TPU v7x, 32 devices: a whole 2x2x4 slice. The times are simulated.
32 devices in a mesh: groups: 2 (over x), gx: 2 (over core), gy: 8 (over z, y).
Axes of the slice: x: 2, y: 2, z: 4, core: 2. Of those that a mesh axis runs over, the one named last changes fastest.
Arguments:
- tokens: bfloat16 [1024, 8192], P(('groups', 'gy'), 'gx'), parts along dimension 0, may hold values from -6 to 6
- gate_weight: bfloat16 [8192, 16384], P('gx', 'gy'), may hold values from -0.0625 to 0.0625
- up_weight: bfloat16 [8192, 16384], P('gx', 'gy'), may hold values from -0.0625 to 0.0625
- down_weight: bfloat16 [16384, 8192], P('gy', 'gx'), may hold values from -0.046875 to 0.046875
Outputs:
- block_out: bfloat16 [1024, 8192], P(('groups', 'gy'), 'gx'), parts along dimension 0
There are 2 independent parts, one for each index of `groups`. A program takes and returns all parts, laid end to end along the dimension named above; an argument that names none is the same for every part. Nothing has to cross between parts.
All inputs are finite; a program needn't handle non-finite values.
Results may differ from a plain program's by a relative error of at most 0.005.
Values may be sent and summed in bfloat16 or wider, within the bound.
No kernel may reach another device: no remote copies, remote signals or barrier semaphores. Data moves between devices by JAX's collectives and lax.ppermute only.
A program may use at most 192 MiB of HBM per device.

v0:
```python
import jax
import jax.numpy as jnp
from jax import lax
from jax.sharding import PartitionSpec as P


def gated(pair):
    return (jax.nn.silu(pair[0]) * pair[1]).astype(jnp.bfloat16)


def shards(tokens, gate_weight, up_weight, down_weight):
    piece = lax.all_gather(tokens, "gy", axis=0, tiled=True)
    first = jnp.dot(piece, gate_weight, preferred_element_type=jnp.float32)
    second = jnp.dot(piece, up_weight, preferred_element_type=jnp.float32)
    partial_value = jnp.stack([first, second])
    summed = lax.psum(partial_value, "gx")
    hidden = gated(summed)
    result = lax.psum_scatter(
        jnp.dot(hidden, down_weight, preferred_element_type=jnp.float32),
        "gy",
        scatter_dimension=0,
        tiled=True,
    )
    return result.astype(jnp.bfloat16)


def solution(mesh):
    return jax.shard_map(
        shards,
        mesh=mesh,
        in_specs=(P(("groups", "gy"), "gx"), P("gx", "gy"), P("gx", "gy"), P("gy", "gx")),
        out_specs=P(("groups", "gy"), "gx"),
        check_vma=False,
    )
```

profile of v0, /device:TPU:0, one launch (start us, length us, event | category | flops | bytes accessed | tf_op | source)
XLA Modules:
  0.0 328.1 jit_solution(15422170795566650534)
XLA Ops:
  6.5 0.0 all-gather.2.cloned.1.call-start
  6.5 0.7 all-gather.2.cloned.1.call-update
  7.3 0.0 all-reduce.2.cloned.1.call-start
  7.3 78.3 %all-gather.2.cloned.1.call-done = bf16[512,4096]{1,0:T(8,128)(2,1)} async-done(((bf16[64,4096]{1,0:T(8,128)(2,1)}), bf16[512,4096]{1,0:T(8,128)(2,1)}) %all-gather.2.cloned.1.call-update) | async-done | bytes 4194320 | tf_op jit(solution)/shard_map/all_gather | solution.py:12
  85.6 0.0 copy-start
  85.6 13.9 %convolution_bitcast_fusion = f32[1,512,2048]{2,1,0:T(8,128)S(1)} fusion(bf16[512,4096]{1,0:T(8,128)(2,1)} %all-gather.2.cloned.1.call-done, bf16[4096,2048]{1,0:T(8,128)(2,1)} %param.6), kind=kOutput, calls=%fused_computation.5 | convolution fusion | flops 8589934592 | bytes 25165824 | tf_op jit(solution)/shard_map/dot_general | solution.py:14
  99.5 0.0 copy-done
  99.5 11.7 %convolution_bitcast_fusion.1 = f32[1,512,2048]{2,1,0:T(8,128)S(1)} fusion(bf16[512,4096]{1,0:T(8,128)(2,1)S(1)} %copy-done, bf16[4096,2048]{1,0:T(8,128)(2,1)} %param.5), kind=kOutput, calls=%fused_computation.6 | convolution fusion | flops 8589934592 | bytes 25165824 | tf_op jit(solution)/shard_map/dot_general | solution.py:13
  111.2 3.8 %pad_maximum_fusion = f32[2,512,2048]{2,1,0:T(8,128)} fusion(f32[1,512,2048]{2,1,0:T(8,128)S(1)} %convolution_bitcast_fusion, f32[1,512,2048]{2,1,0:T(8,128)S(1)} %convolution_bitcast_fusion.1), kind=kLoop, calls=%fused_computation | loop fusion | flops 2097152 | bytes 16777216 | tf_op jit(solution)/shard_map/stack | solution.py:15
  115.0 0.0 all-reduce.2.cloned.1.call-update
  115.0 0.0 reduce-scatter.2.cloned.1.call-start
  115.1 37.2 %all-reduce.2.cloned.1.call-done = f32[2,512,2048]{2,1,0:T(8,128)} async-done(((f32[2,512,2048]{2,1,0:T(8,128)}), f32[2,512,2048]{2,1,0:T(8,128)}) %all-reduce.2.cloned.1.call-update) | async-done | bytes 8388624 | tf_op jit(solution)/shard_map/psum | solution.py:16
  152.3 16.9 %fusion.2 = f32[512,4096]{1,0:T(8,128)} fusion(bf16[2048,4096]{1,0:T(8,128)(2,1)} %param.7, f32[2,512,2048]{2,1,0:T(8,128)} %all-reduce.2.cloned.1.call-done), kind=kOutput, calls=%fused_computation.7 | convolution fusion | flops 8596226048 | bytes 33554432 | tf_op jit(solution)/shard_map/dot_general | solution.py:19
  169.2 0.0 reduce-scatter.2.cloned.1.call-update
  169.2 150.3 %reduce-scatter.2.cloned.1.call-done = f32[64,4096]{1,0:T(8,128)} async-done(((f32[512,4096]{1,0:T(8,128)}), f32[64,4096]{1,0:T(8,128)}) %reduce-scatter.2.cloned.1.call-update) | async-done | bytes 1048592 | tf_op jit(solution)/shard_map/reduce_scatter | solution.py:18
  319.5 2.1 convert_element_type.7
Async XLA Ops:
  6.5 79.1 %all-gather.2.cloned.1.call-start = ((), (), s32[]{:S(2)}) async-start(), calls=%async_computation.1 | async-start | bytes 4718592 | tf_op jit(solution)/shard_map/all_gather | solution.py:12
  7.3 145.0 %all-reduce.2.cloned.1.call-start = ((), (), s32[]{:S(2)}) async-start(), calls=%async_computation.2 | async-start | bytes 16777216 | tf_op jit(solution)/shard_map/psum | solution.py:16
  85.6 13.9 %copy-start = (bf16[512,4096]{1,0:T(8,128)(2,1)S(1)}, bf16[512,4096]{1,0:T(8,128)(2,1)}, u32[]{:S(2)}) copy-start(bf16[512,4096]{1,0:T(8,128)(2,1)} %all-gather.2.cloned.1.call-done) | copy-start | bytes 12582916
  115.0 204.5 %reduce-scatter.2.cloned.1.call-start = ((), (), s32[]{:S(2)}) async-start(), calls=%async_computation.3 | async-start | bytes 9437184 | tf_op jit(solution)/shard_map/reduce_scatter | solution.py:18
Sparse Core Ops, SparseCore 0:
  9.5 76.0 all-gather.1
  115.1 37.1 all-reduce.1
  169.3 150.1 reduce-scatter.1
where the time goes:
time: 328 us
  waiting for transfers between devices  267 us (81%)
  matrix products  42.4 us (13%)
  between operations  13.1 us (4%)
  other arithmetic  5.87 us (2%)
    reduce_scatter x1, waiting for transfers between devices, shards(): lax.psum_scatter(jnp.dot(hidden, down_weight, preferred_element_type=jnp....  150 us
    all_gather x1, waiting for transfers between devices, shards(): piece = lax.all_gather(tokens, 'gy', axis=0, tiled=True)  78.3 us
    psum x1, waiting for transfers between devices, shards(): summed = lax.psum(partial_value, 'gx')  37.2 us
    dot_general x1, matrix products, shards(): jnp.dot(hidden, down_weight, preferred_element_type=jnp.float32)  16.9 us
    dot_general x1, matrix products, shards(): second = jnp.dot(piece, up_weight, preferred_element_type=jnp.float32)  13.9 us
    dot_general x1, matrix products, shards(): first = jnp.dot(piece, gate_weight, preferred_element_type=jnp.float32)  11.7 us
  transfers between devices with their start and end apart: 3, of which 3 were waited for; matrix products, arithmetic and copies ran while one was open for 0% of the time, Pallas kernels for 0%

commit v1 on v0

v1 whole, which is shorter than its diff:
```python
import jax
import jax.numpy as jnp
from jax import lax
from jax.sharding import PartitionSpec as P

F32, BF16 = jnp.float32, jnp.bfloat16


def ring_of(n):
    return list(range(0, n, 2)) + list(range(n - 1, 0, -2))


def make_shards(n):
    ring = ring_of(n)
    half = n // 2
    to_right = [(ring[i], ring[(i + 1) % n]) for i in range(n)]
    to_left = [(ring[(i + 1) % n], ring[i]) for i in range(n)]
    swap = [(0, 1), (1, 0)]

    def right(x):
        return lax.ppermute(x, "gy", to_right)

    def left(x):
        return lax.ppermute(x, "gy", to_left)

    def other(x):
        return lax.ppermute(x, "gx", swap)

    def shards(tokens, gate_weight, up_weight, down_weight):
        rows = tokens.shape[0]
        cut = rows // 2
        core = lax.axis_index("gx")
        first = core == 0

        blocks = [[tokens]]
        r = l = tokens
        for d in range(1, half):
            r, l = right(r), left(l)
            blocks.append([r, l])
        blocks.append([right(r[:cut]), left(l[cut:])])

        spans = [[0, 1]] + [[d] for d in range(2, half - 1)] + [[half - 1, half]]
        partial = {}
        for span in spans:
            x = jnp.concatenate([b for d in span for b in blocks[d]], axis=0)
            g = jnp.dot(x, gate_weight, preferred_element_type=F32)
            u = jnp.dot(x, up_weight, preferred_element_type=F32)
            w = g.shape[1] // 2
            low = jnp.stack([g[:, :w], u[:, :w]])
            high = jnp.stack([g[:, w:], u[:, w:]])
            mine = jnp.where(first, low, high)
            got = other(jnp.where(first, high, low))
            both = mine + got
            h = (jax.nn.silu(both[0]) * both[1]).astype(BF16)
            o = other(h)
            hidden = jnp.concatenate(
                [jnp.where(first, h, o), jnp.where(first, o, h)], axis=1
            )
            out = jnp.dot(hidden, down_weight, preferred_element_type=F32)
            at = 0
            for d in span:
                pieces = []
                for b in blocks[d]:
                    pieces.append(out[at : at + b.shape[0]])
                    at += b.shape[0]
                partial[d] = pieces

        back_l, back_r = partial[half]
        l = left(back_l.astype(BF16))
        r = right(back_r.astype(BF16))
        for d in range(half - 1, 0, -1):
            pl_, pr_ = partial[d]
            if d == half - 1:
                sl = jnp.concatenate([pl_[:cut] + l.astype(F32), pl_[cut:]], axis=0)
                sr = jnp.concatenate([pr_[:cut], pr_[cut:] + r.astype(F32)], axis=0)
            else:
                sl = pl_ + l.astype(F32)
                sr = pr_ + r.astype(F32)
            l, r = left(sl.astype(BF16)), right(sr.astype(BF16))
        total = partial[0][0] + l.astype(F32) + r.astype(F32)
        return total.astype(BF16)

    return shards


def solution(mesh):
    return jax.shard_map(
        make_shards(mesh.shape["gy"]),
        mesh=mesh,
        in_specs=(P(("groups", "gy"), "gx"), P("gx", "gy"), P("gx", "gy"), P("gy", "gx")),
        out_specs=P(("groups", "gy"), "gx"),
        check_vma=False,
    )
```

time: 328 us -> 126 us (0.38)
  waiting for transfers between devices: 267 us -> 52.2 us
  starting transfers between devices: 0.08 us -> 18.8 us
  between operations: 13.1 us -> 0.51 us
  local copies, waits for them, and re-layouts: 0.01 us -> 5.51 us
    reduce_scatter x1 -> x0, waiting for transfers between devices: 150 us -> none  [shards(): lax.psum_scatter(jnp.dot(hidden, down_weight, preferred_element_type=jnp....]
    all_gather x1 -> x0, waiting for transfers between devices: 78.3 us -> none  [shards(): piece = lax.all_gather(tokens, 'gy', axis=0, tiled=True)]
    ppermute x0 -> x22, waiting for transfers between devices: none -> 52.2 us  [the longest x8 27.5 us: right(): return lax.ppermute(x, 'gy', to_right)]
    psum x1 -> x0, waiting for transfers between devices: 37.2 us -> none  [shards(): summed = lax.psum(partial_value, 'gx')]
    ppermute x0 -> x22, starting transfers between devices: none -> 18.8 us  [the longest x8 14.5 us: right(): return lax.ppermute(x, 'gy', to_right)]
    unnamed x2 -> x30, local copies, waits for them, and re-layouts: 0.01 us -> 4.45 us
    another operation x1, other arithmetic: 3.8 us -> 0.09 us  [shards(): partial_value = jnp.stack([first, second])]
    dot_general x3 -> x9, matrix products: 42.4 us -> 43.2 us  [the longest x3 19.8 us: shards(): u = jnp.dot(x, up_weight, preferred_element_type=F32)]
  transfers between devices with their start and end apart: 3 -> 22, of which waited for: 3 -> 14; matrix products, arithmetic and copies ran while one was open for 0% -> 37% of each run, Pallas kernels for 0% -> 0%
where the time goes in v1:
time: 126 us; the launch traced here: 125 us
  waiting for transfers between devices  52.2 us (41%)
  matrix products  43.2 us (34%)
  starting transfers between devices  18.8 us (15%)
  local copies, waits for them, and re-layouts  5.51 us (4%)
  other arithmetic  5.19 us (4%)
    ppermute x8, waiting for transfers between devices, right(): return lax.ppermute(x, 'gy', to_right)  27.5 us
    ppermute x8, waiting for transfers between devices, left(): return lax.ppermute(x, 'gy', to_left)  23.1 us
    dot_general x3, matrix products, shards(): u = jnp.dot(x, up_weight, preferred_element_type=F32)  19.8 us
    ppermute x8, starting transfers between devices, right(): return lax.ppermute(x, 'gy', to_right)  14.5 us
    dot_general x3, matrix products, shards(): g = jnp.dot(x, gate_weight, preferred_element_type=F32)  13.8 us
    dot_general x3, matrix products, shards(): out = jnp.dot(hidden, down_weight, preferred_element_type=F32)  9.62 us
    unnamed x30, local copies, waits for them, and re-layouts  4.45 us
    ppermute x8, starting transfers between devices, left(): return lax.ppermute(x, 'gy', to_left)  3.38 us
  transfers between devices with their start and end apart: 22, of which 14 were waited for; matrix products, arithmetic and copies ran while one was open for 37% of the time, Pallas kernels for 0%

profile of v1, /device:TPU:0, one launch (start us, length us, event | category | flops | bytes accessed | tf_op | source)
XLA Modules:
  0.0 125.4 jit_solution(4665233926565482372)
XLA Ops:
  0.0 3.0 %collective-permute-start = (bf16[64,4096]{1,0:T(8,128)(2,1)}, bf16[64,4096]{1,0:T(8,128)(2,1)S(1)}, u32[]{:S(2)}, u32[]{:S(2)}) collective-permute-start(bf16[64,4096]{1,0:T(8,128)(2,1)} %param.4), channel_id=1, source_target_pairs={{0,2},{2,4},{4,6},{6,7},{7,5},{5,3},{3,1},{1,0},{8,10},{10,12},{12... | collective-permute-start | bytes 1572872 | tf_op jit(solution)/shard_map/ppermute | solution.py:21
  3.0 1.1 constant_dynamic-update-slice_fusion.2
  4.2 10.9 %collective-permute-done = bf16[64,4096]{1,0:T(8,128)(2,1)S(1)} collective-permute-done((bf16[64,4096]{1,0:T(8,128)(2,1)}, bf16[64,4096]{1,0:T(8,128)(2,1)S(1)}, u32[]{:S(2)}, u32[]{:S(2)}) %collective-permute-start) | collective-permute-done | bytes 524320 | tf_op jit(solution)/shard_map/ppermute | solution.py:21
  15.1 1.8 %collective-permute-start.4 = (bf16[64,4096]{1,0:T(8,128)(2,1)S(1)}, bf16[64,4096]{1,0:T(8,128)(2,1)S(1)}, u32[]{:S(2)}, u32[]{:S(2)}) collective-permute-start(bf16[64,4096]{1,0:T(8,128)(2,1)S(1)} %collective-permute-done), channel_id=1, source_target_pairs={{0,2},{2,4},{4,6},{6,7},{7,5},{5,3},{3,1},{1,0},{8,10},{10,12},{12... | collective-permute-start | bytes 1572872 | tf_op jit(solution)/shard_map/ppermute | solution.py:21
  17.3 7.8 %fusion.34 = f32[192,2048]{1,0:T(8,128)S(1)} fusion(bf16[192,4096]{1,0:T(8,128)(2,1)S(1)} %constant_dynamic-update-slice_fusion, bf16[4096,2048]{1,0:T(8,128)(2,1)} %param.5), kind=kOutput, calls=%fused_computation.85 | convolution fusion | flops 3221225472 | bytes 19922944 | tf_op jit(solution)/shard_map/dot_general | solution.py:46
  25.1 3.1 %collective-permute-done.4 = bf16[64,4096]{1,0:T(8,128)(2,1)S(1)} collective-permute-done((bf16[64,4096]{1,0:T(8,128)(2,1)S(1)}, bf16[64,4096]{1,0:T(8,128)(2,1)S(1)}, u32[]{:S(2)}, u32[]{:S(2)}) %collective-permute-start.4) | collective-permute-done | bytes 524320 | tf_op jit(solution)/shard_map/ppermute | solution.py:21
  28.2 1.2 collective-permute-done.5
  29.5 2.4 %fusion.36 = f32[128,2048]{1,0:T(8,128)S(1)} fusion(bf16[128,4096]{1,0:T(8,128)(2,1)S(1)} %constant_dynamic-update-slice_fusion.3, bf16[4096,2048]{1,0:T(8,128)(2,1)S(1)} %bitcast.82), kind=kOutput, calls=%fused_computation.87 | convolution fusion | flops 2147483648 | bytes 18874368 | tf_op jit(solution)/shard_map/dot_general | solution.py:46
  31.9 1.6 %collective-permute-start.8 = (bf16[64,4096]{1,0:T(8,128)(2,1)S(1)}, bf16[64,4096]{1,0:T(8,128)(2,1)S(1)}, u32[]{:S(2)}, u32[]{:S(2)}) collective-permute-start(bf16[64,4096]{1,0:T(8,128)(2,1)S(1)} %collective-permute-done.4), channel_id=1, source_target_pairs={{0,2},{2,4},{4,6},{6,7},{7,5},{5,3},{3,1},{1,0},{8,10},{10,12},{12... | collective-permute-start | bytes 1572872 | tf_op jit(solution)/shard_map/ppermute | solution.py:21
  33.5 0.5 collective-permute-start.9
  34.0 8.2 %fusion.37 = f32[128,2048]{1,0:T(8,128)S(1)} fusion(bf16[128,4096]{1,0:T(8,128)(2,1)S(1)} %constant_dynamic-update-slice_fusion.3, bf16[4096,2048]{1,0:T(8,128)(2,1)} %param.6), kind=kOutput, calls=%fused_computation.88 | convolution fusion | flops 2147483648 | bytes 18874368 | tf_op jit(solution)/shard_map/dot_general | solution.py:47
  42.7 0.9 collective-permute-done.8
  43.6 1.6 %collective-permute-start.10 = (bf16[32,4096]{1,0:T(8,128)(2,1)S(1)}, bf16[32,4096]{1,0:T(8,128)(2,1)S(1)}, u32[]{:S(2)}, u32[]{:S(2)}) collective-permute-start(bf16[32,4096]{1,0:T(8,128)(2,1)S(1)} %slice.149), channel_id=1, source_target_pairs={{0,2},{2,4},{4,6},{6,7},{7,5},{5,3},{3,1},{1,0},{8,10},{10,12},{12... | collective-permute-start | bytes 786440 | tf_op jit(solution)/shard_map/ppermute | solution.py:21
  45.2 0.5 collective-permute-start.11
  45.8 5.6 %collective-permute-done.10 = bf16[32,4096]{1,0:T(8,128)(2,1)S(1)} collective-permute-done((bf16[32,4096]{1,0:T(8,128)(2,1)S(1)}, bf16[32,4096]{1,0:T(8,128)(2,1)S(1)}, u32[]{:S(2)}, u32[]{:S(2)}) %collective-permute-start.10) | collective-permute-done | bytes 262176 | tf_op jit(solution)/shard_map/ppermute | solution.py:21
  51.5 1.4 %collective-permute-done.11 = bf16[32,4096]{1,0:T(8,128)(2,1)S(1)} collective-permute-done((bf16[32,4096]{1,0:T(8,128)(2,1)S(1)}, bf16[32,4096]{1,0:T(8,128)(2,1)S(1)}, u32[]{:S(2)}, u32[]{:S(2)}) %collective-permute-start.11) | collective-permute-done | bytes 262176 | tf_op jit(solution)/shard_map/ppermute | solution.py:24
  52.8 3.6 %fusion.38 = f32[192,2048]{1,0:T(8,128)S(1)} fusion(bf16[192,4096]{1,0:T(8,128)(2,1)S(1)} %constant_dynamic-update-slice_fusion.5, bf16[4096,2048]{1,0:T(8,128)(2,1)S(1)} %bitcast.82), kind=kOutput, calls=%fused_computation.89 | convolution fusion | flops 3221225472 | bytes 19922944 | tf_op jit(solution)/shard_map/dot_general | solution.py:46
  56.5 8.0 %fusion.39 = f32[192,2048]{1,0:T(8,128)S(1)} fusion(bf16[192,4096]{1,0:T(8,128)(2,1)S(1)} %constant_dynamic-update-slice_fusion.5, bf16[4096,2048]{1,0:T(8,128)(2,1)} %param.6), kind=kOutput, calls=%fused_computation.90 | convolution fusion | flops 3221225472 | bytes 19922944 | tf_op jit(solution)/shard_map/dot_general | solution.py:47
  64.5 0.4 slice_bitcast_fusion.4
  65.3 0.6 slice-done.6
  65.9 1.4 %slice-done.7 = s8[4194304]{0:T(1024)(128)(4,1)S(1)} async-done(((s8[16777216]{0:T(1024)(128)(4,1)}), s8[4194304]{0:T(1024)(128)(4,1)S(1)}, s32[]{:S(2)}) %slice-start.7) | async-done | bytes 4194328
  67.3 3.6 %fusion.35 = f32[192,2048]{1,0:T(8,128)S(1)} fusion(bf16[192,4096]{1,0:T(8,128)(2,1)S(1)} %constant_dynamic-update-slice_fusion, bf16[4096,2048]{1,0:T(8,128)(2,1)S(1)} %bitcast.84), kind=kOutput, calls=%fused_computation.86 | convolution fusion | flops 3221225472 | bytes 19922944 | tf_op jit(solution)/shard_map/dot_general | solution.py:47
  71.2 0.4 fusion.1
  71.7 0.3 select_add_fusion.2
  72.0 0.5 select_add_fusion
  72.8 0.6 collective-permute-start.13
  73.6 1.5 %collective-permute-done.2 = f32[2,192,1024]{2,1,0:T(8,128)S(1)} collective-permute-done((f32[2,192,1024]{2,1,0:T(8,128)S(1)}, f32[2,192,1024]{2,1,0:T(8,128)S(1)}, u32[]{:S(2)}, u32[]{:S(2)}) %collective-permute-start.2) | collective-permute-done | bytes 1572896 | tf_op jit(solution)/shard_map/ppermute | solution.py:27
  75.1 0.5 select_add_fusion.1
  75.6 0.3 broadcast_select_fusion.1
  76.0 1.1 slice-done.11
  77.1 3.6 %fusion.33 = (bf16[192,4096]{1,0:T(8,128)(2,1)S(1)}, f32[192,4096]{1,0:T(8,128)S(1)}) fusion(bf16[2048,4096]{1,0:T(8,128)(2,1)S(1)} %bitcast.86, bf16[192,1024]{1,0:T(8,128)(2,1)S(1)} %get-tuple-element.28, bf16[192,1024]{1,0:T(8,128)(2,1)S(1)} %get-tuple-element.27), kind=kOutput, calls=%fused_computation.84 | convolution fusion | flops 3223584768 | bytes 22282240 | tf_op jit(solution)/shard_map/dot_general | solution.py:59
  80.8 0.5 collective-permute-start.14
  81.3 1.6 %collective-permute-start.18 = (bf16[32,4096]{1,0:T(8,128)(2,1)S(1)}, bf16[32,4096]{1,0:T(8,128)(2,1)S(1)}, u32[]{:S(2)}, u32[]{:S(2)}) collective-permute-start(bf16[32,4096]{1,0:T(8,128)(2,1)S(1)} %get-tuple-element.12), channel_id=1, source_target_pairs={{0,2},{2,4},{4,6},{6,7},{7,5},{5,3},{3,1},{1,0},{8,10},{10,12},{12... | collective-permute-start | bytes 786440 | tf_op jit(solution)/shard_map/ppermute | solution.py:21
  83.4 4.7 %collective-permute-done.14 = bf16[32,4096]{1,0:T(8,128)(2,1)S(1)} collective-permute-done((bf16[32,4096]{1,0:T(8,128)(2,1)S(1)}, bf16[32,4096]{1,0:T(8,128)(2,1)S(1)}, u32[]{:S(2)}, u32[]{:S(2)}) %collective-permute-start.14) | collective-permute-done | bytes 262176 | tf_op jit(solution)/shard_map/ppermute | solution.py:24
  88.4 1.6 %collective-permute-start.19 = (bf16[64,4096]{1,0:T(8,128)(2,1)S(1)}, bf16[64,4096]{1,0:T(8,128)(2,1)S(1)}, u32[]{:S(2)}, u32[]{:S(2)}) collective-permute-start(bf16[64,4096]{1,0:T(8,128)(2,1)S(1)} %pad_maximum_fusion.7), channel_id=1, source_target_pairs={{0,2},{2,4},{4,6},{6,7},{7,5},{5,3},{3,1},{1,0},{8,10},{10,12},{12... | collective-permute-start | bytes 1572872 | tf_op jit(solution)/shard_map/ppermute | solution.py:21
  90.1 0.7 collective-permute-start.15
  90.8 2.4 %fusion.25 = f32[128,4096]{1,0:T(8,128)S(1)} fusion(bf16[2048,4096]{1,0:T(8,128)(2,1)S(1)} %bitcast.86, bf16[128,1024]{1,0:T(8,128)(2,1)S(1)} %get-tuple-element.32, bf16[128,1024]{1,0:T(8,128)(2,1)S(1)} %get-tuple-element.31), kind=kOutput, calls=%fused_computation.59 | convolution fusion | flops 2148532224 | bytes 19398656 | tf_op jit(solution)/shard_map/dot_general | solution.py:59
  93.3 0.3 broadcast_select_fusion.3
  93.6 6.7 %collective-permute-done.19 = bf16[64,4096]{1,0:T(8,128)(2,1)S(1)} collective-permute-done((bf16[64,4096]{1,0:T(8,128)(2,1)S(1)}, bf16[64,4096]{1,0:T(8,128)(2,1)S(1)}, u32[]{:S(2)}, u32[]{:S(2)}) %collective-permute-start.19) | collective-permute-done | bytes 524320 | tf_op jit(solution)/shard_map/ppermute | solution.py:21
  100.3 1.9 %collective-permute-done.15 = bf16[64,4096]{1,0:T(8,128)(2,1)S(1)} collective-permute-done((bf16[64,4096]{1,0:T(8,128)(2,1)S(1)}, bf16[64,4096]{1,0:T(8,128)(2,1)S(1)}, u32[]{:S(2)}, u32[]{:S(2)}) %collective-permute-start.15) | collective-permute-done | bytes 524320 | tf_op jit(solution)/shard_map/ppermute | solution.py:24
  102.4 0.5 collective-permute-start.16
  102.9 1.6 %collective-permute-start.20 = (bf16[64,4096]{1,0:T(8,128)(2,1)S(1)}, bf16[64,4096]{1,0:T(8,128)(2,1)S(1)}, u32[]{:S(2)}, u32[]{:S(2)}) collective-permute-start(bf16[64,4096]{1,0:T(8,128)(2,1)S(1)} %get-tuple-element.10), channel_id=1, source_target_pairs={{0,2},{2,4},{4,6},{6,7},{7,5},{5,3},{3,1},{1,0},{8,10},{10,12},{12... | collective-permute-start | bytes 1572872 | tf_op jit(solution)/shard_map/ppermute | solution.py:21
  104.5 3.6 %fusion.13 = f32[192,4096]{1,0:T(8,128)S(1)} fusion(bf16[2048,4096]{1,0:T(8,128)(2,1)S(1)} %bitcast.86, bf16[192,1024]{1,0:T(8,128)(2,1)S(1)} %get-tuple-element.30, bf16[192,1024]{1,0:T(8,128)(2,1)S(1)} %get-tuple-element.29), kind=kOutput, calls=%fused_computation.39 | convolution fusion | flops 3222798336 | bytes 20709376 | tf_op jit(solution)/shard_map/dot_general | solution.py:59
  108.1 6.2 %collective-permute-done.16 = bf16[64,4096]{1,0:T(8,128)(2,1)S(1)} collective-permute-done((bf16[64,4096]{1,0:T(8,128)(2,1)S(1)}, bf16[64,4096]{1,0:T(8,128)(2,1)S(1)}, u32[]{:S(2)}, u32[]{:S(2)}) %collective-permute-start.16) | collective-permute-done | bytes 524320 | tf_op jit(solution)/shard_map/ppermute | solution.py:24
  114.5 0.5 collective-permute-start.17
  115.0 1.6 %collective-permute-start.21 = (bf16[64,4096]{1,0:T(8,128)(2,1)S(1)}, bf16[64,4096]{1,0:T(8,128)(2,1)S(1)}, u32[]{:S(2)}, u32[]{:S(2)}) collective-permute-start(bf16[64,4096]{1,0:T(8,128)(2,1)S(1)} %get-tuple-element.6), channel_id=1, source_target_pairs={{0,2},{2,4},{4,6},{6,7},{7,5},{5,3},{3,1},{1,0},{8,10},{10,12},{12... | collective-permute-start | bytes 1572872 | tf_op jit(solution)/shard_map/ppermute | solution.py:21
  116.6 7.8 %collective-permute-done.17 = bf16[64,4096]{1,0:T(8,128)(2,1)S(1)} collective-permute-done((bf16[64,4096]{1,0:T(8,128)(2,1)S(1)}, bf16[64,4096]{1,0:T(8,128)(2,1)S(1)}, u32[]{:S(2)}, u32[]{:S(2)}) %collective-permute-start.17) | collective-permute-done | bytes 524320 | tf_op jit(solution)/shard_map/ppermute | solution.py:24
  124.4 1.0 fusion.7
  (65 shorter events, 3.6 us)
Async XLA Ops:
  0.0 15.1 %collective-permute-start = (bf16[64,4096]{1,0:T(8,128)(2,1)}, bf16[64,4096]{1,0:T(8,128)(2,1)S(1)}, u32[]{:S(2)}, u32[]{:S(2)}) collective-permute-start(bf16[64,4096]{1,0:T(8,128)(2,1)} %param.4), channel_id=1, source_target_pairs={{0,2},{2,4},{4,6},{6,7},{7,5},{5,3},{3,1},{1,0},{8,10},{10,12},{12... | collective-permute-start | bytes 1572872 | tf_op jit(solution)/shard_map/ppermute | solution.py:21
  3.0 13.9 %collective-permute-start.1 = (bf16[64,4096]{1,0:T(8,128)(2,1)}, bf16[64,4096]{1,0:T(8,128)(2,1)S(1)}, u32[]{:S(2)}, u32[]{:S(2)}) collective-permute-start(bf16[64,4096]{1,0:T(8,128)(2,1)} %param.4), channel_id=1, source_target_pairs={{2,0},{4,2},{6,4},{7,6},{5,7},{3,5},{1,3},{0,1},{10,8},{12,10},{14... | collective-permute-start | bytes 1572872 | tf_op jit(solution)/shard_map/ppermute | solution.py:24
  15.1 13.1 %collective-permute-start.4 = (bf16[64,4096]{1,0:T(8,128)(2,1)S(1)}, bf16[64,4096]{1,0:T(8,128)(2,1)S(1)}, u32[]{:S(2)}, u32[]{:S(2)}) collective-permute-start(bf16[64,4096]{1,0:T(8,128)(2,1)S(1)} %collective-permute-done), channel_id=1, source_target_pairs={{0,2},{2,4},{4,6},{6,7},{7,5},{5,3},{3,1},{1,0},{8,10},{10,12},{12... | collective-permute-start | bytes 1572872 | tf_op jit(solution)/shard_map/ppermute | solution.py:21
  16.9 12.5 %collective-permute-start.5 = (bf16[64,4096]{1,0:T(8,128)(2,1)S(1)}, bf16[64,4096]{1,0:T(8,128)(2,1)S(1)}, u32[]{:S(2)}, u32[]{:S(2)}) collective-permute-start(bf16[64,4096]{1,0:T(8,128)(2,1)S(1)} %collective-permute-done.1), channel_id=1, source_target_pairs={{2,0},{4,2},{6,4},{7,6},{5,7},{3,5},{1,3},{0,1},{10,8},{12,10},{14... | collective-permute-start | bytes 1572872 | tf_op jit(solution)/shard_map/ppermute | solution.py:24
  17.2 12.3 %slice-start = ((s8[16777216]{0:T(1024)(128)(4,1)}), s8[4194304]{0:T(1024)(128)(4,1)S(1)}, s32[]{:S(2)}) async-start(s8[16777216]{0:T(1024)(128)(4,1)} %bitcast.81), calls=%async_computation | async-start | bytes 8388608
  17.2 12.2 %slice-start.1 = ((s8[16777216]{0:T(1024)(128)(4,1)}), s8[4194304]{0:T(1024)(128)(4,1)S(1)}, s32[]{:S(2)}) async-start(s8[16777216]{0:T(1024)(128)(4,1)} %bitcast.81), calls=%async_computation.1 | async-start | bytes 8388608
  17.2 12.2 %slice-start.2 = ((s8[16777216]{0:T(1024)(128)(4,1)}), s8[4194304]{0:T(1024)(128)(4,1)S(1)}, s32[]{:S(2)}) async-start(s8[16777216]{0:T(1024)(128)(4,1)} %bitcast.81), calls=%async_computation.2 | async-start | bytes 8388608
  17.3 12.2 %slice-start.3 = ((s8[16777216]{0:T(1024)(128)(4,1)}), s8[4194304]{0:T(1024)(128)(4,1)S(1)}, s32[]{:S(2)}) async-start(s8[16777216]{0:T(1024)(128)(4,1)} %bitcast.81), calls=%async_computation.3 | async-start | bytes 8388608
  31.9 11.6 %collective-permute-start.8 = (bf16[64,4096]{1,0:T(8,128)(2,1)S(1)}, bf16[64,4096]{1,0:T(8,128)(2,1)S(1)}, u32[]{:S(2)}, u32[]{:S(2)}) collective-permute-start(bf16[64,4096]{1,0:T(8,128)(2,1)S(1)} %collective-permute-done.4), channel_id=1, source_target_pairs={{0,2},{2,4},{4,6},{6,7},{7,5},{5,3},{3,1},{1,0},{8,10},{10,12},{12... | collective-permute-start | bytes 1572872 | tf_op jit(solution)/shard_map/ppermute | solution.py:21
  33.5 11.7 %collective-permute-start.9 = (bf16[64,4096]{1,0:T(8,128)(2,1)S(1)}, bf16[64,4096]{1,0:T(8,128)(2,1)S(1)}, u32[]{:S(2)}, u32[]{:S(2)}) collective-permute-start(bf16[64,4096]{1,0:T(8,128)(2,1)S(1)} %collective-permute-done.5), channel_id=1, source_target_pairs={{2,0},{4,2},{6,4},{7,6},{5,7},{3,5},{1,3},{0,1},{10,8},{12,10},{14... | collective-permute-start | bytes 1572872 | tf_op jit(solution)/shard_map/ppermute | solution.py:24
  42.6 29.1 %collective-permute-start.6 = (f32[2,128,1024]{2,1,0:T(8,128)S(1)}, f32[2,128,1024]{2,1,0:T(8,128)S(1)}, u32[]{:S(2)}, u32[]{:S(2)}) collective-permute-start(f32[2,128,1024]{2,1,0:T(8,128)S(1)} %fusion.8), channel_id=1, source_target_pairs={{0,8},{8,0},{1,9},{9,1},{2,10},{10,2},{3,11},{11,3},{4,12},{12,4},... | collective-permute-start | bytes 3145736 | tf_op jit(solution)/shard_map/ppermute | solution.py:27
  43.6 7.9 %collective-permute-start.10 = (bf16[32,4096]{1,0:T(8,128)(2,1)S(1)}, bf16[32,4096]{1,0:T(8,128)(2,1)S(1)}, u32[]{:S(2)}, u32[]{:S(2)}) collective-permute-start(bf16[32,4096]{1,0:T(8,128)(2,1)S(1)} %slice.149), channel_id=1, source_target_pairs={{0,2},{2,4},{4,6},{6,7},{7,5},{5,3},{3,1},{1,0},{8,10},{10,12},{12... | collective-permute-start | bytes 786440 | tf_op jit(solution)/shard_map/ppermute | solution.py:21
  45.2 7.6 %collective-permute-start.11 = (bf16[32,4096]{1,0:T(8,128)(2,1)S(1)}, bf16[32,4096]{1,0:T(8,128)(2,1)S(1)}, u32[]{:S(2)}, u32[]{:S(2)}) collective-permute-start(bf16[32,4096]{1,0:T(8,128)(2,1)S(1)} %slice.150), channel_id=1, source_target_pairs={{2,0},{4,2},{6,4},{7,6},{5,7},{3,5},{1,3},{0,1},{10,8},{12,10},{14... | collective-permute-start | bytes 786440 | tf_op jit(solution)/shard_map/ppermute | solution.py:24
  56.5 8.8 %slice-start.4 = ((s8[16777216]{0:T(1024)(128)(4,1)}), s8[4194304]{0:T(1024)(128)(4,1)S(1)}, s32[]{:S(2)}) async-start(s8[16777216]{0:T(1024)(128)(4,1)} %bitcast.83), calls=%async_computation.4 | async-start | bytes 8388608
  56.5 8.8 %slice-start.5 = ((s8[16777216]{0:T(1024)(128)(4,1)}), s8[4194304]{0:T(1024)(128)(4,1)S(1)}, s32[]{:S(2)}) async-start(s8[16777216]{0:T(1024)(128)(4,1)} %bitcast.83), calls=%async_computation.5 | async-start | bytes 8388608
  56.5 9.4 %slice-start.6 = ((s8[16777216]{0:T(1024)(128)(4,1)}), s8[4194304]{0:T(1024)(128)(4,1)S(1)}, s32[]{:S(2)}) async-start(s8[16777216]{0:T(1024)(128)(4,1)} %bitcast.83), calls=%async_computation.6 | async-start | bytes 8388608
  64.5 2.8 %slice-start.7 = ((s8[16777216]{0:T(1024)(128)(4,1)}), s8[4194304]{0:T(1024)(128)(4,1)S(1)}, s32[]{:S(2)}) async-start(s8[16777216]{0:T(1024)(128)(4,1)} %bitcast.83), calls=%async_computation.7 | async-start | bytes 8388608
  65.2 6.8 %collective-permute-start.12 = (f32[2,192,1024]{2,1,0:T(8,128)S(1)}, f32[2,192,1024]{2,1,0:T(8,128)S(1)}, u32[]{:S(2)}, u32[]{:S(2)}) collective-permute-start(f32[2,192,1024]{2,1,0:T(8,128)S(1)} %fusion), channel_id=1, source_target_pairs={{0,8},{8,0},{1,9},{9,1},{2,10},{10,2},{3,11},{11,3},{4,12},{12,4},... | collective-permute-start | bytes 4718600 | tf_op jit(solution)/shard_map/ppermute | solution.py:27
  71.0 5.0 %slice-start.8 = ((s8[16777216]{0:T(1024)(128)(4,1)}), s8[4194304]{0:T(1024)(128)(4,1)S(1)}, s32[]{:S(2)}) async-start(s8[16777216]{0:T(1024)(128)(4,1)} %bitcast.85), calls=%async_computation.8 | async-start | bytes 8388608
  71.2 4.8 %slice-start.9 = ((s8[16777216]{0:T(1024)(128)(4,1)}), s8[4194304]{0:T(1024)(128)(4,1)S(1)}, s32[]{:S(2)}) async-start(s8[16777216]{0:T(1024)(128)(4,1)} %bitcast.85), calls=%async_computation.9 | async-start | bytes 8388608
  71.6 3.5 %collective-permute-start.2 = (f32[2,192,1024]{2,1,0:T(8,128)S(1)}, f32[2,192,1024]{2,1,0:T(8,128)S(1)}, u32[]{:S(2)}, u32[]{:S(2)}) collective-permute-start(f32[2,192,1024]{2,1,0:T(8,128)S(1)} %fusion.1), channel_id=1, source_target_pairs={{0,8},{8,0},{1,9},{9,1},{2,10},{10,2},{3,11},{11,3},{4,12},{12,4},... | collective-permute-start | bytes 4718600 | tf_op jit(solution)/shard_map/ppermute | solution.py:27
  72.0 4.0 %slice-start.10 = ((s8[16777216]{0:T(1024)(128)(4,1)}), s8[4194304]{0:T(1024)(128)(4,1)S(1)}, s32[]{:S(2)}) async-start(s8[16777216]{0:T(1024)(128)(4,1)} %bitcast.85), calls=%async_computation.10 | async-start | bytes 8388608
  72.8 2.9 %collective-permute-start.13 = (bf16[192,1024]{1,0:T(8,128)(2,1)S(1)}, bf16[192,1024]{1,0:T(8,128)(2,1)S(1)}, u32[]{:S(2)}, u32[]{:S(2)}) collective-permute-start(bf16[192,1024]{1,0:T(8,128)(2,1)S(1)} %fusion.10), channel_id=1, source_target_pairs={{0,8},{8,0},{1,9},{9,1},{2,10},{10,2},{3,11},{11,3},{4,12},{12,4},... | collective-permute-start | bytes 1179656 | tf_op jit(solution)/shard_map/ppermute | solution.py:27
  73.5 3.6 %slice-start.11 = ((s8[16777216]{0:T(1024)(128)(4,1)}), s8[4194304]{0:T(1024)(128)(4,1)S(1)}, s32[]{:S(2)}) async-start(s8[16777216]{0:T(1024)(128)(4,1)} %bitcast.85), calls=%async_computation.11 | async-start | bytes 8388608
  73.5 9.7 %collective-permute-start.7 = (bf16[128,1024]{1,0:T(8,128)(2,1)S(1)}, bf16[128,1024]{1,0:T(8,128)(2,1)S(1)}, u32[]{:S(2)}, u32[]{:S(2)}) collective-permute-start(bf16[128,1024]{1,0:T(8,128)(2,1)S(1)} %fusion.24), channel_id=1, source_target_pairs={{0,8},{8,0},{1,9},{9,1},{2,10},{10,2},{3,11},{11,3},{4,12},{12,4},... | collective-permute-start | bytes 786440 | tf_op jit(solution)/shard_map/ppermute | solution.py:27
  80.8 7.4 %collective-permute-start.14 = (bf16[32,4096]{1,0:T(8,128)(2,1)S(1)}, bf16[32,4096]{1,0:T(8,128)(2,1)S(1)}, u32[]{:S(2)}, u32[]{:S(2)}) collective-permute-start(bf16[32,4096]{1,0:T(8,128)(2,1)S(1)} %get-tuple-element.11), channel_id=1, source_target_pairs={{2,0},{4,2},{6,4},{7,6},{5,7},{3,5},{1,3},{0,1},{10,8},{12,10},{14... | collective-permute-start | bytes 786440 | tf_op jit(solution)/shard_map/ppermute | solution.py:24
  81.3 7.0 %collective-permute-start.18 = (bf16[32,4096]{1,0:T(8,128)(2,1)S(1)}, bf16[32,4096]{1,0:T(8,128)(2,1)S(1)}, u32[]{:S(2)}, u32[]{:S(2)}) collective-permute-start(bf16[32,4096]{1,0:T(8,128)(2,1)S(1)} %get-tuple-element.12), channel_id=1, source_target_pairs={{0,2},{2,4},{4,6},{6,7},{7,5},{5,3},{3,1},{1,0},{8,10},{10,12},{12... | collective-permute-start | bytes 786440 | tf_op jit(solution)/shard_map/ppermute | solution.py:21
  83.1 10.2 %collective-permute-start.3 = (bf16[192,1024]{1,0:T(8,128)(2,1)S(1)}, bf16[192,1024]{1,0:T(8,128)(2,1)S(1)}, u32[]{:S(2)}, u32[]{:S(2)}) collective-permute-start(bf16[192,1024]{1,0:T(8,128)(2,1)S(1)} %fusion.12), channel_id=1, source_target_pairs={{0,8},{8,0},{1,9},{9,1},{2,10},{10,2},{3,11},{11,3},{4,12},{12,4},... | collective-permute-start | bytes 1179656 | tf_op jit(solution)/shard_map/ppermute | solution.py:27
  88.4 11.9 %collective-permute-start.19 = (bf16[64,4096]{1,0:T(8,128)(2,1)S(1)}, bf16[64,4096]{1,0:T(8,128)(2,1)S(1)}, u32[]{:S(2)}, u32[]{:S(2)}) collective-permute-start(bf16[64,4096]{1,0:T(8,128)(2,1)S(1)} %pad_maximum_fusion.7), channel_id=1, source_target_pairs={{0,2},{2,4},{4,6},{6,7},{7,5},{5,3},{3,1},{1,0},{8,10},{10,12},{12... | collective-permute-start | bytes 1572872 | tf_op jit(solution)/shard_map/ppermute | solution.py:21
  90.1 12.1 %collective-permute-start.15 = (bf16[64,4096]{1,0:T(8,128)(2,1)S(1)}, bf16[64,4096]{1,0:T(8,128)(2,1)S(1)}, u32[]{:S(2)}, u32[]{:S(2)}) collective-permute-start(bf16[64,4096]{1,0:T(8,128)(2,1)S(1)} %pad_maximum_fusion.6), channel_id=1, source_target_pairs={{2,0},{4,2},{6,4},{7,6},{5,7},{3,5},{1,3},{0,1},{10,8},{12,10},{14... | collective-permute-start | bytes 1572872 | tf_op jit(solution)/shard_map/ppermute | solution.py:24
  102.4 11.9 %collective-permute-start.16 = (bf16[64,4096]{1,0:T(8,128)(2,1)S(1)}, bf16[64,4096]{1,0:T(8,128)(2,1)S(1)}, u32[]{:S(2)}, u32[]{:S(2)}) collective-permute-start(bf16[64,4096]{1,0:T(8,128)(2,1)S(1)} %get-tuple-element.9), channel_id=1, source_target_pairs={{2,0},{4,2},{6,4},{7,6},{5,7},{3,5},{1,3},{0,1},{10,8},{12,10},{14... | collective-permute-start | bytes 1572872 | tf_op jit(solution)/shard_map/ppermute | solution.py:24
  102.9 11.4 %collective-permute-start.20 = (bf16[64,4096]{1,0:T(8,128)(2,1)S(1)}, bf16[64,4096]{1,0:T(8,128)(2,1)S(1)}, u32[]{:S(2)}, u32[]{:S(2)}) collective-permute-start(bf16[64,4096]{1,0:T(8,128)(2,1)S(1)} %get-tuple-element.10), channel_id=1, source_target_pairs={{0,2},{2,4},{4,6},{6,7},{7,5},{5,3},{3,1},{1,0},{8,10},{10,12},{12... | collective-permute-start | bytes 1572872 | tf_op jit(solution)/shard_map/ppermute | solution.py:21
  114.5 9.9 %collective-permute-start.17 = (bf16[64,4096]{1,0:T(8,128)(2,1)S(1)}, bf16[64,4096]{1,0:T(8,128)(2,1)S(1)}, u32[]{:S(2)}, u32[]{:S(2)}) collective-permute-start(bf16[64,4096]{1,0:T(8,128)(2,1)S(1)} %get-tuple-element.5), channel_id=1, source_target_pairs={{2,0},{4,2},{6,4},{7,6},{5,7},{3,5},{1,3},{0,1},{10,8},{12,10},{14... | collective-permute-start | bytes 1572872 | tf_op jit(solution)/shard_map/ppermute | solution.py:24
  115.0 9.4 %collective-permute-start.21 = (bf16[64,4096]{1,0:T(8,128)(2,1)S(1)}, bf16[64,4096]{1,0:T(8,128)(2,1)S(1)}, u32[]{:S(2)}, u32[]{:S(2)}) collective-permute-start(bf16[64,4096]{1,0:T(8,128)(2,1)S(1)} %get-tuple-element.6), channel_id=1, source_target_pairs={{0,2},{2,4},{4,6},{6,7},{7,5},{5,3},{3,1},{1,0},{8,10},{10,12},{12... | collective-permute-start | bytes 1572872 | tf_op jit(solution)/shard_map/ppermute | solution.py:21

commit v2 on v0

v2 whole, which is shorter than its diff:
```python
import functools

import jax
import jax.numpy as jnp
from jax import lax
from jax.experimental import pallas as pl
from jax.experimental.pallas import tpu as pltpu
from jax.sharding import PartitionSpec as P

F32, BF16 = jnp.float32, jnp.bfloat16
VMEM = pl.BlockSpec(memory_space=pltpu.VMEM)
ANY = pl.BlockSpec(memory_space=pl.ANY)
SMEM = pl.BlockSpec(memory_space=pltpu.SMEM)


def ring_of(n):
    return list(range(0, n, 2)) + list(range(n - 1, 0, -2))


def held(x, after):
    for t in after:
        t = t[(0,) * t.ndim]
        x = jnp.where(t == t, x, t.astype(x.dtype))
    return x


def bring(w, after, parts=8):
    step = w.shape[0] // parts

    def body(w_ref, *refs):
        o_ref, sem = refs[-2:]
        copies = [
            pltpu.make_async_copy(
                w_ref.at[pl.ds(i * step, step)],
                o_ref.at[pl.ds(i * step, step)],
                sem.at[i],
            )
            for i in range(parts)
        ]
        for copy in copies:
            copy.start()
        for copy in copies:
            copy.wait()

    return pl.pallas_call(
        body,
        in_specs=[ANY] * (1 + len(after)),
        out_specs=VMEM,
        out_shape=pltpu.VMEM(w.shape, w.dtype),
        scratch_shapes=[pltpu.SemaphoreType.DMA((parts,))],
        compiler_params=pltpu.CompilerParams(vmem_limit_bytes=1 << 20),
        cost_estimate=pl.CostEstimate(
            flops=0, bytes_accessed=w.size * 2, transcendentals=0
        ),
    )(pltpu.with_memory_space_constraint(w, pltpu.HBM), *after)


def call(body, out_shape, part, arrays, kept, after, flops):
    size = sum(a.size * a.dtype.itemsize for a in arrays)
    used = 1 + len(arrays) + len(kept)

    def kernel(*refs):
        body(*refs[:used], refs[used + len(after)])

    out, *kept = pl.pallas_call(
        kernel,
        in_specs=[SMEM] + [VMEM] * (used - 1) + [ANY] * len(after),
        out_specs=[VMEM] * (1 + len(kept)),
        out_shape=[out_shape] + [pltpu.VMEM(w.shape, w.dtype) for w in kept],
        input_output_aliases={1 + len(arrays) + i: 1 + i for i in range(len(kept))},
        compiler_params=pltpu.CompilerParams(vmem_limit_bytes=4 << 20),
        cost_estimate=pl.CostEstimate(
            flops=flops, bytes_accessed=size, transcendentals=0
        ),
    )(part, *arrays, *kept, *after)
    return out, kept


def gate_up(x, weights, part, after):
    m, k = x.shape
    w = weights[0].shape[1] // 2
    tile = min(w, 256)

    def body(part_ref, x_ref, g_ref, u_ref, o_ref):
        start = part_ref[0] * w

        @pl.loop(0, w // tile)
        def _(j):
            here = pl.multiple_of(j * tile, tile)
            cols = pl.ds(pl.multiple_of(start + here, tile), tile)
            for i, ref in enumerate((g_ref, u_ref)):
                o_ref[i, :, pl.ds(here, tile)] = jnp.dot(
                    x_ref[...], ref[:, cols], preferred_element_type=F32
                )

    shape = jax.ShapeDtypeStruct((2, m, w), F32)
    return call(body, shape, part, [x], weights, after, 4 * m * k * w)


def down(mine, others, weights, part, after):
    m, w = mine.shape
    n = weights[0].shape[1]
    tile = 256

    def body(part_ref, a_ref, b_ref, d_ref, o_ref):
        first = pl.multiple_of(part_ref[0] * w, w)
        second = pl.multiple_of(w - part_ref[0] * w, w)

        @pl.loop(0, n // tile)
        def _(j):
            cols = pl.ds(pl.multiple_of(j * tile, tile), tile)
            o_ref[:, cols] = jnp.dot(
                a_ref[...], d_ref[pl.ds(first, w), cols], preferred_element_type=F32
            ) + jnp.dot(
                b_ref[...], d_ref[pl.ds(second, w), cols], preferred_element_type=F32
            )

    shape = jax.ShapeDtypeStruct((m, n), F32)
    return call(body, shape, part, [mine, others], weights, after, 4 * m * w * n)


def make_shards(n):
    ring = ring_of(n)
    half = n // 2
    to_right = [(ring[i], ring[(i + 1) % n]) for i in range(n)]
    to_left = [(ring[(i + 1) % n], ring[i]) for i in range(n)]
    swap = [(0, 1), (1, 0)]

    def right(x):
        return lax.ppermute(x, "gy", to_right)

    def left(x):
        return lax.ppermute(x, "gy", to_left)

    def other(x):
        return lax.ppermute(x, "gx", swap)

    def shards(tokens, gate_weight, up_weight, down_weight):
        rows = tokens.shape[0]
        cut = rows // 2
        core = lax.axis_index("gx").astype(jnp.int32)
        keep, give = core.reshape(1), (1 - core).reshape(1)

        a, b = tokens[:cut], tokens[cut:]
        blocks = {0: [a, b]}
        theirs, ours, hidden, partial = {}, {}, {}, {}
        last = []
        wide, back = [bring(gate_weight, []), bring(up_weight, [])], []

        def multiply(span, part):
            x = jnp.concatenate([p for d in span for p in blocks[d]], axis=0)
            out, wide[:] = gate_up(x, wide, part, last)
            last[:] = [out]
            return out

        def give_part(span):
            theirs[span] = other(multiply(span, give))

        def keep_part(span):
            ours[span] = multiply(span, keep)

        def gated(span):
            both = ours[span] + theirs[span]
            h = (jax.nn.silu(both[0]) * both[1]).astype(BF16)
            hidden[span] = h, other(h)

        def put_down(span):
            out, back[:] = down(*hidden[span], back, keep, last)
            last[:] = [out]
            at = 0
            for d in span:
                partial[d] = [
                    out[at + i * cut : at + (i + 1) * cut]
                    for i in range(len(blocks[d]))
                ]
                at += len(blocks[d]) * cut

        ra, rb, la, lb = a, b, a, b
        spans = [(0, 1)] + [(d,) for d in range(2, half + 1)]
        ra, lb = right(ra), left(lb)
        rb, la = right(rb), left(la)
        blocks[1] = [ra, rb, la, lb]
        for d in range(2, half):
            now = spans[d - 2]
            if d > 2:
                ra, lb = held(ra, last), held(lb, last)
            ra, lb = right(ra), left(lb)
            give_part(now)
            if d > 2:
                gated(spans[d - 3])
            rb, la = right(held(rb, last)), left(held(la, last))
            keep_part(now)
            blocks[d] = [ra, rb, la, lb]
        blocks[half] = [right(held(ra, last)), left(held(lb, last))]
        before, far, end = spans[-3:]
        back[:] = [bring(down_weight, last)]
        give_part(before)
        gated(spans[-4]) if len(spans) > 3 else None
        keep_part(before)
        gated(before)
        give_part(far)
        keep_part(far)
        gated(far)
        give_part(end)
        put_down(far)
        keep_part(end)
        gated(end)
        put_down(end)
        for span in spans[-3::-1]:
            put_down(span)

        l_b = left(partial[half - 1][1].astype(BF16))
        r_a = right(partial[half - 1][2].astype(BF16))
        l_a = left(partial[half][0].astype(BF16))
        r_b = right(partial[half][1].astype(BF16))
        for d in range(half - 1, 0, -1):
            if d < half - 1:
                l_b = left((partial[d][1] + l_b.astype(F32)).astype(BF16))
                r_a = right((partial[d][2] + r_a.astype(F32)).astype(BF16))
            l_a = left((partial[d][0] + l_a.astype(F32)).astype(BF16))
            r_b = right((partial[d][3] + r_b.astype(F32)).astype(BF16))
        oa = partial[0][0] + l_a.astype(F32) + r_a.astype(F32)
        ob = partial[0][1] + l_b.astype(F32) + r_b.astype(F32)
        return jnp.concatenate([oa, ob], axis=0).astype(BF16)

    return shards


def solution(mesh):
    return jax.shard_map(
        make_shards(mesh.shape["gy"]),
        mesh=mesh,
        in_specs=(P(("groups", "gy"), "gx"), P("gx", "gy"), P("gx", "gy"), P("gy", "gx")),
        out_specs=P(("groups", "gy"), "gx"),
        check_vma=False,
    )
```

time: 328 us -> 336 us (1.024)
  waiting for transfers between devices: 267 us -> 44 us
  local copies, waits for them, and re-layouts: 0.01 us -> 169 us
  Pallas kernels: 0 us -> 80.1 us
  matrix products: 42.4 us -> 0 us
  starting transfers between devices: 0.08 us -> 31.5 us
  between operations: 13.1 us -> 8.13 us
    unnamed x2 -> x77, local copies, waits for them, and re-layouts: 0.01 us -> 165 us
    reduce_scatter x1 -> x0, waiting for transfers between devices: 150 us -> none  [shards(): lax.psum_scatter(jnp.dot(hidden, down_weight, preferred_element_type=jnp....]
    pallas_call x0 -> x17, Pallas kernels: none -> 80.1 us  [the longest x14 56.2 us: call(): pl.pallas_call(kernel, in_specs=[SMEM] + [VMEM] * (used - 1) + [ANY] * le...]
    all_gather x1 -> x0, waiting for transfers between devices: 78.3 us -> none  [shards(): piece = lax.all_gather(tokens, 'gy', axis=0, tiled=True)]
    ppermute x0 -> x36, waiting for transfers between devices: none -> 44 us  [the longest x14 23.1 us: left(): return lax.ppermute(x, 'gy', to_left)]
    dot_general x3 -> x0, matrix products: 42.4 us -> none  [the longest x1 16.9 us: shards(): jnp.dot(hidden, down_weight, preferred_element_type=jnp.float32)]
    psum x1 -> x0, waiting for transfers between devices: 37.2 us -> none  [shards(): summed = lax.psum(partial_value, 'gx')]
    ppermute x0 -> x36, starting transfers between devices: none -> 31.5 us  [the longest x14 19.6 us: right(): return lax.ppermute(x, 'gy', to_right)]
  transfers between devices with their start and end apart: 3 -> 36, of which waited for: 3 -> 11; matrix products, arithmetic and copies ran while one was open for 0% -> 1% of each run, Pallas kernels for 0% -> 21%
where the time goes in v2:
time: 336 us
  local copies, waits for them, and re-layouts  169 us (50%)
  Pallas kernels  80.1 us (24%)
  waiting for transfers between devices  44 us (13%)
  starting transfers between devices  31.5 us (9%)
  between operations  8.13 us (2%)
    unnamed x77, local copies, waits for them, and re-layouts  165 us
    pallas_call x14, Pallas kernels, call(): pl.pallas_call(kernel, in_specs=[SMEM] + [VMEM] * (used - 1) + [ANY] * le...  56.2 us
    pallas_call x3, Pallas kernels, bring(): pl.pallas_call(body, in_specs=[ANY] * (1 + len(after)), out_specs=VMEM, o...  23.9 us
    ppermute x14, waiting for transfers between devices, left(): return lax.ppermute(x, 'gy', to_left)  23.1 us
    ppermute x14, waiting for transfers between devices, right(): return lax.ppermute(x, 'gy', to_right)  20.7 us
    ppermute x14, starting transfers between devices, right(): return lax.ppermute(x, 'gy', to_right)  19.6 us
    ppermute x14, starting transfers between devices, left(): return lax.ppermute(x, 'gy', to_left)  10.5 us
  transfers between devices with their start and end apart: 36, of which 11 were waited for; matrix products, arithmetic and copies ran while one was open for 1% of the time, Pallas kernels for 21%

profile of v2, /device:TPU:0, one launch (start us, length us, event | category | flops | bytes accessed | tf_op | source)
XLA Modules:
  0.0 335.7 jit_solution(194853481776887727)
XLA Ops:
  6.2 5.9 %shard_map.46.refs_2_ = bf16[4096,2048]{1,0:T(8,128)(2,1)S(1)} custom-call(bf16[4096,2048]{1,0:T(8,128)(2,1)} %w_ref.3), custom_call_target="tpu_custom_call" | custom-call | bytes 16777216 | tf_op jit(solution)/shard_map/pallas_call | solution.py:45
  12.2 5.8 %copy-done = bf16[4096,2048]{1,0:T(8,128)(2,1)} copy-done((bf16[4096,2048]{1,0:T(8,128)(2,1)}, bf16[4096,2048]{1,0:T(8,128)(2,1)S(1)}, u32[]{:S(2)}) %copy-start) | copy-done | bytes 16777240
  18.0 6.0 %shard_map.47.refs_3_ = bf16[4096,2048]{1,0:T(8,128)(2,1)S(1)} custom-call(bf16[4096,2048]{1,0:T(8,128)(2,1)} %w_ref.4), custom_call_target="tpu_custom_call" | custom-call | bytes 16777216 | tf_op jit(solution)/shard_map/pallas_call | solution.py:45
  24.0 5.8 %copy-done.17 = bf16[4096,2048]{1,0:T(8,128)(2,1)} copy-done((bf16[4096,2048]{1,0:T(8,128)(2,1)}, bf16[4096,2048]{1,0:T(8,128)(2,1)S(1)}, u32[]{:S(2)}) %copy-start.17) | copy-done | bytes 16777240
  30.0 5.8 %copy-done.1 = bf16[4096,2048]{1,0:T(8,128)(2,1)S(1)} copy-done((bf16[4096,2048]{1,0:T(8,128)(2,1)S(1)}, bf16[4096,2048]{1,0:T(8,128)(2,1)}, u32[]{:S(2)}) %copy-start.1) | copy-done | bytes 16777240
  35.7 5.8 %copy-done.18 = bf16[4096,2048]{1,0:T(8,128)(2,1)S(1)} copy-done((bf16[4096,2048]{1,0:T(8,128)(2,1)S(1)}, bf16[4096,2048]{1,0:T(8,128)(2,1)}, u32[]{:S(2)}) %copy-start.18) | copy-done | bytes 16777240
  41.5 4.1 %shard_map.48 = (f32[2,192,1024]{2,1,0:T(8,128)S(1)}, bf16[4096,2048]{1,0:T(8,128)(2,1)S(1)}, bf16[4096,2048]{1,0:T(8,128)(2,1)S(1)}) custom-call(s32[1]{0:T(128)} %bitcast.1.refs_0_, bf16[192,4096]{1,0:T(8,128)(2,1)S(1)} %constant_dynamic-update-slice_fusion.refs_1_, ...), custom_call_target="tpu_custom_call", output_to_operand_aliasing={{1}: (2, {}), {2}: (3, {})} | custom-call | flops 3221225472 | bytes 1572864 | tf_op jit(solution)/shard_map/pallas_call | solution.py:65
  45.6 5.8 %copy-done.2 = bf16[4096,2048]{1,0:T(8,128)(2,1)} copy-done((bf16[4096,2048]{1,0:T(8,128)(2,1)}, bf16[4096,2048]{1,0:T(8,128)(2,1)S(1)}, u32[]{:S(2)}) %copy-start.2) | copy-done | bytes 16777240
  53.6 5.8 %copy-done.3 = bf16[4096,2048]{1,0:T(8,128)(2,1)S(1)} copy-done((bf16[4096,2048]{1,0:T(8,128)(2,1)S(1)}, bf16[4096,2048]{1,0:T(8,128)(2,1)}, u32[]{:S(2)}) %copy-start.3) | copy-done | bytes 16777240
  59.4 4.1 %shard_map.49 = (f32[2,192,1024]{2,1,0:T(8,128)S(1)}, bf16[4096,2048]{1,0:T(8,128)(2,1)S(1)}, bf16[4096,2048]{1,0:T(8,128)(2,1)S(1)}) custom-call(s32[1]{0:T(128)} %bitcast.refs_0_, bf16[192,4096]{1,0:T(8,128)(2,1)S(1)} %constant_dynamic-update-slice_fusion.refs_1_, bf16[4096,2048]{1,0:T(8,128)(2,1)S(1)} %copy-done.3, ...), custom_call_target="tpu_custom_call", output_to_operand_aliasing={{1}: (2, {}), {2}: (3, {})} | custom-call | flops 3221225472 | bytes 1572864 | tf_op jit(solution)/shard_map/pallas_call | solution.py:65
  63.5 5.8 %copy-done.4 = bf16[4096,2048]{1,0:T(8,128)(2,1)} copy-done((bf16[4096,2048]{1,0:T(8,128)(2,1)}, bf16[4096,2048]{1,0:T(8,128)(2,1)S(1)}, u32[]{:S(2)}) %copy-start.4) | copy-done | bytes 16777240
  76.1 10.3 %collective-permute-done.6 = bf16[32,4096]{1,0:T(8,128)(2,1)S(1)} collective-permute-done((bf16[32,4096]{1,0:T(8,128)(2,1)S(1)}, bf16[32,4096]{1,0:T(8,128)(2,1)S(1)}, u32[]{:S(2)}, u32[]{:S(2)}) %collective-permute-start.6) | collective-permute-done | bytes 262176 | tf_op jit(solution)/shard_map/ppermute | solution.py:130
  89.4 5.8 %copy-done.5 = bf16[4096,2048]{1,0:T(8,128)(2,1)S(1)} copy-done((bf16[4096,2048]{1,0:T(8,128)(2,1)S(1)}, bf16[4096,2048]{1,0:T(8,128)(2,1)}, u32[]{:S(2)}) %copy-start.5) | copy-done | bytes 16777240
  98.2 5.8 %copy-done.6 = bf16[4096,2048]{1,0:T(8,128)(2,1)} copy-done((bf16[4096,2048]{1,0:T(8,128)(2,1)}, bf16[4096,2048]{1,0:T(8,128)(2,1)S(1)}, u32[]{:S(2)}) %copy-start.6) | copy-done | bytes 16777240
  108.6 5.8 %copy-done.7 = bf16[4096,2048]{1,0:T(8,128)(2,1)S(1)} copy-done((bf16[4096,2048]{1,0:T(8,128)(2,1)S(1)}, bf16[4096,2048]{1,0:T(8,128)(2,1)}, u32[]{:S(2)}) %copy-start.7) | copy-done | bytes 16777240
  114.4 3.1 shard_map.51
  117.5 5.8 %copy-done.8 = bf16[4096,2048]{1,0:T(8,128)(2,1)} copy-done((bf16[4096,2048]{1,0:T(8,128)(2,1)}, bf16[4096,2048]{1,0:T(8,128)(2,1)S(1)}, u32[]{:S(2)}) %copy-start.8) | copy-done | bytes 16777240
  126.2 5.8 %copy-done.9 = bf16[4096,2048]{1,0:T(8,128)(2,1)S(1)} copy-done((bf16[4096,2048]{1,0:T(8,128)(2,1)S(1)}, bf16[4096,2048]{1,0:T(8,128)(2,1)}, u32[]{:S(2)}) %copy-start.9) | copy-done | bytes 16777240
  132.0 3.1 shard_map.52
  135.2 5.8 %copy-done.10 = bf16[4096,2048]{1,0:T(8,128)(2,1)} copy-done((bf16[4096,2048]{1,0:T(8,128)(2,1)}, bf16[4096,2048]{1,0:T(8,128)(2,1)S(1)}, u32[]{:S(2)}) %copy-start.10) | copy-done | bytes 16777240
  142.3 5.8 %copy-done.11 = bf16[4096,2048]{1,0:T(8,128)(2,1)S(1)} copy-done((bf16[4096,2048]{1,0:T(8,128)(2,1)S(1)}, bf16[4096,2048]{1,0:T(8,128)(2,1)}, u32[]{:S(2)}) %copy-start.11) | copy-done | bytes 16777240
  151.2 5.8 %copy-done.12 = bf16[4096,2048]{1,0:T(8,128)(2,1)} copy-done((bf16[4096,2048]{1,0:T(8,128)(2,1)}, bf16[4096,2048]{1,0:T(8,128)(2,1)S(1)}, u32[]{:S(2)}) %copy-start.12) | copy-done | bytes 16777240
  157.6 8.2 %collective-permute-done.17 = bf16[32,4096]{1,0:T(8,128)(2,1)S(1)} collective-permute-done((bf16[32,4096]{1,0:T(8,128)(2,1)S(1)}, bf16[32,4096]{1,0:T(8,128)(2,1)S(1)}, u32[]{:S(2)}, u32[]{:S(2)}) %collective-permute-start.17) | collective-permute-done | bytes 262176 | tf_op jit(solution)/shard_map/ppermute | solution.py:133
  167.9 5.8 %copy-done.13 = bf16[4096,2048]{1,0:T(8,128)(2,1)S(1)} copy-done((bf16[4096,2048]{1,0:T(8,128)(2,1)S(1)}, bf16[4096,2048]{1,0:T(8,128)(2,1)}, u32[]{:S(2)}) %copy-start.13) | copy-done | bytes 16777240
  176.9 3.2 shard_map.55
  180.1 5.8 %copy-done.14 = bf16[4096,2048]{1,0:T(8,128)(2,1)} copy-done((bf16[4096,2048]{1,0:T(8,128)(2,1)}, bf16[4096,2048]{1,0:T(8,128)(2,1)S(1)}, u32[]{:S(2)}) %copy-start.14) | copy-done | bytes 16777240
  186.9 5.8 %copy-done.15 = bf16[4096,2048]{1,0:T(8,128)(2,1)S(1)} copy-done((bf16[4096,2048]{1,0:T(8,128)(2,1)S(1)}, bf16[4096,2048]{1,0:T(8,128)(2,1)}, u32[]{:S(2)}) %copy-start.15) | copy-done | bytes 16777240
  192.6 3.5 %shard_map.56 = (f32[2,64,1024]{2,1,0:T(8,128)S(1)}, bf16[4096,2048]{1,0:T(8,128)(2,1)S(1)}, bf16[4096,2048]{1,0:T(8,128)(2,1)S(1)}) custom-call(s32[1]{0:T(128)} %bitcast.1.refs_0_, bf16[64,4096]{1,0:T(8,128)(2,1)S(1)} %constant_dynamic-update-slice_fusion.9.refs_1_, ...), custom_call_target="tpu_custom_call", output_to_operand_aliasing={{1}: (2, {}), {2}: (3, {})} | custom-call | flops 1073741824 | bytes 524288 | tf_op jit(solution)/shard_map/pallas_call | solution.py:65
  196.1 5.8 %copy-done.16 = bf16[4096,2048]{1,0:T(8,128)(2,1)} copy-done((bf16[4096,2048]{1,0:T(8,128)(2,1)}, bf16[4096,2048]{1,0:T(8,128)(2,1)S(1)}, u32[]{:S(2)}) %copy-start.16) | copy-done | bytes 16777240
  202.0 12.0 %shard_map.57.refs_3_ = bf16[2048,4096]{1,0:T(8,128)(2,1)S(1)} custom-call(bf16[2048,4096]{1,0:T(8,128)(2,1)} %w_ref.5, f32[2,128,1024]{2,1,0:T(8,128)S(1)} %get-tuple-element.51.refs_4_.refs_0_), custom_call_target="tpu_custom_call" | custom-call | bytes 16777216 | tf_op jit(solution)/shard_map/pallas_call | solution.py:45
  214.0 8.5 %copy-done.21 = bf16[2048,4096]{1,0:T(8,128)(2,1)} copy-done((bf16[2048,4096]{1,0:T(8,128)(2,1)}, bf16[2048,4096]{1,0:T(8,128)(2,1)S(1)}, u32[]{:S(2)}) %copy-start.21) | copy-done | bytes 16777240
  222.7 5.9 %copy-done.22 = bf16[2048,4096]{1,0:T(8,128)(2,1)S(1)} copy-done((bf16[2048,4096]{1,0:T(8,128)(2,1)S(1)}, bf16[2048,4096]{1,0:T(8,128)(2,1)}, u32[]{:S(2)}) %copy-start.22) | copy-done | bytes 16777240
  228.7 5.4 %shard_map.58 = (f32[128,4096]{1,0:T(8,128)S(1)}, bf16[2048,4096]{1,0:T(8,128)(2,1)S(1)}) custom-call(s32[1]{0:T(128)} %bitcast.refs_0_, bf16[128,1024]{1,0:T(8,128)(2,1)S(1)} %fusion.3.refs_1_, bf16[128,1024]{1,0:T(8,128)(2,1)S(1)} %collective-permute-done.19.refs_2_, bf16[2048,4096]{1,0:T(8,128)(2,1)S(1)} %copy-done.22, ...), custom_call_target="tpu_custom_call", output_to_operand_aliasing={{1}: (3, {})} | custom-call | flops 2147483648 | bytes 524288 | tf_op jit(solution)/shard_map/pallas_call | solution.py:65
  234.1 5.8 %copy-done.23 = bf16[2048,4096]{1,0:T(8,128)(2,1)} copy-done((bf16[2048,4096]{1,0:T(8,128)(2,1)}, bf16[2048,4096]{1,0:T(8,128)(2,1)S(1)}, u32[]{:S(2)}) %copy-start.23) | copy-done | bytes 16777240
  239.9 5.8 %copy-done.20 = bf16[4096,2048]{1,0:T(8,128)(2,1)S(1)} copy-done((bf16[4096,2048]{1,0:T(8,128)(2,1)S(1)}, bf16[4096,2048]{1,0:T(8,128)(2,1)}, u32[]{:S(2)}) %copy-start.20) | copy-done | bytes 16777240
  245.7 3.5 %shard_map.59 = (f32[2,64,1024]{2,1,0:T(8,128)S(1)}, bf16[4096,2048]{1,0:T(8,128)(2,1)S(1)}, bf16[4096,2048]{1,0:T(8,128)(2,1)S(1)}) custom-call(s32[1]{0:T(128)} %bitcast.refs_0_, bf16[64,4096]{1,0:T(8,128)(2,1)S(1)} %constant_dynamic-update-slice_fusion.9.refs_1_, bf16[4096,2048]{1,0:T(8,128)(2,1)S(1)} %bitcast.51, ...), custom_call_target="tpu_custom_call", output_to_operand_aliasing={{1}: (2, {}), {2}: (3, {})} | custom-call | flops 1073741824 | bytes 524288 | tf_op jit(solution)/shard_map/pallas_call | solution.py:65
  250.7 5.8 %copy-done.24 = bf16[2048,4096]{1,0:T(8,128)(2,1)S(1)} copy-done((bf16[2048,4096]{1,0:T(8,128)(2,1)S(1)}, bf16[2048,4096]{1,0:T(8,128)(2,1)}, u32[]{:S(2)}) %copy-start.24) | copy-done | bytes 16777240
  256.5 5.1 %shard_map.60 = (f32[64,4096]{1,0:T(8,128)S(1)}, bf16[2048,4096]{1,0:T(8,128)(2,1)S(1)}) custom-call(s32[1]{0:T(128)} %bitcast.refs_0_, bf16[64,1024]{1,0:T(8,128)(2,1)S(1)} %fusion.7.refs_1_, bf16[64,1024]{1,0:T(8,128)(2,1)S(1)} %collective-permute-done.21.refs_2_, bf16[2048,4096]{1,0:T(8,128)(2,1)S(1)} %copy-done.24, ...), custom_call_target="tpu_custom_call", output_to_operand_aliasing={{1}: (3, {})} | custom-call | flops 1073741824 | bytes 262144 | tf_op jit(solution)/shard_map/pallas_call | solution.py:65
  261.6 5.8 %copy-done.25 = bf16[2048,4096]{1,0:T(8,128)(2,1)} copy-done((bf16[2048,4096]{1,0:T(8,128)(2,1)}, bf16[2048,4096]{1,0:T(8,128)(2,1)S(1)}, u32[]{:S(2)}) %copy-start.25) | copy-done | bytes 16777240
  271.7 5.0 %collective-permute-done.22 = bf16[32,4096]{1,0:T(8,128)(2,1)S(1)} collective-permute-done((bf16[32,4096]{1,0:T(8,128)(2,1)S(1)}, bf16[32,4096]{1,0:T(8,128)(2,1)S(1)}, u32[]{:S(2)}, u32[]{:S(2)}) %collective-permute-start.22) | collective-permute-done | bytes 262176 | tf_op jit(solution)/shard_map/ppermute | solution.py:133
  279.7 5.8 %copy-done.26 = bf16[2048,4096]{1,0:T(8,128)(2,1)S(1)} copy-done((bf16[2048,4096]{1,0:T(8,128)(2,1)S(1)}, bf16[2048,4096]{1,0:T(8,128)(2,1)}, u32[]{:S(2)}) %copy-start.26) | copy-done | bytes 16777240
  285.5 5.4 %shard_map.61 = (f32[128,4096]{1,0:T(8,128)S(1)}, bf16[2048,4096]{1,0:T(8,128)(2,1)S(1)}) custom-call(s32[1]{0:T(128)} %bitcast.refs_0_, bf16[128,1024]{1,0:T(8,128)(2,1)S(1)} %fusion.5.refs_1_, bf16[128,1024]{1,0:T(8,128)(2,1)S(1)} %collective-permute-done.11.refs_2_, bf16[2048,4096]{1,0:T(8,128)(2,1)S(1)} %copy-done.26, ...), custom_call_target="tpu_custom_call", output_to_operand_aliasing={{1}: (3, {})} | custom-call | flops 2147483648 | bytes 524288 | tf_op jit(solution)/shard_map/pallas_call | solution.py:65
  290.9 5.8 %copy-done.27 = bf16[2048,4096]{1,0:T(8,128)(2,1)} copy-done((bf16[2048,4096]{1,0:T(8,128)(2,1)}, bf16[2048,4096]{1,0:T(8,128)(2,1)S(1)}, u32[]{:S(2)}) %copy-start.27) | copy-done | bytes 16777240
  299.1 5.8 %copy-done.28 = bf16[2048,4096]{1,0:T(8,128)(2,1)S(1)} copy-done((bf16[2048,4096]{1,0:T(8,128)(2,1)S(1)}, bf16[2048,4096]{1,0:T(8,128)(2,1)}, u32[]{:S(2)}) %copy-start.28) | copy-done | bytes 16777240
  304.8 6.4 %shard_map.62 = (f32[192,4096]{1,0:T(8,128)S(1)}, bf16[2048,4096]{1,0:T(8,128)(2,1)S(1)}) custom-call(s32[1]{0:T(128)} %bitcast.refs_0_, bf16[192,1024]{1,0:T(8,128)(2,1)S(1)} %fusion.1.refs_1_, bf16[192,1024]{1,0:T(8,128)(2,1)S(1)} %collective-permute-done.5.refs_2_, bf16[2048,4096]{1,0:T(8,128)(2,1)S(1)} %copy-done.28, ...), custom_call_target="tpu_custom_call", output_to_operand_aliasing={{1}: (3, {})} | custom-call | flops 3221225472 | bytes 786432 | tf_op jit(solution)/shard_map/pallas_call | solution.py:65
  315.5 5.0 %collective-permute-done.34 = bf16[32,4096]{1,0:T(8,128)(2,1)S(1)} collective-permute-done((bf16[32,4096]{1,0:T(8,128)(2,1)S(1)}, bf16[32,4096]{1,0:T(8,128)(2,1)S(1)}, u32[]{:S(2)}, u32[]{:S(2)}) %collective-permute-start.34) | collective-permute-done | bytes 262176 | tf_op jit(solution)/shard_map/ppermute | solution.py:130
  322.1 4.3 %collective-permute-done.25 = bf16[32,4096]{1,0:T(8,128)(2,1)S(1)} collective-permute-done((bf16[32,4096]{1,0:T(8,128)(2,1)S(1)}, bf16[32,4096]{1,0:T(8,128)(2,1)S(1)}, u32[]{:S(2)}, u32[]{:S(2)}) %collective-permute-start.25) | collective-permute-done | bytes 262176 | tf_op jit(solution)/shard_map/ppermute | solution.py:133
  328.6 4.9 %collective-permute-done.35 = bf16[32,4096]{1,0:T(8,128)(2,1)S(1)} collective-permute-done((bf16[32,4096]{1,0:T(8,128)(2,1)S(1)}, bf16[32,4096]{1,0:T(8,128)(2,1)S(1)}, u32[]{:S(2)}, u32[]{:S(2)}) %collective-permute-start.35) | collective-permute-done | bytes 262176 | tf_op jit(solution)/shard_map/ppermute | solution.py:130
  (152 shorter events, 54.1 us)
Async XLA Ops:
  1.1 28.8 %collective-permute-start.3 = (bf16[32,4096]{1,0:T(8,128)(2,1)S(1)}, bf16[32,4096]{1,0:T(8,128)(2,1)S(1)}, u32[]{:S(2)}, u32[]{:S(2)}) collective-permute-start(bf16[32,4096]{1,0:T(8,128)(2,1)S(1)} %get-tuple-element.90), channel_id=1, source_target_pairs={{2,0},{4,2},{6,4},{7,6},{5,7},{3,5},{1,3},{0,1},{10,8},{12,10},{14... | collective-permute-start | bytes 786440 | tf_op jit(solution)/shard_map/ppermute | solution.py:133
  4.1 25.7 %collective-permute-start.1 = (bf16[32,4096]{1,0:T(8,128)(2,1)S(1)}, bf16[32,4096]{1,0:T(8,128)(2,1)S(1)}, u32[]{:S(2)}, u32[]{:S(2)}) collective-permute-start(bf16[32,4096]{1,0:T(8,128)(2,1)S(1)} %get-tuple-element.90), channel_id=1, source_target_pairs={{0,2},{2,4},{4,6},{6,7},{7,5},{5,3},{3,1},{1,0},{8,10},{10,12},{12... | collective-permute-start | bytes 786440 | tf_op jit(solution)/shard_map/ppermute | solution.py:130
  4.2 25.7 %collective-permute-start.2 = (bf16[32,4096]{1,0:T(8,128)(2,1)S(1)}, bf16[32,4096]{1,0:T(8,128)(2,1)S(1)}, u32[]{:S(2)}, u32[]{:S(2)}) collective-permute-start(bf16[32,4096]{1,0:T(8,128)(2,1)S(1)} %get-tuple-element.91), channel_id=1, source_target_pairs={{2,0},{4,2},{6,4},{7,6},{5,7},{3,5},{1,3},{0,1},{10,8},{12,10},{14... | collective-permute-start | bytes 786440 | tf_op jit(solution)/shard_map/ppermute | solution.py:133
  6.1 23.7 %collective-permute-start = (bf16[32,4096]{1,0:T(8,128)(2,1)S(1)}, bf16[32,4096]{1,0:T(8,128)(2,1)S(1)}, u32[]{:S(2)}, u32[]{:S(2)}) collective-permute-start(bf16[32,4096]{1,0:T(8,128)(2,1)S(1)} %get-tuple-element.91), channel_id=1, source_target_pairs={{0,2},{2,4},{4,6},{6,7},{7,5},{5,3},{3,1},{1,0},{8,10},{10,12},{12... | collective-permute-start | bytes 786440 | tf_op jit(solution)/shard_map/ppermute | solution.py:130
  18.0 11.7 %copy-start.29 = (bf16[64,4096]{1,0:T(8,128)(2,1)S(1)}, bf16[64,4096]{1,0:T(8,128)(2,1)}, u32[]{:S(2)}) copy-start(bf16[64,4096]{1,0:T(8,128)(2,1)} %param.4) | copy-start | bytes 1572868
  45.6 5.8 %copy-start.2 = (bf16[4096,2048]{1,0:T(8,128)(2,1)}, bf16[4096,2048]{1,0:T(8,128)(2,1)S(1)}, u32[]{:S(2)}) copy-start(bf16[4096,2048]{1,0:T(8,128)(2,1)S(1)} %get-tuple-element.40.refs_2_) | copy-start | bytes 50331652
  63.5 5.8 %copy-start.4 = (bf16[4096,2048]{1,0:T(8,128)(2,1)}, bf16[4096,2048]{1,0:T(8,128)(2,1)S(1)}, u32[]{:S(2)}) copy-start(bf16[4096,2048]{1,0:T(8,128)(2,1)S(1)} %get-tuple-element.44.refs_2_) | copy-start | bytes 50331652
  71.8 178.3 %collective-permute-start.4 = (f32[2,192,1024]{2,1,0:T(8,128)S(1)}, f32[2,192,1024]{2,1,0:T(8,128)S(1)}, u32[]{:S(2)}, u32[]{:S(2)}) collective-permute-start(f32[2,192,1024]{2,1,0:T(8,128)S(1)} %get-tuple-element.42.refs_4_), channel_id=1, source_target_pairs={{0,8},{8,0},{1,9},{9,1},{2,10},{10,2},{3,11},{11,3},{4,12},{12,4},... | collective-permute-start | bytes 4718600 | tf_op jit(solution)/shard_map/ppermute | solution.py:136
  71.9 14.6 %collective-permute-start.7 = (bf16[32,4096]{1,0:T(8,128)(2,1)S(1)}, bf16[32,4096]{1,0:T(8,128)(2,1)S(1)}, u32[]{:S(2)}, u32[]{:S(2)}) collective-permute-start(bf16[32,4096]{1,0:T(8,128)(2,1)S(1)} %broadcast_select_fusion.7), channel_id=1, source_target_pairs={{0,2},{2,4},{4,6},{6,7},{7,5},{5,3},{3,1},{1,0},{8,10},{10,12},{12... | collective-permute-start | bytes 786440 | tf_op jit(solution)/shard_map/ppermute | solution.py:130
  73.9 12.5 %collective-permute-start.6 = (bf16[32,4096]{1,0:T(8,128)(2,1)S(1)}, bf16[32,4096]{1,0:T(8,128)(2,1)S(1)}, u32[]{:S(2)}, u32[]{:S(2)}) collective-permute-start(bf16[32,4096]{1,0:T(8,128)(2,1)S(1)} %collective-permute-done), channel_id=1, source_target_pairs={{0,2},{2,4},{4,6},{6,7},{7,5},{5,3},{3,1},{1,0},{8,10},{10,12},{12... | collective-permute-start | bytes 786440 | tf_op jit(solution)/shard_map/ppermute | solution.py:130
  75.5 11.0 %collective-permute-start.8 = (bf16[32,4096]{1,0:T(8,128)(2,1)S(1)}, bf16[32,4096]{1,0:T(8,128)(2,1)S(1)}, u32[]{:S(2)}, u32[]{:S(2)}) collective-permute-start(bf16[32,4096]{1,0:T(8,128)(2,1)S(1)} %broadcast_select_fusion.6), channel_id=1, source_target_pairs={{2,0},{4,2},{6,4},{7,6},{5,7},{3,5},{1,3},{0,1},{10,8},{12,10},{14... | collective-permute-start | bytes 786440 | tf_op jit(solution)/shard_map/ppermute | solution.py:133
  76.0 13.3 %collective-permute-start.9 = (bf16[32,4096]{1,0:T(8,128)(2,1)S(1)}, bf16[32,4096]{1,0:T(8,128)(2,1)S(1)}, u32[]{:S(2)}, u32[]{:S(2)}) collective-permute-start(bf16[32,4096]{1,0:T(8,128)(2,1)S(1)} %collective-permute-done.3), channel_id=1, source_target_pairs={{2,0},{4,2},{6,4},{7,6},{5,7},{3,5},{1,3},{0,1},{10,8},{12,10},{14... | collective-permute-start | bytes 786440 | tf_op jit(solution)/shard_map/ppermute | solution.py:133
  98.2 5.8 %copy-start.6 = (bf16[4096,2048]{1,0:T(8,128)(2,1)}, bf16[4096,2048]{1,0:T(8,128)(2,1)S(1)}, u32[]{:S(2)}) copy-start(bf16[4096,2048]{1,0:T(8,128)(2,1)S(1)} %get-tuple-element.46.refs_2_) | copy-start | bytes 50331652
  106.5 59.3 %collective-permute-start.14 = (bf16[32,4096]{1,0:T(8,128)(2,1)S(1)}, bf16[32,4096]{1,0:T(8,128)(2,1)S(1)}, u32[]{:S(2)}, u32[]{:S(2)}) collective-permute-start(bf16[32,4096]{1,0:T(8,128)(2,1)S(1)} %get-tuple-element.96), channel_id=1, source_target_pairs={{2,0},{4,2},{6,4},{7,6},{5,7},{3,5},{1,3},{0,1},{10,8},{12,10},{14... | collective-permute-start | bytes 786440 | tf_op jit(solution)/shard_map/ppermute | solution.py:133
  107.1 50.0 %collective-permute-start.12 = (bf16[32,4096]{1,0:T(8,128)(2,1)S(1)}, bf16[32,4096]{1,0:T(8,128)(2,1)S(1)}, u32[]{:S(2)}, u32[]{:S(2)}) collective-permute-start(bf16[32,4096]{1,0:T(8,128)(2,1)S(1)} %get-tuple-element.99), channel_id=1, source_target_pairs={{0,2},{2,4},{4,6},{6,7},{7,5},{5,3},{3,1},{1,0},{8,10},{10,12},{12... | collective-permute-start | bytes 786440 | tf_op jit(solution)/shard_map/ppermute | solution.py:130
  117.5 5.8 %copy-start.8 = (bf16[4096,2048]{1,0:T(8,128)(2,1)}, bf16[4096,2048]{1,0:T(8,128)(2,1)S(1)}, u32[]{:S(2)}) copy-start(bf16[4096,2048]{1,0:T(8,128)(2,1)S(1)} %get-tuple-element.49.refs_2_) | copy-start | bytes 50331652
  124.6 32.9 %collective-permute-start.16 = (bf16[32,4096]{1,0:T(8,128)(2,1)S(1)}, bf16[32,4096]{1,0:T(8,128)(2,1)S(1)}, u32[]{:S(2)}, u32[]{:S(2)}) collective-permute-start(bf16[32,4096]{1,0:T(8,128)(2,1)S(1)} %broadcast_select_fusion.1), channel_id=1, source_target_pairs={{0,2},{2,4},{4,6},{6,7},{7,5},{5,3},{3,1},{1,0},{8,10},{10,12},{12... | collective-permute-start | bytes 786440 | tf_op jit(solution)/shard_map/ppermute | solution.py:130
  141.0 81.5 %collective-permute-start.10 = (f32[2,128,1024]{2,1,0:T(8,128)S(1)}, f32[2,128,1024]{2,1,0:T(8,128)S(1)}, u32[]{:S(2)}, u32[]{:S(2)}) collective-permute-start(f32[2,128,1024]{2,1,0:T(8,128)S(1)} %get-tuple-element.54.refs_4_), channel_id=1, source_target_pairs={{0,8},{8,0},{1,9},{9,1},{2,10},{10,2},{3,11},{11,3},{4,12},{12,4},... | collective-permute-start | bytes 3145736 | tf_op jit(solution)/shard_map/ppermute | solution.py:136
  157.0 8.7 %collective-permute-start.17 = (bf16[32,4096]{1,0:T(8,128)(2,1)S(1)}, bf16[32,4096]{1,0:T(8,128)(2,1)S(1)}, u32[]{:S(2)}, u32[]{:S(2)}) collective-permute-start(bf16[32,4096]{1,0:T(8,128)(2,1)S(1)} %broadcast_select_fusion), channel_id=1, source_target_pairs={{2,0},{4,2},{6,4},{7,6},{5,7},{3,5},{1,3},{0,1},{10,8},{12,10},{14... | collective-permute-start | bytes 786440 | tf_op jit(solution)/shard_map/ppermute | solution.py:133
  165.8 20.1 %collective-permute-start.15 = (bf16[32,4096]{1,0:T(8,128)(2,1)S(1)}, bf16[32,4096]{1,0:T(8,128)(2,1)S(1)}, u32[]{:S(2)}, u32[]{:S(2)}) collective-permute-start(bf16[32,4096]{1,0:T(8,128)(2,1)S(1)} %get-tuple-element.93), channel_id=1, source_target_pairs={{2,0},{4,2},{6,4},{7,6},{5,7},{3,5},{1,3},{0,1},{10,8},{12,10},{14... | collective-permute-start | bytes 786440 | tf_op jit(solution)/shard_map/ppermute | solution.py:133
  166.3 19.6 %collective-permute-start.13 = (bf16[32,4096]{1,0:T(8,128)(2,1)S(1)}, bf16[32,4096]{1,0:T(8,128)(2,1)S(1)}, u32[]{:S(2)}, u32[]{:S(2)}) collective-permute-start(bf16[32,4096]{1,0:T(8,128)(2,1)S(1)} %get-tuple-element.95), channel_id=1, source_target_pairs={{0,2},{2,4},{4,6},{6,7},{7,5},{5,3},{3,1},{1,0},{8,10},{10,12},{12... | collective-permute-start | bytes 786440 | tf_op jit(solution)/shard_map/ppermute | solution.py:130
  176.8 9.2 %collective-permute-start.18 = (f32[2,128,1024]{2,1,0:T(8,128)S(1)}, f32[2,128,1024]{2,1,0:T(8,128)S(1)}, u32[]{:S(2)}, u32[]{:S(2)}) collective-permute-start(f32[2,128,1024]{2,1,0:T(8,128)S(1)} %get-tuple-element.60.refs_4_), channel_id=1, source_target_pairs={{0,8},{8,0},{1,9},{9,1},{2,10},{10,2},{3,11},{11,3},{4,12},{12,4},... | collective-permute-start | bytes 3145736 | tf_op jit(solution)/shard_map/ppermute | solution.py:136
  186.3 36.4 %collective-permute-start.19 = (bf16[128,1024]{1,0:T(8,128)(2,1)S(1)}, bf16[128,1024]{1,0:T(8,128)(2,1)S(1)}, u32[]{:S(2)}, u32[]{:S(2)}) collective-permute-start(bf16[128,1024]{1,0:T(8,128)(2,1)S(1)} %fusion.3.refs_1_), channel_id=1, source_target_pairs={{0,8},{8,0},{1,9},{9,1},{2,10},{10,2},{3,11},{11,3},{4,12},{12,4},... | collective-permute-start | bytes 786440 | tf_op jit(solution)/shard_map/ppermute | solution.py:136
  202.0 12.0 %copy-start.19 = (bf16[4096,2048]{1,0:T(8,128)(2,1)}, bf16[4096,2048]{1,0:T(8,128)(2,1)S(1)}, u32[]{:S(2)}) copy-start(bf16[4096,2048]{1,0:T(8,128)(2,1)S(1)} %get-tuple-element.65.refs_3_) | copy-start | bytes 50331652
  202.0 47.2 %collective-permute-start.20 = (f32[2,64,1024]{2,1,0:T(8,128)S(1)}, f32[2,64,1024]{2,1,0:T(8,128)S(1)}, u32[]{:S(2)}, u32[]{:S(2)}) collective-permute-start(f32[2,64,1024]{2,1,0:T(8,128)S(1)} %get-tuple-element.66.refs_4_), channel_id=1, source_target_pairs={{0,8},{8,0},{1,9},{9,1},{2,10},{10,2},{3,11},{11,3},{4,12},{12,4},... | collective-permute-start | bytes 1572872 | tf_op jit(solution)/shard_map/ppermute | solution.py:136
  202.0 37.9 %slice-start = ((s8[16777216]{0:T(1024)(128)(4,1)}), s8[4194304]{0:T(1024)(128)(4,1)S(1)}, s32[]{:S(2)}) async-start(s8[16777216]{0:T(1024)(128)(4,1)} %bitcast.50), calls=%async_computation | async-start | bytes 8388608
  202.0 37.9 %slice-start.1 = ((s8[16777216]{0:T(1024)(128)(4,1)}), s8[4194304]{0:T(1024)(128)(4,1)S(1)}, s32[]{:S(2)}) async-start(s8[16777216]{0:T(1024)(128)(4,1)} %bitcast.50), calls=%async_computation.1 | async-start | bytes 8388608
  202.0 37.9 %slice-start.2 = ((s8[16777216]{0:T(1024)(128)(4,1)}), s8[4194304]{0:T(1024)(128)(4,1)S(1)}, s32[]{:S(2)}) async-start(s8[16777216]{0:T(1024)(128)(4,1)} %bitcast.50), calls=%async_computation.2 | async-start | bytes 8388608
  214.0 8.5 %copy-start.21 = (bf16[2048,4096]{1,0:T(8,128)(2,1)}, bf16[2048,4096]{1,0:T(8,128)(2,1)S(1)}, u32[]{:S(2)}) copy-start(bf16[2048,4096]{1,0:T(8,128)(2,1)S(1)} %shard_map.57.refs_3_) | copy-start | bytes 50331652
  222.7 17.2 %slice-start.3 = ((s8[16777216]{0:T(1024)(128)(4,1)}), s8[4194304]{0:T(1024)(128)(4,1)S(1)}, s32[]{:S(2)}) async-start(s8[16777216]{0:T(1024)(128)(4,1)} %bitcast.50), calls=%async_computation.3 | async-start | bytes 8388608
  222.7 5.9 %copy-start.22 = (bf16[2048,4096]{1,0:T(8,128)(2,1)S(1)}, bf16[2048,4096]{1,0:T(8,128)(2,1)}, u32[]{:S(2)}) copy-start(bf16[2048,4096]{1,0:T(8,128)(2,1)} %copy-done.21) | copy-start | bytes 50331652
  249.3 1.4 collective-permute-start.21
  249.5 30.1 %collective-permute-start.11 = (bf16[128,1024]{1,0:T(8,128)(2,1)S(1)}, bf16[128,1024]{1,0:T(8,128)(2,1)S(1)}, u32[]{:S(2)}, u32[]{:S(2)}) collective-permute-start(bf16[128,1024]{1,0:T(8,128)(2,1)S(1)} %fusion.5.refs_1_), channel_id=1, source_target_pairs={{0,8},{8,0},{1,9},{9,1},{2,10},{10,2},{3,11},{11,3},{4,12},{12,4},... | collective-permute-start | bytes 786440 | tf_op jit(solution)/shard_map/ppermute | solution.py:136
  267.5 9.2 %collective-permute-start.22 = (bf16[32,4096]{1,0:T(8,128)(2,1)S(1)}, bf16[32,4096]{1,0:T(8,128)(2,1)S(1)}, u32[]{:S(2)}, u32[]{:S(2)}) collective-permute-start(bf16[32,4096]{1,0:T(8,128)(2,1)S(1)} %get-tuple-element.88), channel_id=1, source_target_pairs={{2,0},{4,2},{6,4},{7,6},{5,7},{3,5},{1,3},{0,1},{10,8},{12,10},{14... | collective-permute-start | bytes 786440 | tf_op jit(solution)/shard_map/ppermute | solution.py:133
  268.0 9.2 %collective-permute-start.32 = (bf16[32,4096]{1,0:T(8,128)(2,1)S(1)}, bf16[32,4096]{1,0:T(8,128)(2,1)S(1)}, u32[]{:S(2)}, u32[]{:S(2)}) collective-permute-start(bf16[32,4096]{1,0:T(8,128)(2,1)S(1)} %get-tuple-element.89), channel_id=1, source_target_pairs={{0,2},{2,4},{4,6},{6,7},{7,5},{5,3},{3,1},{1,0},{8,10},{10,12},{12... | collective-permute-start | bytes 786440 | tf_op jit(solution)/shard_map/ppermute | solution.py:130
  269.6 27.1 %collective-permute-start.26 = (bf16[32,4096]{1,0:T(8,128)(2,1)S(1)}, bf16[32,4096]{1,0:T(8,128)(2,1)S(1)}, u32[]{:S(2)}, u32[]{:S(2)}) collective-permute-start(bf16[32,4096]{1,0:T(8,128)(2,1)S(1)} %get-tuple-element.86), channel_id=1, source_target_pairs={{0,2},{2,4},{4,6},{6,7},{7,5},{5,3},{3,1},{1,0},{8,10},{10,12},{12... | collective-permute-start | bytes 786440 | tf_op jit(solution)/shard_map/ppermute | solution.py:130
  271.2 25.6 %collective-permute-start.29 = (bf16[32,4096]{1,0:T(8,128)(2,1)S(1)}, bf16[32,4096]{1,0:T(8,128)(2,1)S(1)}, u32[]{:S(2)}, u32[]{:S(2)}) collective-permute-start(bf16[32,4096]{1,0:T(8,128)(2,1)S(1)} %get-tuple-element.87), channel_id=1, source_target_pairs={{2,0},{4,2},{6,4},{7,6},{5,7},{3,5},{1,3},{0,1},{10,8},{12,10},{14... | collective-permute-start | bytes 786440 | tf_op jit(solution)/shard_map/ppermute | solution.py:133
  277.3 19.4 %collective-permute-start.23 = (bf16[32,4096]{1,0:T(8,128)(2,1)S(1)}, bf16[32,4096]{1,0:T(8,128)(2,1)S(1)}, u32[]{:S(2)}, u32[]{:S(2)}) collective-permute-start(bf16[32,4096]{1,0:T(8,128)(2,1)S(1)} %get-tuple-element.84), channel_id=1, source_target_pairs={{2,0},{4,2},{6,4},{7,6},{5,7},{3,5},{1,3},{0,1},{10,8},{12,10},{14... | collective-permute-start | bytes 786440 | tf_op jit(solution)/shard_map/ppermute | solution.py:133
  277.8 18.9 %collective-permute-start.33 = (bf16[32,4096]{1,0:T(8,128)(2,1)S(1)}, bf16[32,4096]{1,0:T(8,128)(2,1)S(1)}, u32[]{:S(2)}, u32[]{:S(2)}) collective-permute-start(bf16[32,4096]{1,0:T(8,128)(2,1)S(1)} %get-tuple-element.85), channel_id=1, source_target_pairs={{0,2},{2,4},{4,6},{6,7},{7,5},{5,3},{3,1},{1,0},{8,10},{10,12},{12... | collective-permute-start | bytes 786440 | tf_op jit(solution)/shard_map/ppermute | solution.py:130
  279.6 19.4 %collective-permute-start.5 = (bf16[192,1024]{1,0:T(8,128)(2,1)S(1)}, bf16[192,1024]{1,0:T(8,128)(2,1)S(1)}, u32[]{:S(2)}, u32[]{:S(2)}) collective-permute-start(bf16[192,1024]{1,0:T(8,128)(2,1)S(1)} %fusion.1.refs_1_), channel_id=1, source_target_pairs={{0,8},{8,0},{1,9},{9,1},{2,10},{10,2},{3,11},{11,3},{4,12},{12,4},... | collective-permute-start | bytes 1179656 | tf_op jit(solution)/shard_map/ppermute | solution.py:136
  297.0 16.4 %collective-permute-start.24 = (bf16[32,4096]{1,0:T(8,128)(2,1)S(1)}, bf16[32,4096]{1,0:T(8,128)(2,1)S(1)}, u32[]{:S(2)}, u32[]{:S(2)}) collective-permute-start(bf16[32,4096]{1,0:T(8,128)(2,1)S(1)} %get-tuple-element.80), channel_id=1, source_target_pairs={{2,0},{4,2},{6,4},{7,6},{5,7},{3,5},{1,3},{0,1},{10,8},{12,10},{14... | collective-permute-start | bytes 786440 | tf_op jit(solution)/shard_map/ppermute | solution.py:133
  297.5 15.8 %collective-permute-start.27 = (bf16[32,4096]{1,0:T(8,128)(2,1)S(1)}, bf16[32,4096]{1,0:T(8,128)(2,1)S(1)}, u32[]{:S(2)}, u32[]{:S(2)}) collective-permute-start(bf16[32,4096]{1,0:T(8,128)(2,1)S(1)} %get-tuple-element.83), channel_id=1, source_target_pairs={{0,2},{2,4},{4,6},{6,7},{7,5},{5,3},{3,1},{1,0},{8,10},{10,12},{12... | collective-permute-start | bytes 786440 | tf_op jit(solution)/shard_map/ppermute | solution.py:130
  311.3 9.2 %collective-permute-start.34 = (bf16[32,4096]{1,0:T(8,128)(2,1)S(1)}, bf16[32,4096]{1,0:T(8,128)(2,1)S(1)}, u32[]{:S(2)}, u32[]{:S(2)}) collective-permute-start(bf16[32,4096]{1,0:T(8,128)(2,1)S(1)} %get-tuple-element.81), channel_id=1, source_target_pairs={{0,2},{2,4},{4,6},{6,7},{7,5},{5,3},{3,1},{1,0},{8,10},{10,12},{12... | collective-permute-start | bytes 786440 | tf_op jit(solution)/shard_map/ppermute | solution.py:130
  312.9 9.2 %collective-permute-start.30 = (bf16[32,4096]{1,0:T(8,128)(2,1)S(1)}, bf16[32,4096]{1,0:T(8,128)(2,1)S(1)}, u32[]{:S(2)}, u32[]{:S(2)}) collective-permute-start(bf16[32,4096]{1,0:T(8,128)(2,1)S(1)} %get-tuple-element.82), channel_id=1, source_target_pairs={{2,0},{4,2},{6,4},{7,6},{5,7},{3,5},{1,3},{0,1},{10,8},{12,10},{14... | collective-permute-start | bytes 786440 | tf_op jit(solution)/shard_map/ppermute | solution.py:133
  313.4 13.0 %collective-permute-start.25 = (bf16[32,4096]{1,0:T(8,128)(2,1)S(1)}, bf16[32,4096]{1,0:T(8,128)(2,1)S(1)}, u32[]{:S(2)}, u32[]{:S(2)}) collective-permute-start(bf16[32,4096]{1,0:T(8,128)(2,1)S(1)} %get-tuple-element.78), channel_id=1, source_target_pairs={{2,0},{4,2},{6,4},{7,6},{5,7},{3,5},{1,3},{0,1},{10,8},{12,10},{14... | collective-permute-start | bytes 786440 | tf_op jit(solution)/shard_map/ppermute | solution.py:133
  314.0 12.4 %collective-permute-start.28 = (bf16[32,4096]{1,0:T(8,128)(2,1)S(1)}, bf16[32,4096]{1,0:T(8,128)(2,1)S(1)}, u32[]{:S(2)}, u32[]{:S(2)}) collective-permute-start(bf16[32,4096]{1,0:T(8,128)(2,1)S(1)} %get-tuple-element.79), channel_id=1, source_target_pairs={{0,2},{2,4},{4,6},{6,7},{7,5},{5,3},{3,1},{1,0},{8,10},{10,12},{12... | collective-permute-start | bytes 786440 | tf_op jit(solution)/shard_map/ppermute | solution.py:130
  326.6 7.0 %collective-permute-start.35 = (bf16[32,4096]{1,0:T(8,128)(2,1)S(1)}, bf16[32,4096]{1,0:T(8,128)(2,1)S(1)}, u32[]{:S(2)}, u32[]{:S(2)}) collective-permute-start(bf16[32,4096]{1,0:T(8,128)(2,1)S(1)} %get-tuple-element.76), channel_id=1, source_target_pairs={{0,2},{2,4},{4,6},{6,7},{7,5},{5,3},{3,1},{1,0},{8,10},{10,12},{12... | collective-permute-start | bytes 786440 | tf_op jit(solution)/shard_map/ppermute | solution.py:130
  328.1 6.7 %collective-permute-start.31 = (bf16[32,4096]{1,0:T(8,128)(2,1)S(1)}, bf16[32,4096]{1,0:T(8,128)(2,1)S(1)}, u32[]{:S(2)}, u32[]{:S(2)}) collective-permute-start(bf16[32,4096]{1,0:T(8,128)(2,1)S(1)} %get-tuple-element.77), channel_id=1, source_target_pairs={{2,0},{4,2},{6,4},{7,6},{5,7},{3,5},{1,3},{0,1},{10,8},{12,10},{14... | collective-permute-start | bytes 786440 | tf_op jit(solution)/shard_map/ppermute | solution.py:133
  (22 other events, 127.5 us)

commit v3 on v0

v3 whole, which is shorter than its diff:
```python
import jax
import jax.numpy as jnp
from jax import lax
from jax.experimental import pallas as pl
from jax.experimental.pallas import tpu as pltpu
from jax.sharding import PartitionSpec as P

F32, BF16 = jnp.float32, jnp.bfloat16
ANY = pl.BlockSpec(memory_space=pl.ANY)
VMEM = pl.BlockSpec(memory_space=pltpu.VMEM)


def ring_of(n):
    return list(range(0, n, 2)) + list(range(n - 1, 0, -2))


def in_hbm(x):
    return pltpu.with_memory_space_constraint(x, pltpu.HBM)


def params(flops, read):
    return dict(
        compiler_params=pltpu.CompilerParams(vmem_limit_bytes=24 << 20),
        cost_estimate=pl.CostEstimate(
            flops=flops, bytes_accessed=read, transcendentals=0
        ),
    )


def gate_up(x, gate_weight, up_weight, part, after):
    m, k = x.shape
    w = gate_weight.shape[1] // 2
    tile, deep = min(w, 256), k // 2
    tiles = w // tile

    def body(part_ref, x_ref, g_ref, u_ref, *refs):
        o_ref = refs[-1]
        step = pl.program_id(1)
        rows = x_ref[:, pl.ds(pl.multiple_of(step * deep, deep), deep)]
        g = jnp.dot(rows, g_ref[...], preferred_element_type=F32)
        u = jnp.dot(rows, u_ref[...], preferred_element_type=F32)

        @pl.when(step == 0)
        def _():
            o_ref[0] = g
            o_ref[1] = u

        @pl.when(step != 0)
        def _():
            o_ref[0] += g
            o_ref[1] += u

    weight = pl.BlockSpec((deep, tile), lambda j, s, part: (s, part[0] * tiles + j))
    return pl.pallas_call(
        body,
        grid_spec=pltpu.PrefetchScalarGridSpec(
            num_scalar_prefetch=1,
            grid=(tiles, 2),
            in_specs=[VMEM, weight, weight] + [ANY] * len(after),
            out_specs=pl.BlockSpec((2, m, tile), lambda j, s, part: (0, 0, j)),
        ),
        out_shape=jax.ShapeDtypeStruct((2, m, w), F32),
        **params(4 * m * k * w, 4 * k * w),
    )(part, x, in_hbm(gate_weight), in_hbm(up_weight), *after)


def down(mine, others, weight, part, cut):
    m, w = mine.shape
    n = weight.shape[1]
    tile = 512

    def body(part_ref, a_ref, b_ref, d_ref, l_ref, r_ref, o_ref, h_ref):
        @pl.when(pl.program_id(0) == 0)
        def _():
            h_ref[:, pl.ds(pl.multiple_of(part_ref[0] * w, w), w)] = a_ref[...]
            h_ref[:, pl.ds(pl.multiple_of(w - part_ref[0] * w, w), w)] = b_ref[...]

        out = jnp.dot(h_ref[...], d_ref[...], preferred_element_type=F32)
        l_ref[...] = out[:cut].astype(BF16)
        r_ref[...] = out[cut : 2 * cut].astype(BF16)
        o_ref[...] = out[2 * cut :]

    return pl.pallas_call(
        body,
        grid_spec=pltpu.PrefetchScalarGridSpec(
            num_scalar_prefetch=1,
            grid=(n // tile,),
            in_specs=[VMEM, VMEM, pl.BlockSpec((2 * w, tile), lambda j, part: (0, j))],
            out_specs=[
                pl.BlockSpec((r, tile), lambda j, part: (0, j))
                for r in (cut, cut, m - 2 * cut)
            ],
            scratch_shapes=[pltpu.VMEM((m, 2 * w), BF16)],
        ),
        out_shape=[
            jax.ShapeDtypeStruct((cut, n), BF16),
            jax.ShapeDtypeStruct((cut, n), BF16),
            jax.ShapeDtypeStruct((m - 2 * cut, n), F32),
        ],
        **params(4 * m * w * n, 4 * w * n),
    )(part, mine, others, in_hbm(weight))


def gate(*arrays, after=()):
    return pl.pallas_call(
        lambda *refs: None,
        in_specs=[ANY] * (len(arrays) + len(after)),
        out_specs=[ANY] * len(arrays),
        out_shape=[jax.ShapeDtypeStruct(x.shape, x.dtype) for x in arrays],
        input_output_aliases={i: i for i in range(len(arrays))},
        cost_estimate=pl.CostEstimate(flops=0, bytes_accessed=0, transcendentals=0),
    )(*arrays, *after)


def make_shards(n):
    ring = ring_of(n)
    half = n // 2
    to_right = [(ring[i], ring[(i + 1) % n]) for i in range(n)]
    to_left = [(ring[(i + 1) % n], ring[i]) for i in range(n)]
    swap = [(0, 1), (1, 0)]

    def right(x):
        return lax.ppermute(x, "gy", to_right)

    def left(x):
        return lax.ppermute(x, "gy", to_left)

    def other(x):
        return lax.ppermute(x, "gx", swap)

    def shards(tokens, gate_weight, up_weight, down_weight):
        rows = tokens.shape[0]
        cut = rows // 2
        core = lax.axis_index("gx").astype(jnp.int32)
        keep, give = core.reshape(1), (1 - core).reshape(1)
        a, b = tokens[:cut], tokens[cut:]

        def kernels(x, after):
            theirs = gate_up(x, gate_weight, up_weight, give, after)
            (theirs,) = yield [theirs]
            got = other(theirs)
            ours = gate_up(x, gate_weight, up_weight, keep, [theirs])
            ours, got = yield [ours, got]
            h = (jax.nn.silu(ours[0] + got[0]) * (ours[1] + got[1])).astype(BF16)
            yield down(h, other(h), down_weight, keep, cut)

        def gather(r, l, hops):
            found = []
            for _ in range(hops):
                r, l = right(r), left(l)
                found = [r, l] + found
            return found

        def stack(pieces):
            return jnp.concatenate(pieces, axis=0)

        def add(part, block):
            return (part + block.astype(F32)).astype(BF16)

        early = gather(a, b, half - 1)
        early[0], early[1], r, l = gate(early[0], early[1], b, a)
        far = gather(early[0], early[1], 1) + early
        steps = kernels(stack(far), [])
        near, step = [], next(steps)
        for hop in range(half - 1):
            r, l = right(r), left(l)
            if hop < 2:
                r, l, *back = gate(r, l, *step)
                step = steps.send(back)
            elif hop < half - 2:
                r, l = gate(r, l)
            near = [r, l] + near
        l, r, sums = step

        steps = kernels(stack(near + [a, b]), [sums])
        step = next(steps)
        l, r = left(l), right(r)
        for hop in range(half - 1):
            if hop < 2:
                l, r, *back = gate(l, r, *step)
                step = steps.send(back)
            else:
                l, r = gate(l, r, after=step if hop == 2 else ())
            i = 2 * hop * cut
            l = left(add(sums[i : i + cut], l))
            r = right(add(sums[i + cut : i + 2 * cut], r))
        far_a, far_b = l, r
        l, r, sums = step
        l, r = left(l), right(r)
        for hop in range(half - 2):
            if hop == 0:
                l, r, far_a, far_b = gate(l, r, far_a, far_b)
            else:
                l, r = gate(l, r)
            i = 2 * hop * cut
            l = left(add(sums[i : i + cut], l))
            r = right(add(sums[i + cut : i + 2 * cut], r))
        l, r = gate(l, r)
        total_a = sums[-2 * cut : -cut] + far_a.astype(F32) + r.astype(F32)
        total_b = sums[-cut:] + far_b.astype(F32) + l.astype(F32)
        return jnp.concatenate([total_a, total_b], axis=0).astype(BF16)

    return shards


def solution(mesh):
    return jax.shard_map(
        make_shards(mesh.shape["gy"]),
        mesh=mesh,
        in_specs=(P(("groups", "gy"), "gx"), P("gx", "gy"), P("gx", "gy"), P("gy", "gx")),
        out_specs=P(("groups", "gy"), "gx"),
        check_vma=False,
    )
```

time: 328 us -> 183 us (0.56)
  waiting for transfers between devices: 267 us -> 52.3 us
  Pallas kernels: 0 us -> 64.7 us
  matrix products: 42.4 us -> 0 us
  starting transfers between devices: 0.08 us -> 30 us
  local copies, waits for them, and re-layouts: 0.01 us -> 21.1 us
  between operations: 13.1 us -> 0.48 us
  other arithmetic: 5.87 us -> 13.7 us
    reduce_scatter x1 -> x0, waiting for transfers between devices: 150 us -> none  [shards(): lax.psum_scatter(jnp.dot(hidden, down_weight, preferred_element_type=jnp....]
    all_gather x1 -> x0, waiting for transfers between devices: 78.3 us -> none  [shards(): piece = lax.all_gather(tokens, 'gy', axis=0, tiled=True)]
    pallas_call x0 -> x15, Pallas kernels: none -> 64.7 us  [the longest x4 42.6 us: gate_up(): pl.pallas_call(body, grid_spec=pltpu.PrefetchScalarGridSpec(num_scalar_pr...]
    ppermute x0 -> x32, waiting for transfers between devices: none -> 52.3 us  [the longest x14 28.9 us: left(): return lax.ppermute(x, 'gy', to_left)]
    dot_general x3 -> x0, matrix products: 42.4 us -> none  [the longest x1 16.9 us: shards(): jnp.dot(hidden, down_weight, preferred_element_type=jnp.float32)]
    psum x1 -> x0, waiting for transfers between devices: 37.2 us -> none  [shards(): summed = lax.psum(partial_value, 'gx')]
    ppermute x0 -> x32, starting transfers between devices: none -> 30 us  [the longest x14 16.8 us: right(): return lax.ppermute(x, 'gy', to_right)]
    unnamed x2 -> x85, local copies, waits for them, and re-layouts: 0.01 us -> 20 us
  transfers between devices with their start and end apart: 3 -> 32, of which waited for: 3 -> 15; matrix products, arithmetic and copies ran while one was open for 0% -> 5% of each run, Pallas kernels for 0% -> 29%
where the time goes in v3:
time: 183 us; the launch traced here: 182 us
  Pallas kernels  64.7 us (35%)
  waiting for transfers between devices  52.3 us (29%)
  starting transfers between devices  30 us (16%)
  local copies, waits for them, and re-layouts  21.1 us (12%)
  other arithmetic  13.7 us (7%)
    pallas_call x4, Pallas kernels, gate_up(): pl.pallas_call(body, grid_spec=pltpu.PrefetchScalarGridSpec(num_scalar_pr...  42.6 us
    ppermute x14, waiting for transfers between devices, left(): return lax.ppermute(x, 'gy', to_left)  28.9 us
    ppermute x14, waiting for transfers between devices, right(): return lax.ppermute(x, 'gy', to_right)  23.4 us
    pallas_call x2, Pallas kernels, down(): pl.pallas_call(body, grid_spec=pltpu.PrefetchScalarGridSpec(num_scalar_pr...  22 us
    unnamed x85, local copies, waits for them, and re-layouts  20 us
    ppermute x14, starting transfers between devices, right(): return lax.ppermute(x, 'gy', to_right)  16.8 us
    ppermute x14, starting transfers between devices, left(): return lax.ppermute(x, 'gy', to_left)  13 us
    convert_element_type x5, other arithmetic, add(): return (part + block.astype(F32)).astype(BF16)  6.15 us
  transfers between devices with their start and end apart: 32, of which 15 were waited for; matrix products, arithmetic and copies ran while one was open for 5% of the time, Pallas kernels for 29%

profile of v3, /device:TPU:0, one launch (start us, length us, event | category | flops | bytes accessed | tf_op | source)
XLA Modules:
  0.0 182.3 jit_solution(12878003284620364408)
XLA Ops:
  1.1 3.0 %collective-permute-start.3 = (bf16[32,4096]{1,0:T(8,128)(2,1)S(1)}, bf16[32,4096]{1,0:T(8,128)(2,1)S(1)}, u32[]{:S(2)}, u32[]{:S(2)}) collective-permute-start(bf16[32,4096]{1,0:T(8,128)(2,1)S(1)} %get-tuple-element.85.refs_2_), channel_id=1, source_target_pairs={{2,0},{4,2},{6,4},{7,6},{5,7},{3,5},{1,3},{0,1},{10,8},{12,10},{14... | collective-permute-start | bytes 786440 | tf_op jit(solution)/shard_map/ppermute | solution.py:126
  4.2 6.2 %collective-permute-done.3 = bf16[32,4096]{1,0:T(8,128)(2,1)S(1)} collective-permute-done((bf16[32,4096]{1,0:T(8,128)(2,1)S(1)}, bf16[32,4096]{1,0:T(8,128)(2,1)S(1)}, u32[]{:S(2)}, u32[]{:S(2)}) %collective-permute-start.3) | collective-permute-done | bytes 262176 | tf_op jit(solution)/shard_map/ppermute | solution.py:126
  10.5 1.7 collective-permute-start.4
  12.5 5.5 %collective-permute-done.4 = bf16[32,4096]{1,0:T(8,128)(2,1)S(1)} collective-permute-done((bf16[32,4096]{1,0:T(8,128)(2,1)S(1)}, bf16[32,4096]{1,0:T(8,128)(2,1)S(1)}, u32[]{:S(2)}, u32[]{:S(2)}) %collective-permute-start.4) | collective-permute-done | bytes 262176 | tf_op jit(solution)/shard_map/ppermute | solution.py:126
  18.0 1.4 collective-permute-start.5
  20.0 4.5 %collective-permute-done.5.refs_1_ = bf16[32,4096]{1,0:T(8,128)(2,1)S(1)} collective-permute-done((bf16[32,4096]{1,0:T(8,128)(2,1)S(1)}, bf16[32,4096]{1,0:T(8,128)(2,1)S(1)}, u32[]{:S(2)}, u32[]{:S(2)}) %collective-permute-start.5) | collective-permute-done | bytes 262176 | tf_op jit(solution)/shard_map/ppermute | solution.py:126
  24.5 1.2 collective-permute-done.2.refs_0_
  27.2 1.6 collective-permute-start.6
  29.2 1.3 collective-permute-start.9
  30.5 4.2 %collective-permute-done.8 = bf16[32,4096]{1,0:T(8,128)(2,1)} collective-permute-done((bf16[32,4096]{1,0:T(8,128)(2,1)}, bf16[32,4096]{1,0:T(8,128)(2,1)}, u32[]{:S(2)}, u32[]{:S(2)}) %collective-permute-start.8) | collective-permute-done | bytes 262176 | tf_op jit(solution)/shard_map/ppermute | solution.py:123
  35.7 3.4 %collective-permute-done.9 = bf16[32,4096]{1,0:T(8,128)(2,1)S(1)} collective-permute-done((bf16[32,4096]{1,0:T(8,128)(2,1)}, bf16[32,4096]{1,0:T(8,128)(2,1)S(1)}, u32[]{:S(2)}, u32[]{:S(2)}) %collective-permute-start.9) | collective-permute-done | bytes 262176 | tf_op jit(solution)/shard_map/ppermute | solution.py:126
  41.2 10.7 %shard_map.47.refs_2_ = f32[2,256,1024]{2,1,0:T(8,128)S(1)} custom-call(s32[1]{0:T(128)} %bitcast.1.part_ref, bf16[256,4096]{1,0:T(8,128)(2,1)S(1)} %constant_dynamic-update-slice_fusion.x_ref, bf16[4096,2048]{1,0:T(8,128)(2,1)} %g_ref.7, bf16[4096,2048]{1,0:T(8,128)(2,1)} %u_ref.7), custom_call_target="tpu_custom_call" | custom-call | flops 4294967296 | bytes 16777216 | tf_op jit(solution)/shard_map/pallas_call | solution.py:54
  51.9 1.3 copy-done
  54.7 1.6 collective-permute-start.10
  56.7 1.6 copy-done.1
  58.3 10.7 %shard_map.49.refs_2_ = f32[2,256,1024]{2,1,0:T(8,128)S(1)} custom-call(s32[1]{0:T(128)} %bitcast.part_ref, bf16[256,4096]{1,0:T(8,128)(2,1)S(1)} %constant_dynamic-update-slice_fusion.x_ref, bf16[4096,2048]{1,0:T(8,128)(2,1)} %g_ref.7, bf16[4096,2048]{1,0:T(8,128)(2,1)} %u_ref.7, f32[2,256,1024]{2,1,0:T(8,128)S(1)} %copy-done.1), custom_call_target="tpu_custom_call" | custom-call | flops 4294967296 | bytes 16777216 | tf_op jit(solution)/shard_map/pallas_call | solution.py:54
  69.0 1.3 copy-done.3
  71.1 1.6 collective-permute-start.16
  73.1 2.7 %fusion.4.a_ref = bf16[256,1024]{1,0:T(8,128)(2,1)S(1)} fusion(f32[2,256,1024]{2,1,0:T(8,128)} %get-tuple-element.47, f32[2,256,1024]{2,1,0:T(8,128)} %get-tuple-element.46), kind=kLoop, calls=%fused_computation.8 | loop fusion | flops 2097152 | bytes 4718592 | tf_op jit(solution)/shard_map/convert_element_type | solution.py:144
  76.0 3.5 %collective-permute-done.16 = bf16[32,4096]{1,0:T(8,128)(2,1)S(1)} collective-permute-done((bf16[32,4096]{1,0:T(8,128)(2,1)}, bf16[32,4096]{1,0:T(8,128)(2,1)S(1)}, u32[]{:S(2)}, u32[]{:S(2)}) %collective-permute-start.16) | collective-permute-done | bytes 262176 | tf_op jit(solution)/shard_map/ppermute | solution.py:123
  79.5 1.3 collective-permute-done.17
  81.0 11.4 %shard_map.51 = (bf16[32,4096]{1,0:T(8,128)(2,1)S(1)}, bf16[32,4096]{1,0:T(8,128)(2,1)S(1)}, f32[192,4096]{1,0:T(8,128)S(1)}) custom-call(s32[1]{0:T(128)} %bitcast.part_ref, bf16[256,1024]{1,0:T(8,128)(2,1)S(1)} %fusion.4.a_ref, bf16[256,1024]{1,0:T(8,128)(2,1)S(1)} %collective-permute-done.13.b_ref, bf16[2048,4096]{1,0:T(8,128)(2,1)} %d_ref.3), custom_call_target="tpu_custom_call" | custom-call | flops 4294967296 | bytes 16777216 | tf_op jit(solution)/shard_map/pallas_call | solution.py:83
  92.9 1.6 collective-permute-start.15
  94.5 10.7 %shard_map.52.refs_2_ = f32[2,256,1024]{2,1,0:T(8,128)S(1)} custom-call(s32[1]{0:T(128)} %bitcast.1.part_ref, bf16[256,4096]{1,0:T(8,128)(2,1)S(1)} %constant_dynamic-update-slice_fusion.8.x_ref, bf16[4096,2048]{1,0:T(8,128)(2,1)} %g_ref.7, bf16[4096,2048]{1,0:T(8,128)(2,1)} %u_ref.7, f32[192,4096]{1,0:T(8,128)S(1)} %get-tuple-element.48.refs_0_), custom_call_target="tpu_custom_call" | custom-call | flops 4294967296 | bytes 16777216 | tf_op jit(solution)/shard_map/pallas_call | solution.py:54
  105.2 1.4 copy-done.4
  107.3 1.3 add_convert_fusion.10
  108.6 1.6 collective-permute-start.19
  110.7 1.6 copy-done.10
  112.3 10.7 %shard_map.54.refs_2_ = f32[2,256,1024]{2,1,0:T(8,128)S(1)} custom-call(s32[1]{0:T(128)} %bitcast.part_ref, bf16[256,4096]{1,0:T(8,128)(2,1)S(1)} %copy-done.10, bf16[4096,2048]{1,0:T(8,128)(2,1)} %g_ref.7, bf16[4096,2048]{1,0:T(8,128)(2,1)} %u_ref.7, f32[2,256,1024]{2,1,0:T(8,128)S(1)} %copy-done.5), custom_call_target="tpu_custom_call" | custom-call | flops 4294967296 | bytes 16777216 | tf_op jit(solution)/shard_map/pallas_call | solution.py:54
  122.9 1.3 copy-done.2
  125.0 2.7 %fusion.a_ref = bf16[256,1024]{1,0:T(8,128)(2,1)S(1)} fusion(f32[2,256,1024]{2,1,0:T(8,128)} %get-tuple-element.57, f32[2,256,1024]{2,1,0:T(8,128)} %get-tuple-element.56), kind=kLoop, calls=%fused_computation.1 | loop fusion | flops 2097152 | bytes 4718592 | tf_op jit(solution)/shard_map/convert_element_type | solution.py:144
  128.8 1.6 collective-permute-start.25
  130.9 10.6 %shard_map.56 = (bf16[32,4096]{1,0:T(8,128)(2,1)S(1)}, bf16[32,4096]{1,0:T(8,128)(2,1)S(1)}, f32[192,4096]{1,0:T(8,128)S(1)}) custom-call(s32[1]{0:T(128)} %bitcast.part_ref, bf16[256,1024]{1,0:T(8,128)(2,1)S(1)} %fusion.a_ref, bf16[256,1024]{1,0:T(8,128)(2,1)S(1)} %collective-permute-done.21.b_ref, bf16[2048,4096]{1,0:T(8,128)(2,1)} %d_ref.3), custom_call_target="tpu_custom_call" | custom-call | flops 4294967296 | bytes 16777216 | tf_op jit(solution)/shard_map/pallas_call | solution.py:83
  141.6 1.7 copy-done.6
  145.5 1.6 add_convert_fusion.6
  147.1 1.6 collective-permute-start.27
  149.6 1.6 collective-permute-start.23
  151.2 5.2 %collective-permute-done.27.refs_3_ = bf16[32,4096]{1,0:T(8,128)(2,1)} collective-permute-done((bf16[32,4096]{1,0:T(8,128)(2,1)S(1)}, bf16[32,4096]{1,0:T(8,128)(2,1)}, u32[]{:S(2)}, u32[]{:S(2)}) %collective-permute-start.27) | collective-permute-done | bytes 262176 | tf_op jit(solution)/shard_map/ppermute | solution.py:123
  156.4 1.6 collective-permute-done.26.refs_2_
  158.0 4.2 %collective-permute-done.22.refs_0_ = bf16[32,4096]{1,0:T(8,128)(2,1)} collective-permute-done((bf16[32,4096]{1,0:T(8,128)(2,1)}, bf16[32,4096]{1,0:T(8,128)(2,1)}, u32[]{:S(2)}, u32[]{:S(2)}) %collective-permute-start.22) | collective-permute-done | bytes 262176 | tf_op jit(solution)/shard_map/ppermute | solution.py:126
  162.2 1.1 add_convert_fusion.4
  163.4 1.4 collective-permute-start.29
  165.4 4.9 %collective-permute-done.29.refs_1_ = bf16[32,4096]{1,0:T(8,128)(2,1)S(1)} collective-permute-done((bf16[32,4096]{1,0:T(8,128)(2,1)S(1)}, bf16[32,4096]{1,0:T(8,128)(2,1)S(1)}, u32[]{:S(2)}, u32[]{:S(2)}) %collective-permute-start.29) | collective-permute-done | bytes 262176 | tf_op jit(solution)/shard_map/ppermute | solution.py:123
  170.4 1.2 collective-permute-done.28.refs_0_
  171.5 1.1 add_convert_fusion.2
  173.6 1.2 collective-permute-start.30
  174.7 4.3 %collective-permute-done.31.refs_1_ = bf16[32,4096]{1,0:T(8,128)(2,1)S(1)} collective-permute-done((bf16[32,4096]{1,0:T(8,128)(2,1)S(1)}, bf16[32,4096]{1,0:T(8,128)(2,1)S(1)}, u32[]{:S(2)}, u32[]{:S(2)}) %collective-permute-start.31) | collective-permute-done | bytes 262176 | tf_op jit(solution)/shard_map/ppermute | solution.py:123
  180.1 1.3 add_convert_fusion.1
  (128 shorter events, 21.2 us)
Async XLA Ops:
  1.1 24.6 %copy-start.26 = (bf16[32,4096]{1,0:T(8,128)(2,1)}, bf16[32,4096]{1,0:T(8,128)(2,1)S(1)}, u32[]{:S(2)}) copy-start(bf16[32,4096]{1,0:T(8,128)(2,1)S(1)} %get-tuple-element.85.refs_2_) | copy-start | bytes 786436
  1.1 24.6 %copy-start.27 = (bf16[32,4096]{1,0:T(8,128)(2,1)}, bf16[32,4096]{1,0:T(8,128)(2,1)S(1)}, u32[]{:S(2)}) copy-start(bf16[32,4096]{1,0:T(8,128)(2,1)S(1)} %get-tuple-element.86.refs_3_) | copy-start | bytes 786436
  1.1 9.4 %collective-permute-start.3 = (bf16[32,4096]{1,0:T(8,128)(2,1)S(1)}, bf16[32,4096]{1,0:T(8,128)(2,1)S(1)}, u32[]{:S(2)}, u32[]{:S(2)}) collective-permute-start(bf16[32,4096]{1,0:T(8,128)(2,1)S(1)} %get-tuple-element.85.refs_2_), channel_id=1, source_target_pairs={{2,0},{4,2},{6,4},{7,6},{5,7},{3,5},{1,3},{0,1},{10,8},{12,10},{14... | collective-permute-start | bytes 786440 | tf_op jit(solution)/shard_map/ppermute | solution.py:126
  4.1 8.0 %collective-permute-start = (bf16[32,4096]{1,0:T(8,128)(2,1)S(1)}, bf16[32,4096]{1,0:T(8,128)(2,1)S(1)}, u32[]{:S(2)}, u32[]{:S(2)}) collective-permute-start(bf16[32,4096]{1,0:T(8,128)(2,1)S(1)} %get-tuple-element.86.refs_3_), channel_id=1, source_target_pairs={{0,2},{2,4},{4,6},{6,7},{7,5},{5,3},{3,1},{1,0},{8,10},{10,12},{12... | collective-permute-start | bytes 786440 | tf_op jit(solution)/shard_map/ppermute | solution.py:123
  10.5 7.5 %collective-permute-start.4 = (bf16[32,4096]{1,0:T(8,128)(2,1)S(1)}, bf16[32,4096]{1,0:T(8,128)(2,1)S(1)}, u32[]{:S(2)}, u32[]{:S(2)}) collective-permute-start(bf16[32,4096]{1,0:T(8,128)(2,1)S(1)} %collective-permute-done.3), channel_id=1, source_target_pairs={{2,0},{4,2},{6,4},{7,6},{5,7},{3,5},{1,3},{0,1},{10,8},{12,10},{14... | collective-permute-start | bytes 786440 | tf_op jit(solution)/shard_map/ppermute | solution.py:126
  12.2 7.2 %collective-permute-start.1 = (bf16[32,4096]{1,0:T(8,128)(2,1)S(1)}, bf16[32,4096]{1,0:T(8,128)(2,1)S(1)}, u32[]{:S(2)}, u32[]{:S(2)}) collective-permute-start(bf16[32,4096]{1,0:T(8,128)(2,1)S(1)} %collective-permute-done), channel_id=1, source_target_pairs={{0,2},{2,4},{4,6},{6,7},{7,5},{5,3},{3,1},{1,0},{8,10},{10,12},{12... | collective-permute-start | bytes 786440 | tf_op jit(solution)/shard_map/ppermute | solution.py:123
  18.0 6.6 %collective-permute-start.5 = (bf16[32,4096]{1,0:T(8,128)(2,1)S(1)}, bf16[32,4096]{1,0:T(8,128)(2,1)S(1)}, u32[]{:S(2)}, u32[]{:S(2)}) collective-permute-start(bf16[32,4096]{1,0:T(8,128)(2,1)S(1)} %collective-permute-done.4), channel_id=1, source_target_pairs={{2,0},{4,2},{6,4},{7,6},{5,7},{3,5},{1,3},{0,1},{10,8},{12,10},{14... | collective-permute-start | bytes 786440 | tf_op jit(solution)/shard_map/ppermute | solution.py:126
  19.3 11.1 %copy-start.34 = (bf16[32,4096]{1,0:T(8,128)(2,1)}, bf16[32,4096]{1,0:T(8,128)(2,1)S(1)}, u32[]{:S(2)}) copy-start(bf16[32,4096]{1,0:T(8,128)(2,1)S(1)} %collective-permute-done.1) | copy-start | bytes 786436
  19.3 6.4 %collective-permute-start.2 = (bf16[32,4096]{1,0:T(8,128)(2,1)S(1)}, bf16[32,4096]{1,0:T(8,128)(2,1)S(1)}, u32[]{:S(2)}, u32[]{:S(2)}) collective-permute-start(bf16[32,4096]{1,0:T(8,128)(2,1)S(1)} %collective-permute-done.1), channel_id=1, source_target_pairs={{0,2},{2,4},{4,6},{6,7},{7,5},{5,3},{3,1},{1,0},{8,10},{10,12},{12... | collective-permute-start | bytes 786440 | tf_op jit(solution)/shard_map/ppermute | solution.py:123
  26.4 8.3 %collective-permute-start.8 = (bf16[32,4096]{1,0:T(8,128)(2,1)}, bf16[32,4096]{1,0:T(8,128)(2,1)}, u32[]{:S(2)}, u32[]{:S(2)}) collective-permute-start(bf16[32,4096]{1,0:T(8,128)(2,1)} %get-tuple-element.41), channel_id=1, source_target_pairs={{0,2},{2,4},{4,6},{6,7},{7,5},{5,3},{3,1},{1,0},{8,10},{10,12},{12... | collective-permute-start | bytes 786440 | tf_op jit(solution)/shard_map/ppermute | solution.py:123
  27.2 26.1 %collective-permute-start.6 = (bf16[32,4096]{1,0:T(8,128)(2,1)}, bf16[32,4096]{1,0:T(8,128)(2,1)S(1)}, u32[]{:S(2)}, u32[]{:S(2)}) collective-permute-start(bf16[32,4096]{1,0:T(8,128)(2,1)} %get-tuple-element.39), channel_id=1, source_target_pairs={{0,2},{2,4},{4,6},{6,7},{7,5},{5,3},{3,1},{1,0},{8,10},{10,12},{12... | collective-permute-start | bytes 786440 | tf_op jit(solution)/shard_map/ppermute | solution.py:123
  28.7 24.5 %collective-permute-start.7 = (bf16[32,4096]{1,0:T(8,128)(2,1)}, bf16[32,4096]{1,0:T(8,128)(2,1)S(1)}, u32[]{:S(2)}, u32[]{:S(2)}) collective-permute-start(bf16[32,4096]{1,0:T(8,128)(2,1)} %get-tuple-element.40), channel_id=1, source_target_pairs={{2,0},{4,2},{6,4},{7,6},{5,7},{3,5},{1,3},{0,1},{10,8},{12,10},{14... | collective-permute-start | bytes 786440 | tf_op jit(solution)/shard_map/ppermute | solution.py:126
  29.2 9.9 %collective-permute-start.9 = (bf16[32,4096]{1,0:T(8,128)(2,1)}, bf16[32,4096]{1,0:T(8,128)(2,1)S(1)}, u32[]{:S(2)}, u32[]{:S(2)}) collective-permute-start(bf16[32,4096]{1,0:T(8,128)(2,1)} %get-tuple-element.42), channel_id=1, source_target_pairs={{2,0},{4,2},{6,4},{7,6},{5,7},{3,5},{1,3},{0,1},{10,8},{12,10},{14... | collective-permute-start | bytes 786440 | tf_op jit(solution)/shard_map/ppermute | solution.py:126
  34.7 6.4 %copy-start.35 = (bf16[32,4096]{1,0:T(8,128)(2,1)S(1)}, bf16[32,4096]{1,0:T(8,128)(2,1)}, u32[]{:S(2)}) copy-start(bf16[32,4096]{1,0:T(8,128)(2,1)} %copy-done.34) | copy-start | bytes 786436
  54.7 15.6 %collective-permute-start.12 = (f32[2,256,1024]{2,1,0:T(8,128)}, f32[2,256,1024]{2,1,0:T(8,128)}, u32[]{:S(2)}, u32[]{:S(2)}) collective-permute-start(f32[2,256,1024]{2,1,0:T(8,128)} %get-tuple-element.45.refs_0_), channel_id=1, source_target_pairs={{0,8},{8,0},{1,9},{9,1},{2,10},{10,2},{3,11},{11,3},{4,12},{12,4},... | collective-permute-start | bytes 6291464 | tf_op jit(solution)/shard_map/ppermute | solution.py:129
  54.7 15.6 %collective-permute-start.10 = (bf16[32,4096]{1,0:T(8,128)(2,1)}, bf16[32,4096]{1,0:T(8,128)(2,1)S(1)}, u32[]{:S(2)}, u32[]{:S(2)}) collective-permute-start(bf16[32,4096]{1,0:T(8,128)(2,1)} %get-tuple-element.43), channel_id=1, source_target_pairs={{0,2},{2,4},{4,6},{6,7},{7,5},{5,3},{3,1},{1,0},{8,10},{10,12},{12... | collective-permute-start | bytes 786440 | tf_op jit(solution)/shard_map/ppermute | solution.py:123
  56.3 14.0 %collective-permute-start.11 = (bf16[32,4096]{1,0:T(8,128)(2,1)}, bf16[32,4096]{1,0:T(8,128)(2,1)S(1)}, u32[]{:S(2)}, u32[]{:S(2)}) collective-permute-start(bf16[32,4096]{1,0:T(8,128)(2,1)} %get-tuple-element.44), channel_id=1, source_target_pairs={{2,0},{4,2},{6,4},{7,6},{5,7},{3,5},{1,3},{0,1},{10,8},{12,10},{14... | collective-permute-start | bytes 786440 | tf_op jit(solution)/shard_map/ppermute | solution.py:126
  71.1 8.4 %collective-permute-start.16 = (bf16[32,4096]{1,0:T(8,128)(2,1)}, bf16[32,4096]{1,0:T(8,128)(2,1)S(1)}, u32[]{:S(2)}, u32[]{:S(2)}) collective-permute-start(bf16[32,4096]{1,0:T(8,128)(2,1)} %get-tuple-element.51), channel_id=1, source_target_pairs={{0,2},{2,4},{4,6},{6,7},{7,5},{5,3},{3,1},{1,0},{8,10},{10,12},{12... | collective-permute-start | bytes 786440 | tf_op jit(solution)/shard_map/ppermute | solution.py:123
  72.7 8.1 %collective-permute-start.17 = (bf16[32,4096]{1,0:T(8,128)(2,1)}, bf16[32,4096]{1,0:T(8,128)(2,1)S(1)}, u32[]{:S(2)}, u32[]{:S(2)}) collective-permute-start(bf16[32,4096]{1,0:T(8,128)(2,1)} %get-tuple-element.52), channel_id=1, source_target_pairs={{2,0},{4,2},{6,4},{7,6},{5,7},{3,5},{1,3},{0,1},{10,8},{12,10},{14... | collective-permute-start | bytes 786440 | tf_op jit(solution)/shard_map/ppermute | solution.py:126
  73.1 7.7 %copy-start.20 = (bf16[32,4096]{1,0:T(8,128)(2,1)S(1)}, bf16[32,4096]{1,0:T(8,128)(2,1)}, u32[]{:S(2)}) copy-start(bf16[32,4096]{1,0:T(8,128)(2,1)} %get-tuple-element.51) | copy-start | bytes 786436
  73.1 7.7 %copy-start.22 = (bf16[32,4096]{1,0:T(8,128)(2,1)S(1)}, bf16[32,4096]{1,0:T(8,128)(2,1)}, u32[]{:S(2)}) copy-start(bf16[32,4096]{1,0:T(8,128)(2,1)} %get-tuple-element.52) | copy-start | bytes 786436
  75.9 5.0 %copy-start.16 = (bf16[32,4096]{1,0:T(8,128)(2,1)S(1)}, bf16[32,4096]{1,0:T(8,128)(2,1)}, u32[]{:S(2)}) copy-start(bf16[32,4096]{1,0:T(8,128)(2,1)} %get-tuple-element.43) | copy-start | bytes 786436
  75.9 5.0 %copy-start.18 = (bf16[32,4096]{1,0:T(8,128)(2,1)S(1)}, bf16[32,4096]{1,0:T(8,128)(2,1)}, u32[]{:S(2)}) copy-start(bf16[32,4096]{1,0:T(8,128)(2,1)} %get-tuple-element.44) | copy-start | bytes 786436
  75.9 5.1 %copy-start.14 = (bf16[64,4096]{1,0:T(8,128)(2,1)S(1)}, bf16[64,4096]{1,0:T(8,128)(2,1)}, u32[]{:S(2)}) copy-start(bf16[64,4096]{1,0:T(8,128)(2,1)} %param.4) | copy-start | bytes 1572868
  75.9 5.1 %collective-permute-start.13 = (bf16[256,1024]{1,0:T(8,128)(2,1)S(1)}, bf16[256,1024]{1,0:T(8,128)(2,1)S(1)}, u32[]{:S(2)}, u32[]{:S(2)}) collective-permute-start(bf16[256,1024]{1,0:T(8,128)(2,1)S(1)} %fusion.4.a_ref), channel_id=1, source_target_pairs={{0,8},{8,0},{1,9},{9,1},{2,10},{10,2},{3,11},{11,3},{4,12},{12,4},... | collective-permute-start | bytes 1572872 | tf_op jit(solution)/shard_map/ppermute | solution.py:129
  81.0 13.5 %copy-start.9 = (bf16[256,4096]{1,0:T(8,128)(2,1)}, bf16[256,4096]{1,0:T(8,128)(2,1)S(1)}, u32[]{:S(2)}) copy-start(bf16[256,4096]{1,0:T(8,128)(2,1)S(1)} %constant_dynamic-update-slice_fusion.8.x_ref) | copy-start | bytes 6291460
  92.4 35.3 %copy-start.8 = (f32[192,4096]{1,0:T(8,128)}, f32[192,4096]{1,0:T(8,128)S(1)}, u32[]{:S(2)}) copy-start(f32[192,4096]{1,0:T(8,128)S(1)} %get-tuple-element.48.refs_0_) | copy-start | bytes 9437188
  92.4 14.1 %collective-permute-start.14 = (bf16[32,4096]{1,0:T(8,128)(2,1)S(1)}, bf16[32,4096]{1,0:T(8,128)(2,1)S(1)}, u32[]{:S(2)}, u32[]{:S(2)}) collective-permute-start(bf16[32,4096]{1,0:T(8,128)(2,1)S(1)} %get-tuple-element.49), channel_id=1, source_target_pairs={{2,0},{4,2},{6,4},{7,6},{5,7},{3,5},{1,3},{0,1},{10,8},{12,10},{14... | collective-permute-start | bytes 786440 | tf_op jit(solution)/shard_map/ppermute | solution.py:126
  92.9 13.6 %collective-permute-start.15 = (bf16[32,4096]{1,0:T(8,128)(2,1)S(1)}, bf16[32,4096]{1,0:T(8,128)(2,1)}, u32[]{:S(2)}, u32[]{:S(2)}) collective-permute-start(bf16[32,4096]{1,0:T(8,128)(2,1)S(1)} %get-tuple-element.50), channel_id=1, source_target_pairs={{0,2},{2,4},{4,6},{6,7},{7,5},{5,3},{3,1},{1,0},{8,10},{10,12},{12... | collective-permute-start | bytes 786440 | tf_op jit(solution)/shard_map/ppermute | solution.py:123
  107.3 3.4 %copy-start.5 = (f32[2,256,1024]{2,1,0:T(8,128)S(1)}, f32[2,256,1024]{2,1,0:T(8,128)}, u32[]{:S(2)}) copy-start(f32[2,256,1024]{2,1,0:T(8,128)} %get-tuple-element.55.refs_0_) | copy-start | bytes 6291460
  107.3 17.0 %collective-permute-start.20 = (f32[2,256,1024]{2,1,0:T(8,128)}, f32[2,256,1024]{2,1,0:T(8,128)}, u32[]{:S(2)}, u32[]{:S(2)}) collective-permute-start(f32[2,256,1024]{2,1,0:T(8,128)} %get-tuple-element.55.refs_0_), channel_id=1, source_target_pairs={{0,8},{8,0},{1,9},{9,1},{2,10},{10,2},{3,11},{11,3},{4,12},{12,4},... | collective-permute-start | bytes 6291464 | tf_op jit(solution)/shard_map/ppermute | solution.py:129
  108.6 15.7 %collective-permute-start.19 = (bf16[32,4096]{1,0:T(8,128)(2,1)S(1)}, bf16[32,4096]{1,0:T(8,128)(2,1)S(1)}, u32[]{:S(2)}, u32[]{:S(2)}) collective-permute-start(bf16[32,4096]{1,0:T(8,128)(2,1)S(1)} %get-tuple-element.83), channel_id=1, source_target_pairs={{0,2},{2,4},{4,6},{6,7},{7,5},{5,3},{3,1},{1,0},{8,10},{10,12},{12... | collective-permute-start | bytes 786440 | tf_op jit(solution)/shard_map/ppermute | solution.py:123
  110.1 14.1 %collective-permute-start.18 = (bf16[32,4096]{1,0:T(8,128)(2,1)S(1)}, bf16[32,4096]{1,0:T(8,128)(2,1)}, u32[]{:S(2)}, u32[]{:S(2)}) collective-permute-start(bf16[32,4096]{1,0:T(8,128)(2,1)S(1)} %get-tuple-element.84), channel_id=1, source_target_pairs={{2,0},{4,2},{6,4},{7,6},{5,7},{3,5},{1,3},{0,1},{10,8},{12,10},{14... | collective-permute-start | bytes 786440 | tf_op jit(solution)/shard_map/ppermute | solution.py:126
  125.0 2.8 %copy-start.30 = (bf16[32,4096]{1,0:T(8,128)(2,1)S(1)}, bf16[32,4096]{1,0:T(8,128)(2,1)}, u32[]{:S(2)}) copy-start(bf16[32,4096]{1,0:T(8,128)(2,1)} %get-tuple-element.62) | copy-start | bytes 786436
  127.7 3.2 %collective-permute-start.21 = (bf16[256,1024]{1,0:T(8,128)(2,1)S(1)}, bf16[256,1024]{1,0:T(8,128)(2,1)S(1)}, u32[]{:S(2)}, u32[]{:S(2)}) collective-permute-start(bf16[256,1024]{1,0:T(8,128)(2,1)S(1)} %fusion.a_ref), channel_id=1, source_target_pairs={{0,8},{8,0},{1,9},{9,1},{2,10},{10,2},{3,11},{11,3},{4,12},{12,4},... | collective-permute-start | bytes 1572872 | tf_op jit(solution)/shard_map/ppermute | solution.py:129
  128.8 15.8 %collective-permute-start.25 = (bf16[32,4096]{1,0:T(8,128)(2,1)S(1)}, bf16[32,4096]{1,0:T(8,128)(2,1)S(1)}, u32[]{:S(2)}, u32[]{:S(2)}) collective-permute-start(bf16[32,4096]{1,0:T(8,128)(2,1)S(1)} %get-tuple-element.81), channel_id=1, source_target_pairs={{0,2},{2,4},{4,6},{6,7},{7,5},{5,3},{3,1},{1,0},{8,10},{10,12},{12... | collective-permute-start | bytes 786440 | tf_op jit(solution)/shard_map/ppermute | solution.py:123
  130.4 14.3 %collective-permute-start.24 = (bf16[32,4096]{1,0:T(8,128)(2,1)S(1)}, bf16[32,4096]{1,0:T(8,128)(2,1)S(1)}, u32[]{:S(2)}, u32[]{:S(2)}) collective-permute-start(bf16[32,4096]{1,0:T(8,128)(2,1)S(1)} %get-tuple-element.82), channel_id=1, source_target_pairs={{2,0},{4,2},{6,4},{7,6},{5,7},{3,5},{1,3},{0,1},{10,8},{12,10},{14... | collective-permute-start | bytes 786440 | tf_op jit(solution)/shard_map/ppermute | solution.py:126
  141.6 1.7 copy-start.6
  145.5 4.1 %copy-start.12 = (bf16[32,4096]{1,0:T(8,128)(2,1)S(1)}, bf16[32,4096]{1,0:T(8,128)(2,1)}, u32[]{:S(2)}) copy-start(bf16[32,4096]{1,0:T(8,128)(2,1)} %copy-done.11) | copy-start | bytes 786436
  145.5 16.7 %copy-start.7 = (f32[192,4096]{1,0:T(8,128)S(1)}, f32[192,4096]{1,0:T(8,128)}, u32[]{:S(2)}) copy-start(f32[192,4096]{1,0:T(8,128)} %copy-done.6) | copy-start | bytes 9437188
  147.1 9.3 %collective-permute-start.27 = (bf16[32,4096]{1,0:T(8,128)(2,1)S(1)}, bf16[32,4096]{1,0:T(8,128)(2,1)}, u32[]{:S(2)}, u32[]{:S(2)}) collective-permute-start(bf16[32,4096]{1,0:T(8,128)(2,1)S(1)} %get-tuple-element.79), channel_id=1, source_target_pairs={{0,2},{2,4},{4,6},{6,7},{7,5},{5,3},{3,1},{1,0},{8,10},{10,12},{12... | collective-permute-start | bytes 786440 | tf_op jit(solution)/shard_map/ppermute | solution.py:123
  148.7 9.3 %collective-permute-start.26 = (bf16[32,4096]{1,0:T(8,128)(2,1)S(1)}, bf16[32,4096]{1,0:T(8,128)(2,1)}, u32[]{:S(2)}, u32[]{:S(2)}) collective-permute-start(bf16[32,4096]{1,0:T(8,128)(2,1)S(1)} %get-tuple-element.80), channel_id=1, source_target_pairs={{2,0},{4,2},{6,4},{7,6},{5,7},{3,5},{1,3},{0,1},{10,8},{12,10},{14... | collective-permute-start | bytes 786440 | tf_op jit(solution)/shard_map/ppermute | solution.py:126
  149.2 13.1 %collective-permute-start.22 = (bf16[32,4096]{1,0:T(8,128)(2,1)}, bf16[32,4096]{1,0:T(8,128)(2,1)}, u32[]{:S(2)}, u32[]{:S(2)}) collective-permute-start(bf16[32,4096]{1,0:T(8,128)(2,1)} %copy-done.13), channel_id=1, source_target_pairs={{2,0},{4,2},{6,4},{7,6},{5,7},{3,5},{1,3},{0,1},{10,8},{12,10},{14... | collective-permute-start | bytes 786440 | tf_op jit(solution)/shard_map/ppermute | solution.py:126
  149.6 12.6 %collective-permute-start.23 = (bf16[32,4096]{1,0:T(8,128)(2,1)S(1)}, bf16[32,4096]{1,0:T(8,128)(2,1)}, u32[]{:S(2)}, u32[]{:S(2)}) collective-permute-start(bf16[32,4096]{1,0:T(8,128)(2,1)S(1)} %copy-done.12), channel_id=1, source_target_pairs={{0,2},{2,4},{4,6},{6,7},{7,5},{5,3},{3,1},{1,0},{8,10},{10,12},{12... | collective-permute-start | bytes 786440 | tf_op jit(solution)/shard_map/ppermute | solution.py:123
  163.4 7.0 %collective-permute-start.29 = (bf16[32,4096]{1,0:T(8,128)(2,1)S(1)}, bf16[32,4096]{1,0:T(8,128)(2,1)S(1)}, u32[]{:S(2)}, u32[]{:S(2)}) collective-permute-start(bf16[32,4096]{1,0:T(8,128)(2,1)S(1)} %get-tuple-element.77), channel_id=1, source_target_pairs={{0,2},{2,4},{4,6},{6,7},{7,5},{5,3},{3,1},{1,0},{8,10},{10,12},{12... | collective-permute-start | bytes 786440 | tf_op jit(solution)/shard_map/ppermute | solution.py:123
  164.8 6.8 %collective-permute-start.28 = (bf16[32,4096]{1,0:T(8,128)(2,1)S(1)}, bf16[32,4096]{1,0:T(8,128)(2,1)}, u32[]{:S(2)}, u32[]{:S(2)}) collective-permute-start(bf16[32,4096]{1,0:T(8,128)(2,1)S(1)} %get-tuple-element.78), channel_id=1, source_target_pairs={{2,0},{4,2},{6,4},{7,6},{5,7},{3,5},{1,3},{0,1},{10,8},{12,10},{14... | collective-permute-start | bytes 786440 | tf_op jit(solution)/shard_map/ppermute | solution.py:126
  172.7 6.4 %collective-permute-start.31 = (bf16[32,4096]{1,0:T(8,128)(2,1)S(1)}, bf16[32,4096]{1,0:T(8,128)(2,1)S(1)}, u32[]{:S(2)}, u32[]{:S(2)}) collective-permute-start(bf16[32,4096]{1,0:T(8,128)(2,1)S(1)} %get-tuple-element.75), channel_id=1, source_target_pairs={{0,2},{2,4},{4,6},{6,7},{7,5},{5,3},{3,1},{1,0},{8,10},{10,12},{12... | collective-permute-start | bytes 786440 | tf_op jit(solution)/shard_map/ppermute | solution.py:123
  173.6 6.5 %collective-permute-start.30 = (bf16[32,4096]{1,0:T(8,128)(2,1)S(1)}, bf16[32,4096]{1,0:T(8,128)(2,1)}, u32[]{:S(2)}, u32[]{:S(2)}) collective-permute-start(bf16[32,4096]{1,0:T(8,128)(2,1)S(1)} %get-tuple-element.76), channel_id=1, source_target_pairs={{2,0},{4,2},{6,4},{7,6},{5,7},{3,5},{1,3},{0,1},{10,8},{12,10},{14... | collective-permute-start | bytes 786440 | tf_op jit(solution)/shard_map/ppermute | solution.py:126
  (20 other events, 20.0 us)

commit v4 on v3

--- a/solution.py
+++ b/solution.py
@@ -20,7 +20,7 @@
 
 def params(flops, read):
     return dict(
-        compiler_params=pltpu.CompilerParams(vmem_limit_bytes=24 << 20),
+        compiler_params=pltpu.CompilerParams(vmem_limit_bytes=16 << 20),
         cost_estimate=pl.CostEstimate(
             flops=flops, bytes_accessed=read, transcendentals=0
         ),
@@ -30,34 +30,28 @@
 def gate_up(x, gate_weight, up_weight, part, after):
     m, k = x.shape
     w = gate_weight.shape[1] // 2
-    tile, deep = min(w, 256), k // 2
-    tiles = w // tile
+    deep = 512
 
     def body(part_ref, x_ref, g_ref, u_ref, *refs):
         o_ref = refs[-1]
-        step = pl.program_id(1)
-        rows = x_ref[:, pl.ds(pl.multiple_of(step * deep, deep), deep)]
-        g = jnp.dot(rows, g_ref[...], preferred_element_type=F32)
-        u = jnp.dot(rows, u_ref[...], preferred_element_type=F32)
+        step = pl.program_id(0)
 
         @pl.when(step == 0)
         def _():
-            o_ref[0] = g
-            o_ref[1] = u
-
-        @pl.when(step != 0)
-        def _():
-            o_ref[0] += g
-            o_ref[1] += u
-
-    weight = pl.BlockSpec((deep, tile), lambda j, s, part: (s, part[0] * tiles + j))
+            o_ref[...] = jnp.zeros_like(o_ref)
+
+        cols = pl.ds(pl.multiple_of(step * deep, deep), deep)
+        o_ref[0] += jnp.dot(x_ref[:, cols], g_ref[...], preferred_element_type=F32)
+        o_ref[1] += jnp.dot(x_ref[:, cols], u_ref[...], preferred_element_type=F32)
+
+    weight = pl.BlockSpec((deep, w), lambda s, part: (s, part[0]))
     return pl.pallas_call(
         body,
         grid_spec=pltpu.PrefetchScalarGridSpec(
             num_scalar_prefetch=1,
-            grid=(tiles, 2),
+            grid=(k // deep,),
             in_specs=[VMEM, weight, weight] + [ANY] * len(after),
-            out_specs=pl.BlockSpec((2, m, tile), lambda j, s, part: (0, 0, j)),
+            out_specs=VMEM,
         ),
         out_shape=jax.ShapeDtypeStruct((2, m, w), F32),
         **params(4 * m * k * w, 4 * k * w),
@@ -67,30 +61,43 @@
 def down(mine, others, weight, part, cut):
     m, w = mine.shape
     n = weight.shape[1]
-    tile = 512
-
-    def body(part_ref, a_ref, b_ref, d_ref, l_ref, r_ref, o_ref, h_ref):
-        @pl.when(pl.program_id(0) == 0)
+    tile, deep = n // 2, min(2 * w, 512)
+    steps = 2 * w // deep
+
+    def body(part_ref, a_ref, b_ref, d_ref, l_ref, r_ref, o_ref, h_ref, s_ref):
+        j, step = pl.program_id(0), pl.program_id(1)
+
+        @pl.when((j == 0) & (step == 0))
         def _():
             h_ref[:, pl.ds(pl.multiple_of(part_ref[0] * w, w), w)] = a_ref[...]
             h_ref[:, pl.ds(pl.multiple_of(w - part_ref[0] * w, w), w)] = b_ref[...]
 
-        out = jnp.dot(h_ref[...], d_ref[...], preferred_element_type=F32)
-        l_ref[...] = out[:cut].astype(BF16)
-        r_ref[...] = out[cut : 2 * cut].astype(BF16)
-        o_ref[...] = out[2 * cut :]
+        @pl.when(step == 0)
+        def _():
+            s_ref[...] = jnp.zeros_like(s_ref)
+
+        rows = h_ref[:, pl.ds(pl.multiple_of(step * deep, deep), deep)]
+        s_ref[...] += jnp.dot(rows, d_ref[...], preferred_element_type=F32)
+
+        @pl.when(step == steps - 1)
+        def _():
+            cols = pl.ds(pl.multiple_of(j * tile, tile), tile)
+            l_ref[:, cols] = s_ref[:cut].astype(BF16)
+            r_ref[:, cols] = s_ref[cut : 2 * cut].astype(BF16)
+            o_ref[:, cols] = s_ref[2 * cut :]
 
     return pl.pallas_call(
         body,
         grid_spec=pltpu.PrefetchScalarGridSpec(
             num_scalar_prefetch=1,
-            grid=(n // tile,),
-            in_specs=[VMEM, VMEM, pl.BlockSpec((2 * w, tile), lambda j, part: (0, j))],
-            out_specs=[
-                pl.BlockSpec((r, tile), lambda j, part: (0, j))
-                for r in (cut, cut, m - 2 * cut)
+            grid=(2, steps),
+            in_specs=[
+                VMEM,
+                VMEM,
+                pl.BlockSpec((deep, tile), lambda j, s, part: (s, j)),
             ],
-            scratch_shapes=[pltpu.VMEM((m, 2 * w), BF16)],
+            out_specs=[VMEM, VMEM, VMEM],
+            scratch_shapes=[pltpu.VMEM((m, 2 * w), BF16), pltpu.VMEM((m, tile), F32)],
         ),
         out_shape=[
             jax.ShapeDtypeStruct((cut, n), BF16),
@@ -108,6 +115,7 @@
         out_specs=[ANY] * len(arrays),
         out_shape=[jax.ShapeDtypeStruct(x.shape, x.dtype) for x in arrays],
         input_output_aliases={i: i for i in range(len(arrays))},
+        compiler_params=pltpu.CompilerParams(vmem_limit_bytes=1 << 18),
         cost_estimate=pl.CostEstimate(flops=0, bytes_accessed=0, transcendentals=0),
     )(*arrays, *after)
 
@@ -158,7 +166,8 @@
             return (part + block.astype(F32)).astype(BF16)
 
         early = gather(a, b, half - 1)
-        early[0], early[1], r, l = gate(early[0], early[1], b, a)
+        early[0], early[1] = gate(early[0], early[1])
+        r, l = gate(b, a, after=early[:2])
         far = gather(early[0], early[1], 1) + early
         steps = kernels(stack(far), [])
         near, step = [], next(steps)

time: 183 us -> 150 us (0.82)
  local copies, waits for them, and re-layouts: 21.1 us -> 1.37 us
  other arithmetic: 13.7 us -> 2.65 us
    unnamed x85 -> x15, local copies, waits for them, and re-layouts: 20 us -> 0.25 us
    ppermute x14, waiting for transfers between devices: 28.9 us -> 10.8 us  [left(): return lax.ppermute(x, 'gy', to_left)]
    ppermute x14, waiting for transfers between devices: 23.4 us -> 40 us  [right(): return lax.ppermute(x, 'gy', to_right)]
    convert_element_type x5, other arithmetic: 6.15 us -> 0.55 us  [add(): return (part + block.astype(F32)).astype(BF16)]
    ppermute x14, starting transfers between devices: 16.8 us -> 22.1 us  [right(): return lax.ppermute(x, 'gy', to_right)]
    ppermute x14, starting transfers between devices: 13 us -> 7.73 us  [left(): return lax.ppermute(x, 'gy', to_left)]
    convert_element_type x2, other arithmetic: 5.39 us -> 1.08 us  [kernels(): h = (jax.nn.silu(ours[0] + got[0]) * (ours[1] + got[1])).astype(BF16)]
  transfers between devices with their start and end apart: 32 -> 32, of which waited for: 15 -> 15; matrix products, arithmetic and copies ran while one was open for 5% -> 1% of each run, Pallas kernels for 29% -> 35%
where the time goes in v4:
time: 150 us; the launch traced here: 149 us
  Pallas kernels  64 us (43%)
  waiting for transfers between devices  50.7 us (34%)
  starting transfers between devices  30.1 us (20%)
  other arithmetic  2.65 us (2%)
    pallas_call x4, Pallas kernels, gate_up(): pl.pallas_call(body, grid_spec=pltpu.PrefetchScalarGridSpec(num_scalar_pr...  42 us
    ppermute x14, waiting for transfers between devices, right(): return lax.ppermute(x, 'gy', to_right)  40 us
    ppermute x14, starting transfers between devices, right(): return lax.ppermute(x, 'gy', to_right)  22.1 us
    pallas_call x2, Pallas kernels, down(): pl.pallas_call(body, grid_spec=pltpu.PrefetchScalarGridSpec(num_scalar_pr...  21.9 us
    ppermute x14, waiting for transfers between devices, left(): return lax.ppermute(x, 'gy', to_left)  10.8 us
    ppermute x14, starting transfers between devices, left(): return lax.ppermute(x, 'gy', to_left)  7.73 us
  transfers between devices with their start and end apart: 32, of which 15 were waited for; matrix products, arithmetic and copies ran while one was open for 1% of the time, Pallas kernels for 35%

profile of v4, /device:TPU:0, one launch (start us, length us, event | category | flops | bytes accessed | tf_op | source)
XLA Modules:
  0.0 149.3 jit_solution(13385842274452892915)
XLA Ops:
  0.0 1.1 fusion.8
  1.1 3.1 %collective-permute-start = (bf16[32,4096]{1,0:T(8,128)(2,1)S(1)}, bf16[32,4096]{1,0:T(8,128)(2,1)S(1)}, u32[]{:S(2)}, u32[]{:S(2)}) collective-permute-start(bf16[32,4096]{1,0:T(8,128)(2,1)S(1)} %get-tuple-element.85.refs_1_), channel_id=1, source_target_pairs={{0,2},{2,4},{4,6},{6,7},{7,5},{5,3},{3,1},{1,0},{8,10},{10,12},{12... | collective-permute-start | bytes 786440 | tf_op jit(solution)/shard_map/ppermute | solution.py:131
  4.2 6.2 %collective-permute-done = bf16[32,4096]{1,0:T(8,128)(2,1)S(1)} collective-permute-done((bf16[32,4096]{1,0:T(8,128)(2,1)S(1)}, bf16[32,4096]{1,0:T(8,128)(2,1)S(1)}, u32[]{:S(2)}, u32[]{:S(2)}) %collective-permute-start) | collective-permute-done | bytes 262176 | tf_op jit(solution)/shard_map/ppermute | solution.py:131
  10.4 1.8 %collective-permute-start.1 = (bf16[32,4096]{1,0:T(8,128)(2,1)S(1)}, bf16[32,4096]{1,0:T(8,128)(2,1)S(1)}, u32[]{:S(2)}, u32[]{:S(2)}) collective-permute-start(bf16[32,4096]{1,0:T(8,128)(2,1)S(1)} %collective-permute-done), channel_id=1, source_target_pairs={{0,2},{2,4},{4,6},{6,7},{7,5},{5,3},{3,1},{1,0},{8,10},{10,12},{12... | collective-permute-start | bytes 786440 | tf_op jit(solution)/shard_map/ppermute | solution.py:131
  12.4 5.5 %collective-permute-done.1 = bf16[32,4096]{1,0:T(8,128)(2,1)S(1)} collective-permute-done((bf16[32,4096]{1,0:T(8,128)(2,1)S(1)}, bf16[32,4096]{1,0:T(8,128)(2,1)S(1)}, u32[]{:S(2)}, u32[]{:S(2)}) %collective-permute-start.1) | collective-permute-done | bytes 262176 | tf_op jit(solution)/shard_map/ppermute | solution.py:131
  17.9 1.5 collective-permute-start.2
  19.4 0.5 collective-permute-start.5
  19.9 4.5 %collective-permute-done.2.refs_0_ = bf16[32,4096]{1,0:T(8,128)(2,1)S(1)} collective-permute-done((bf16[32,4096]{1,0:T(8,128)(2,1)S(1)}, bf16[32,4096]{1,0:T(8,128)(2,1)S(1)}, u32[]{:S(2)}, u32[]{:S(2)}) %collective-permute-start.2) | collective-permute-done | bytes 262176 | tf_op jit(solution)/shard_map/ppermute | solution.py:131
  24.5 1.3 collective-permute-done.5.refs_1_
  25.7 1.6 %collective-permute-start.8 = (bf16[32,4096]{1,0:T(8,128)(2,1)S(1)}, bf16[32,4096]{1,0:T(8,128)(2,1)S(1)}, u32[]{:S(2)}, u32[]{:S(2)}) collective-permute-start(bf16[32,4096]{1,0:T(8,128)(2,1)S(1)} %get-tuple-element.39.refs_2_), channel_id=1, source_target_pairs={{0,2},{2,4},{4,6},{6,7},{7,5},{5,3},{3,1},{1,0},{8,10},{10,12},{12... | collective-permute-start | bytes 786440 | tf_op jit(solution)/shard_map/ppermute | solution.py:131
  27.8 1.6 %collective-permute-start.6 = (bf16[32,4096]{1,0:T(8,128)(2,1)S(1)}, bf16[32,4096]{1,0:T(8,128)(2,1)S(1)}, u32[]{:S(2)}, u32[]{:S(2)}) collective-permute-start(bf16[32,4096]{1,0:T(8,128)(2,1)S(1)} %get-tuple-element.41), channel_id=1, source_target_pairs={{0,2},{2,4},{4,6},{6,7},{7,5},{5,3},{3,1},{1,0},{8,10},{10,12},{12... | collective-permute-start | bytes 786440 | tf_op jit(solution)/shard_map/ppermute | solution.py:131
  29.8 3.9 %collective-permute-done.8 = bf16[32,4096]{1,0:T(8,128)(2,1)S(1)} collective-permute-done((bf16[32,4096]{1,0:T(8,128)(2,1)S(1)}, bf16[32,4096]{1,0:T(8,128)(2,1)S(1)}, u32[]{:S(2)}, u32[]{:S(2)}) %collective-permute-start.8) | collective-permute-done | bytes 262176 | tf_op jit(solution)/shard_map/ppermute | solution.py:131
  33.7 1.3 collective-permute-done.9
  35.2 10.5 %shard_map.48.refs_2_ = f32[2,256,1024]{2,1,0:T(8,128)S(1)} custom-call(s32[1]{0:T(128)} %bitcast.1.part_ref, bf16[256,4096]{1,0:T(8,128)(2,1)S(1)} %constant_dynamic-update-slice_fusion.x_ref, bf16[4096,2048]{1,0:T(8,128)(2,1)} %g_ref.7, bf16[4096,2048]{1,0:T(8,128)(2,1)} %u_ref.7), custom_call_target="tpu_custom_call" | custom-call | flops 4294967296 | bytes 16777216 | tf_op jit(solution)/shard_map/pallas_call | solution.py:48
  45.8 1.6 %collective-permute-start.10 = (bf16[32,4096]{1,0:T(8,128)(2,1)S(1)}, bf16[32,4096]{1,0:T(8,128)(2,1)S(1)}, u32[]{:S(2)}, u32[]{:S(2)}) collective-permute-start(bf16[32,4096]{1,0:T(8,128)(2,1)S(1)} %get-tuple-element.43), channel_id=1, source_target_pairs={{0,2},{2,4},{4,6},{6,7},{7,5},{5,3},{3,1},{1,0},{8,10},{10,12},{12... | collective-permute-start | bytes 786440 | tf_op jit(solution)/shard_map/ppermute | solution.py:131
  47.9 10.5 %shard_map.50.refs_2_ = f32[2,256,1024]{2,1,0:T(8,128)S(1)} custom-call(s32[1]{0:T(128)} %bitcast.part_ref, bf16[256,4096]{1,0:T(8,128)(2,1)S(1)} %constant_dynamic-update-slice_fusion.x_ref, bf16[4096,2048]{1,0:T(8,128)(2,1)} %g_ref.7, bf16[4096,2048]{1,0:T(8,128)(2,1)} %u_ref.7, f32[2,256,1024]{2,1,0:T(8,128)S(1)} %get-tuple-element.45.refs_0_), custom_call_target="tpu_custom_call" | custom-call | flops 4294967296 | bytes 16777216 | tf_op jit(solution)/shard_map/pallas_call | solution.py:48
  58.4 1.6 %collective-permute-start.16 = (bf16[32,4096]{1,0:T(8,128)(2,1)S(1)}, bf16[32,4096]{1,0:T(8,128)(2,1)S(1)}, u32[]{:S(2)}, u32[]{:S(2)}) collective-permute-start(bf16[32,4096]{1,0:T(8,128)(2,1)S(1)} %get-tuple-element.51), channel_id=1, source_target_pairs={{0,2},{2,4},{4,6},{6,7},{7,5},{5,3},{3,1},{1,0},{8,10},{10,12},{12... | collective-permute-start | bytes 786440 | tf_op jit(solution)/shard_map/ppermute | solution.py:131
  60.0 0.5 collective-permute-start.17
  60.5 0.5 fusion.4.a_ref
  61.1 5.4 %collective-permute-done.16 = bf16[32,4096]{1,0:T(8,128)(2,1)S(1)} collective-permute-done((bf16[32,4096]{1,0:T(8,128)(2,1)S(1)}, bf16[32,4096]{1,0:T(8,128)(2,1)S(1)}, u32[]{:S(2)}, u32[]{:S(2)}) %collective-permute-start.16) | collective-permute-done | bytes 262176 | tf_op jit(solution)/shard_map/ppermute | solution.py:131
  66.6 1.3 collective-permute-done.17
  68.1 11.0 %shard_map.52 = (bf16[32,4096]{1,0:T(8,128)(2,1)S(1)}, bf16[32,4096]{1,0:T(8,128)(2,1)S(1)}, f32[192,4096]{1,0:T(8,128)S(1)}) custom-call(s32[1]{0:T(128)} %bitcast.part_ref, bf16[256,1024]{1,0:T(8,128)(2,1)S(1)} %fusion.4.a_ref, bf16[256,1024]{1,0:T(8,128)(2,1)S(1)} %collective-permute-done.13.b_ref, bf16[2048,4096]{1,0:T(8,128)(2,1)} %d_ref.3), custom_call_target="tpu_custom_call" | custom-call | flops 4294967296 | bytes 16777216 | tf_op jit(solution)/shard_map/pallas_call | solution.py:89
  79.0 0.5 collective-permute-start.14
  79.5 1.6 %collective-permute-start.15 = (bf16[32,4096]{1,0:T(8,128)(2,1)S(1)}, bf16[32,4096]{1,0:T(8,128)(2,1)S(1)}, u32[]{:S(2)}, u32[]{:S(2)}) collective-permute-start(bf16[32,4096]{1,0:T(8,128)(2,1)S(1)} %get-tuple-element.50), channel_id=1, source_target_pairs={{0,2},{2,4},{4,6},{6,7},{7,5},{5,3},{3,1},{1,0},{8,10},{10,12},{12... | collective-permute-start | bytes 786440 | tf_op jit(solution)/shard_map/ppermute | solution.py:131
  81.1 10.5 %shard_map.53.refs_2_ = f32[2,256,1024]{2,1,0:T(8,128)S(1)} custom-call(s32[1]{0:T(128)} %bitcast.1.part_ref, bf16[256,4096]{1,0:T(8,128)(2,1)S(1)} %constant_dynamic-update-slice_fusion.8.x_ref, bf16[4096,2048]{1,0:T(8,128)(2,1)} %g_ref.7, bf16[4096,2048]{1,0:T(8,128)(2,1)} %u_ref.7, f32[192,4096]{1,0:T(8,128)S(1)} %get-tuple-element.48.refs_0_), custom_call_target="tpu_custom_call" | custom-call | flops 4294967296 | bytes 16777216 | tf_op jit(solution)/shard_map/pallas_call | solution.py:48
  91.8 1.6 %collective-permute-start.19 = (bf16[32,4096]{1,0:T(8,128)(2,1)S(1)}, bf16[32,4096]{1,0:T(8,128)(2,1)S(1)}, u32[]{:S(2)}, u32[]{:S(2)}) collective-permute-start(bf16[32,4096]{1,0:T(8,128)(2,1)S(1)} %get-tuple-element.83), channel_id=1, source_target_pairs={{0,2},{2,4},{4,6},{6,7},{7,5},{5,3},{3,1},{1,0},{8,10},{10,12},{12... | collective-permute-start | bytes 786440 | tf_op jit(solution)/shard_map/ppermute | solution.py:131
  93.4 0.5 collective-permute-start.18
  93.9 10.5 %shard_map.55.refs_2_ = f32[2,256,1024]{2,1,0:T(8,128)S(1)} custom-call(s32[1]{0:T(128)} %bitcast.part_ref, bf16[256,4096]{1,0:T(8,128)(2,1)S(1)} %constant_dynamic-update-slice_fusion.8.x_ref, bf16[4096,2048]{1,0:T(8,128)(2,1)} %g_ref.7, bf16[4096,2048]{1,0:T(8,128)(2,1)} %u_ref.7, f32[2,256,1024]{2,1,0:T(8,128)S(1)} %get-tuple-element.55.refs_0_), custom_call_target="tpu_custom_call" | custom-call | flops 4294967296 | bytes 16777216 | tf_op jit(solution)/shard_map/pallas_call | solution.py:48
  104.5 0.5 fusion.a_ref
  105.2 1.6 %collective-permute-start.25 = (bf16[32,4096]{1,0:T(8,128)(2,1)S(1)}, bf16[32,4096]{1,0:T(8,128)(2,1)S(1)}, u32[]{:S(2)}, u32[]{:S(2)}) collective-permute-start(bf16[32,4096]{1,0:T(8,128)(2,1)S(1)} %get-tuple-element.81), channel_id=1, source_target_pairs={{0,2},{2,4},{4,6},{6,7},{7,5},{5,3},{3,1},{1,0},{8,10},{10,12},{12... | collective-permute-start | bytes 786440 | tf_op jit(solution)/shard_map/ppermute | solution.py:131
  106.8 0.5 collective-permute-start.24
  107.3 11.0 %shard_map.57 = (bf16[32,4096]{1,0:T(8,128)(2,1)S(1)}, bf16[32,4096]{1,0:T(8,128)(2,1)S(1)}, f32[192,4096]{1,0:T(8,128)S(1)}) custom-call(s32[1]{0:T(128)} %bitcast.part_ref, bf16[256,1024]{1,0:T(8,128)(2,1)S(1)} %fusion.a_ref, bf16[256,1024]{1,0:T(8,128)(2,1)S(1)} %collective-permute-done.21.b_ref, bf16[2048,4096]{1,0:T(8,128)(2,1)} %d_ref.3), custom_call_target="tpu_custom_call" | custom-call | flops 4294967296 | bytes 16777216 | tf_op jit(solution)/shard_map/pallas_call | solution.py:89
  118.4 1.6 %collective-permute-start.27 = (bf16[32,4096]{1,0:T(8,128)(2,1)S(1)}, bf16[32,4096]{1,0:T(8,128)(2,1)S(1)}, u32[]{:S(2)}, u32[]{:S(2)}) collective-permute-start(bf16[32,4096]{1,0:T(8,128)(2,1)S(1)} %get-tuple-element.79), channel_id=1, source_target_pairs={{0,2},{2,4},{4,6},{6,7},{7,5},{5,3},{3,1},{1,0},{8,10},{10,12},{12... | collective-permute-start | bytes 786440 | tf_op jit(solution)/shard_map/ppermute | solution.py:131
  120.0 0.5 collective-permute-start.26
  120.5 0.5 collective-permute-start.22
  120.9 1.6 %collective-permute-start.23 = (bf16[32,4096]{1,0:T(8,128)(2,1)S(1)}, bf16[32,4096]{1,0:T(8,128)(2,1)S(1)}, u32[]{:S(2)}, u32[]{:S(2)}) collective-permute-start(bf16[32,4096]{1,0:T(8,128)(2,1)S(1)} %get-tuple-element.60.refs_3_), channel_id=1, source_target_pairs={{0,2},{2,4},{4,6},{6,7},{7,5},{5,3},{3,1},{1,0},{8,10},{10,12},{12... | collective-permute-start | bytes 786440 | tf_op jit(solution)/shard_map/ppermute | solution.py:131
  122.5 5.1 %collective-permute-done.27.refs_3_ = bf16[32,4096]{1,0:T(8,128)(2,1)S(1)} collective-permute-done((bf16[32,4096]{1,0:T(8,128)(2,1)S(1)}, bf16[32,4096]{1,0:T(8,128)(2,1)S(1)}, u32[]{:S(2)}, u32[]{:S(2)}) %collective-permute-start.27) | collective-permute-done | bytes 262176 | tf_op jit(solution)/shard_map/ppermute | solution.py:131
  127.6 1.6 %collective-permute-done.26.refs_2_ = bf16[32,4096]{1,0:T(8,128)(2,1)S(1)} collective-permute-done((bf16[32,4096]{1,0:T(8,128)(2,1)S(1)}, bf16[32,4096]{1,0:T(8,128)(2,1)S(1)}, u32[]{:S(2)}, u32[]{:S(2)}) %collective-permute-start.26) | collective-permute-done | bytes 262176 | tf_op jit(solution)/shard_map/ppermute | solution.py:134
  129.2 4.3 %collective-permute-done.22.refs_0_ = bf16[32,4096]{1,0:T(8,128)(2,1)S(1)} collective-permute-done((bf16[32,4096]{1,0:T(8,128)(2,1)S(1)}, bf16[32,4096]{1,0:T(8,128)(2,1)S(1)}, u32[]{:S(2)}, u32[]{:S(2)}) %collective-permute-start.22) | collective-permute-done | bytes 262176 | tf_op jit(solution)/shard_map/ppermute | solution.py:134
  133.6 0.8 collective-permute-start.29
  134.4 1.3 collective-permute-start.28
  135.7 4.9 %collective-permute-done.29.refs_1_ = bf16[32,4096]{1,0:T(8,128)(2,1)S(1)} collective-permute-done((bf16[32,4096]{1,0:T(8,128)(2,1)S(1)}, bf16[32,4096]{1,0:T(8,128)(2,1)S(1)}, u32[]{:S(2)}, u32[]{:S(2)}) %collective-permute-start.29) | collective-permute-done | bytes 262176 | tf_op jit(solution)/shard_map/ppermute | solution.py:131
  140.6 0.5 collective-permute-done.28.refs_0_
  141.2 0.6 collective-permute-start.31
  141.9 1.4 collective-permute-start.30
  143.3 4.3 %collective-permute-done.31.refs_1_ = bf16[32,4096]{1,0:T(8,128)(2,1)S(1)} collective-permute-done((bf16[32,4096]{1,0:T(8,128)(2,1)S(1)}, bf16[32,4096]{1,0:T(8,128)(2,1)S(1)}, u32[]{:S(2)}, u32[]{:S(2)}) %collective-permute-start.31) | collective-permute-done | bytes 262176 | tf_op jit(solution)/shard_map/ppermute | solution.py:131
  147.6 0.6 collective-permute-done.30.refs_0_
  148.4 0.8 pad_maximum_fusion
  (59 shorter events, 3.0 us)
Async XLA Ops:
  1.1 9.3 %collective-permute-start = (bf16[32,4096]{1,0:T(8,128)(2,1)S(1)}, bf16[32,4096]{1,0:T(8,128)(2,1)S(1)}, u32[]{:S(2)}, u32[]{:S(2)}) collective-permute-start(bf16[32,4096]{1,0:T(8,128)(2,1)S(1)} %get-tuple-element.85.refs_1_), channel_id=1, source_target_pairs={{0,2},{2,4},{4,6},{6,7},{7,5},{5,3},{3,1},{1,0},{8,10},{10,12},{12... | collective-permute-start | bytes 786440 | tf_op jit(solution)/shard_map/ppermute | solution.py:131
  4.1 8.0 %collective-permute-start.3 = (bf16[32,4096]{1,0:T(8,128)(2,1)S(1)}, bf16[32,4096]{1,0:T(8,128)(2,1)S(1)}, u32[]{:S(2)}, u32[]{:S(2)}) collective-permute-start(bf16[32,4096]{1,0:T(8,128)(2,1)S(1)} %get-tuple-element.86.refs_0_), channel_id=1, source_target_pairs={{2,0},{4,2},{6,4},{7,6},{5,7},{3,5},{1,3},{0,1},{10,8},{12,10},{14... | collective-permute-start | bytes 786440 | tf_op jit(solution)/shard_map/ppermute | solution.py:134
  10.4 7.5 %collective-permute-start.1 = (bf16[32,4096]{1,0:T(8,128)(2,1)S(1)}, bf16[32,4096]{1,0:T(8,128)(2,1)S(1)}, u32[]{:S(2)}, u32[]{:S(2)}) collective-permute-start(bf16[32,4096]{1,0:T(8,128)(2,1)S(1)} %collective-permute-done), channel_id=1, source_target_pairs={{0,2},{2,4},{4,6},{6,7},{7,5},{5,3},{3,1},{1,0},{8,10},{10,12},{12... | collective-permute-start | bytes 786440 | tf_op jit(solution)/shard_map/ppermute | solution.py:131
  12.2 7.2 %collective-permute-start.4 = (bf16[32,4096]{1,0:T(8,128)(2,1)S(1)}, bf16[32,4096]{1,0:T(8,128)(2,1)S(1)}, u32[]{:S(2)}, u32[]{:S(2)}) collective-permute-start(bf16[32,4096]{1,0:T(8,128)(2,1)S(1)} %collective-permute-done.3), channel_id=1, source_target_pairs={{2,0},{4,2},{6,4},{7,6},{5,7},{3,5},{1,3},{0,1},{10,8},{12,10},{14... | collective-permute-start | bytes 786440 | tf_op jit(solution)/shard_map/ppermute | solution.py:134
  17.9 6.6 %collective-permute-start.2 = (bf16[32,4096]{1,0:T(8,128)(2,1)S(1)}, bf16[32,4096]{1,0:T(8,128)(2,1)S(1)}, u32[]{:S(2)}, u32[]{:S(2)}) collective-permute-start(bf16[32,4096]{1,0:T(8,128)(2,1)S(1)} %collective-permute-done.1), channel_id=1, source_target_pairs={{0,2},{2,4},{4,6},{6,7},{7,5},{5,3},{3,1},{1,0},{8,10},{10,12},{12... | collective-permute-start | bytes 786440 | tf_op jit(solution)/shard_map/ppermute | solution.py:131
  19.4 6.4 %collective-permute-start.5 = (bf16[32,4096]{1,0:T(8,128)(2,1)S(1)}, bf16[32,4096]{1,0:T(8,128)(2,1)S(1)}, u32[]{:S(2)}, u32[]{:S(2)}) collective-permute-start(bf16[32,4096]{1,0:T(8,128)(2,1)S(1)} %collective-permute-done.4), channel_id=1, source_target_pairs={{2,0},{4,2},{6,4},{7,6},{5,7},{3,5},{1,3},{0,1},{10,8},{12,10},{14... | collective-permute-start | bytes 786440 | tf_op jit(solution)/shard_map/ppermute | solution.py:134
  25.7 7.9 %collective-permute-start.8 = (bf16[32,4096]{1,0:T(8,128)(2,1)S(1)}, bf16[32,4096]{1,0:T(8,128)(2,1)S(1)}, u32[]{:S(2)}, u32[]{:S(2)}) collective-permute-start(bf16[32,4096]{1,0:T(8,128)(2,1)S(1)} %get-tuple-element.39.refs_2_), channel_id=1, source_target_pairs={{0,2},{2,4},{4,6},{6,7},{7,5},{5,3},{3,1},{1,0},{8,10},{10,12},{12... | collective-permute-start | bytes 786440 | tf_op jit(solution)/shard_map/ppermute | solution.py:131
  27.3 7.6 %collective-permute-start.9 = (bf16[32,4096]{1,0:T(8,128)(2,1)S(1)}, bf16[32,4096]{1,0:T(8,128)(2,1)S(1)}, u32[]{:S(2)}, u32[]{:S(2)}) collective-permute-start(bf16[32,4096]{1,0:T(8,128)(2,1)S(1)} %get-tuple-element.40.refs_3_), channel_id=1, source_target_pairs={{2,0},{4,2},{6,4},{7,6},{5,7},{3,5},{1,3},{0,1},{10,8},{12,10},{14... | collective-permute-start | bytes 786440 | tf_op jit(solution)/shard_map/ppermute | solution.py:134
  27.8 17.9 %collective-permute-start.6 = (bf16[32,4096]{1,0:T(8,128)(2,1)S(1)}, bf16[32,4096]{1,0:T(8,128)(2,1)S(1)}, u32[]{:S(2)}, u32[]{:S(2)}) collective-permute-start(bf16[32,4096]{1,0:T(8,128)(2,1)S(1)} %get-tuple-element.41), channel_id=1, source_target_pairs={{0,2},{2,4},{4,6},{6,7},{7,5},{5,3},{3,1},{1,0},{8,10},{10,12},{12... | collective-permute-start | bytes 786440 | tf_op jit(solution)/shard_map/ppermute | solution.py:131
  29.3 16.3 %collective-permute-start.7 = (bf16[32,4096]{1,0:T(8,128)(2,1)S(1)}, bf16[32,4096]{1,0:T(8,128)(2,1)S(1)}, u32[]{:S(2)}, u32[]{:S(2)}) collective-permute-start(bf16[32,4096]{1,0:T(8,128)(2,1)S(1)} %get-tuple-element.42), channel_id=1, source_target_pairs={{2,0},{4,2},{6,4},{7,6},{5,7},{3,5},{1,3},{0,1},{10,8},{12,10},{14... | collective-permute-start | bytes 786440 | tf_op jit(solution)/shard_map/ppermute | solution.py:134
  45.7 12.7 %collective-permute-start.12 = (f32[2,256,1024]{2,1,0:T(8,128)S(1)}, f32[2,256,1024]{2,1,0:T(8,128)S(1)}, u32[]{:S(2)}, u32[]{:S(2)}) collective-permute-start(f32[2,256,1024]{2,1,0:T(8,128)S(1)} %get-tuple-element.45.refs_0_), channel_id=1, source_target_pairs={{0,8},{8,0},{1,9},{9,1},{2,10},{10,2},{3,11},{11,3},{4,12},{12,4},... | collective-permute-start | bytes 6291464 | tf_op jit(solution)/shard_map/ppermute | solution.py:137
  45.8 12.6 %collective-permute-start.10 = (bf16[32,4096]{1,0:T(8,128)(2,1)S(1)}, bf16[32,4096]{1,0:T(8,128)(2,1)S(1)}, u32[]{:S(2)}, u32[]{:S(2)}) collective-permute-start(bf16[32,4096]{1,0:T(8,128)(2,1)S(1)} %get-tuple-element.43), channel_id=1, source_target_pairs={{0,2},{2,4},{4,6},{6,7},{7,5},{5,3},{3,1},{1,0},{8,10},{10,12},{12... | collective-permute-start | bytes 786440 | tf_op jit(solution)/shard_map/ppermute | solution.py:131
  47.4 11.0 %collective-permute-start.11 = (bf16[32,4096]{1,0:T(8,128)(2,1)S(1)}, bf16[32,4096]{1,0:T(8,128)(2,1)S(1)}, u32[]{:S(2)}, u32[]{:S(2)}) collective-permute-start(bf16[32,4096]{1,0:T(8,128)(2,1)S(1)} %get-tuple-element.44), channel_id=1, source_target_pairs={{2,0},{4,2},{6,4},{7,6},{5,7},{3,5},{1,3},{0,1},{10,8},{12,10},{14... | collective-permute-start | bytes 786440 | tf_op jit(solution)/shard_map/ppermute | solution.py:134
  58.4 8.2 %collective-permute-start.16 = (bf16[32,4096]{1,0:T(8,128)(2,1)S(1)}, bf16[32,4096]{1,0:T(8,128)(2,1)S(1)}, u32[]{:S(2)}, u32[]{:S(2)}) collective-permute-start(bf16[32,4096]{1,0:T(8,128)(2,1)S(1)} %get-tuple-element.51), channel_id=1, source_target_pairs={{0,2},{2,4},{4,6},{6,7},{7,5},{5,3},{3,1},{1,0},{8,10},{10,12},{12... | collective-permute-start | bytes 786440 | tf_op jit(solution)/shard_map/ppermute | solution.py:131
  60.0 7.8 %collective-permute-start.17 = (bf16[32,4096]{1,0:T(8,128)(2,1)S(1)}, bf16[32,4096]{1,0:T(8,128)(2,1)S(1)}, u32[]{:S(2)}, u32[]{:S(2)}) collective-permute-start(bf16[32,4096]{1,0:T(8,128)(2,1)S(1)} %get-tuple-element.52), channel_id=1, source_target_pairs={{2,0},{4,2},{6,4},{7,6},{5,7},{3,5},{1,3},{0,1},{10,8},{12,10},{14... | collective-permute-start | bytes 786440 | tf_op jit(solution)/shard_map/ppermute | solution.py:134
  61.0 7.0 %copy-start = (bf16[64,4096]{1,0:T(8,128)(2,1)S(1)}, bf16[64,4096]{1,0:T(8,128)(2,1)}, u32[]{:S(2)}) copy-start(bf16[64,4096]{1,0:T(8,128)(2,1)} %param.4) | copy-start | bytes 1572868
  61.1 7.0 %collective-permute-start.13 = (bf16[256,1024]{1,0:T(8,128)(2,1)S(1)}, bf16[256,1024]{1,0:T(8,128)(2,1)S(1)}, u32[]{:S(2)}, u32[]{:S(2)}) collective-permute-start(bf16[256,1024]{1,0:T(8,128)(2,1)S(1)} %fusion.4.a_ref), channel_id=1, source_target_pairs={{0,8},{8,0},{1,9},{9,1},{2,10},{10,2},{3,11},{11,3},{4,12},{12,4},... | collective-permute-start | bytes 1572872 | tf_op jit(solution)/shard_map/ppermute | solution.py:137
  79.0 12.6 %collective-permute-start.14 = (bf16[32,4096]{1,0:T(8,128)(2,1)S(1)}, bf16[32,4096]{1,0:T(8,128)(2,1)S(1)}, u32[]{:S(2)}, u32[]{:S(2)}) collective-permute-start(bf16[32,4096]{1,0:T(8,128)(2,1)S(1)} %get-tuple-element.49), channel_id=1, source_target_pairs={{2,0},{4,2},{6,4},{7,6},{5,7},{3,5},{1,3},{0,1},{10,8},{12,10},{14... | collective-permute-start | bytes 786440 | tf_op jit(solution)/shard_map/ppermute | solution.py:134
  79.5 12.1 %collective-permute-start.15 = (bf16[32,4096]{1,0:T(8,128)(2,1)S(1)}, bf16[32,4096]{1,0:T(8,128)(2,1)S(1)}, u32[]{:S(2)}, u32[]{:S(2)}) collective-permute-start(bf16[32,4096]{1,0:T(8,128)(2,1)S(1)} %get-tuple-element.50), channel_id=1, source_target_pairs={{0,2},{2,4},{4,6},{6,7},{7,5},{5,3},{3,1},{1,0},{8,10},{10,12},{12... | collective-permute-start | bytes 786440 | tf_op jit(solution)/shard_map/ppermute | solution.py:131
  91.7 12.8 %collective-permute-start.20 = (f32[2,256,1024]{2,1,0:T(8,128)S(1)}, f32[2,256,1024]{2,1,0:T(8,128)S(1)}, u32[]{:S(2)}, u32[]{:S(2)}) collective-permute-start(f32[2,256,1024]{2,1,0:T(8,128)S(1)} %get-tuple-element.55.refs_0_), channel_id=1, source_target_pairs={{0,8},{8,0},{1,9},{9,1},{2,10},{10,2},{3,11},{11,3},{4,12},{12,4},... | collective-permute-start | bytes 6291464 | tf_op jit(solution)/shard_map/ppermute | solution.py:137
  91.8 12.6 %collective-permute-start.19 = (bf16[32,4096]{1,0:T(8,128)(2,1)S(1)}, bf16[32,4096]{1,0:T(8,128)(2,1)S(1)}, u32[]{:S(2)}, u32[]{:S(2)}) collective-permute-start(bf16[32,4096]{1,0:T(8,128)(2,1)S(1)} %get-tuple-element.83), channel_id=1, source_target_pairs={{0,2},{2,4},{4,6},{6,7},{7,5},{5,3},{3,1},{1,0},{8,10},{10,12},{12... | collective-permute-start | bytes 786440 | tf_op jit(solution)/shard_map/ppermute | solution.py:131
  93.4 11.0 %collective-permute-start.18 = (bf16[32,4096]{1,0:T(8,128)(2,1)S(1)}, bf16[32,4096]{1,0:T(8,128)(2,1)S(1)}, u32[]{:S(2)}, u32[]{:S(2)}) collective-permute-start(bf16[32,4096]{1,0:T(8,128)(2,1)S(1)} %get-tuple-element.84), channel_id=1, source_target_pairs={{2,0},{4,2},{6,4},{7,6},{5,7},{3,5},{1,3},{0,1},{10,8},{12,10},{14... | collective-permute-start | bytes 786440 | tf_op jit(solution)/shard_map/ppermute | solution.py:134
  105.0 2.3 %collective-permute-start.21 = (bf16[256,1024]{1,0:T(8,128)(2,1)S(1)}, bf16[256,1024]{1,0:T(8,128)(2,1)S(1)}, u32[]{:S(2)}, u32[]{:S(2)}) collective-permute-start(bf16[256,1024]{1,0:T(8,128)(2,1)S(1)} %fusion.a_ref), channel_id=1, source_target_pairs={{0,8},{8,0},{1,9},{9,1},{2,10},{10,2},{3,11},{11,3},{4,12},{12,4},... | collective-permute-start | bytes 1572872 | tf_op jit(solution)/shard_map/ppermute | solution.py:137
  105.2 13.0 %collective-permute-start.25 = (bf16[32,4096]{1,0:T(8,128)(2,1)S(1)}, bf16[32,4096]{1,0:T(8,128)(2,1)S(1)}, u32[]{:S(2)}, u32[]{:S(2)}) collective-permute-start(bf16[32,4096]{1,0:T(8,128)(2,1)S(1)} %get-tuple-element.81), channel_id=1, source_target_pairs={{0,2},{2,4},{4,6},{6,7},{7,5},{5,3},{3,1},{1,0},{8,10},{10,12},{12... | collective-permute-start | bytes 786440 | tf_op jit(solution)/shard_map/ppermute | solution.py:131
  106.8 11.5 %collective-permute-start.24 = (bf16[32,4096]{1,0:T(8,128)(2,1)S(1)}, bf16[32,4096]{1,0:T(8,128)(2,1)S(1)}, u32[]{:S(2)}, u32[]{:S(2)}) collective-permute-start(bf16[32,4096]{1,0:T(8,128)(2,1)S(1)} %get-tuple-element.82), channel_id=1, source_target_pairs={{2,0},{4,2},{6,4},{7,6},{5,7},{3,5},{1,3},{0,1},{10,8},{12,10},{14... | collective-permute-start | bytes 786440 | tf_op jit(solution)/shard_map/ppermute | solution.py:134
  118.4 9.2 %collective-permute-start.27 = (bf16[32,4096]{1,0:T(8,128)(2,1)S(1)}, bf16[32,4096]{1,0:T(8,128)(2,1)S(1)}, u32[]{:S(2)}, u32[]{:S(2)}) collective-permute-start(bf16[32,4096]{1,0:T(8,128)(2,1)S(1)} %get-tuple-element.79), channel_id=1, source_target_pairs={{0,2},{2,4},{4,6},{6,7},{7,5},{5,3},{3,1},{1,0},{8,10},{10,12},{12... | collective-permute-start | bytes 786440 | tf_op jit(solution)/shard_map/ppermute | solution.py:131
  120.0 9.2 %collective-permute-start.26 = (bf16[32,4096]{1,0:T(8,128)(2,1)S(1)}, bf16[32,4096]{1,0:T(8,128)(2,1)S(1)}, u32[]{:S(2)}, u32[]{:S(2)}) collective-permute-start(bf16[32,4096]{1,0:T(8,128)(2,1)S(1)} %get-tuple-element.80), channel_id=1, source_target_pairs={{2,0},{4,2},{6,4},{7,6},{5,7},{3,5},{1,3},{0,1},{10,8},{12,10},{14... | collective-permute-start | bytes 786440 | tf_op jit(solution)/shard_map/ppermute | solution.py:134
  120.5 13.0 %collective-permute-start.22 = (bf16[32,4096]{1,0:T(8,128)(2,1)S(1)}, bf16[32,4096]{1,0:T(8,128)(2,1)S(1)}, u32[]{:S(2)}, u32[]{:S(2)}) collective-permute-start(bf16[32,4096]{1,0:T(8,128)(2,1)S(1)} %get-tuple-element.59.refs_2_), channel_id=1, source_target_pairs={{2,0},{4,2},{6,4},{7,6},{5,7},{3,5},{1,3},{0,1},{10,8},{12,10},{14... | collective-permute-start | bytes 786440 | tf_op jit(solution)/shard_map/ppermute | solution.py:134
  120.9 12.5 %collective-permute-start.23 = (bf16[32,4096]{1,0:T(8,128)(2,1)S(1)}, bf16[32,4096]{1,0:T(8,128)(2,1)S(1)}, u32[]{:S(2)}, u32[]{:S(2)}) collective-permute-start(bf16[32,4096]{1,0:T(8,128)(2,1)S(1)} %get-tuple-element.60.refs_3_), channel_id=1, source_target_pairs={{0,2},{2,4},{4,6},{6,7},{7,5},{5,3},{3,1},{1,0},{8,10},{10,12},{12... | collective-permute-start | bytes 786440 | tf_op jit(solution)/shard_map/ppermute | solution.py:131
  133.6 7.0 %collective-permute-start.29 = (bf16[32,4096]{1,0:T(8,128)(2,1)S(1)}, bf16[32,4096]{1,0:T(8,128)(2,1)S(1)}, u32[]{:S(2)}, u32[]{:S(2)}) collective-permute-start(bf16[32,4096]{1,0:T(8,128)(2,1)S(1)} %get-tuple-element.77), channel_id=1, source_target_pairs={{0,2},{2,4},{4,6},{6,7},{7,5},{5,3},{3,1},{1,0},{8,10},{10,12},{12... | collective-permute-start | bytes 786440 | tf_op jit(solution)/shard_map/ppermute | solution.py:131
  134.4 6.7 %collective-permute-start.28 = (bf16[32,4096]{1,0:T(8,128)(2,1)S(1)}, bf16[32,4096]{1,0:T(8,128)(2,1)S(1)}, u32[]{:S(2)}, u32[]{:S(2)}) collective-permute-start(bf16[32,4096]{1,0:T(8,128)(2,1)S(1)} %get-tuple-element.78), channel_id=1, source_target_pairs={{2,0},{4,2},{6,4},{7,6},{5,7},{3,5},{1,3},{0,1},{10,8},{12,10},{14... | collective-permute-start | bytes 786440 | tf_op jit(solution)/shard_map/ppermute | solution.py:134
  141.2 6.4 %collective-permute-start.31 = (bf16[32,4096]{1,0:T(8,128)(2,1)S(1)}, bf16[32,4096]{1,0:T(8,128)(2,1)S(1)}, u32[]{:S(2)}, u32[]{:S(2)}) collective-permute-start(bf16[32,4096]{1,0:T(8,128)(2,1)S(1)} %get-tuple-element.75), channel_id=1, source_target_pairs={{0,2},{2,4},{4,6},{6,7},{7,5},{5,3},{3,1},{1,0},{8,10},{10,12},{12... | collective-permute-start | bytes 786440 | tf_op jit(solution)/shard_map/ppermute | solution.py:131
  141.9 6.4 %collective-permute-start.30 = (bf16[32,4096]{1,0:T(8,128)(2,1)S(1)}, bf16[32,4096]{1,0:T(8,128)(2,1)S(1)}, u32[]{:S(2)}, u32[]{:S(2)}) collective-permute-start(bf16[32,4096]{1,0:T(8,128)(2,1)S(1)} %get-tuple-element.76), channel_id=1, source_target_pairs={{2,0},{4,2},{6,4},{7,6},{5,7},{3,5},{1,3},{0,1},{10,8},{12,10},{14... | collective-permute-start | bytes 786440 | tf_op jit(solution)/shard_map/ppermute | solution.py:134

commit v5 on v4

--- a/solution.py
+++ b/solution.py
@@ -7,6 +7,7 @@
 
 F32, BF16 = jnp.float32, jnp.bfloat16
 ANY = pl.BlockSpec(memory_space=pl.ANY)
+SMEM = pl.BlockSpec(memory_space=pltpu.SMEM)
 VMEM = pl.BlockSpec(memory_space=pltpu.VMEM)
 
 
@@ -20,7 +21,7 @@
 
 def params(flops, read):
     return dict(
-        compiler_params=pltpu.CompilerParams(vmem_limit_bytes=16 << 20),
+        compiler_params=pltpu.CompilerParams(vmem_limit_bytes=24 << 20),
         cost_estimate=pl.CostEstimate(
             flops=flops, bytes_accessed=read, transcendentals=0
         ),
@@ -31,29 +32,41 @@
     m, k = x.shape
     w = gate_weight.shape[1] // 2
     deep = 512
-
-    def body(part_ref, x_ref, g_ref, u_ref, *refs):
-        o_ref = refs[-1]
-        step = pl.program_id(0)
-
-        @pl.when(step == 0)
-        def _():
-            o_ref[...] = jnp.zeros_like(o_ref)
-
-        cols = pl.ds(pl.multiple_of(step * deep, deep), deep)
-        o_ref[0] += jnp.dot(x_ref[:, cols], g_ref[...], preferred_element_type=F32)
-        o_ref[1] += jnp.dot(x_ref[:, cols], u_ref[...], preferred_element_type=F32)
-
-    weight = pl.BlockSpec((deep, w), lambda s, part: (s, part[0]))
+    steps = k // deep
+
+    def body(part_ref, x_ref, *refs):
+        weights, (o_ref, held_ref, sems) = refs[:2], refs[-3:]
+        cols = pl.ds(pl.multiple_of(part_ref[0] * w, w), w)
+
+        def fetch(i, s):
+            rows = pl.ds(pl.multiple_of(s * deep, deep), deep)
+            return pltpu.make_async_copy(
+                weights[i].at[rows, cols], held_ref.at[i, s], sems.at[i, s]
+            )
+
+        for s in range(steps):
+            for i in range(2):
+                fetch(i, s).start()
+        o_ref[...] = jnp.zeros_like(o_ref)
+
+        @pl.loop(0, steps)
+        def _(s):
+            here = pl.ds(pl.multiple_of(s * deep, deep), deep)
+            for i in range(2):
+                fetch(i, s).wait()
+                o_ref[i] += jnp.dot(
+                    x_ref[:, here], held_ref[i, s], preferred_element_type=F32
+                )
+
     return pl.pallas_call(
         body,
-        grid_spec=pltpu.PrefetchScalarGridSpec(
-            num_scalar_prefetch=1,
-            grid=(k // deep,),
-            in_specs=[VMEM, weight, weight] + [ANY] * len(after),
-            out_specs=VMEM,
-        ),
+        in_specs=[SMEM, VMEM] + [ANY] * (2 + len(after)),
+        out_specs=VMEM,
         out_shape=jax.ShapeDtypeStruct((2, m, w), F32),
+        scratch_shapes=[
+            pltpu.VMEM((2, steps, deep, w), BF16),
+            pltpu.SemaphoreType.DMA((2, steps)),
+        ],
         **params(4 * m * k * w, 4 * k * w),
     )(part, x, in_hbm(gate_weight), in_hbm(up_weight), *after)
 
@@ -61,48 +74,41 @@
 def down(mine, others, weight, part, cut):
     m, w = mine.shape
     n = weight.shape[1]
-    tile, deep = n // 2, min(2 * w, 512)
-    steps = 2 * w // deep
-
-    def body(part_ref, a_ref, b_ref, d_ref, l_ref, r_ref, o_ref, h_ref, s_ref):
-        j, step = pl.program_id(0), pl.program_id(1)
-
-        @pl.when((j == 0) & (step == 0))
-        def _():
-            h_ref[:, pl.ds(pl.multiple_of(part_ref[0] * w, w), w)] = a_ref[...]
-            h_ref[:, pl.ds(pl.multiple_of(w - part_ref[0] * w, w), w)] = b_ref[...]
-
-        @pl.when(step == 0)
-        def _():
-            s_ref[...] = jnp.zeros_like(s_ref)
-
-        rows = h_ref[:, pl.ds(pl.multiple_of(step * deep, deep), deep)]
-        s_ref[...] += jnp.dot(rows, d_ref[...], preferred_element_type=F32)
-
-        @pl.when(step == steps - 1)
-        def _():
+    tile = 512
+    steps = n // tile
+
+    def body(part_ref, a_ref, b_ref, d_ref, l_ref, r_ref, o_ref, h_ref, held_ref, sems):
+        def fetch(j):
             cols = pl.ds(pl.multiple_of(j * tile, tile), tile)
-            l_ref[:, cols] = s_ref[:cut].astype(BF16)
-            r_ref[:, cols] = s_ref[cut : 2 * cut].astype(BF16)
-            o_ref[:, cols] = s_ref[2 * cut :]
+            return pltpu.make_async_copy(d_ref.at[:, cols], held_ref.at[j], sems.at[j])
+
+        for j in range(steps):
+            fetch(j).start()
+        h_ref[:, pl.ds(pl.multiple_of(part_ref[0] * w, w), w)] = a_ref[...]
+        h_ref[:, pl.ds(pl.multiple_of(w - part_ref[0] * w, w), w)] = b_ref[...]
+
+        @pl.loop(0, steps)
+        def _(j):
+            cols = pl.ds(pl.multiple_of(j * tile, tile), tile)
+            fetch(j).wait()
+            out = jnp.dot(h_ref[...], held_ref[j], preferred_element_type=F32)
+            l_ref[:, cols] = out[:cut].astype(BF16)
+            r_ref[:, cols] = out[cut : 2 * cut].astype(BF16)
+            o_ref[:, cols] = out[2 * cut :]
 
     return pl.pallas_call(
         body,
-        grid_spec=pltpu.PrefetchScalarGridSpec(
-            num_scalar_prefetch=1,
-            grid=(2, steps),
-            in_specs=[
-                VMEM,
-                VMEM,
-                pl.BlockSpec((deep, tile), lambda j, s, part: (s, j)),
-            ],
-            out_specs=[VMEM, VMEM, VMEM],
-            scratch_shapes=[pltpu.VMEM((m, 2 * w), BF16), pltpu.VMEM((m, tile), F32)],
-        ),
+        in_specs=[SMEM, VMEM, VMEM, ANY],
+        out_specs=[VMEM] * 3,
         out_shape=[
             jax.ShapeDtypeStruct((cut, n), BF16),
             jax.ShapeDtypeStruct((cut, n), BF16),
             jax.ShapeDtypeStruct((m - 2 * cut, n), F32),
+        ],
+        scratch_shapes=[
+            pltpu.VMEM((m, 2 * w), BF16),
+            pltpu.VMEM((steps, 2 * w, tile), BF16),
+            pltpu.SemaphoreType.DMA((steps,)),
         ],
         **params(4 * m * w * n, 4 * w * n),
     )(part, mine, others, in_hbm(weight))

time: 150 us -> 135 us (0.900)
  Pallas kernels: 64 us -> 49.1 us
    pallas_call x6, Pallas kernels: 63.9 us -> 49.1 us  [the longest x4 34.4 us: gate_up(): pl.pallas_call(body, in_specs=[SMEM, VMEM] + [ANY] * (2 + len(after)), ou...]
  transfers between devices with their start and end apart: 32 -> 32, of which waited for: 15 -> 16; matrix products, arithmetic and copies ran while one was open for 1% -> 1% of each run, Pallas kernels for 35% -> 31%
where the time goes in v5:
time: 135 us; the launch traced here: 134 us
  waiting for transfers between devices  50.8 us (38%)
  Pallas kernels  49.1 us (36%)
  starting transfers between devices  30.1 us (22%)
  other arithmetic  2.62 us (2%)
  local copies, waits for them, and re-layouts  1.37 us (1%)
    ppermute x14, waiting for transfers between devices, right(): return lax.ppermute(x, 'gy', to_right)  40 us
    pallas_call x4, Pallas kernels, gate_up(): pl.pallas_call(body, in_specs=[SMEM, VMEM] + [ANY] * (2 + len(after)), ou...  34.4 us
    ppermute x14, starting transfers between devices, right(): return lax.ppermute(x, 'gy', to_right)  21.5 us
    pallas_call x2, Pallas kernels, down(): pl.pallas_call(body, in_specs=[SMEM, VMEM, VMEM, ANY], out_specs=[VMEM] *...  14.6 us
    ppermute x14, waiting for transfers between devices, left(): return lax.ppermute(x, 'gy', to_left)  10.7 us
    ppermute x14, starting transfers between devices, left(): return lax.ppermute(x, 'gy', to_left)  8.34 us
  transfers between devices with their start and end apart: 32, of which 16 were waited for; matrix products, arithmetic and copies ran while one was open for 1% of the time, Pallas kernels for 31%

profile of v5, /device:TPU:0, one launch (start us, length us, event | category | flops | bytes accessed | tf_op | source)
XLA Modules:
  0.0 134.4 jit_solution(6847674851429758328)
XLA Ops:
  0.0 1.1 fusion.8
  1.1 3.1 %collective-permute-start = (bf16[32,4096]{1,0:T(8,128)(2,1)S(1)}, bf16[32,4096]{1,0:T(8,128)(2,1)S(1)}, u32[]{:S(2)}, u32[]{:S(2)}) collective-permute-start(bf16[32,4096]{1,0:T(8,128)(2,1)S(1)} %get-tuple-element.85.refs_1_), channel_id=1, source_target_pairs={{0,2},{2,4},{4,6},{6,7},{7,5},{5,3},{3,1},{1,0},{8,10},{10,12},{12... | collective-permute-start | bytes 786440 | tf_op jit(solution)/shard_map/ppermute | solution.py:137
  4.2 6.2 %collective-permute-done = bf16[32,4096]{1,0:T(8,128)(2,1)S(1)} collective-permute-done((bf16[32,4096]{1,0:T(8,128)(2,1)S(1)}, bf16[32,4096]{1,0:T(8,128)(2,1)S(1)}, u32[]{:S(2)}, u32[]{:S(2)}) %collective-permute-start) | collective-permute-done | bytes 262176 | tf_op jit(solution)/shard_map/ppermute | solution.py:137
  10.4 1.8 %collective-permute-start.1 = (bf16[32,4096]{1,0:T(8,128)(2,1)S(1)}, bf16[32,4096]{1,0:T(8,128)(2,1)S(1)}, u32[]{:S(2)}, u32[]{:S(2)}) collective-permute-start(bf16[32,4096]{1,0:T(8,128)(2,1)S(1)} %collective-permute-done), channel_id=1, source_target_pairs={{0,2},{2,4},{4,6},{6,7},{7,5},{5,3},{3,1},{1,0},{8,10},{10,12},{12... | collective-permute-start | bytes 786440 | tf_op jit(solution)/shard_map/ppermute | solution.py:137
  12.4 5.5 %collective-permute-done.1 = bf16[32,4096]{1,0:T(8,128)(2,1)S(1)} collective-permute-done((bf16[32,4096]{1,0:T(8,128)(2,1)S(1)}, bf16[32,4096]{1,0:T(8,128)(2,1)S(1)}, u32[]{:S(2)}, u32[]{:S(2)}) %collective-permute-start.1) | collective-permute-done | bytes 262176 | tf_op jit(solution)/shard_map/ppermute | solution.py:137
  17.9 1.5 %collective-permute-start.2 = (bf16[32,4096]{1,0:T(8,128)(2,1)S(1)}, bf16[32,4096]{1,0:T(8,128)(2,1)S(1)}, u32[]{:S(2)}, u32[]{:S(2)}) collective-permute-start(bf16[32,4096]{1,0:T(8,128)(2,1)S(1)} %collective-permute-done.1), channel_id=1, source_target_pairs={{0,2},{2,4},{4,6},{6,7},{7,5},{5,3},{3,1},{1,0},{8,10},{10,12},{12... | collective-permute-start | bytes 786440 | tf_op jit(solution)/shard_map/ppermute | solution.py:137
  19.4 0.5 collective-permute-start.5
  19.9 4.5 %collective-permute-done.2.refs_0_ = bf16[32,4096]{1,0:T(8,128)(2,1)S(1)} collective-permute-done((bf16[32,4096]{1,0:T(8,128)(2,1)S(1)}, bf16[32,4096]{1,0:T(8,128)(2,1)S(1)}, u32[]{:S(2)}, u32[]{:S(2)}) %collective-permute-start.2) | collective-permute-done | bytes 262176 | tf_op jit(solution)/shard_map/ppermute | solution.py:137
  24.5 1.3 collective-permute-done.5.refs_1_
  25.7 1.6 %collective-permute-start.8 = (bf16[32,4096]{1,0:T(8,128)(2,1)S(1)}, bf16[32,4096]{1,0:T(8,128)(2,1)S(1)}, u32[]{:S(2)}, u32[]{:S(2)}) collective-permute-start(bf16[32,4096]{1,0:T(8,128)(2,1)S(1)} %get-tuple-element.39.refs_2_), channel_id=1, source_target_pairs={{0,2},{2,4},{4,6},{6,7},{7,5},{5,3},{3,1},{1,0},{8,10},{10,12},{12... | collective-permute-start | bytes 786440 | tf_op jit(solution)/shard_map/ppermute | solution.py:137
  27.8 1.6 %collective-permute-start.6 = (bf16[32,4096]{1,0:T(8,128)(2,1)S(1)}, bf16[32,4096]{1,0:T(8,128)(2,1)S(1)}, u32[]{:S(2)}, u32[]{:S(2)}) collective-permute-start(bf16[32,4096]{1,0:T(8,128)(2,1)S(1)} %get-tuple-element.41), channel_id=1, source_target_pairs={{0,2},{2,4},{4,6},{6,7},{7,5},{5,3},{3,1},{1,0},{8,10},{10,12},{12... | collective-permute-start | bytes 786440 | tf_op jit(solution)/shard_map/ppermute | solution.py:137
  29.8 3.9 %collective-permute-done.8 = bf16[32,4096]{1,0:T(8,128)(2,1)S(1)} collective-permute-done((bf16[32,4096]{1,0:T(8,128)(2,1)S(1)}, bf16[32,4096]{1,0:T(8,128)(2,1)S(1)}, u32[]{:S(2)}, u32[]{:S(2)}) %collective-permute-start.8) | collective-permute-done | bytes 262176 | tf_op jit(solution)/shard_map/ppermute | solution.py:137
  33.7 1.3 collective-permute-done.9
  35.2 8.6 %shard_map.48.refs_2_ = f32[2,256,1024]{2,1,0:T(8,128)S(1)} custom-call(s32[1]{0:T(128)} %bitcast.1.part_ref, bf16[256,4096]{1,0:T(8,128)(2,1)S(1)} %constant_dynamic-update-slice_fusion.x_ref, bf16[4096,2048]{1,0:T(8,128)(2,1)} %refs_0_.7, bf16[4096,2048]{1,0:T(8,128)(2,1)} %refs_1_.7), custom_call_target="tpu_custom_call" | custom-call | flops 4294967296 | bytes 16777216 | tf_op jit(solution)/shard_map/pallas_call | solution.py:61
  43.9 1.6 %collective-permute-start.10 = (bf16[32,4096]{1,0:T(8,128)(2,1)S(1)}, bf16[32,4096]{1,0:T(8,128)(2,1)S(1)}, u32[]{:S(2)}, u32[]{:S(2)}) collective-permute-start(bf16[32,4096]{1,0:T(8,128)(2,1)S(1)} %get-tuple-element.43), channel_id=1, source_target_pairs={{0,2},{2,4},{4,6},{6,7},{7,5},{5,3},{3,1},{1,0},{8,10},{10,12},{12... | collective-permute-start | bytes 786440 | tf_op jit(solution)/shard_map/ppermute | solution.py:137
  46.0 8.6 %shard_map.50.refs_2_ = f32[2,256,1024]{2,1,0:T(8,128)S(1)} custom-call(s32[1]{0:T(128)} %bitcast.part_ref, bf16[256,4096]{1,0:T(8,128)(2,1)S(1)} %constant_dynamic-update-slice_fusion.x_ref, bf16[4096,2048]{1,0:T(8,128)(2,1)} %refs_0_.7, bf16[4096,2048]{1,0:T(8,128)(2,1)} %refs_1_.7, f32[2,256,1024]{2,1,0:T(8,128)S(1)} %get-tuple-element.45.refs_2_), custom_call_target="tpu_custom_call" | custom-call | flops 4294967296 | bytes 16777216 | tf_op jit(solution)/shard_map/pallas_call | solution.py:61
  54.6 1.6 %collective-permute-start.16 = (bf16[32,4096]{1,0:T(8,128)(2,1)S(1)}, bf16[32,4096]{1,0:T(8,128)(2,1)S(1)}, u32[]{:S(2)}, u32[]{:S(2)}) collective-permute-start(bf16[32,4096]{1,0:T(8,128)(2,1)S(1)} %get-tuple-element.51), channel_id=1, source_target_pairs={{0,2},{2,4},{4,6},{6,7},{7,5},{5,3},{3,1},{1,0},{8,10},{10,12},{12... | collective-permute-start | bytes 786440 | tf_op jit(solution)/shard_map/ppermute | solution.py:137
  56.7 0.5 fusion.4.a_ref
  57.3 5.4 %collective-permute-done.16 = bf16[32,4096]{1,0:T(8,128)(2,1)S(1)} collective-permute-done((bf16[32,4096]{1,0:T(8,128)(2,1)S(1)}, bf16[32,4096]{1,0:T(8,128)(2,1)S(1)}, u32[]{:S(2)}, u32[]{:S(2)}) %collective-permute-start.16) | collective-permute-done | bytes 262176 | tf_op jit(solution)/shard_map/ppermute | solution.py:137
  62.8 1.3 collective-permute-done.17
  64.3 7.3 %shard_map.52 = (bf16[32,4096]{1,0:T(8,128)(2,1)S(1)}, bf16[32,4096]{1,0:T(8,128)(2,1)S(1)}, f32[192,4096]{1,0:T(8,128)S(1)}) custom-call(s32[1]{0:T(128)} %bitcast.part_ref, bf16[256,1024]{1,0:T(8,128)(2,1)S(1)} %fusion.4.a_ref, bf16[256,1024]{1,0:T(8,128)(2,1)S(1)} %collective-permute-done.13.b_ref, bf16[2048,4096]{1,0:T(8,128)(2,1)} %d_ref.3), custom_call_target="tpu_custom_call" | custom-call | flops 4294967296 | bytes 16777216 | tf_op jit(solution)/shard_map/pallas_call | solution.py:99
  71.6 0.5 collective-permute-start.14
  72.1 1.6 %collective-permute-start.15 = (bf16[32,4096]{1,0:T(8,128)(2,1)S(1)}, bf16[32,4096]{1,0:T(8,128)(2,1)S(1)}, u32[]{:S(2)}, u32[]{:S(2)}) collective-permute-start(bf16[32,4096]{1,0:T(8,128)(2,1)S(1)} %get-tuple-element.50), channel_id=1, source_target_pairs={{0,2},{2,4},{4,6},{6,7},{7,5},{5,3},{3,1},{1,0},{8,10},{10,12},{12... | collective-permute-start | bytes 786440 | tf_op jit(solution)/shard_map/ppermute | solution.py:137
  73.7 8.6 %shard_map.53.refs_2_ = f32[2,256,1024]{2,1,0:T(8,128)S(1)} custom-call(s32[1]{0:T(128)} %bitcast.1.part_ref, bf16[256,4096]{1,0:T(8,128)(2,1)S(1)} %constant_dynamic-update-slice_fusion.8.x_ref, bf16[4096,2048]{1,0:T(8,128)(2,1)} %refs_0_.7, bf16[4096,2048]{1,0:T(8,128)(2,1)} %refs_1_.7, f32[192,4096]{1,0:T(8,128)S(1)} %get-tuple-element.48.refs_2_), custom_call_target="tpu_custom_call" | custom-call | flops 4294967296 | bytes 16777216 | tf_op jit(solution)/shard_map/pallas_call | solution.py:61
  82.5 1.6 %collective-permute-start.19 = (bf16[32,4096]{1,0:T(8,128)(2,1)S(1)}, bf16[32,4096]{1,0:T(8,128)(2,1)S(1)}, u32[]{:S(2)}, u32[]{:S(2)}) collective-permute-start(bf16[32,4096]{1,0:T(8,128)(2,1)S(1)} %get-tuple-element.83), channel_id=1, source_target_pairs={{0,2},{2,4},{4,6},{6,7},{7,5},{5,3},{3,1},{1,0},{8,10},{10,12},{12... | collective-permute-start | bytes 786440 | tf_op jit(solution)/shard_map/ppermute | solution.py:137
  84.1 0.5 collective-permute-start.18
  84.6 8.6 %shard_map.55.refs_2_ = f32[2,256,1024]{2,1,0:T(8,128)S(1)} custom-call(s32[1]{0:T(128)} %bitcast.part_ref, bf16[256,4096]{1,0:T(8,128)(2,1)S(1)} %constant_dynamic-update-slice_fusion.8.x_ref, bf16[4096,2048]{1,0:T(8,128)(2,1)} %refs_0_.7, bf16[4096,2048]{1,0:T(8,128)(2,1)} %refs_1_.7, f32[2,256,1024]{2,1,0:T(8,128)S(1)} %get-tuple-element.55.refs_2_), custom_call_target="tpu_custom_call" | custom-call | flops 4294967296 | bytes 16777216 | tf_op jit(solution)/shard_map/pallas_call | solution.py:61
  93.2 0.5 fusion.a_ref
  94.0 1.6 %collective-permute-start.25 = (bf16[32,4096]{1,0:T(8,128)(2,1)S(1)}, bf16[32,4096]{1,0:T(8,128)(2,1)S(1)}, u32[]{:S(2)}, u32[]{:S(2)}) collective-permute-start(bf16[32,4096]{1,0:T(8,128)(2,1)S(1)} %get-tuple-element.81), channel_id=1, source_target_pairs={{0,2},{2,4},{4,6},{6,7},{7,5},{5,3},{3,1},{1,0},{8,10},{10,12},{12... | collective-permute-start | bytes 786440 | tf_op jit(solution)/shard_map/ppermute | solution.py:137
  95.5 0.5 collective-permute-start.24
  96.0 7.3 %shard_map.57 = (bf16[32,4096]{1,0:T(8,128)(2,1)S(1)}, bf16[32,4096]{1,0:T(8,128)(2,1)S(1)}, f32[192,4096]{1,0:T(8,128)S(1)}) custom-call(s32[1]{0:T(128)} %bitcast.part_ref, bf16[256,1024]{1,0:T(8,128)(2,1)S(1)} %fusion.a_ref, bf16[256,1024]{1,0:T(8,128)(2,1)S(1)} %collective-permute-done.21.b_ref, bf16[2048,4096]{1,0:T(8,128)(2,1)} %d_ref.3), custom_call_target="tpu_custom_call" | custom-call | flops 4294967296 | bytes 16777216 | tf_op jit(solution)/shard_map/pallas_call | solution.py:99
  103.4 0.6 collective-permute-done.24.refs_0_
  104.0 1.0 collective-permute-start.27
  105.1 1.1 collective-permute-start.26
  106.1 0.5 collective-permute-start.22
  106.6 1.5 %collective-permute-start.23 = (bf16[32,4096]{1,0:T(8,128)(2,1)S(1)}, bf16[32,4096]{1,0:T(8,128)(2,1)S(1)}, u32[]{:S(2)}, u32[]{:S(2)}) collective-permute-start(bf16[32,4096]{1,0:T(8,128)(2,1)S(1)} %get-tuple-element.60.refs_3_), channel_id=1, source_target_pairs={{0,2},{2,4},{4,6},{6,7},{7,5},{5,3},{3,1},{1,0},{8,10},{10,12},{12... | collective-permute-start | bytes 786440 | tf_op jit(solution)/shard_map/ppermute | solution.py:137
  108.1 5.2 %collective-permute-done.27.refs_3_ = bf16[32,4096]{1,0:T(8,128)(2,1)S(1)} collective-permute-done((bf16[32,4096]{1,0:T(8,128)(2,1)S(1)}, bf16[32,4096]{1,0:T(8,128)(2,1)S(1)}, u32[]{:S(2)}, u32[]{:S(2)}) %collective-permute-start.27) | collective-permute-done | bytes 262176 | tf_op jit(solution)/shard_map/ppermute | solution.py:137
  113.3 0.9 collective-permute-done.26.refs_2_
  114.3 4.3 %collective-permute-done.22.refs_0_ = bf16[32,4096]{1,0:T(8,128)(2,1)S(1)} collective-permute-done((bf16[32,4096]{1,0:T(8,128)(2,1)S(1)}, bf16[32,4096]{1,0:T(8,128)(2,1)S(1)}, u32[]{:S(2)}, u32[]{:S(2)}) %collective-permute-start.22) | collective-permute-done | bytes 262176 | tf_op jit(solution)/shard_map/ppermute | solution.py:140
  118.7 0.8 collective-permute-start.29
  119.5 1.2 collective-permute-start.28
  120.8 4.9 %collective-permute-done.29.refs_1_ = bf16[32,4096]{1,0:T(8,128)(2,1)S(1)} collective-permute-done((bf16[32,4096]{1,0:T(8,128)(2,1)S(1)}, bf16[32,4096]{1,0:T(8,128)(2,1)S(1)}, u32[]{:S(2)}, u32[]{:S(2)}) %collective-permute-start.29) | collective-permute-done | bytes 262176 | tf_op jit(solution)/shard_map/ppermute | solution.py:137
  125.7 0.5 collective-permute-done.28.refs_0_
  126.3 0.6 collective-permute-start.31
  127.0 1.4 %collective-permute-start.30 = (bf16[32,4096]{1,0:T(8,128)(2,1)S(1)}, bf16[32,4096]{1,0:T(8,128)(2,1)S(1)}, u32[]{:S(2)}, u32[]{:S(2)}) collective-permute-start(bf16[32,4096]{1,0:T(8,128)(2,1)S(1)} %get-tuple-element.76), channel_id=1, source_target_pairs={{2,0},{4,2},{6,4},{7,6},{5,7},{3,5},{1,3},{0,1},{10,8},{12,10},{14... | collective-permute-start | bytes 786440 | tf_op jit(solution)/shard_map/ppermute | solution.py:140
  128.4 4.3 %collective-permute-done.31.refs_1_ = bf16[32,4096]{1,0:T(8,128)(2,1)S(1)} collective-permute-done((bf16[32,4096]{1,0:T(8,128)(2,1)S(1)}, bf16[32,4096]{1,0:T(8,128)(2,1)S(1)}, u32[]{:S(2)}, u32[]{:S(2)}) %collective-permute-start.31) | collective-permute-done | bytes 262176 | tf_op jit(solution)/shard_map/ppermute | solution.py:137
  132.7 0.6 collective-permute-done.30.refs_0_
  133.5 0.8 pad_maximum_fusion
  (59 shorter events, 3.4 us)
Async XLA Ops:
  1.1 9.3 %collective-permute-start = (bf16[32,4096]{1,0:T(8,128)(2,1)S(1)}, bf16[32,4096]{1,0:T(8,128)(2,1)S(1)}, u32[]{:S(2)}, u32[]{:S(2)}) collective-permute-start(bf16[32,4096]{1,0:T(8,128)(2,1)S(1)} %get-tuple-element.85.refs_1_), channel_id=1, source_target_pairs={{0,2},{2,4},{4,6},{6,7},{7,5},{5,3},{3,1},{1,0},{8,10},{10,12},{12... | collective-permute-start | bytes 786440 | tf_op jit(solution)/shard_map/ppermute | solution.py:137
  4.1 8.0 %collective-permute-start.3 = (bf16[32,4096]{1,0:T(8,128)(2,1)S(1)}, bf16[32,4096]{1,0:T(8,128)(2,1)S(1)}, u32[]{:S(2)}, u32[]{:S(2)}) collective-permute-start(bf16[32,4096]{1,0:T(8,128)(2,1)S(1)} %get-tuple-element.86.refs_0_), channel_id=1, source_target_pairs={{2,0},{4,2},{6,4},{7,6},{5,7},{3,5},{1,3},{0,1},{10,8},{12,10},{14... | collective-permute-start | bytes 786440 | tf_op jit(solution)/shard_map/ppermute | solution.py:140
  10.4 7.5 %collective-permute-start.1 = (bf16[32,4096]{1,0:T(8,128)(2,1)S(1)}, bf16[32,4096]{1,0:T(8,128)(2,1)S(1)}, u32[]{:S(2)}, u32[]{:S(2)}) collective-permute-start(bf16[32,4096]{1,0:T(8,128)(2,1)S(1)} %collective-permute-done), channel_id=1, source_target_pairs={{0,2},{2,4},{4,6},{6,7},{7,5},{5,3},{3,1},{1,0},{8,10},{10,12},{12... | collective-permute-start | bytes 786440 | tf_op jit(solution)/shard_map/ppermute | solution.py:137
  12.2 7.2 %collective-permute-start.4 = (bf16[32,4096]{1,0:T(8,128)(2,1)S(1)}, bf16[32,4096]{1,0:T(8,128)(2,1)S(1)}, u32[]{:S(2)}, u32[]{:S(2)}) collective-permute-start(bf16[32,4096]{1,0:T(8,128)(2,1)S(1)} %collective-permute-done.3), channel_id=1, source_target_pairs={{2,0},{4,2},{6,4},{7,6},{5,7},{3,5},{1,3},{0,1},{10,8},{12,10},{14... | collective-permute-start | bytes 786440 | tf_op jit(solution)/shard_map/ppermute | solution.py:140
  17.9 6.6 %collective-permute-start.2 = (bf16[32,4096]{1,0:T(8,128)(2,1)S(1)}, bf16[32,4096]{1,0:T(8,128)(2,1)S(1)}, u32[]{:S(2)}, u32[]{:S(2)}) collective-permute-start(bf16[32,4096]{1,0:T(8,128)(2,1)S(1)} %collective-permute-done.1), channel_id=1, source_target_pairs={{0,2},{2,4},{4,6},{6,7},{7,5},{5,3},{3,1},{1,0},{8,10},{10,12},{12... | collective-permute-start | bytes 786440 | tf_op jit(solution)/shard_map/ppermute | solution.py:137
  19.4 6.4 %collective-permute-start.5 = (bf16[32,4096]{1,0:T(8,128)(2,1)S(1)}, bf16[32,4096]{1,0:T(8,128)(2,1)S(1)}, u32[]{:S(2)}, u32[]{:S(2)}) collective-permute-start(bf16[32,4096]{1,0:T(8,128)(2,1)S(1)} %collective-permute-done.4), channel_id=1, source_target_pairs={{2,0},{4,2},{6,4},{7,6},{5,7},{3,5},{1,3},{0,1},{10,8},{12,10},{14... | collective-permute-start | bytes 786440 | tf_op jit(solution)/shard_map/ppermute | solution.py:140
  25.7 7.9 %collective-permute-start.8 = (bf16[32,4096]{1,0:T(8,128)(2,1)S(1)}, bf16[32,4096]{1,0:T(8,128)(2,1)S(1)}, u32[]{:S(2)}, u32[]{:S(2)}) collective-permute-start(bf16[32,4096]{1,0:T(8,128)(2,1)S(1)} %get-tuple-element.39.refs_2_), channel_id=1, source_target_pairs={{0,2},{2,4},{4,6},{6,7},{7,5},{5,3},{3,1},{1,0},{8,10},{10,12},{12... | collective-permute-start | bytes 786440 | tf_op jit(solution)/shard_map/ppermute | solution.py:137
  27.3 7.6 %collective-permute-start.9 = (bf16[32,4096]{1,0:T(8,128)(2,1)S(1)}, bf16[32,4096]{1,0:T(8,128)(2,1)S(1)}, u32[]{:S(2)}, u32[]{:S(2)}) collective-permute-start(bf16[32,4096]{1,0:T(8,128)(2,1)S(1)} %get-tuple-element.40.refs_3_), channel_id=1, source_target_pairs={{2,0},{4,2},{6,4},{7,6},{5,7},{3,5},{1,3},{0,1},{10,8},{12,10},{14... | collective-permute-start | bytes 786440 | tf_op jit(solution)/shard_map/ppermute | solution.py:140
  27.8 16.0 %collective-permute-start.6 = (bf16[32,4096]{1,0:T(8,128)(2,1)S(1)}, bf16[32,4096]{1,0:T(8,128)(2,1)S(1)}, u32[]{:S(2)}, u32[]{:S(2)}) collective-permute-start(bf16[32,4096]{1,0:T(8,128)(2,1)S(1)} %get-tuple-element.41), channel_id=1, source_target_pairs={{0,2},{2,4},{4,6},{6,7},{7,5},{5,3},{3,1},{1,0},{8,10},{10,12},{12... | collective-permute-start | bytes 786440 | tf_op jit(solution)/shard_map/ppermute | solution.py:137
  29.3 14.4 %collective-permute-start.7 = (bf16[32,4096]{1,0:T(8,128)(2,1)S(1)}, bf16[32,4096]{1,0:T(8,128)(2,1)S(1)}, u32[]{:S(2)}, u32[]{:S(2)}) collective-permute-start(bf16[32,4096]{1,0:T(8,128)(2,1)S(1)} %get-tuple-element.42), channel_id=1, source_target_pairs={{2,0},{4,2},{6,4},{7,6},{5,7},{3,5},{1,3},{0,1},{10,8},{12,10},{14... | collective-permute-start | bytes 786440 | tf_op jit(solution)/shard_map/ppermute | solution.py:140
  43.8 10.8 %collective-permute-start.12 = (f32[2,256,1024]{2,1,0:T(8,128)S(1)}, f32[2,256,1024]{2,1,0:T(8,128)S(1)}, u32[]{:S(2)}, u32[]{:S(2)}) collective-permute-start(f32[2,256,1024]{2,1,0:T(8,128)S(1)} %get-tuple-element.45.refs_2_), channel_id=1, source_target_pairs={{0,8},{8,0},{1,9},{9,1},{2,10},{10,2},{3,11},{11,3},{4,12},{12,4},... | collective-permute-start | bytes 6291464 | tf_op jit(solution)/shard_map/ppermute | solution.py:143
  43.9 10.7 %collective-permute-start.10 = (bf16[32,4096]{1,0:T(8,128)(2,1)S(1)}, bf16[32,4096]{1,0:T(8,128)(2,1)S(1)}, u32[]{:S(2)}, u32[]{:S(2)}) collective-permute-start(bf16[32,4096]{1,0:T(8,128)(2,1)S(1)} %get-tuple-element.43), channel_id=1, source_target_pairs={{0,2},{2,4},{4,6},{6,7},{7,5},{5,3},{3,1},{1,0},{8,10},{10,12},{12... | collective-permute-start | bytes 786440 | tf_op jit(solution)/shard_map/ppermute | solution.py:137
  45.5 9.1 %collective-permute-start.11 = (bf16[32,4096]{1,0:T(8,128)(2,1)S(1)}, bf16[32,4096]{1,0:T(8,128)(2,1)S(1)}, u32[]{:S(2)}, u32[]{:S(2)}) collective-permute-start(bf16[32,4096]{1,0:T(8,128)(2,1)S(1)} %get-tuple-element.44), channel_id=1, source_target_pairs={{2,0},{4,2},{6,4},{7,6},{5,7},{3,5},{1,3},{0,1},{10,8},{12,10},{14... | collective-permute-start | bytes 786440 | tf_op jit(solution)/shard_map/ppermute | solution.py:140
  54.6 8.1 %collective-permute-start.16 = (bf16[32,4096]{1,0:T(8,128)(2,1)S(1)}, bf16[32,4096]{1,0:T(8,128)(2,1)S(1)}, u32[]{:S(2)}, u32[]{:S(2)}) collective-permute-start(bf16[32,4096]{1,0:T(8,128)(2,1)S(1)} %get-tuple-element.51), channel_id=1, source_target_pairs={{0,2},{2,4},{4,6},{6,7},{7,5},{5,3},{3,1},{1,0},{8,10},{10,12},{12... | collective-permute-start | bytes 786440 | tf_op jit(solution)/shard_map/ppermute | solution.py:137
  56.3 7.8 %collective-permute-start.17 = (bf16[32,4096]{1,0:T(8,128)(2,1)S(1)}, bf16[32,4096]{1,0:T(8,128)(2,1)S(1)}, u32[]{:S(2)}, u32[]{:S(2)}) collective-permute-start(bf16[32,4096]{1,0:T(8,128)(2,1)S(1)} %get-tuple-element.52), channel_id=1, source_target_pairs={{2,0},{4,2},{6,4},{7,6},{5,7},{3,5},{1,3},{0,1},{10,8},{12,10},{14... | collective-permute-start | bytes 786440 | tf_op jit(solution)/shard_map/ppermute | solution.py:140
  57.2 7.0 %copy-start = (bf16[64,4096]{1,0:T(8,128)(2,1)S(1)}, bf16[64,4096]{1,0:T(8,128)(2,1)}, u32[]{:S(2)}) copy-start(bf16[64,4096]{1,0:T(8,128)(2,1)} %param.4) | copy-start | bytes 1572868
  57.3 7.0 %collective-permute-start.13 = (bf16[256,1024]{1,0:T(8,128)(2,1)S(1)}, bf16[256,1024]{1,0:T(8,128)(2,1)S(1)}, u32[]{:S(2)}, u32[]{:S(2)}) collective-permute-start(bf16[256,1024]{1,0:T(8,128)(2,1)S(1)} %fusion.4.a_ref), channel_id=1, source_target_pairs={{0,8},{8,0},{1,9},{9,1},{2,10},{10,2},{3,11},{11,3},{4,12},{12,4},... | collective-permute-start | bytes 1572872 | tf_op jit(solution)/shard_map/ppermute | solution.py:143
  71.6 10.7 %collective-permute-start.14 = (bf16[32,4096]{1,0:T(8,128)(2,1)S(1)}, bf16[32,4096]{1,0:T(8,128)(2,1)S(1)}, u32[]{:S(2)}, u32[]{:S(2)}) collective-permute-start(bf16[32,4096]{1,0:T(8,128)(2,1)S(1)} %get-tuple-element.49), channel_id=1, source_target_pairs={{2,0},{4,2},{6,4},{7,6},{5,7},{3,5},{1,3},{0,1},{10,8},{12,10},{14... | collective-permute-start | bytes 786440 | tf_op jit(solution)/shard_map/ppermute | solution.py:140
  72.1 10.2 %collective-permute-start.15 = (bf16[32,4096]{1,0:T(8,128)(2,1)S(1)}, bf16[32,4096]{1,0:T(8,128)(2,1)S(1)}, u32[]{:S(2)}, u32[]{:S(2)}) collective-permute-start(bf16[32,4096]{1,0:T(8,128)(2,1)S(1)} %get-tuple-element.50), channel_id=1, source_target_pairs={{0,2},{2,4},{4,6},{6,7},{7,5},{5,3},{3,1},{1,0},{8,10},{10,12},{12... | collective-permute-start | bytes 786440 | tf_op jit(solution)/shard_map/ppermute | solution.py:137
  82.3 10.9 %collective-permute-start.20 = (f32[2,256,1024]{2,1,0:T(8,128)S(1)}, f32[2,256,1024]{2,1,0:T(8,128)S(1)}, u32[]{:S(2)}, u32[]{:S(2)}) collective-permute-start(f32[2,256,1024]{2,1,0:T(8,128)S(1)} %get-tuple-element.55.refs_2_), channel_id=1, source_target_pairs={{0,8},{8,0},{1,9},{9,1},{2,10},{10,2},{3,11},{11,3},{4,12},{12,4},... | collective-permute-start | bytes 6291464 | tf_op jit(solution)/shard_map/ppermute | solution.py:143
  82.5 10.7 %collective-permute-start.19 = (bf16[32,4096]{1,0:T(8,128)(2,1)S(1)}, bf16[32,4096]{1,0:T(8,128)(2,1)S(1)}, u32[]{:S(2)}, u32[]{:S(2)}) collective-permute-start(bf16[32,4096]{1,0:T(8,128)(2,1)S(1)} %get-tuple-element.83), channel_id=1, source_target_pairs={{0,2},{2,4},{4,6},{6,7},{7,5},{5,3},{3,1},{1,0},{8,10},{10,12},{12... | collective-permute-start | bytes 786440 | tf_op jit(solution)/shard_map/ppermute | solution.py:137
  84.1 9.1 %collective-permute-start.18 = (bf16[32,4096]{1,0:T(8,128)(2,1)S(1)}, bf16[32,4096]{1,0:T(8,128)(2,1)S(1)}, u32[]{:S(2)}, u32[]{:S(2)}) collective-permute-start(bf16[32,4096]{1,0:T(8,128)(2,1)S(1)} %get-tuple-element.84), channel_id=1, source_target_pairs={{2,0},{4,2},{6,4},{7,6},{5,7},{3,5},{1,3},{0,1},{10,8},{12,10},{14... | collective-permute-start | bytes 786440 | tf_op jit(solution)/shard_map/ppermute | solution.py:140
  93.8 2.3 %collective-permute-start.21 = (bf16[256,1024]{1,0:T(8,128)(2,1)S(1)}, bf16[256,1024]{1,0:T(8,128)(2,1)S(1)}, u32[]{:S(2)}, u32[]{:S(2)}) collective-permute-start(bf16[256,1024]{1,0:T(8,128)(2,1)S(1)} %fusion.a_ref), channel_id=1, source_target_pairs={{0,8},{8,0},{1,9},{9,1},{2,10},{10,2},{3,11},{11,3},{4,12},{12,4},... | collective-permute-start | bytes 1572872 | tf_op jit(solution)/shard_map/ppermute | solution.py:143
  94.0 9.4 %collective-permute-start.25 = (bf16[32,4096]{1,0:T(8,128)(2,1)S(1)}, bf16[32,4096]{1,0:T(8,128)(2,1)S(1)}, u32[]{:S(2)}, u32[]{:S(2)}) collective-permute-start(bf16[32,4096]{1,0:T(8,128)(2,1)S(1)} %get-tuple-element.81), channel_id=1, source_target_pairs={{0,2},{2,4},{4,6},{6,7},{7,5},{5,3},{3,1},{1,0},{8,10},{10,12},{12... | collective-permute-start | bytes 786440 | tf_op jit(solution)/shard_map/ppermute | solution.py:137
  95.5 8.4 %collective-permute-start.24 = (bf16[32,4096]{1,0:T(8,128)(2,1)S(1)}, bf16[32,4096]{1,0:T(8,128)(2,1)S(1)}, u32[]{:S(2)}, u32[]{:S(2)}) collective-permute-start(bf16[32,4096]{1,0:T(8,128)(2,1)S(1)} %get-tuple-element.82), channel_id=1, source_target_pairs={{2,0},{4,2},{6,4},{7,6},{5,7},{3,5},{1,3},{0,1},{10,8},{12,10},{14... | collective-permute-start | bytes 786440 | tf_op jit(solution)/shard_map/ppermute | solution.py:140
  104.0 9.3 %collective-permute-start.27 = (bf16[32,4096]{1,0:T(8,128)(2,1)S(1)}, bf16[32,4096]{1,0:T(8,128)(2,1)S(1)}, u32[]{:S(2)}, u32[]{:S(2)}) collective-permute-start(bf16[32,4096]{1,0:T(8,128)(2,1)S(1)} %get-tuple-element.79), channel_id=1, source_target_pairs={{0,2},{2,4},{4,6},{6,7},{7,5},{5,3},{3,1},{1,0},{8,10},{10,12},{12... | collective-permute-start | bytes 786440 | tf_op jit(solution)/shard_map/ppermute | solution.py:137
  105.1 9.2 %collective-permute-start.26 = (bf16[32,4096]{1,0:T(8,128)(2,1)S(1)}, bf16[32,4096]{1,0:T(8,128)(2,1)S(1)}, u32[]{:S(2)}, u32[]{:S(2)}) collective-permute-start(bf16[32,4096]{1,0:T(8,128)(2,1)S(1)} %get-tuple-element.80), channel_id=1, source_target_pairs={{2,0},{4,2},{6,4},{7,6},{5,7},{3,5},{1,3},{0,1},{10,8},{12,10},{14... | collective-permute-start | bytes 786440 | tf_op jit(solution)/shard_map/ppermute | solution.py:140
  106.1 12.4 %collective-permute-start.22 = (bf16[32,4096]{1,0:T(8,128)(2,1)S(1)}, bf16[32,4096]{1,0:T(8,128)(2,1)S(1)}, u32[]{:S(2)}, u32[]{:S(2)}) collective-permute-start(bf16[32,4096]{1,0:T(8,128)(2,1)S(1)} %get-tuple-element.59.refs_2_), channel_id=1, source_target_pairs={{2,0},{4,2},{6,4},{7,6},{5,7},{3,5},{1,3},{0,1},{10,8},{12,10},{14... | collective-permute-start | bytes 786440 | tf_op jit(solution)/shard_map/ppermute | solution.py:140
  106.6 11.9 %collective-permute-start.23 = (bf16[32,4096]{1,0:T(8,128)(2,1)S(1)}, bf16[32,4096]{1,0:T(8,128)(2,1)S(1)}, u32[]{:S(2)}, u32[]{:S(2)}) collective-permute-start(bf16[32,4096]{1,0:T(8,128)(2,1)S(1)} %get-tuple-element.60.refs_3_), channel_id=1, source_target_pairs={{0,2},{2,4},{4,6},{6,7},{7,5},{5,3},{3,1},{1,0},{8,10},{10,12},{12... | collective-permute-start | bytes 786440 | tf_op jit(solution)/shard_map/ppermute | solution.py:137
  118.7 7.0 %collective-permute-start.29 = (bf16[32,4096]{1,0:T(8,128)(2,1)S(1)}, bf16[32,4096]{1,0:T(8,128)(2,1)S(1)}, u32[]{:S(2)}, u32[]{:S(2)}) collective-permute-start(bf16[32,4096]{1,0:T(8,128)(2,1)S(1)} %get-tuple-element.77), channel_id=1, source_target_pairs={{0,2},{2,4},{4,6},{6,7},{7,5},{5,3},{3,1},{1,0},{8,10},{10,12},{12... | collective-permute-start | bytes 786440 | tf_op jit(solution)/shard_map/ppermute | solution.py:137
  119.5 6.7 %collective-permute-start.28 = (bf16[32,4096]{1,0:T(8,128)(2,1)S(1)}, bf16[32,4096]{1,0:T(8,128)(2,1)S(1)}, u32[]{:S(2)}, u32[]{:S(2)}) collective-permute-start(bf16[32,4096]{1,0:T(8,128)(2,1)S(1)} %get-tuple-element.78), channel_id=1, source_target_pairs={{2,0},{4,2},{6,4},{7,6},{5,7},{3,5},{1,3},{0,1},{10,8},{12,10},{14... | collective-permute-start | bytes 786440 | tf_op jit(solution)/shard_map/ppermute | solution.py:140
  126.3 6.4 %collective-permute-start.31 = (bf16[32,4096]{1,0:T(8,128)(2,1)S(1)}, bf16[32,4096]{1,0:T(8,128)(2,1)S(1)}, u32[]{:S(2)}, u32[]{:S(2)}) collective-permute-start(bf16[32,4096]{1,0:T(8,128)(2,1)S(1)} %get-tuple-element.75), channel_id=1, source_target_pairs={{0,2},{2,4},{4,6},{6,7},{7,5},{5,3},{3,1},{1,0},{8,10},{10,12},{12... | collective-permute-start | bytes 786440 | tf_op jit(solution)/shard_map/ppermute | solution.py:137
  127.0 6.4 %collective-permute-start.30 = (bf16[32,4096]{1,0:T(8,128)(2,1)S(1)}, bf16[32,4096]{1,0:T(8,128)(2,1)S(1)}, u32[]{:S(2)}, u32[]{:S(2)}) collective-permute-start(bf16[32,4096]{1,0:T(8,128)(2,1)S(1)} %get-tuple-element.76), channel_id=1, source_target_pairs={{2,0},{4,2},{6,4},{7,6},{5,7},{3,5},{1,3},{0,1},{10,8},{12,10},{14... | collective-permute-start | bytes 786440 | tf_op jit(solution)/shard_map/ppermute | solution.py:140

commit v6 on v0

v6 whole, which is shorter than its diff:
```python
import jax
import jax.numpy as jnp
from jax import lax
from jax.experimental import pallas as pl
from jax.experimental.pallas import tpu as pltpu
from jax.sharding import PartitionSpec as P

F32, BF16 = jnp.float32, jnp.bfloat16
ANY = pl.BlockSpec(memory_space=pl.ANY)
SMEM = pl.BlockSpec(memory_space=pltpu.SMEM)
VMEM = pl.BlockSpec(memory_space=pltpu.VMEM)


def ring_of(n):
    return list(range(0, n, 2)) + list(range(n - 1, 0, -2))


def in_hbm(x):
    return pltpu.with_memory_space_constraint(x, pltpu.HBM)


def in_vmem(x):
    return pltpu.with_memory_space_constraint(x, pltpu.VMEM)


def params(vmem, flops, read):
    return dict(
        compiler_params=pltpu.CompilerParams(vmem_limit_bytes=vmem),
        cost_estimate=pl.CostEstimate(
            flops=flops, bytes_accessed=read, transcendentals=0
        ),
    )


def gate(*arrays, after=()):
    return pl.pallas_call(
        lambda *refs: None,
        in_specs=[ANY] * (len(arrays) + len(after)),
        out_specs=[ANY] * len(arrays),
        out_shape=[jax.ShapeDtypeStruct(x.shape, x.dtype) for x in arrays],
        input_output_aliases={i: i for i in range(len(arrays))},
        **params(1 << 18, 0, 0),
    )(*arrays, *after)


def split(r, l):
    cut, n = r.shape[0] // 2, r.shape[1]
    if cut % 16:
        return r[:cut], l[cut:]

    def body(r_ref, l_ref, a_ref, b_ref):
        a_ref[...] = r_ref[:cut]
        b_ref[...] = l_ref[cut:]

    return pl.pallas_call(
        body,
        in_specs=[VMEM, VMEM],
        out_specs=[VMEM, VMEM],
        out_shape=[jax.ShapeDtypeStruct((cut, n), r.dtype)] * 2,
        **params(4 << 20, 0, 8 * cut * n),
    )(r, l)


def bring(weights, parts, after, pieces=8):
    k, w = weights[0].shape[0], weights[0].shape[1] // 2
    step = k // pieces
    count = len(weights) * len(parts)

    def body(*refs):
        sources, refs = refs[: len(weights)], refs[len(weights) :]
        targets, sems = refs[-1 - count : -1], refs[-1]
        copies = []
        for i, target in enumerate(targets):
            start = pl.multiple_of(refs[i // len(weights)][0] * w, w)
            for s in range(pieces):
                rows = pl.ds(s * step, step)
                copies.append(
                    pltpu.make_async_copy(
                        sources[i % len(weights)].at[rows, pl.ds(start, w)],
                        target.at[rows],
                        sems.at[i, s],
                    )
                )
        for copy in copies:
            copy.start()
        for copy in copies:
            copy.wait()

    return pl.pallas_call(
        body,
        in_specs=[ANY] * len(weights) + [SMEM] * len(parts) + [ANY] * len(after),
        out_specs=[VMEM] * count,
        out_shape=[pltpu.VMEM((k, w), weights[0].dtype)] * count,
        scratch_shapes=[pltpu.SemaphoreType.DMA((count, pieces))],
        **params(1 << 18, 0, 4 * sum(w.size for w in weights)),
    )(*map(in_hbm, weights), *parts, *after)


def gate_up(pieces, weights, after):
    if any(p.shape[0] % 16 for p in pieces):
        pieces = [jnp.concatenate(pieces, axis=0)]
    m, k = sum(p.shape[0] for p in pieces), pieces[0].shape[1]
    w = weights[0].shape[1]
    tile = min(w, 256)
    count, halves = len(pieces), len(weights) // 2

    def body(*refs):
        weight_refs = refs[count : count + len(weights)]
        out_refs, x_ref = refs[-1 - halves : -1], refs[-1]
        at = 0
        for ref in refs[:count]:
            x_ref[at : at + ref.shape[0]] = ref[...]
            at += ref.shape[0]

        @pl.loop(0, w // tile)
        def _(j):
            cols = pl.ds(pl.multiple_of(j * tile, tile), tile)
            for i, ref in enumerate(weight_refs):
                out_refs[i // 2][i % 2, :, cols] = jnp.dot(
                    x_ref[...], ref[:, cols], preferred_element_type=F32
                )

    shape = jax.ShapeDtypeStruct((2, m, w), F32)
    return pl.pallas_call(
        body,
        in_specs=[VMEM] * (count + len(weights)) + [ANY] * len(after),
        out_specs=[VMEM] * halves,
        out_shape=[shape] * halves,
        scratch_shapes=[pltpu.VMEM((m, k), BF16)],
        **params(6 << 20, 4 * halves * m * k * w, 4 * halves * k * w),
    )(*pieces, *map(in_vmem, weights), *after)


def gated(ours, theirs):
    _, m, w = ours.shape
    tile = min(w, 256)

    def body(a_ref, b_ref, o_ref):
        @pl.loop(0, w // tile)
        def _(j):
            cols = pl.ds(pl.multiple_of(j * tile, tile), tile)
            v = a_ref[0, :, cols] + b_ref[0, :, cols]
            u = a_ref[1, :, cols] + b_ref[1, :, cols]
            o_ref[:, cols] = (v / (1.0 + jnp.exp(-v)) * u).astype(BF16)

    return pl.pallas_call(
        body,
        in_specs=[VMEM, VMEM],
        out_specs=VMEM,
        out_shape=jax.ShapeDtypeStruct((m, w), BF16),
        **params(4 << 20, 8 * m * w, 16 * m * w),
    )(ours, theirs)


def down(halves, weight, part, outs, after):
    m = sum(h.shape[0] for h, _ in halves)
    w = halves[0][0].shape[1]
    n = weight.shape[1]
    tile, deep = 512, min(2 * w, 512)
    steps = n // tile
    if any(h.shape[0] % 16 for h, _ in halves):
        halves = [tuple(jnp.concatenate(hs, axis=0) for hs in zip(*halves))]
    count = len(halves)

    def body(part_ref, *refs):
        d_ref, (h_ref, held_ref, sems) = refs[2 * count], refs[-3:]
        out_refs = refs[-3 - len(outs) : -3]

        def fetch(j, i):
            rows = pl.ds(i * deep, deep)
            cols = pl.ds(pl.multiple_of(j * tile, tile), tile)
            return pltpu.make_async_copy(
                d_ref.at[rows, cols], held_ref.at[j, rows], sems.at[j, i]
            )

        for j in range(steps):
            for i in range(2 * w // deep):
                fetch(j, i).start()
        at = 0
        for i in range(count):
            rows = slice(at, at + refs[2 * i].shape[0])
            at = rows.stop
            first = pl.multiple_of(part_ref[0] * w, w)
            h_ref[rows, pl.ds(first, w)] = refs[2 * i][...]
            h_ref[rows, pl.ds(pl.multiple_of(w - first, w), w)] = refs[2 * i + 1][...]

        @pl.loop(0, steps)
        def _(j):
            cols = pl.ds(pl.multiple_of(j * tile, tile), tile)
            for i in range(2 * w // deep):
                fetch(j, i).wait()
            out = jnp.dot(h_ref[...], held_ref[j], preferred_element_type=F32)
            for (at, size, dtype), ref in zip(outs, out_refs):
                ref[:, cols] = out[at : at + size].astype(dtype)

    return pl.pallas_call(
        body,
        in_specs=[SMEM] + [VMEM] * (2 * count) + [ANY] * (1 + len(after)),
        out_specs=[VMEM] * len(outs),
        out_shape=[jax.ShapeDtypeStruct((size, n), dtype) for _, size, dtype in outs],
        scratch_shapes=[
            pltpu.VMEM((m, 2 * w), BF16),
            pltpu.VMEM((steps, 2 * w, tile), BF16),
            pltpu.SemaphoreType.DMA((steps, 2 * w // deep)),
        ],
        **params(24 << 20, 4 * m * w * n, 4 * w * n),
    )(part, *[h for pair in halves for h in pair], in_hbm(weight), *after)


def make_shards(n):
    ring = ring_of(n)
    half = n // 2
    to_right = [(ring[i], ring[(i + 1) % n]) for i in range(n)]
    to_left = [(ring[(i + 1) % n], ring[i]) for i in range(n)]
    swap = [(0, 1), (1, 0)]

    def right(x):
        return lax.ppermute(x, "gy", to_right)

    def left(x):
        return lax.ppermute(x, "gy", to_left)

    def other(x):
        return lax.ppermute(x, "gx", swap)

    def add(part, block):
        return (part + block.astype(F32)).astype(BF16)

    def shards(tokens, gate_weight, up_weight, down_weight):
        rows = tokens.shape[0]
        cut = rows // 2
        core = lax.axis_index("gx").astype(jnp.int32)
        keep, give = core.reshape(1), (1 - core).reshape(1)

        r, l = right(tokens), left(tokens)
        wide = bring([gate_weight, up_weight], [give, keep], [])
        r, l = gate(r, l, after=wide[-1:])
        groups, sums = [[tokens, r, l]], []
        for d in range(2, half):
            r, l = right(r), left(l)
            theirs, ours = gate_up(groups[-1], wide, sums[-1:])
            r, l, theirs, ours = gate(r, l, theirs, ours)
            groups.append([r, l])
            sums += [theirs, ours]
        far_l, far_r = split(r, l)
        far_l, far_r = right(far_l), left(far_r)
        got = [other(theirs) for theirs in sums[::2]]
        far_l, far_r, r, l, *got = gate(far_l, far_r, r, l, *got)

        def hide(ours, got):
            h = gated(ours, got)
            return h, other(h)

        (theirs,) = gate_up([far_l, far_r, r, l], wide[:2], [])
        far_got = other(theirs)
        (ours,) = gate_up([far_l, far_r, r, l], wide[2:], [theirs])
        far = hide(ours, far_got)
        near = [hide(*pair) for pair in zip(sums[1::2], got)]
        at = [(i * cut, cut) for i in range(6)]
        outs = [(*at[3], BF16), (*at[4], BF16), (*at[0], BF16), (*at[1], BF16)]
        outs += [(*at[2], F32), (*at[5], F32)]
        b_l, b_r, a_l, a_r, next_l, next_r = down([far], down_weight, keep, outs, [])

        b_l, b_r = left(b_l), right(b_r)
        a_l, a_r = left(a_l), right(a_r)
        size = rows * (2 * half - 3)
        (rest,) = down(near, down_weight, keep, [(0, size, F32)], [next_l])

        def parts(d):
            first = rows * (2 * d - 1)
            return [rest[first + i * cut : first + (i + 1) * cut] for i in range(4)]

        after = [rest]
        for d in range(half - 2, -1, -1):
            b_l, b_r = gate(b_l, b_r, after=after)
            if d > 0:
                _, left_b, right_a, _ = parts(d)
                b_l, b_r = add(left_b, b_l), add(right_a, b_r)
                after = [b_l, b_r]
                b_l, b_r = left(b_l), right(b_r)
            else:
                after = [b_l, b_r]
            a_l, a_r = gate(a_l, a_r, after=after)
            a_l, a_r = add(next_l, a_l), add(next_r, a_r)
            after = [a_l, a_r]
            a_l, a_r = left(a_l), right(a_r)
            if d > 0:
                next_l, _, _, next_r = parts(d)
        a_l, a_r = gate(a_l, a_r)
        total_a = rest[:cut] + a_l.astype(F32) + b_r.astype(F32)
        total_b = rest[cut:rows] + a_r.astype(F32) + b_l.astype(F32)
        return jnp.concatenate([total_a, total_b], axis=0).astype(BF16)

    return shards


def solution(mesh):
    return jax.shard_map(
        make_shards(mesh.shape["gy"]),
        mesh=mesh,
        in_specs=(P(("groups", "gy"), "gx"), P("gx", "gy"), P("gx", "gy"), P("gy", "gx")),
        out_specs=P(("groups", "gy"), "gx"),
        check_vma=False,
    )
```

time: 328 us -> 119 us (0.36)
  waiting for transfers between devices: 267 us -> 43.6 us
  Pallas kernels: 0 us -> 48.8 us
  matrix products: 42.4 us -> 0 us
  starting transfers between devices: 0.08 us -> 25 us
  between operations: 13.1 us -> 0.16 us
  other arithmetic: 5.87 us -> 1.55 us
    reduce_scatter x1 -> x0, waiting for transfers between devices: 150 us -> none  [shards(): lax.psum_scatter(jnp.dot(hidden, down_weight, preferred_element_type=jnp....]
    all_gather x1 -> x0, waiting for transfers between devices: 78.3 us -> none  [shards(): piece = lax.all_gather(tokens, 'gy', axis=0, tiled=True)]
    pallas_call x0 -> x22, Pallas kernels: none -> 48.8 us  [the longest x4 21.7 us: gate_up(): pl.pallas_call(body, in_specs=[VMEM] * (count + len(weights)) + [ANY] * l...]
    ppermute x0 -> x28, waiting for transfers between devices: none -> 43.6 us  [the longest x11 28.2 us: right(): return lax.ppermute(x, 'gy', to_right)]
    dot_general x3 -> x0, matrix products: 42.4 us -> none  [the longest x1 16.9 us: shards(): jnp.dot(hidden, down_weight, preferred_element_type=jnp.float32)]
    psum x1 -> x0, waiting for transfers between devices: 37.2 us -> none  [shards(): summed = lax.psum(partial_value, 'gx')]
    ppermute x0 -> x28, starting transfers between devices: none -> 25 us  [the longest x11 16.4 us: right(): return lax.ppermute(x, 'gy', to_right)]
    another operation x1, other arithmetic: 3.8 us -> 0.2 us  [shards(): partial_value = jnp.stack([first, second])]
  transfers between devices with their start and end apart: 3 -> 28, of which waited for: 3 -> 20; matrix products, arithmetic and copies ran while one was open for 0% -> 0% of each run, Pallas kernels for 0% -> 37%
where the time goes in v6:
time: 119 us
  Pallas kernels  48.8 us (41%)
  waiting for transfers between devices  43.6 us (37%)
  starting transfers between devices  25 us (21%)
  other arithmetic  1.55 us (1%)
    ppermute x11, waiting for transfers between devices, right(): return lax.ppermute(x, 'gy', to_right)  28.2 us
    pallas_call x4, Pallas kernels, gate_up(): pl.pallas_call(body, in_specs=[VMEM] * (count + len(weights)) + [ANY] * l...  21.7 us
    ppermute x11, starting transfers between devices, right(): return lax.ppermute(x, 'gy', to_right)  16.4 us
    pallas_call x2, Pallas kernels, down(): pl.pallas_call(body, in_specs=[SMEM] + [VMEM] * (2 * count) + [ANY] * (1...  15.4 us
    ppermute x11, waiting for transfers between devices, left(): return lax.ppermute(x, 'gy', to_left)  15.2 us
    pallas_call x1, Pallas kernels, bring(): pl.pallas_call(body, in_specs=[ANY] * len(weights) + [SMEM] * len(parts)...  10.8 us
    ppermute x11, starting transfers between devices, left(): return lax.ppermute(x, 'gy', to_left)  7.31 us
  transfers between devices with their start and end apart: 28, of which 20 were waited for; matrix products, arithmetic and copies ran while one was open for 0% of the time, Pallas kernels for 37%

profile of v6, /device:TPU:0, one launch (start us, length us, event | category | flops | bytes accessed | tf_op | source)
XLA Modules:
  0.0 119.1 jit_solution(4303846271434812852)
XLA Ops:
  0.0 3.0 %collective-permute-start = (bf16[64,4096]{1,0:T(8,128)(2,1)}, bf16[64,4096]{1,0:T(8,128)(2,1)S(1)}, u32[]{:S(2)}, u32[]{:S(2)}) collective-permute-start(bf16[64,4096]{1,0:T(8,128)(2,1)} %refs_0_.3), channel_id=1, source_target_pairs={{0,2},{2,4},{4,6},{6,7},{7,5},{5,3},{3,1},{1,0},{8,10},{10,12},{12... | collective-permute-start | bytes 1572872 | tf_op jit(solution)/shard_map/ppermute | solution.py:218
  3.0 10.8 %shard_map.46 = (bf16[4096,1024]{1,0:T(8,128)(2,1)S(1)}, bf16[4096,1024]{1,0:T(8,128)(2,1)S(1)}, bf16[4096,1024]{1,0:T(8,128)(2,1)S(1)}, bf16[4096,1024]{1,0:T(8,128)(2,1)S(1)}) custom-call(bf16[4096,2048]{1,0:T(8,128)(2,1)} %refs_0_.2, bf16[4096,2048]{1,0:T(8,128)(2,1)} %refs_1_.1, s32[1]{0:T(128)} %bitcast.1.refs_2_, s32[1]{0:T(128)} %bitcast.refs_3_.part_ref), custom_call_target="tpu_custom_call" | custom-call | bytes 67108864 | tf_op jit(solution)/shard_map/pallas_call | solution.py:89
  13.9 1.2 %collective-permute-done.refs_0_ = bf16[64,4096]{1,0:T(8,128)(2,1)S(1)} collective-permute-done((bf16[64,4096]{1,0:T(8,128)(2,1)}, bf16[64,4096]{1,0:T(8,128)(2,1)S(1)}, u32[]{:S(2)}, u32[]{:S(2)}) %collective-permute-start) | collective-permute-done | bytes 524320 | tf_op jit(solution)/shard_map/ppermute | solution.py:218
  15.1 1.5 %collective-permute-done.1.refs_1_ = bf16[64,4096]{1,0:T(8,128)(2,1)S(1)} collective-permute-done((bf16[64,4096]{1,0:T(8,128)(2,1)}, bf16[64,4096]{1,0:T(8,128)(2,1)S(1)}, u32[]{:S(2)}, u32[]{:S(2)}) %collective-permute-start.1) | collective-permute-done | bytes 524320 | tf_op jit(solution)/shard_map/ppermute | solution.py:221
  16.6 1.6 %collective-permute-start.2 = (bf16[64,4096]{1,0:T(8,128)(2,1)S(1)}, bf16[64,4096]{1,0:T(8,128)(2,1)S(1)}, u32[]{:S(2)}, u32[]{:S(2)}) collective-permute-start(bf16[64,4096]{1,0:T(8,128)(2,1)S(1)} %get-tuple-element.52.refs_1_), channel_id=1, source_target_pairs={{0,2},{2,4},{4,6},{6,7},{7,5},{5,3},{3,1},{1,0},{8,10},{10,12},{12... | collective-permute-start | bytes 1572872 | tf_op jit(solution)/shard_map/ppermute | solution.py:218
  18.2 0.4 collective-permute-start.3
  18.6 7.6 %shard_map.48 = (f32[2,192,1024]{2,1,0:T(8,128)S(1)}, f32[2,192,1024]{2,1,0:T(8,128)S(1)}) custom-call(bf16[64,4096]{1,0:T(8,128)(2,1)S(1)} %copy-done, bf16[64,4096]{1,0:T(8,128)(2,1)S(1)} %get-tuple-element.52.refs_1_, bf16[64,4096]{1,0:T(8,128)(2,1)S(1)} %get-tuple-element.53.refs_2_, bf16[4096,1024]{1,0:T(8,128)(2,1)S(1)} %get-tuple-element.54.refs_3_.refs_2_.refs_4_, ...), custom_call_target="tpu_custom_call" | custom-call | flops 6442450944 | bytes 33554432 | tf_op jit(solution)/shard_map/pallas_call | solution.py:124
  26.3 2.8 %collective-permute-done.2.refs_0_ = bf16[64,4096]{1,0:T(8,128)(2,1)S(1)} collective-permute-done((bf16[64,4096]{1,0:T(8,128)(2,1)S(1)}, bf16[64,4096]{1,0:T(8,128)(2,1)S(1)}, u32[]{:S(2)}, u32[]{:S(2)}) %collective-permute-start.2) | collective-permute-done | bytes 524320 | tf_op jit(solution)/shard_map/ppermute | solution.py:218
  29.1 1.3 %collective-permute-done.3.refs_1_ = bf16[64,4096]{1,0:T(8,128)(2,1)S(1)} collective-permute-done((bf16[64,4096]{1,0:T(8,128)(2,1)S(1)}, bf16[64,4096]{1,0:T(8,128)(2,1)S(1)}, u32[]{:S(2)}, u32[]{:S(2)}) %collective-permute-start.3) | collective-permute-done | bytes 524320 | tf_op jit(solution)/shard_map/ppermute | solution.py:221
  30.4 1.6 %collective-permute-start.4 = (bf16[64,4096]{1,0:T(8,128)(2,1)S(1)}, bf16[64,4096]{1,0:T(8,128)(2,1)S(1)}, u32[]{:S(2)}, u32[]{:S(2)}) collective-permute-start(bf16[64,4096]{1,0:T(8,128)(2,1)S(1)} %get-tuple-element.60.refs_0_), channel_id=1, source_target_pairs={{0,2},{2,4},{4,6},{6,7},{7,5},{5,3},{3,1},{1,0},{8,10},{10,12},{12... | collective-permute-start | bytes 1572872 | tf_op jit(solution)/shard_map/ppermute | solution.py:218
  32.4 5.6 %shard_map.50 = (f32[2,128,1024]{2,1,0:T(8,128)S(1)}, f32[2,128,1024]{2,1,0:T(8,128)S(1)}) custom-call(bf16[64,4096]{1,0:T(8,128)(2,1)S(1)} %get-tuple-element.60.refs_0_, bf16[64,4096]{1,0:T(8,128)(2,1)S(1)} %get-tuple-element.61.refs_1_, bf16[4096,1024]{1,0:T(8,128)(2,1)S(1)} %get-tuple-element.54.refs_3_.refs_2_.refs_4_, ...), custom_call_target="tpu_custom_call" | custom-call | flops 4294967296 | bytes 33554432 | tf_op jit(solution)/shard_map/pallas_call | solution.py:124
  38.1 3.6 %collective-permute-done.4.refs_0_ = bf16[64,4096]{1,0:T(8,128)(2,1)S(1)} collective-permute-done((bf16[64,4096]{1,0:T(8,128)(2,1)S(1)}, bf16[64,4096]{1,0:T(8,128)(2,1)S(1)}, u32[]{:S(2)}, u32[]{:S(2)}) %collective-permute-start.4) | collective-permute-done | bytes 524320 | tf_op jit(solution)/shard_map/ppermute | solution.py:218
  41.7 1.3 %collective-permute-done.5.refs_1_ = bf16[64,4096]{1,0:T(8,128)(2,1)S(1)} collective-permute-done((bf16[64,4096]{1,0:T(8,128)(2,1)S(1)}, bf16[64,4096]{1,0:T(8,128)(2,1)S(1)}, u32[]{:S(2)}, u32[]{:S(2)}) %collective-permute-start.5) | collective-permute-done | bytes 524320 | tf_op jit(solution)/shard_map/ppermute | solution.py:221
  43.0 1.6 %collective-permute-start.6 = (bf16[32,4096]{1,0:T(8,128)(2,1)S(1)}, bf16[32,4096]{1,0:T(8,128)(2,1)S(1)}, u32[]{:S(2)}, u32[]{:S(2)}) collective-permute-start(bf16[32,4096]{1,0:T(8,128)(2,1)S(1)} %get-tuple-element.66), channel_id=1, source_target_pairs={{0,2},{2,4},{4,6},{6,7},{7,5},{5,3},{3,1},{1,0},{8,10},{10,12},{12... | collective-permute-start | bytes 786440 | tf_op jit(solution)/shard_map/ppermute | solution.py:218
  44.6 0.5 collective-permute-start.7
  45.1 6.7 %collective-permute-done.6.refs_0_ = bf16[32,4096]{1,0:T(8,128)(2,1)S(1)} collective-permute-done((bf16[32,4096]{1,0:T(8,128)(2,1)S(1)}, bf16[32,4096]{1,0:T(8,128)(2,1)S(1)}, u32[]{:S(2)}, u32[]{:S(2)}) %collective-permute-start.6) | collective-permute-done | bytes 262176 | tf_op jit(solution)/shard_map/ppermute | solution.py:218
  51.8 1.2 %collective-permute-done.7.refs_1_ = bf16[32,4096]{1,0:T(8,128)(2,1)S(1)} collective-permute-done((bf16[32,4096]{1,0:T(8,128)(2,1)S(1)}, bf16[32,4096]{1,0:T(8,128)(2,1)S(1)}, u32[]{:S(2)}, u32[]{:S(2)}) %collective-permute-start.7) | collective-permute-done | bytes 262176 | tf_op jit(solution)/shard_map/ppermute | solution.py:221
  53.0 4.2 %shard_map.56.refs_6_ = f32[2,192,1024]{2,1,0:T(8,128)S(1)} custom-call(bf16[32,4096]{1,0:T(8,128)(2,1)S(1)} %get-tuple-element.73.refs_0_, bf16[32,4096]{1,0:T(8,128)(2,1)S(1)} %get-tuple-element.74.refs_1_, bf16[64,4096]{1,0:T(8,128)(2,1)S(1)} %get-tuple-element.75.refs_2_, bf16[64,4096]{1,0:T(8,128)(2,1)S(1)} %get-tuple-element.76.refs_3_, ...), custom_call_target="tpu_custom_call" | custom-call | flops 3221225472 | bytes 16777216 | tf_op jit(solution)/shard_map/pallas_call | solution.py:124
  57.4 4.2 %shard_map.57.a_ref = f32[2,192,1024]{2,1,0:T(8,128)S(1)} custom-call(bf16[32,4096]{1,0:T(8,128)(2,1)S(1)} %get-tuple-element.73.refs_0_, bf16[32,4096]{1,0:T(8,128)(2,1)S(1)} %get-tuple-element.74.refs_1_, bf16[64,4096]{1,0:T(8,128)(2,1)S(1)} %get-tuple-element.75.refs_2_, bf16[64,4096]{1,0:T(8,128)(2,1)S(1)} %get-tuple-element.76.refs_3_, ...), custom_call_target="tpu_custom_call" | custom-call | flops 3221225472 | bytes 16777216 | tf_op jit(solution)/shard_map/pallas_call | solution.py:124
  61.9 0.6 collective-permute-start.13
  63.1 0.6 collective-permute-start.11
  63.8 6.8 %shard_map.59 = (bf16[32,4096]{1,0:T(8,128)(2,1)S(1)}, bf16[32,4096]{1,0:T(8,128)(2,1)S(1)}, bf16[32,4096]{1,0:T(8,128)(2,1)S(1)}, bf16[32,4096]{1,0:T(8,128)(2,...) custom-call(s32[1]{0:T(128)} %bitcast.refs_3_.part_ref, bf16[192,1024]{1,0:T(8,128)(2,1)S(1)} %shard_map.58.refs_0_, ...), custom_call_target="tpu_custom_call" | custom-call | flops 3221225472 | bytes 16777216 | tf_op jit(solution)/shard_map/pallas_call | solution.py:196
  70.6 0.6 collective-permute-start.14
  71.2 1.5 %collective-permute-start.15 = (bf16[32,4096]{1,0:T(8,128)(2,1)S(1)}, bf16[32,4096]{1,0:T(8,128)(2,1)S(1)}, u32[]{:S(2)}, u32[]{:S(2)}) collective-permute-start(bf16[32,4096]{1,0:T(8,128)(2,1)S(1)} %get-tuple-element.79), channel_id=1, source_target_pairs={{0,2},{2,4},{4,6},{6,7},{7,5},{5,3},{3,1},{1,0},{8,10},{10,12},{12... | collective-permute-start | bytes 786440 | tf_op jit(solution)/shard_map/ppermute | solution.py:218
  72.7 0.5 collective-permute-start.16
  73.2 1.5 %collective-permute-start.17 = (bf16[32,4096]{1,0:T(8,128)(2,1)S(1)}, bf16[32,4096]{1,0:T(8,128)(2,1)S(1)}, u32[]{:S(2)}, u32[]{:S(2)}) collective-permute-start(bf16[32,4096]{1,0:T(8,128)(2,1)S(1)} %get-tuple-element.81), channel_id=1, source_target_pairs={{0,2},{2,4},{4,6},{6,7},{7,5},{5,3},{3,1},{1,0},{8,10},{10,12},{12... | collective-permute-start | bytes 786440 | tf_op jit(solution)/shard_map/ppermute | solution.py:218
  74.7 8.6 %shard_map.60.refs_2_ = f32[320,4096]{1,0:T(8,128)S(1)} custom-call(s32[1]{0:T(128)} %bitcast.refs_3_.part_ref, bf16[192,1024]{1,0:T(8,128)(2,1)S(1)} %shard_map.54.refs_0_, bf16[192,1024]{1,0:T(8,128)(2,1)S(1)} %collective-permute-done.10.refs_1_, bf16[128,1024]{1,0:T(8,128)(2,1)S(1)} %shard_map.55.refs_2_, ...), custom_call_target="tpu_custom_call" | custom-call | flops 5368709120 | bytes 16777216 | tf_op jit(solution)/shard_map/pallas_call | solution.py:196
  83.3 1.5 %collective-permute-done.16.refs_0_ = bf16[32,4096]{1,0:T(8,128)(2,1)S(1)} collective-permute-done((bf16[32,4096]{1,0:T(8,128)(2,1)S(1)}, bf16[32,4096]{1,0:T(8,128)(2,1)S(1)}, u32[]{:S(2)}, u32[]{:S(2)}) %collective-permute-start.16) | collective-permute-done | bytes 262176 | tf_op jit(solution)/shard_map/ppermute | solution.py:221
  85.2 1.6 %collective-permute-start.21 = (bf16[32,4096]{1,0:T(8,128)(2,1)S(1)}, bf16[32,4096]{1,0:T(8,128)(2,1)S(1)}, u32[]{:S(2)}, u32[]{:S(2)}) collective-permute-start(bf16[32,4096]{1,0:T(8,128)(2,1)S(1)} %get-tuple-element.105.refs_3_), channel_id=1, source_target_pairs={{0,2},{2,4},{4,6},{6,7},{7,5},{5,3},{3,1},{1,0},{8,10},{10,12},{12... | collective-permute-start | bytes 786440 | tf_op jit(solution)/shard_map/ppermute | solution.py:218
  86.7 0.5 collective-permute-start.20
  87.3 0.5 collective-permute-start.18
  87.9 1.6 %collective-permute-start.19 = (bf16[32,4096]{1,0:T(8,128)(2,1)S(1)}, bf16[32,4096]{1,0:T(8,128)(2,1)S(1)}, u32[]{:S(2)}, u32[]{:S(2)}) collective-permute-start(bf16[32,4096]{1,0:T(8,128)(2,1)S(1)} %add_convert_fusion.refs_3_), channel_id=1, source_target_pairs={{0,2},{2,4},{4,6},{6,7},{7,5},{5,3},{3,1},{1,0},{8,10},{10,12},{12... | collective-permute-start | bytes 786440 | tf_op jit(solution)/shard_map/ppermute | solution.py:218
  89.5 5.0 %collective-permute-done.21.refs_1_ = bf16[32,4096]{1,0:T(8,128)(2,1)S(1)} collective-permute-done((bf16[32,4096]{1,0:T(8,128)(2,1)S(1)}, bf16[32,4096]{1,0:T(8,128)(2,1)S(1)}, u32[]{:S(2)}, u32[]{:S(2)}) %collective-permute-start.21) | collective-permute-done | bytes 262176 | tf_op jit(solution)/shard_map/ppermute | solution.py:218
  94.5 1.5 %collective-permute-done.20.refs_0_ = bf16[32,4096]{1,0:T(8,128)(2,1)S(1)} collective-permute-done((bf16[32,4096]{1,0:T(8,128)(2,1)S(1)}, bf16[32,4096]{1,0:T(8,128)(2,1)S(1)}, u32[]{:S(2)}, u32[]{:S(2)}) %collective-permute-start.20) | collective-permute-done | bytes 262176 | tf_op jit(solution)/shard_map/ppermute | solution.py:221
  96.1 0.8 collective-permute-start.25
  96.9 1.3 %collective-permute-start.24 = (bf16[32,4096]{1,0:T(8,128)(2,1)S(1)}, bf16[32,4096]{1,0:T(8,128)(2,1)S(1)}, u32[]{:S(2)}, u32[]{:S(2)}) collective-permute-start(bf16[32,4096]{1,0:T(8,128)(2,1)S(1)} %get-tuple-element.104.refs_2_), channel_id=1, source_target_pairs={{2,0},{4,2},{6,4},{7,6},{5,7},{3,5},{1,3},{0,1},{10,8},{12,10},{14... | collective-permute-start | bytes 786440 | tf_op jit(solution)/shard_map/ppermute | solution.py:221
  98.2 3.4 %collective-permute-done.18.refs_0_ = bf16[32,4096]{1,0:T(8,128)(2,1)S(1)} collective-permute-done((bf16[32,4096]{1,0:T(8,128)(2,1)S(1)}, bf16[32,4096]{1,0:T(8,128)(2,1)S(1)}, u32[]{:S(2)}, u32[]{:S(2)}) %collective-permute-start.18) | collective-permute-done | bytes 262176 | tf_op jit(solution)/shard_map/ppermute | solution.py:221
  101.7 0.8 collective-permute-start.23
  102.5 1.3 %collective-permute-start.22 = (bf16[32,4096]{1,0:T(8,128)(2,1)S(1)}, bf16[32,4096]{1,0:T(8,128)(2,1)S(1)}, u32[]{:S(2)}, u32[]{:S(2)}) collective-permute-start(bf16[32,4096]{1,0:T(8,128)(2,1)S(1)} %get-tuple-element.102.refs_2_), channel_id=1, source_target_pairs={{2,0},{4,2},{6,4},{7,6},{5,7},{3,5},{1,3},{0,1},{10,8},{12,10},{14... | collective-permute-start | bytes 786440 | tf_op jit(solution)/shard_map/ppermute | solution.py:221
  103.8 1.9 %collective-permute-done.25.refs_1_ = bf16[32,4096]{1,0:T(8,128)(2,1)S(1)} collective-permute-done((bf16[32,4096]{1,0:T(8,128)(2,1)S(1)}, bf16[32,4096]{1,0:T(8,128)(2,1)S(1)}, u32[]{:S(2)}, u32[]{:S(2)}) %collective-permute-start.25) | collective-permute-done | bytes 262176 | tf_op jit(solution)/shard_map/ppermute | solution.py:218
  105.7 1.5 %collective-permute-done.24.refs_0_ = bf16[32,4096]{1,0:T(8,128)(2,1)S(1)} collective-permute-done((bf16[32,4096]{1,0:T(8,128)(2,1)S(1)}, bf16[32,4096]{1,0:T(8,128)(2,1)S(1)}, u32[]{:S(2)}, u32[]{:S(2)}) %collective-permute-start.24) | collective-permute-done | bytes 262176 | tf_op jit(solution)/shard_map/ppermute | solution.py:221
  107.2 2.4 %collective-permute-done.23.refs_1_ = bf16[32,4096]{1,0:T(8,128)(2,1)S(1)} collective-permute-done((bf16[32,4096]{1,0:T(8,128)(2,1)S(1)}, bf16[32,4096]{1,0:T(8,128)(2,1)S(1)}, u32[]{:S(2)}, u32[]{:S(2)}) %collective-permute-start.23) | collective-permute-done | bytes 262176 | tf_op jit(solution)/shard_map/ppermute | solution.py:218
  109.6 1.1 collective-permute-done.22.refs_0_
  110.9 0.8 collective-permute-start.27
  111.7 1.3 %collective-permute-start.26 = (bf16[32,4096]{1,0:T(8,128)(2,1)S(1)}, bf16[32,4096]{1,0:T(8,128)(2,1)S(1)}, u32[]{:S(2)}, u32[]{:S(2)}) collective-permute-start(bf16[32,4096]{1,0:T(8,128)(2,1)S(1)} %get-tuple-element.100), channel_id=1, source_target_pairs={{2,0},{4,2},{6,4},{7,6},{5,7},{3,5},{1,3},{0,1},{10,8},{12,10},{14... | collective-permute-start | bytes 786440 | tf_op jit(solution)/shard_map/ppermute | solution.py:221
  113.0 4.3 %collective-permute-done.27.refs_1_ = bf16[32,4096]{1,0:T(8,128)(2,1)S(1)} collective-permute-done((bf16[32,4096]{1,0:T(8,128)(2,1)S(1)}, bf16[32,4096]{1,0:T(8,128)(2,1)S(1)}, u32[]{:S(2)}, u32[]{:S(2)}) %collective-permute-start.27) | collective-permute-done | bytes 262176 | tf_op jit(solution)/shard_map/ppermute | solution.py:218
  117.3 0.8 collective-permute-done.26.refs_0_
  118.3 0.8 pad_maximum_fusion
  (40 shorter events, 2.6 us)
Async XLA Ops:
  0.0 15.1 %collective-permute-start = (bf16[64,4096]{1,0:T(8,128)(2,1)}, bf16[64,4096]{1,0:T(8,128)(2,1)S(1)}, u32[]{:S(2)}, u32[]{:S(2)}) collective-permute-start(bf16[64,4096]{1,0:T(8,128)(2,1)} %refs_0_.3), channel_id=1, source_target_pairs={{0,2},{2,4},{4,6},{6,7},{7,5},{5,3},{3,1},{1,0},{8,10},{10,12},{12... | collective-permute-start | bytes 1572872 | tf_op jit(solution)/shard_map/ppermute | solution.py:218
  3.0 13.6 %collective-permute-start.1 = (bf16[64,4096]{1,0:T(8,128)(2,1)}, bf16[64,4096]{1,0:T(8,128)(2,1)S(1)}, u32[]{:S(2)}, u32[]{:S(2)}) collective-permute-start(bf16[64,4096]{1,0:T(8,128)(2,1)} %refs_0_.3), channel_id=1, source_target_pairs={{2,0},{4,2},{6,4},{7,6},{5,7},{3,5},{1,3},{0,1},{10,8},{12,10},{14... | collective-permute-start | bytes 1572872 | tf_op jit(solution)/shard_map/ppermute | solution.py:221
  13.9 4.8 %copy-start = (bf16[64,4096]{1,0:T(8,128)(2,1)S(1)}, bf16[64,4096]{1,0:T(8,128)(2,1)}, u32[]{:S(2)}) copy-start(bf16[64,4096]{1,0:T(8,128)(2,1)} %refs_0_.3) | copy-start | bytes 1572868
  16.6 12.5 %collective-permute-start.2 = (bf16[64,4096]{1,0:T(8,128)(2,1)S(1)}, bf16[64,4096]{1,0:T(8,128)(2,1)S(1)}, u32[]{:S(2)}, u32[]{:S(2)}) collective-permute-start(bf16[64,4096]{1,0:T(8,128)(2,1)S(1)} %get-tuple-element.52.refs_1_), channel_id=1, source_target_pairs={{0,2},{2,4},{4,6},{6,7},{7,5},{5,3},{3,1},{1,0},{8,10},{10,12},{12... | collective-permute-start | bytes 1572872 | tf_op jit(solution)/shard_map/ppermute | solution.py:218
  18.2 12.2 %collective-permute-start.3 = (bf16[64,4096]{1,0:T(8,128)(2,1)S(1)}, bf16[64,4096]{1,0:T(8,128)(2,1)S(1)}, u32[]{:S(2)}, u32[]{:S(2)}) collective-permute-start(bf16[64,4096]{1,0:T(8,128)(2,1)S(1)} %get-tuple-element.53.refs_2_), channel_id=1, source_target_pairs={{2,0},{4,2},{6,4},{7,6},{5,7},{3,5},{1,3},{0,1},{10,8},{12,10},{14... | collective-permute-start | bytes 1572872 | tf_op jit(solution)/shard_map/ppermute | solution.py:221
  30.4 11.3 %collective-permute-start.4 = (bf16[64,4096]{1,0:T(8,128)(2,1)S(1)}, bf16[64,4096]{1,0:T(8,128)(2,1)S(1)}, u32[]{:S(2)}, u32[]{:S(2)}) collective-permute-start(bf16[64,4096]{1,0:T(8,128)(2,1)S(1)} %get-tuple-element.60.refs_0_), channel_id=1, source_target_pairs={{0,2},{2,4},{4,6},{6,7},{7,5},{5,3},{3,1},{1,0},{8,10},{10,12},{12... | collective-permute-start | bytes 1572872 | tf_op jit(solution)/shard_map/ppermute | solution.py:218
  32.0 11.0 %collective-permute-start.5 = (bf16[64,4096]{1,0:T(8,128)(2,1)S(1)}, bf16[64,4096]{1,0:T(8,128)(2,1)S(1)}, u32[]{:S(2)}, u32[]{:S(2)}) collective-permute-start(bf16[64,4096]{1,0:T(8,128)(2,1)S(1)} %get-tuple-element.61.refs_1_), channel_id=1, source_target_pairs={{2,0},{4,2},{6,4},{7,6},{5,7},{3,5},{1,3},{0,1},{10,8},{12,10},{14... | collective-permute-start | bytes 1572872 | tf_op jit(solution)/shard_map/ppermute | solution.py:221
  32.4 20.6 %collective-permute-start.8 = (f32[2,192,1024]{2,1,0:T(8,128)S(1)}, f32[2,192,1024]{2,1,0:T(8,128)S(1)}, u32[]{:S(2)}, u32[]{:S(2)}) collective-permute-start(f32[2,192,1024]{2,1,0:T(8,128)S(1)} %get-tuple-element.68), channel_id=1, source_target_pairs={{0,8},{8,0},{1,9},{9,1},{2,10},{10,2},{3,11},{11,3},{4,12},{12,4},... | collective-permute-start | bytes 4718600 | tf_op jit(solution)/shard_map/ppermute | solution.py:224
  43.0 10.1 %collective-permute-start.9 = (f32[2,128,1024]{2,1,0:T(8,128)S(1)}, f32[2,128,1024]{2,1,0:T(8,128)S(1)}, u32[]{:S(2)}, u32[]{:S(2)}) collective-permute-start(f32[2,128,1024]{2,1,0:T(8,128)S(1)} %get-tuple-element.69), channel_id=1, source_target_pairs={{0,8},{8,0},{1,9},{9,1},{2,10},{10,2},{3,11},{11,3},{4,12},{12,4},... | collective-permute-start | bytes 3145736 | tf_op jit(solution)/shard_map/ppermute | solution.py:224
  43.0 8.8 %collective-permute-start.6 = (bf16[32,4096]{1,0:T(8,128)(2,1)S(1)}, bf16[32,4096]{1,0:T(8,128)(2,1)S(1)}, u32[]{:S(2)}, u32[]{:S(2)}) collective-permute-start(bf16[32,4096]{1,0:T(8,128)(2,1)S(1)} %get-tuple-element.66), channel_id=1, source_target_pairs={{0,2},{2,4},{4,6},{6,7},{7,5},{5,3},{3,1},{1,0},{8,10},{10,12},{12... | collective-permute-start | bytes 786440 | tf_op jit(solution)/shard_map/ppermute | solution.py:218
  44.6 8.4 %collective-permute-start.7 = (bf16[32,4096]{1,0:T(8,128)(2,1)S(1)}, bf16[32,4096]{1,0:T(8,128)(2,1)S(1)}, u32[]{:S(2)}, u32[]{:S(2)}) collective-permute-start(bf16[32,4096]{1,0:T(8,128)(2,1)S(1)} %get-tuple-element.67), channel_id=1, source_target_pairs={{2,0},{4,2},{6,4},{7,6},{5,7},{3,5},{1,3},{0,1},{10,8},{12,10},{14... | collective-permute-start | bytes 786440 | tf_op jit(solution)/shard_map/ppermute | solution.py:221
  57.3 4.3 %collective-permute-start.12 = (f32[2,192,1024]{2,1,0:T(8,128)S(1)}, f32[2,192,1024]{2,1,0:T(8,128)S(1)}, u32[]{:S(2)}, u32[]{:S(2)}) collective-permute-start(f32[2,192,1024]{2,1,0:T(8,128)S(1)} %shard_map.56.refs_6_), channel_id=1, source_target_pairs={{0,8},{8,0},{1,9},{9,1},{2,10},{10,2},{3,11},{11,3},{4,12},{12,4},... | collective-permute-start | bytes 4718600 | tf_op jit(solution)/shard_map/ppermute | solution.py:224
  61.9 1.9 %collective-permute-start.13 = (bf16[192,1024]{1,0:T(8,128)(2,1)S(1)}, bf16[192,1024]{1,0:T(8,128)(2,1)S(1)}, u32[]{:S(2)}, u32[]{:S(2)}) collective-permute-start(bf16[192,1024]{1,0:T(8,128)(2,1)S(1)} %shard_map.58.refs_0_), channel_id=1, source_target_pairs={{0,8},{8,0},{1,9},{9,1},{2,10},{10,2},{3,11},{11,3},{4,12},{12,4},... | collective-permute-start | bytes 1179656 | tf_op jit(solution)/shard_map/ppermute | solution.py:224
  62.8 11.9 %collective-permute-start.10 = (bf16[192,1024]{1,0:T(8,128)(2,1)S(1)}, bf16[192,1024]{1,0:T(8,128)(2,1)S(1)}, u32[]{:S(2)}, u32[]{:S(2)}) collective-permute-start(bf16[192,1024]{1,0:T(8,128)(2,1)S(1)} %shard_map.54.refs_0_), channel_id=1, source_target_pairs={{0,8},{8,0},{1,9},{9,1},{2,10},{10,2},{3,11},{11,3},{4,12},{12,4},... | collective-permute-start | bytes 1179656 | tf_op jit(solution)/shard_map/ppermute | solution.py:224
  63.1 10.1 %collective-permute-start.11 = (bf16[128,1024]{1,0:T(8,128)(2,1)S(1)}, bf16[128,1024]{1,0:T(8,128)(2,1)S(1)}, u32[]{:S(2)}, u32[]{:S(2)}) collective-permute-start(bf16[128,1024]{1,0:T(8,128)(2,1)S(1)} %shard_map.55.refs_2_), channel_id=1, source_target_pairs={{0,8},{8,0},{1,9},{9,1},{2,10},{10,2},{3,11},{11,3},{4,12},{12,4},... | collective-permute-start | bytes 786440 | tf_op jit(solution)/shard_map/ppermute | solution.py:224
  70.6 16.7 %collective-permute-start.14 = (bf16[32,4096]{1,0:T(8,128)(2,1)S(1)}, bf16[32,4096]{1,0:T(8,128)(2,1)S(1)}, u32[]{:S(2)}, u32[]{:S(2)}) collective-permute-start(bf16[32,4096]{1,0:T(8,128)(2,1)S(1)} %get-tuple-element.78), channel_id=1, source_target_pairs={{2,0},{4,2},{6,4},{7,6},{5,7},{3,5},{1,3},{0,1},{10,8},{12,10},{14... | collective-permute-start | bytes 786440 | tf_op jit(solution)/shard_map/ppermute | solution.py:221
  71.2 16.1 %collective-permute-start.15 = (bf16[32,4096]{1,0:T(8,128)(2,1)S(1)}, bf16[32,4096]{1,0:T(8,128)(2,1)S(1)}, u32[]{:S(2)}, u32[]{:S(2)}) collective-permute-start(bf16[32,4096]{1,0:T(8,128)(2,1)S(1)} %get-tuple-element.79), channel_id=1, source_target_pairs={{0,2},{2,4},{4,6},{6,7},{7,5},{5,3},{3,1},{1,0},{8,10},{10,12},{12... | collective-permute-start | bytes 786440 | tf_op jit(solution)/shard_map/ppermute | solution.py:218
  72.7 12.2 %collective-permute-start.16 = (bf16[32,4096]{1,0:T(8,128)(2,1)S(1)}, bf16[32,4096]{1,0:T(8,128)(2,1)S(1)}, u32[]{:S(2)}, u32[]{:S(2)}) collective-permute-start(bf16[32,4096]{1,0:T(8,128)(2,1)S(1)} %get-tuple-element.80), channel_id=1, source_target_pairs={{2,0},{4,2},{6,4},{7,6},{5,7},{3,5},{1,3},{0,1},{10,8},{12,10},{14... | collective-permute-start | bytes 786440 | tf_op jit(solution)/shard_map/ppermute | solution.py:221
  73.2 11.9 %collective-permute-start.17 = (bf16[32,4096]{1,0:T(8,128)(2,1)S(1)}, bf16[32,4096]{1,0:T(8,128)(2,1)S(1)}, u32[]{:S(2)}, u32[]{:S(2)}) collective-permute-start(bf16[32,4096]{1,0:T(8,128)(2,1)S(1)} %get-tuple-element.81), channel_id=1, source_target_pairs={{0,2},{2,4},{4,6},{6,7},{7,5},{5,3},{3,1},{1,0},{8,10},{10,12},{12... | collective-permute-start | bytes 786440 | tf_op jit(solution)/shard_map/ppermute | solution.py:218
  85.2 9.3 %collective-permute-start.21 = (bf16[32,4096]{1,0:T(8,128)(2,1)S(1)}, bf16[32,4096]{1,0:T(8,128)(2,1)S(1)}, u32[]{:S(2)}, u32[]{:S(2)}) collective-permute-start(bf16[32,4096]{1,0:T(8,128)(2,1)S(1)} %get-tuple-element.105.refs_3_), channel_id=1, source_target_pairs={{0,2},{2,4},{4,6},{6,7},{7,5},{5,3},{3,1},{1,0},{8,10},{10,12},{12... | collective-permute-start | bytes 786440 | tf_op jit(solution)/shard_map/ppermute | solution.py:218
  86.7 9.2 %collective-permute-start.20 = (bf16[32,4096]{1,0:T(8,128)(2,1)S(1)}, bf16[32,4096]{1,0:T(8,128)(2,1)S(1)}, u32[]{:S(2)}, u32[]{:S(2)}) collective-permute-start(bf16[32,4096]{1,0:T(8,128)(2,1)S(1)} %get-tuple-element.106.refs_2_), channel_id=1, source_target_pairs={{2,0},{4,2},{6,4},{7,6},{5,7},{3,5},{1,3},{0,1},{10,8},{12,10},{14... | collective-permute-start | bytes 786440 | tf_op jit(solution)/shard_map/ppermute | solution.py:221
  87.3 14.3 %collective-permute-start.18 = (bf16[32,4096]{1,0:T(8,128)(2,1)S(1)}, bf16[32,4096]{1,0:T(8,128)(2,1)S(1)}, u32[]{:S(2)}, u32[]{:S(2)}) collective-permute-start(bf16[32,4096]{1,0:T(8,128)(2,1)S(1)} %add_convert_fusion.1.refs_2_), channel_id=1, source_target_pairs={{2,0},{4,2},{6,4},{7,6},{5,7},{3,5},{1,3},{0,1},{10,8},{12,10},{14... | collective-permute-start | bytes 786440 | tf_op jit(solution)/shard_map/ppermute | solution.py:221
  87.9 13.8 %collective-permute-start.19 = (bf16[32,4096]{1,0:T(8,128)(2,1)S(1)}, bf16[32,4096]{1,0:T(8,128)(2,1)S(1)}, u32[]{:S(2)}, u32[]{:S(2)}) collective-permute-start(bf16[32,4096]{1,0:T(8,128)(2,1)S(1)} %add_convert_fusion.refs_3_), channel_id=1, source_target_pairs={{0,2},{2,4},{4,6},{6,7},{7,5},{5,3},{3,1},{1,0},{8,10},{10,12},{12... | collective-permute-start | bytes 786440 | tf_op jit(solution)/shard_map/ppermute | solution.py:218
  96.1 9.6 %collective-permute-start.25 = (bf16[32,4096]{1,0:T(8,128)(2,1)S(1)}, bf16[32,4096]{1,0:T(8,128)(2,1)S(1)}, u32[]{:S(2)}, u32[]{:S(2)}) collective-permute-start(bf16[32,4096]{1,0:T(8,128)(2,1)S(1)} %get-tuple-element.103.refs_3_), channel_id=1, source_target_pairs={{0,2},{2,4},{4,6},{6,7},{7,5},{5,3},{3,1},{1,0},{8,10},{10,12},{12... | collective-permute-start | bytes 786440 | tf_op jit(solution)/shard_map/ppermute | solution.py:218
  96.9 10.3 %collective-permute-start.24 = (bf16[32,4096]{1,0:T(8,128)(2,1)S(1)}, bf16[32,4096]{1,0:T(8,128)(2,1)S(1)}, u32[]{:S(2)}, u32[]{:S(2)}) collective-permute-start(bf16[32,4096]{1,0:T(8,128)(2,1)S(1)} %get-tuple-element.104.refs_2_), channel_id=1, source_target_pairs={{2,0},{4,2},{6,4},{7,6},{5,7},{3,5},{1,3},{0,1},{10,8},{12,10},{14... | collective-permute-start | bytes 786440 | tf_op jit(solution)/shard_map/ppermute | solution.py:221
  101.7 7.9 %collective-permute-start.23 = (bf16[32,4096]{1,0:T(8,128)(2,1)S(1)}, bf16[32,4096]{1,0:T(8,128)(2,1)S(1)}, u32[]{:S(2)}, u32[]{:S(2)}) collective-permute-start(bf16[32,4096]{1,0:T(8,128)(2,1)S(1)} %get-tuple-element.101.refs_3_), channel_id=1, source_target_pairs={{0,2},{2,4},{4,6},{6,7},{7,5},{5,3},{3,1},{1,0},{8,10},{10,12},{12... | collective-permute-start | bytes 786440 | tf_op jit(solution)/shard_map/ppermute | solution.py:218
  102.5 8.2 %collective-permute-start.22 = (bf16[32,4096]{1,0:T(8,128)(2,1)S(1)}, bf16[32,4096]{1,0:T(8,128)(2,1)S(1)}, u32[]{:S(2)}, u32[]{:S(2)}) collective-permute-start(bf16[32,4096]{1,0:T(8,128)(2,1)S(1)} %get-tuple-element.102.refs_2_), channel_id=1, source_target_pairs={{2,0},{4,2},{6,4},{7,6},{5,7},{3,5},{1,3},{0,1},{10,8},{12,10},{14... | collective-permute-start | bytes 786440 | tf_op jit(solution)/shard_map/ppermute | solution.py:221
  110.9 6.4 %collective-permute-start.27 = (bf16[32,4096]{1,0:T(8,128)(2,1)S(1)}, bf16[32,4096]{1,0:T(8,128)(2,1)S(1)}, u32[]{:S(2)}, u32[]{:S(2)}) collective-permute-start(bf16[32,4096]{1,0:T(8,128)(2,1)S(1)} %get-tuple-element.99), channel_id=1, source_target_pairs={{0,2},{2,4},{4,6},{6,7},{7,5},{5,3},{3,1},{1,0},{8,10},{10,12},{12... | collective-permute-start | bytes 786440 | tf_op jit(solution)/shard_map/ppermute | solution.py:218
  111.7 6.4 %collective-permute-start.26 = (bf16[32,4096]{1,0:T(8,128)(2,1)S(1)}, bf16[32,4096]{1,0:T(8,128)(2,1)S(1)}, u32[]{:S(2)}, u32[]{:S(2)}) collective-permute-start(bf16[32,4096]{1,0:T(8,128)(2,1)S(1)} %get-tuple-element.100), channel_id=1, source_target_pairs={{2,0},{4,2},{6,4},{7,6},{5,7},{3,5},{1,3},{0,1},{10,8},{12,10},{14... | collective-permute-start | bytes 786440 | tf_op jit(solution)/shard_map/ppermute | solution.py:221

commit v7 on v6

v7 whole, which is shorter than its diff:
```python
import jax
import jax.numpy as jnp
from jax import lax
from jax.experimental import pallas as pl
from jax.experimental.pallas import tpu as pltpu
from jax.sharding import PartitionSpec as P

F32, BF16 = jnp.float32, jnp.bfloat16
ANY = pl.BlockSpec(memory_space=pl.ANY)
SMEM = pl.BlockSpec(memory_space=pltpu.SMEM)
VMEM = pl.BlockSpec(memory_space=pltpu.VMEM)


def ring_of(n):
    return list(range(0, n, 2)) + list(range(n - 1, 0, -2))


def in_hbm(x):
    return pltpu.with_memory_space_constraint(x, pltpu.HBM)


def in_vmem(x):
    return pltpu.with_memory_space_constraint(x, pltpu.VMEM)


GATE, KERNEL = 22_000_000_000, 5_500_000_000


def params(vmem, work=0):
    return dict(
        compiler_params=pltpu.CompilerParams(vmem_limit_bytes=vmem),
        cost_estimate=pl.CostEstimate(flops=work, bytes_accessed=0, transcendentals=0),
    )


def gate(*arrays, after=(), work=0):
    return pl.pallas_call(
        lambda *refs: None,
        name="gate",
        in_specs=[ANY] * (len(arrays) + len(after)),
        out_specs=[ANY] * len(arrays),
        out_shape=[jax.ShapeDtypeStruct(x.shape, x.dtype) for x in arrays],
        input_output_aliases={i: i for i in range(len(arrays))},
        **params(1 << 18, work),
    )(*arrays, *after)


def fetches(sources, targets, sems, pieces=8):
    copies = []
    for i, ((source, start), target) in enumerate(zip(sources, targets)):
        step = target.shape[0] // pieces
        for s in range(pieces):
            rows = pl.ds(s * step, step)
            cols = pl.ds(start, target.shape[1])
            copies.append(
                pltpu.make_async_copy(
                    source.at[rows, cols], target.at[rows], sems.at[i, s]
                )
            )
    return copies


def bring(weights, part, after):
    k, w = weights[0].shape[0], weights[0].shape[1] // 2
    count = len(weights)

    def body(part_ref, *refs):
        start = pl.multiple_of(part_ref[0] * w, w)
        sources = [(ref, start) for ref in refs[:count]]
        copies = fetches(sources, refs[-1 - count : -1], refs[-1])
        for copy in copies:
            copy.start()
        for copy in copies:
            copy.wait()

    return pl.pallas_call(
        body,
        name="bring",
        in_specs=[SMEM] + [ANY] * (count + len(after)),
        out_specs=[VMEM] * count,
        out_shape=[pltpu.VMEM((k, w), weights[0].dtype)] * count,
        scratch_shapes=[pltpu.SemaphoreType.DMA((count, 8))],
        **params(1 << 18, KERNEL),
    )(part, *map(in_hbm, weights), *after)


def gate_up(pieces, weights, after, load=None):
    if any(p.shape[0] % 16 for p in pieces):
        pieces = [jnp.concatenate(pieces, axis=0)]
    m, k = sum(p.shape[0] for p in pieces), pieces[0].shape[1]
    w = weights[0].shape[1]
    tile = min(w, 256)
    count, halves = len(pieces), len(weights) // 2
    shapes = [jax.ShapeDtypeStruct((2, m, w), F32)] * halves
    scratch = [pltpu.VMEM((m, k), BF16)]
    extra = []
    if load is not None:
        wide = load.shape[1] // 2
        extra = [in_hbm(load)]
        shapes += [pltpu.VMEM((load.shape[0], wide), load.dtype)] * 2
        scratch += [pltpu.SemaphoreType.DMA((2, 8))]

    def body(*refs):
        weight_refs = refs[count : count + len(weights)]
        outs = refs[-len(shapes) - len(scratch) : -len(scratch)]
        out_refs, x_ref = outs[:halves], refs[-len(scratch)]
        copies = []
        if load is not None:
            source = refs[count + len(weights)]
            copies = fetches([(source, 0), (source, wide)], outs[halves:], refs[-1])
        for copy in copies:
            copy.start()
        at = 0
        for ref in refs[:count]:
            x_ref[at : at + ref.shape[0]] = ref[...]
            at += ref.shape[0]

        @pl.loop(0, w // tile)
        def _(j):
            cols = pl.ds(pl.multiple_of(j * tile, tile), tile)
            for i, ref in enumerate(weight_refs):
                out_refs[i // 2][i % 2, :, cols] = jnp.dot(
                    x_ref[...], ref[:, cols], preferred_element_type=F32
                )

        for copy in copies:
            copy.wait()

    return pl.pallas_call(
        body,
        name="gate_up",
        in_specs=[VMEM] * (count + len(weights)) + [ANY] * (len(extra) + len(after)),
        out_specs=[VMEM] * len(shapes),
        out_shape=shapes,
        scratch_shapes=scratch,
        **params(6 << 20, KERNEL),
    )(*pieces, *map(in_vmem, weights), *extra, *after)


def gated(ours, theirs):
    _, m, w = ours.shape
    tile = min(w, 256)

    def body(a_ref, b_ref, o_ref):
        @pl.loop(0, w // tile)
        def _(j):
            cols = pl.ds(pl.multiple_of(j * tile, tile), tile)
            v = a_ref[0, :, cols] + b_ref[0, :, cols]
            u = a_ref[1, :, cols] + b_ref[1, :, cols]
            o_ref[:, cols] = (v / (1.0 + jnp.exp(-v)) * u).astype(BF16)

    return pl.pallas_call(
        body,
        name="gated",
        in_specs=[VMEM, VMEM],
        out_specs=VMEM,
        out_shape=jax.ShapeDtypeStruct((m, w), BF16),
        **params(4 << 20),
    )(ours, theirs)


def down(halves, weights, part, outs, after):
    m = sum(h.shape[0] for h, _ in halves)
    w = halves[0][0].shape[1]
    n = weights[0].shape[1]
    tile = 512
    if any(h.shape[0] % 16 for h, _ in halves):
        halves = [tuple(jnp.concatenate(hs, axis=0) for hs in zip(*halves))]
    count = len(halves)

    def body(part_ref, *refs):
        weight_refs, h_ref = refs[2 * count : 2 * count + 2], refs[-1]
        out_refs = refs[-1 - len(outs) : -1]
        at = 0
        for i in range(count):
            rows = slice(at, at + refs[2 * i].shape[0])
            at = rows.stop
            first = pl.multiple_of(part_ref[0] * w, w)
            h_ref[rows, pl.ds(first, w)] = refs[2 * i][...]
            h_ref[rows, pl.ds(pl.multiple_of(w - first, w), w)] = refs[2 * i + 1][...]

        for i, d_ref in enumerate(weight_refs):

            @pl.loop(0, n // tile)
            def _(j):
                here = pl.multiple_of(j * tile, tile)
                out = jnp.dot(
                    h_ref[...], d_ref[:, pl.ds(here, tile)], preferred_element_type=F32
                )
                cols = pl.ds(i * n + here, tile)
                for (at, size, dtype), ref in zip(outs, out_refs):
                    ref[:, cols] = out[at : at + size].astype(dtype)

    return pl.pallas_call(
        body,
        name="down",
        in_specs=[SMEM] + [VMEM] * (2 * count + 2) + [ANY] * len(after),
        out_specs=[VMEM] * len(outs),
        out_shape=[
            jax.ShapeDtypeStruct((size, 2 * n), dtype) for _, size, dtype in outs
        ],
        scratch_shapes=[pltpu.VMEM((m, 2 * w), BF16)],
        **params(6 << 20),
    )(part, *[h for pair in halves for h in pair], *map(in_vmem, weights), *after)


def make_shards(n):
    ring = ring_of(n)
    half = n // 2
    to_right = [(ring[i], ring[(i + 1) % n]) for i in range(n)]
    to_left = [(ring[(i + 1) % n], ring[i]) for i in range(n)]
    swap = [(0, 1), (1, 0)]

    def right(x, name="right"):
        with jax.named_scope(name):
            return lax.ppermute(x, "gy", to_right)

    def left(x, name="left"):
        with jax.named_scope(name):
            return lax.ppermute(x, "gy", to_left)

    def other(x, name="swap"):
        with jax.named_scope(name):
            return lax.ppermute(x, "gx", swap)

    def add(part, block):
        return (part + block.astype(F32)).astype(BF16)

    def shards(tokens, gate_weight, up_weight, down_weight):
        rows = tokens.shape[0]
        cut = rows // 2
        core = lax.axis_index("gx").astype(jnp.int32)
        keep, give = core.reshape(1), (1 - core).reshape(1)

        a, b = tokens[:cut], tokens[cut:]
        far_r, far_l = right(a, "far_r1"), left(b, "far_l1")
        near_r, near_l = right(b, "near_r1"), left(a, "near_l1")
        wide = bring([gate_weight, up_weight], give, [])
        blocks, groups, sums, got = [[tokens]], [], [], []
        after = wide[-1:]
        for d in range(1, half):
            far_r, far_l = gate(far_r, far_l, after=after, work=GATE)
            held_r, held_l = far_r, far_l
            far_r = right(far_r, f"far_r{d + 1}")
            far_l = left(far_l, f"far_l{d + 1}")
            if d == 1:
                wide += bring([gate_weight, up_weight], keep, [held_r])
                near_r, near_l = gate(near_r, near_l, after=wide[-1:], work=GATE)
            else:
                groups.append(blocks[0] + blocks[1] if d == 2 else blocks[d - 1])
                theirs, ours = gate_up(groups[-1], wide, [held_r])
                near_r, near_l, theirs, ours, *got = gate(
                    near_r, near_l, theirs, ours, *got, work=GATE
                )
                sums.append(ours)
                if d < half - 1:
                    got.append(other(theirs, f"swap{d}"))
            blocks.append([held_r, near_r, near_l, held_l])
            if d < half - 1:
                after = [near_r]
                near_r = right(near_r, f"near_r{d + 1}")
                near_l = left(near_l, f"near_l{d + 1}")
        far_r, far_l, theirs, *got = gate(far_r, far_l, theirs, *got, after=[near_r])
        got.append(other(theirs, "swap_last"))
        last = [far_r, far_l, *blocks[-1]]

        def hide(ours, got):
            h = gated(ours, got)
            return h, other(h)

        (theirs,) = gate_up(last, wide[:2], [])
        last_got = other(theirs)
        ours, *weight = gate_up(last, wide[2:], [theirs], down_weight)
        last = hide(ours, last_got)
        near = [hide(*pair) for pair in zip(sums, got)]
        at = [(i * cut, cut) for i in range(6)]
        outs = [(*at[3], BF16), (*at[4], BF16), (*at[0], BF16), (*at[1], BF16)]
        outs += [(*at[2], F32), (*at[5], F32)]
        b_l, b_r, a_l, a_r, next_l, next_r = down([last], weight, keep, outs, [])

        b_l, b_r = left(b_l), right(b_r)
        a_l, a_r = left(a_l), right(a_r)
        (rest,) = down(near[-1:], weight, keep, [(0, 2 * rows, F32)], [next_l])
        parts = {half - 2: [rest[i * cut : (i + 1) * cut] for i in range(4)]}
        after = [rest]
        for d in range(half - 2, -1, -1):
            b_l, b_r = gate(b_l, b_r, after=after)
            if d > 0:
                _, left_b, right_a, _ = parts[d]
                b_l, b_r = add(left_b, b_l), add(right_a, b_r)
                after = [b_l, b_r]
                b_l, b_r = left(b_l), right(b_r)
            else:
                after = [b_l, b_r]
            if d == half - 2:
                size = rows * (2 * half - 5)
                (rest,) = down(near[:-1], weight, keep, [(0, size, F32)], after)
                for e in range(1, half - 2):
                    first = rows * (2 * e - 1)
                    parts[e] = [
                        rest[first + i * cut : first + (i + 1) * cut] for i in range(4)
                    ]
                after = [rest]
            a_l, a_r = gate(a_l, a_r, after=after)
            a_l, a_r = add(next_l, a_l), add(next_r, a_r)
            after = [a_l, a_r]
            a_l, a_r = left(a_l), right(a_r)
            if d > 0:
                next_l, _, _, next_r = parts[d]
        a_l, a_r = gate(a_l, a_r)
        total_a = rest[:cut] + a_l.astype(F32) + b_r.astype(F32)
        total_b = rest[cut:rows] + a_r.astype(F32) + b_l.astype(F32)
        return jnp.concatenate([total_a, total_b], axis=0).astype(BF16)

    return shards


def solution(mesh):
    return jax.shard_map(
        make_shards(mesh.shape["gy"]),
        mesh=mesh,
        in_specs=(P(("groups", "gy"), "gx"), P("gx", "gy"), P("gx", "gy"), P("gy", "gx")),
        out_specs=P(("groups", "gy"), "gx"),
        check_vma=False,
    )
```

time: 119 us -> 117 us (0.983)
  waiting for transfers between devices: 43.6 us -> 33.3 us
  starting transfers between devices: 25 us -> 31.3 us
    ppermute x11 -> x14, starting transfers between devices: 7.31 us -> 22.6 us  [left(): return lax.ppermute(x, 'gy', to_left)]
    ppermute x11 -> x14, starting transfers between devices: 16.4 us -> 7.32 us  [right(): return lax.ppermute(x, 'gy', to_right)]
    ppermute x11 -> x14, waiting for transfers between devices: 28.2 us -> 19.2 us  [right(): return lax.ppermute(x, 'gy', to_right)]
    ppermute x11 -> x14, waiting for transfers between devices: 15.2 us -> 13.2 us  [left(): return lax.ppermute(x, 'gy', to_left)]
    pallas_call x22 -> x26, Pallas kernels: 48.8 us -> 49.4 us  [the longest x4 23.4 us: gate_up(): pl.pallas_call(body, name='gate_up', in_specs=[VMEM] * (count + len(weigh...]
  transfers between devices with their start and end apart: 28 -> 34, of which waited for: 20 -> 14; matrix products, arithmetic and copies ran while one was open for 0% -> 0% of each run, Pallas kernels for 37% -> 39%
where the time goes in v7:
time: 117 us
  Pallas kernels  49.4 us (42%)
  waiting for transfers between devices  33.3 us (28%)
  starting transfers between devices  31.3 us (27%)
  other arithmetic  1.54 us (1%)
    pallas_call x4, Pallas kernels, gate_up(): pl.pallas_call(body, name='gate_up', in_specs=[VMEM] * (count + len(weigh...  23.4 us
    ppermute x14, starting transfers between devices, left(): return lax.ppermute(x, 'gy', to_left)  22.6 us
    ppermute x14, waiting for transfers between devices, right(): return lax.ppermute(x, 'gy', to_right)  19.2 us
    pallas_call x3, Pallas kernels, down(): pl.pallas_call(body, name='down', in_specs=[SMEM] + [VMEM] * (2 * count +...  13.3 us
    ppermute x14, waiting for transfers between devices, left(): return lax.ppermute(x, 'gy', to_left)  13.2 us
    pallas_call x2, Pallas kernels, bring(): pl.pallas_call(body, name='bring', in_specs=[SMEM] + [ANY] * (count + len...  11.9 us
    ppermute x14, starting transfers between devices, right(): return lax.ppermute(x, 'gy', to_right)  7.32 us
  transfers between devices with their start and end apart: 34, of which 14 were waited for; matrix products, arithmetic and copies ran while one was open for 0% of the time, Pallas kernels for 39%

profile of v7, /device:TPU:0, one launch (start us, length us, event | category | flops | bytes accessed | tf_op | source)
XLA Modules:
  0.0 116.9 jit_solution(2249272779299032673)
XLA Ops:
  0.0 1.1 fusion.12
  1.1 3.0 %collective-permute-start.3 = (bf16[32,4096]{1,0:T(8,128)(2,1)S(1)}, bf16[32,4096]{1,0:T(8,128)(2,1)S(1)}, u32[]{:S(2)}, u32[]{:S(2)}) collective-permute-start(bf16[32,4096]{1,0:T(8,128)(2,1)S(1)} %get-tuple-element.120), channel_id=1, source_target_pairs={{2,0},{4,2},{6,4},{7,6},{5,7},{3,5},{1,3},{0,1},{10,8},{12,10},{14... | collective-permute-start | bytes 786440 | tf_op jit(solution)/shard_map/far_l1/ppermute | solution.py:220
  4.2 2.0 %collective-permute-start.2 = (bf16[32,4096]{1,0:T(8,128)(2,1)S(1)}, bf16[32,4096]{1,0:T(8,128)(2,1)S(1)}, u32[]{:S(2)}, u32[]{:S(2)}) collective-permute-start(bf16[32,4096]{1,0:T(8,128)(2,1)S(1)} %get-tuple-element.119), channel_id=1, source_target_pairs={{0,2},{2,4},{4,6},{6,7},{7,5},{5,3},{3,1},{1,0},{8,10},{10,12},{12... | collective-permute-start | bytes 786440 | tf_op jit(solution)/shard_map/far_r1/ppermute | solution.py:216
  6.2 5.9 %bring.2 = (bf16[4096,1024]{1,0:T(8,128)(2,1)S(1)}, bf16[4096,1024]{1,0:T(8,128)(2,1)S(1)}) custom-call(s32[1]{0:T(128)} %bitcast.1.part_ref, bf16[4096,2048]{1,0:T(8,128)(2,1)} %refs_0_.4, bf16[4096,2048]{1,0:T(8,128)(2,1)} %refs_1_.3), custom_call_target="tpu_custom_call" | custom-call | flops 5500000256 | tf_op jit(solution)/shard_map/bring/pallas_call | solution.py:76
  12.2 5.3 %collective-permute-done.2.refs_0_ = bf16[32,4096]{1,0:T(8,128)(2,1)S(1)} collective-permute-done((bf16[32,4096]{1,0:T(8,128)(2,1)S(1)}, bf16[32,4096]{1,0:T(8,128)(2,1)S(1)}, u32[]{:S(2)}, u32[]{:S(2)}) %collective-permute-start.2) | collective-permute-done | bytes 262176 | tf_op jit(solution)/shard_map/far_r1/ppermute | solution.py:216
  17.9 1.6 %collective-permute-start.7 = (bf16[32,4096]{1,0:T(8,128)(2,1)S(1)}, bf16[32,4096]{1,0:T(8,128)(2,1)S(1)}, u32[]{:S(2)}, u32[]{:S(2)}) collective-permute-start(bf16[32,4096]{1,0:T(8,128)(2,1)S(1)} %get-tuple-element.62.refs_4_), channel_id=1, source_target_pairs={{2,0},{4,2},{6,4},{7,6},{5,7},{3,5},{1,3},{0,1},{10,8},{12,10},{14... | collective-permute-start | bytes 786440 | tf_op jit(solution)/shard_map/far_l2/ppermute | solution.py:220
  19.5 5.9 %bring.3 = (bf16[4096,1024]{1,0:T(8,128)(2,1)S(1)}, bf16[4096,1024]{1,0:T(8,128)(2,1)S(1)}) custom-call(s32[1]{0:T(128)} %bitcast.part_ref, bf16[4096,2048]{1,0:T(8,128)(2,1)} %refs_0_.4, bf16[4096,2048]{1,0:T(8,128)(2,1)} %refs_1_.3, bf16[32,4096]{1,0:T(8,128)(2,1)S(1)} %get-tuple-element.58.refs_2_.refs_1_), custom_call_target="tpu_custom_call" | custom-call | flops 5500000256 | tf_op jit(solution)/shard_map/bring/pallas_call | solution.py:76
  25.5 0.5 collective-permute-start.4
  25.9 1.6 %collective-permute-start.5 = (bf16[32,4096]{1,0:T(8,128)(2,1)S(1)}, bf16[32,4096]{1,0:T(8,128)(2,1)S(1)}, u32[]{:S(2)}, u32[]{:S(2)}) collective-permute-start(bf16[32,4096]{1,0:T(8,128)(2,1)S(1)} %get-tuple-element.61.refs_3_), channel_id=1, source_target_pairs={{2,0},{4,2},{6,4},{7,6},{5,7},{3,5},{1,3},{0,1},{10,8},{12,10},{14... | collective-permute-start | bytes 786440 | tf_op jit(solution)/shard_map/near_l2/ppermute | solution.py:220
  28.0 1.6 %collective-permute-start.9 = (bf16[32,4096]{1,0:T(8,128)(2,1)S(1)}, bf16[32,4096]{1,0:T(8,128)(2,1)S(1)}, u32[]{:S(2)}, u32[]{:S(2)}) collective-permute-start(bf16[32,4096]{1,0:T(8,128)(2,1)S(1)} %get-tuple-element.69.refs_3_), channel_id=1, source_target_pairs={{2,0},{4,2},{6,4},{7,6},{5,7},{3,5},{1,3},{0,1},{10,8},{12,10},{14... | collective-permute-start | bytes 786440 | tf_op jit(solution)/shard_map/far_l3/ppermute | solution.py:220
  29.6 7.6 %gate_up.4 = (f32[2,192,1024]{2,1,0:T(8,128)S(1)}, f32[2,192,1024]{2,1,0:T(8,128)S(1)}) custom-call(bf16[64,4096]{1,0:T(8,128)(2,1)S(1)} %copy-done, bf16[32,4096]{1,0:T(8,128)(2,1)S(1)} %get-tuple-element.58.refs_2_.refs_1_, bf16[32,4096]{1,0:T(8,128)(2,1)S(1)} %get-tuple-element.60.refs_2_, bf16[32,4096]{1,0:T(8,128)(2,1)S(1)} %get-tuple-element.61.refs_3_, ...), custom_call_target="tpu_custom_call" | custom-call | flops 5500000256 | tf_op jit(solution)/shard_map/gate_up/pallas_call | solution.py:129
  37.3 0.5 collective-permute-start.12
  37.8 1.6 %collective-permute-start.13 = (bf16[32,4096]{1,0:T(8,128)(2,1)S(1)}, bf16[32,4096]{1,0:T(8,128)(2,1)S(1)}, u32[]{:S(2)}, u32[]{:S(2)}) collective-permute-start(bf16[32,4096]{1,0:T(8,128)(2,1)S(1)} %get-tuple-element.73.refs_2_), channel_id=1, source_target_pairs={{2,0},{4,2},{6,4},{7,6},{5,7},{3,5},{1,3},{0,1},{10,8},{12,10},{14... | collective-permute-start | bytes 786440 | tf_op jit(solution)/shard_map/near_l3/ppermute | solution.py:220
  39.4 0.4 collective-permute-start.10
  39.8 1.6 %collective-permute-start.11 = (bf16[32,4096]{1,0:T(8,128)(2,1)S(1)}, bf16[32,4096]{1,0:T(8,128)(2,1)S(1)}, u32[]{:S(2)}, u32[]{:S(2)}) collective-permute-start(bf16[32,4096]{1,0:T(8,128)(2,1)S(1)} %get-tuple-element.72.refs_5_), channel_id=1, source_target_pairs={{2,0},{4,2},{6,4},{7,6},{5,7},{3,5},{1,3},{0,1},{10,8},{12,10},{14... | collective-permute-start | bytes 786440 | tf_op jit(solution)/shard_map/far_l4/ppermute | solution.py:220
  41.4 5.6 %gate_up.5 = (f32[2,128,1024]{2,1,0:T(8,128)S(1)}, f32[2,128,1024]{2,1,0:T(8,128)S(1)}) custom-call(bf16[32,4096]{1,0:T(8,128)(2,1)S(1)} %get-tuple-element.65.refs_9_.refs_0_, bf16[32,4096]{1,0:T(8,128)(2,1)S(1)} %get-tuple-element.70.refs_2_.refs_1_, bf16[32,4096]{1,0:T(8,128)(2,1)S(1)} %get-tuple-element.73.refs_2_, ...), custom_call_target="tpu_custom_call" | custom-call | flops 5500000256 | tf_op jit(solution)/shard_map/gate_up/pallas_call | solution.py:129
  47.1 4.5 %collective-permute-done.10.refs_0_ = bf16[32,4096]{1,0:T(8,128)(2,1)S(1)} collective-permute-done((bf16[32,4096]{1,0:T(8,128)(2,1)S(1)}, bf16[32,4096]{1,0:T(8,128)(2,1)S(1)}, u32[]{:S(2)}, u32[]{:S(2)}) %collective-permute-start.10) | collective-permute-done | bytes 262176 | tf_op jit(solution)/shard_map/far_r4/ppermute | solution.py:216
  51.8 4.2 %gate_up.6.refs_9_ = f32[2,192,1024]{2,1,0:T(8,128)S(1)} custom-call(bf16[32,4096]{1,0:T(8,128)(2,1)S(1)} %get-tuple-element.81.refs_0_, bf16[32,4096]{1,0:T(8,128)(2,1)S(1)} %get-tuple-element.82.refs_1_, bf16[32,4096]{1,0:T(8,128)(2,1)S(1)} %get-tuple-element.71.refs_8_.refs_2_, bf16[32,4096]{1,0:T(8,128)(2,1)S(1)} %get-tuple-element.79.refs_4_.refs_3_, ...), custom_call_target="tpu_custom_call" | custom-call | flops 5500000256 | tf_op jit(solution)/shard_map/gate_up/pallas_call | solution.py:129
  56.1 0.5 collective-permute-start.16
  56.6 5.9 %gate_up.7 = (f32[2,192,1024]{2,1,0:T(8,128)S(1)}, bf16[2048,2048]{1,0:T(8,128)(2,1)S(1)}, bf16[2048,2048]{1,0:T(8,128)(2,1)S(1)}) custom-call(bf16[32,4096]{1,0:T(8,128)(2,1)S(1)} %get-tuple-element.81.refs_0_, bf16[32,4096]{1,0:T(8,128)(2,1)S(1)} %get-tuple-element.82.refs_1_, bf16[32,4096]{1,0:T(8,128)(2,1)S(1)} %get-tuple-element.71.refs_8_.refs_2_, ...), custom_call_target="tpu_custom_call" | custom-call | flops 5500000256 | tf_op jit(solution)/shard_map/gate_up/pallas_call | solution.py:129
  63.2 0.5 collective-permute-start.17
  63.7 0.9 collective-permute-done.19.refs_1_
  64.6 4.8 %down.3 = (bf16[32,4096]{1,0:T(8,128)(2,1)S(1)}, bf16[32,4096]{1,0:T(8,128)(2,1)S(1)}, bf16[32,4096]{1,0:T(8,128)(2,1)S(1)}, bf16[32,4096]{1,0:T(8,128)(2,1)S(1)...) custom-call(s32[1]{0:T(128)} %bitcast.part_ref, bf16[192,1024]{1,0:T(8,128)(2,1)S(1)} %gated.5.refs_0_, ...), custom_call_target="tpu_custom_call" | custom-call | tf_op jit(solution)/shard_map/down/pallas_call | solution.py:194
  69.4 1.7 %collective-permute-start.20 = (bf16[32,4096]{1,0:T(8,128)(2,1)S(1)}, bf16[32,4096]{1,0:T(8,128)(2,1)S(1)}, u32[]{:S(2)}, u32[]{:S(2)}) collective-permute-start(bf16[32,4096]{1,0:T(8,128)(2,1)S(1)} %get-tuple-element.90), channel_id=1, source_target_pairs={{2,0},{4,2},{6,4},{7,6},{5,7},{3,5},{1,3},{0,1},{10,8},{12,10},{14... | collective-permute-start | bytes 786440 | tf_op jit(solution)/shard_map/left/ppermute | solution.py:220
  71.9 1.7 %collective-permute-start.22 = (bf16[32,4096]{1,0:T(8,128)(2,1)S(1)}, bf16[32,4096]{1,0:T(8,128)(2,1)S(1)}, u32[]{:S(2)}, u32[]{:S(2)}) collective-permute-start(bf16[32,4096]{1,0:T(8,128)(2,1)S(1)} %get-tuple-element.94), channel_id=1, source_target_pairs={{2,0},{4,2},{6,4},{7,6},{5,7},{3,5},{1,3},{0,1},{10,8},{12,10},{14... | collective-permute-start | bytes 786440 | tf_op jit(solution)/shard_map/left/ppermute | solution.py:220
  73.6 0.4 collective-permute-start.23
  74.0 3.7 %down.4.refs_2_ = f32[128,4096]{1,0:T(8,128)S(1)} custom-call(s32[1]{0:T(128)} %bitcast.part_ref, bf16[128,1024]{1,0:T(8,128)(2,1)S(1)} %gated.4.refs_0_, bf16[128,1024]{1,0:T(8,128)(2,1)S(1)} %collective-permute-done.17.refs_1_, bf16[2048,2048]{1,0:T(8,128)(2,1)S(1)} %get-tuple-element.84.refs_2_, bf16[2048,2048]{1,0:T(8,128)(2,1)S(1)} %get-tuple-element.85.refs_3_, ...), custom_call_target="tpu_custom_call" | custom-call | tf_op jit(solution)/shard_map/down/pallas_call | solution.py:194
  77.7 0.9 collective-permute-done.20.refs_0_
  78.6 1.7 %collective-permute-done.21.refs_1_ = bf16[32,4096]{1,0:T(8,128)(2,1)S(1)} collective-permute-done((bf16[32,4096]{1,0:T(8,128)(2,1)S(1)}, bf16[32,4096]{1,0:T(8,128)(2,1)S(1)}, u32[]{:S(2)}, u32[]{:S(2)}) %collective-permute-start.21) | collective-permute-done | bytes 262176 | tf_op jit(solution)/shard_map/right/ppermute | solution.py:216
  80.4 1.6 %collective-permute-start.26 = (bf16[32,4096]{1,0:T(8,128)(2,1)S(1)}, bf16[32,4096]{1,0:T(8,128)(2,1)S(1)}, u32[]{:S(2)}, u32[]{:S(2)}) collective-permute-start(bf16[32,4096]{1,0:T(8,128)(2,1)S(1)} %get-tuple-element.118.refs_4_), channel_id=1, source_target_pairs={{2,0},{4,2},{6,4},{7,6},{5,7},{3,5},{1,3},{0,1},{10,8},{12,10},{14... | collective-permute-start | bytes 786440 | tf_op jit(solution)/shard_map/left/ppermute | solution.py:220
  82.0 0.5 collective-permute-start.27
  82.5 4.8 %down.5.refs_2_ = f32[192,4096]{1,0:T(8,128)S(1)} custom-call(s32[1]{0:T(128)} %bitcast.part_ref, bf16[192,1024]{1,0:T(8,128)(2,1)S(1)} %gated.3.refs_0_, bf16[192,1024]{1,0:T(8,128)(2,1)S(1)} %collective-permute-done.15.refs_1_, bf16[2048,2048]{1,0:T(8,128)(2,1)S(1)} %get-tuple-element.84.refs_2_, bf16[2048,2048]{1,0:T(8,128)(2,1)S(1)} %get-tuple-element.85.refs_3_, ...), custom_call_target="tpu_custom_call" | custom-call | tf_op jit(solution)/shard_map/down/pallas_call | solution.py:194
  87.4 0.4 collective-permute-start.25
  87.9 1.6 %collective-permute-start.24 = (bf16[32,4096]{1,0:T(8,128)(2,1)S(1)}, bf16[32,4096]{1,0:T(8,128)(2,1)S(1)}, u32[]{:S(2)}, u32[]{:S(2)}) collective-permute-start(bf16[32,4096]{1,0:T(8,128)(2,1)S(1)} %add_convert_fusion.1.refs_2_), channel_id=1, source_target_pairs={{2,0},{4,2},{6,4},{7,6},{5,7},{3,5},{1,3},{0,1},{10,8},{12,10},{14... | collective-permute-start | bytes 786440 | tf_op jit(solution)/shard_map/left/ppermute | solution.py:220
  89.9 1.7 %collective-permute-done.27.refs_1_ = bf16[32,4096]{1,0:T(8,128)(2,1)S(1)} collective-permute-done((bf16[32,4096]{1,0:T(8,128)(2,1)S(1)}, bf16[32,4096]{1,0:T(8,128)(2,1)S(1)}, u32[]{:S(2)}, u32[]{:S(2)}) %collective-permute-start.27) | collective-permute-done | bytes 262176 | tf_op jit(solution)/shard_map/right/ppermute | solution.py:216
  91.6 1.6 %collective-permute-start.30 = (bf16[32,4096]{1,0:T(8,128)(2,1)S(1)}, bf16[32,4096]{1,0:T(8,128)(2,1)S(1)}, u32[]{:S(2)}, u32[]{:S(2)}) collective-permute-start(bf16[32,4096]{1,0:T(8,128)(2,1)S(1)} %get-tuple-element.114.refs_2_), channel_id=1, source_target_pairs={{2,0},{4,2},{6,4},{7,6},{5,7},{3,5},{1,3},{0,1},{10,8},{12,10},{14... | collective-permute-start | bytes 786440 | tf_op jit(solution)/shard_map/left/ppermute | solution.py:220
  93.3 0.5 collective-permute-start.31
  93.7 3.4 %collective-permute-done.25.refs_1_ = bf16[32,4096]{1,0:T(8,128)(2,1)S(1)} collective-permute-done((bf16[32,4096]{1,0:T(8,128)(2,1)S(1)}, bf16[32,4096]{1,0:T(8,128)(2,1)S(1)}, u32[]{:S(2)}, u32[]{:S(2)}) %collective-permute-start.25) | collective-permute-done | bytes 262176 | tf_op jit(solution)/shard_map/right/ppermute | solution.py:216
  97.2 1.6 %collective-permute-start.28 = (bf16[32,4096]{1,0:T(8,128)(2,1)S(1)}, bf16[32,4096]{1,0:T(8,128)(2,1)S(1)}, u32[]{:S(2)}, u32[]{:S(2)}) collective-permute-start(bf16[32,4096]{1,0:T(8,128)(2,1)S(1)} %get-tuple-element.116.refs_2_), channel_id=1, source_target_pairs={{2,0},{4,2},{6,4},{7,6},{5,7},{3,5},{1,3},{0,1},{10,8},{12,10},{14... | collective-permute-start | bytes 786440 | tf_op jit(solution)/shard_map/left/ppermute | solution.py:220
  98.9 0.4 collective-permute-start.29
  99.3 3.4 %collective-permute-done.30.refs_0_ = bf16[32,4096]{1,0:T(8,128)(2,1)S(1)} collective-permute-done((bf16[32,4096]{1,0:T(8,128)(2,1)S(1)}, bf16[32,4096]{1,0:T(8,128)(2,1)S(1)}, u32[]{:S(2)}, u32[]{:S(2)}) %collective-permute-start.30) | collective-permute-done | bytes 262176 | tf_op jit(solution)/shard_map/left/ppermute | solution.py:220
  102.8 3.2 %collective-permute-done.28.refs_0_ = bf16[32,4096]{1,0:T(8,128)(2,1)S(1)} collective-permute-done((bf16[32,4096]{1,0:T(8,128)(2,1)S(1)}, bf16[32,4096]{1,0:T(8,128)(2,1)S(1)}, u32[]{:S(2)}, u32[]{:S(2)}) %collective-permute-start.28) | collective-permute-done | bytes 262176 | tf_op jit(solution)/shard_map/left/ppermute | solution.py:220
  105.9 1.3 %collective-permute-done.29.refs_1_ = bf16[32,4096]{1,0:T(8,128)(2,1)S(1)} collective-permute-done((bf16[32,4096]{1,0:T(8,128)(2,1)S(1)}, bf16[32,4096]{1,0:T(8,128)(2,1)S(1)}, u32[]{:S(2)}, u32[]{:S(2)}) %collective-permute-start.29) | collective-permute-done | bytes 262176 | tf_op jit(solution)/shard_map/right/ppermute | solution.py:216
  107.4 1.6 %collective-permute-start.32 = (bf16[32,4096]{1,0:T(8,128)(2,1)S(1)}, bf16[32,4096]{1,0:T(8,128)(2,1)S(1)}, u32[]{:S(2)}, u32[]{:S(2)}) collective-permute-start(bf16[32,4096]{1,0:T(8,128)(2,1)S(1)} %get-tuple-element.112), channel_id=1, source_target_pairs={{2,0},{4,2},{6,4},{7,6},{5,7},{3,5},{1,3},{0,1},{10,8},{12,10},{14... | collective-permute-start | bytes 786440 | tf_op jit(solution)/shard_map/left/ppermute | solution.py:220
  109.0 0.5 collective-permute-start.33
  109.5 5.2 %collective-permute-done.32.refs_0_ = bf16[32,4096]{1,0:T(8,128)(2,1)S(1)} collective-permute-done((bf16[32,4096]{1,0:T(8,128)(2,1)S(1)}, bf16[32,4096]{1,0:T(8,128)(2,1)S(1)}, u32[]{:S(2)}, u32[]{:S(2)}) %collective-permute-start.32) | collective-permute-done | bytes 262176 | tf_op jit(solution)/shard_map/left/ppermute | solution.py:220
  114.6 1.3 %collective-permute-done.33.refs_1_ = bf16[32,4096]{1,0:T(8,128)(2,1)S(1)} collective-permute-done((bf16[32,4096]{1,0:T(8,128)(2,1)S(1)}, bf16[32,4096]{1,0:T(8,128)(2,1)S(1)}, u32[]{:S(2)}, u32[]{:S(2)}) %collective-permute-start.33) | collective-permute-done | bytes 262176 | tf_op jit(solution)/shard_map/right/ppermute | solution.py:216
  116.1 0.8 pad_maximum_fusion
  (57 shorter events, 4.0 us)
Async XLA Ops:
  1.1 16.4 %collective-permute-start.3 = (bf16[32,4096]{1,0:T(8,128)(2,1)S(1)}, bf16[32,4096]{1,0:T(8,128)(2,1)S(1)}, u32[]{:S(2)}, u32[]{:S(2)}) collective-permute-start(bf16[32,4096]{1,0:T(8,128)(2,1)S(1)} %get-tuple-element.120), channel_id=1, source_target_pairs={{2,0},{4,2},{6,4},{7,6},{5,7},{3,5},{1,3},{0,1},{10,8},{12,10},{14... | collective-permute-start | bytes 786440 | tf_op jit(solution)/shard_map/far_l1/ppermute | solution.py:220
  4.1 21.4 %collective-permute-start = (bf16[32,4096]{1,0:T(8,128)(2,1)S(1)}, bf16[32,4096]{1,0:T(8,128)(2,1)S(1)}, u32[]{:S(2)}, u32[]{:S(2)}) collective-permute-start(bf16[32,4096]{1,0:T(8,128)(2,1)S(1)} %get-tuple-element.120), channel_id=1, source_target_pairs={{0,2},{2,4},{4,6},{6,7},{7,5},{5,3},{3,1},{1,0},{8,10},{10,12},{12... | collective-permute-start | bytes 786440 | tf_op jit(solution)/shard_map/near_r1/ppermute | solution.py:216
  4.2 13.3 %collective-permute-start.2 = (bf16[32,4096]{1,0:T(8,128)(2,1)S(1)}, bf16[32,4096]{1,0:T(8,128)(2,1)S(1)}, u32[]{:S(2)}, u32[]{:S(2)}) collective-permute-start(bf16[32,4096]{1,0:T(8,128)(2,1)S(1)} %get-tuple-element.119), channel_id=1, source_target_pairs={{0,2},{2,4},{4,6},{6,7},{7,5},{5,3},{3,1},{1,0},{8,10},{10,12},{12... | collective-permute-start | bytes 786440 | tf_op jit(solution)/shard_map/far_r1/ppermute | solution.py:216
  6.2 19.3 %collective-permute-start.1 = (bf16[32,4096]{1,0:T(8,128)(2,1)S(1)}, bf16[32,4096]{1,0:T(8,128)(2,1)S(1)}, u32[]{:S(2)}, u32[]{:S(2)}) collective-permute-start(bf16[32,4096]{1,0:T(8,128)(2,1)S(1)} %get-tuple-element.119), channel_id=1, source_target_pairs={{2,0},{4,2},{6,4},{7,6},{5,7},{3,5},{1,3},{0,1},{10,8},{12,10},{14... | collective-permute-start | bytes 786440 | tf_op jit(solution)/shard_map/near_l1/ppermute | solution.py:220
  17.5 10.1 %collective-permute-start.6 = (bf16[32,4096]{1,0:T(8,128)(2,1)S(1)}, bf16[32,4096]{1,0:T(8,128)(2,1)S(1)}, u32[]{:S(2)}, u32[]{:S(2)}) collective-permute-start(bf16[32,4096]{1,0:T(8,128)(2,1)S(1)} %get-tuple-element.58.refs_2_.refs_1_), channel_id=1, source_target_pairs={{0,2},{2,4},{4,6},{6,7},{7,5},{5,3},{3,1},{1,0},{8,10},{10,12},{12... | collective-permute-start | bytes 786440 | tf_op jit(solution)/shard_map/far_r2/ppermute | solution.py:216
  17.9 9.7 %collective-permute-start.7 = (bf16[32,4096]{1,0:T(8,128)(2,1)S(1)}, bf16[32,4096]{1,0:T(8,128)(2,1)S(1)}, u32[]{:S(2)}, u32[]{:S(2)}) collective-permute-start(bf16[32,4096]{1,0:T(8,128)(2,1)S(1)} %get-tuple-element.62.refs_4_), channel_id=1, source_target_pairs={{2,0},{4,2},{6,4},{7,6},{5,7},{3,5},{1,3},{0,1},{10,8},{12,10},{14... | collective-permute-start | bytes 786440 | tf_op jit(solution)/shard_map/far_l2/ppermute | solution.py:220
  25.5 11.7 %collective-permute-start.4 = (bf16[32,4096]{1,0:T(8,128)(2,1)S(1)}, bf16[32,4096]{1,0:T(8,128)(2,1)S(1)}, u32[]{:S(2)}, u32[]{:S(2)}) collective-permute-start(bf16[32,4096]{1,0:T(8,128)(2,1)S(1)} %get-tuple-element.60.refs_2_), channel_id=1, source_target_pairs={{0,2},{2,4},{4,6},{6,7},{7,5},{5,3},{3,1},{1,0},{8,10},{10,12},{12... | collective-permute-start | bytes 786440 | tf_op jit(solution)/shard_map/near_r2/ppermute | solution.py:216
  25.9 3.7 %copy-start = (bf16[64,4096]{1,0:T(8,128)(2,1)S(1)}, bf16[64,4096]{1,0:T(8,128)(2,1)}, u32[]{:S(2)}) copy-start(bf16[64,4096]{1,0:T(8,128)(2,1)} %refs_0_.5) | copy-start | bytes 1572868
  25.9 11.3 %collective-permute-start.5 = (bf16[32,4096]{1,0:T(8,128)(2,1)S(1)}, bf16[32,4096]{1,0:T(8,128)(2,1)S(1)}, u32[]{:S(2)}, u32[]{:S(2)}) collective-permute-start(bf16[32,4096]{1,0:T(8,128)(2,1)S(1)} %get-tuple-element.61.refs_3_), channel_id=1, source_target_pairs={{2,0},{4,2},{6,4},{7,6},{5,7},{3,5},{1,3},{0,1},{10,8},{12,10},{14... | collective-permute-start | bytes 786440 | tf_op jit(solution)/shard_map/near_l2/ppermute | solution.py:220
  27.6 11.8 %collective-permute-start.8 = (bf16[32,4096]{1,0:T(8,128)(2,1)S(1)}, bf16[32,4096]{1,0:T(8,128)(2,1)S(1)}, u32[]{:S(2)}, u32[]{:S(2)}) collective-permute-start(bf16[32,4096]{1,0:T(8,128)(2,1)S(1)} %get-tuple-element.65.refs_9_.refs_0_), channel_id=1, source_target_pairs={{0,2},{2,4},{4,6},{6,7},{7,5},{5,3},{3,1},{1,0},{8,10},{10,12},{12... | collective-permute-start | bytes 786440 | tf_op jit(solution)/shard_map/far_r3/ppermute | solution.py:216
  28.0 11.4 %collective-permute-start.9 = (bf16[32,4096]{1,0:T(8,128)(2,1)S(1)}, bf16[32,4096]{1,0:T(8,128)(2,1)S(1)}, u32[]{:S(2)}, u32[]{:S(2)}) collective-permute-start(bf16[32,4096]{1,0:T(8,128)(2,1)S(1)} %get-tuple-element.69.refs_3_), channel_id=1, source_target_pairs={{2,0},{4,2},{6,4},{7,6},{5,7},{3,5},{1,3},{0,1},{10,8},{12,10},{14... | collective-permute-start | bytes 786440 | tf_op jit(solution)/shard_map/far_l3/ppermute | solution.py:220
  37.2 9.8 %collective-permute-start.14 = (f32[2,192,1024]{2,1,0:T(8,128)S(1)}, f32[2,192,1024]{2,1,0:T(8,128)S(1)}, u32[]{:S(2)}, u32[]{:S(2)}) collective-permute-start(f32[2,192,1024]{2,1,0:T(8,128)S(1)} %get-tuple-element.76), channel_id=1, source_target_pairs={{0,8},{8,0},{1,9},{9,1},{2,10},{10,2},{3,11},{11,3},{4,12},{12,4},... | collective-permute-start | bytes 4718600 | tf_op jit(solution)/shard_map/swap2/ppermute | solution.py:224
  37.3 9.7 %collective-permute-start.12 = (bf16[32,4096]{1,0:T(8,128)(2,1)S(1)}, bf16[32,4096]{1,0:T(8,128)(2,1)S(1)}, u32[]{:S(2)}, u32[]{:S(2)}) collective-permute-start(bf16[32,4096]{1,0:T(8,128)(2,1)S(1)} %get-tuple-element.70.refs_2_.refs_1_), channel_id=1, source_target_pairs={{0,2},{2,4},{4,6},{6,7},{7,5},{5,3},{3,1},{1,0},{8,10},{10,12},{12... | collective-permute-start | bytes 786440 | tf_op jit(solution)/shard_map/near_r3/ppermute | solution.py:216
  37.8 9.3 %collective-permute-start.13 = (bf16[32,4096]{1,0:T(8,128)(2,1)S(1)}, bf16[32,4096]{1,0:T(8,128)(2,1)S(1)}, u32[]{:S(2)}, u32[]{:S(2)}) collective-permute-start(bf16[32,4096]{1,0:T(8,128)(2,1)S(1)} %get-tuple-element.73.refs_2_), channel_id=1, source_target_pairs={{2,0},{4,2},{6,4},{7,6},{5,7},{3,5},{1,3},{0,1},{10,8},{12,10},{14... | collective-permute-start | bytes 786440 | tf_op jit(solution)/shard_map/near_l3/ppermute | solution.py:220
  39.4 12.2 %collective-permute-start.10 = (bf16[32,4096]{1,0:T(8,128)(2,1)S(1)}, bf16[32,4096]{1,0:T(8,128)(2,1)S(1)}, u32[]{:S(2)}, u32[]{:S(2)}) collective-permute-start(bf16[32,4096]{1,0:T(8,128)(2,1)S(1)} %get-tuple-element.71.refs_8_.refs_2_), channel_id=1, source_target_pairs={{0,2},{2,4},{4,6},{6,7},{7,5},{5,3},{3,1},{1,0},{8,10},{10,12},{12... | collective-permute-start | bytes 786440 | tf_op jit(solution)/shard_map/far_r4/ppermute | solution.py:216
  39.8 12.0 %collective-permute-start.11 = (bf16[32,4096]{1,0:T(8,128)(2,1)S(1)}, bf16[32,4096]{1,0:T(8,128)(2,1)S(1)}, u32[]{:S(2)}, u32[]{:S(2)}) collective-permute-start(bf16[32,4096]{1,0:T(8,128)(2,1)S(1)} %get-tuple-element.72.refs_5_), channel_id=1, source_target_pairs={{2,0},{4,2},{6,4},{7,6},{5,7},{3,5},{1,3},{0,1},{10,8},{12,10},{14... | collective-permute-start | bytes 786440 | tf_op jit(solution)/shard_map/far_l4/ppermute | solution.py:220
  56.0 6.5 %collective-permute-start.18 = (f32[2,192,1024]{2,1,0:T(8,128)S(1)}, f32[2,192,1024]{2,1,0:T(8,128)S(1)}, u32[]{:S(2)}, u32[]{:S(2)}) collective-permute-start(f32[2,192,1024]{2,1,0:T(8,128)S(1)} %gate_up.6.refs_9_), channel_id=1, source_target_pairs={{0,8},{8,0},{1,9},{9,1},{2,10},{10,2},{3,11},{11,3},{4,12},{12,4},... | collective-permute-start | bytes 4718600 | tf_op jit(solution)/shard_map/swap/ppermute | solution.py:224
  56.1 6.9 %collective-permute-start.16 = (f32[2,128,1024]{2,1,0:T(8,128)S(1)}, f32[2,128,1024]{2,1,0:T(8,128)S(1)}, u32[]{:S(2)}, u32[]{:S(2)}) collective-permute-start(f32[2,128,1024]{2,1,0:T(8,128)S(1)} %get-tuple-element.87), channel_id=1, source_target_pairs={{0,8},{8,0},{1,9},{9,1},{2,10},{10,2},{3,11},{11,3},{4,12},{12,4},... | collective-permute-start | bytes 3145736 | tf_op jit(solution)/shard_map/swap_last/ppermute | solution.py:224
  62.8 1.8 %collective-permute-start.19 = (bf16[192,1024]{1,0:T(8,128)(2,1)S(1)}, bf16[192,1024]{1,0:T(8,128)(2,1)S(1)}, u32[]{:S(2)}, u32[]{:S(2)}) collective-permute-start(bf16[192,1024]{1,0:T(8,128)(2,1)S(1)} %gated.5.refs_0_), channel_id=1, source_target_pairs={{0,8},{8,0},{1,9},{9,1},{2,10},{10,2},{3,11},{11,3},{4,12},{12,4},... | collective-permute-start | bytes 1179656 | tf_op jit(solution)/shard_map/swap/ppermute | solution.py:224
  63.2 10.3 %collective-permute-start.17 = (bf16[128,1024]{1,0:T(8,128)(2,1)S(1)}, bf16[128,1024]{1,0:T(8,128)(2,1)S(1)}, u32[]{:S(2)}, u32[]{:S(2)}) collective-permute-start(bf16[128,1024]{1,0:T(8,128)(2,1)S(1)} %gated.4.refs_0_), channel_id=1, source_target_pairs={{0,8},{8,0},{1,9},{9,1},{2,10},{10,2},{3,11},{11,3},{4,12},{12,4},... | collective-permute-start | bytes 786440 | tf_op jit(solution)/shard_map/swap/ppermute | solution.py:224
  69.4 9.2 %collective-permute-start.20 = (bf16[32,4096]{1,0:T(8,128)(2,1)S(1)}, bf16[32,4096]{1,0:T(8,128)(2,1)S(1)}, u32[]{:S(2)}, u32[]{:S(2)}) collective-permute-start(bf16[32,4096]{1,0:T(8,128)(2,1)S(1)} %get-tuple-element.90), channel_id=1, source_target_pairs={{2,0},{4,2},{6,4},{7,6},{5,7},{3,5},{1,3},{0,1},{10,8},{12,10},{14... | collective-permute-start | bytes 786440 | tf_op jit(solution)/shard_map/left/ppermute | solution.py:220
  71.1 9.2 %collective-permute-start.21 = (bf16[32,4096]{1,0:T(8,128)(2,1)S(1)}, bf16[32,4096]{1,0:T(8,128)(2,1)S(1)}, u32[]{:S(2)}, u32[]{:S(2)}) collective-permute-start(bf16[32,4096]{1,0:T(8,128)(2,1)S(1)} %get-tuple-element.91), channel_id=1, source_target_pairs={{0,2},{2,4},{4,6},{6,7},{7,5},{5,3},{3,1},{1,0},{8,10},{10,12},{12... | collective-permute-start | bytes 786440 | tf_op jit(solution)/shard_map/right/ppermute | solution.py:216
  71.8 10.6 %collective-permute-start.15 = (bf16[192,1024]{1,0:T(8,128)(2,1)S(1)}, bf16[192,1024]{1,0:T(8,128)(2,1)S(1)}, u32[]{:S(2)}, u32[]{:S(2)}) collective-permute-start(bf16[192,1024]{1,0:T(8,128)(2,1)S(1)} %gated.3.refs_0_), channel_id=1, source_target_pairs={{0,8},{8,0},{1,9},{9,1},{2,10},{10,2},{3,11},{11,3},{4,12},{12,4},... | collective-permute-start | bytes 1179656 | tf_op jit(solution)/shard_map/swap/ppermute | solution.py:224
  71.9 15.4 %collective-permute-start.22 = (bf16[32,4096]{1,0:T(8,128)(2,1)S(1)}, bf16[32,4096]{1,0:T(8,128)(2,1)S(1)}, u32[]{:S(2)}, u32[]{:S(2)}) collective-permute-start(bf16[32,4096]{1,0:T(8,128)(2,1)S(1)} %get-tuple-element.94), channel_id=1, source_target_pairs={{2,0},{4,2},{6,4},{7,6},{5,7},{3,5},{1,3},{0,1},{10,8},{12,10},{14... | collective-permute-start | bytes 786440 | tf_op jit(solution)/shard_map/left/ppermute | solution.py:220
  73.6 13.7 %collective-permute-start.23 = (bf16[32,4096]{1,0:T(8,128)(2,1)S(1)}, bf16[32,4096]{1,0:T(8,128)(2,1)S(1)}, u32[]{:S(2)}, u32[]{:S(2)}) collective-permute-start(bf16[32,4096]{1,0:T(8,128)(2,1)S(1)} %get-tuple-element.95), channel_id=1, source_target_pairs={{0,2},{2,4},{4,6},{6,7},{7,5},{5,3},{3,1},{1,0},{8,10},{10,12},{12... | collective-permute-start | bytes 786440 | tf_op jit(solution)/shard_map/right/ppermute | solution.py:216
  80.4 9.5 %collective-permute-start.26 = (bf16[32,4096]{1,0:T(8,128)(2,1)S(1)}, bf16[32,4096]{1,0:T(8,128)(2,1)S(1)}, u32[]{:S(2)}, u32[]{:S(2)}) collective-permute-start(bf16[32,4096]{1,0:T(8,128)(2,1)S(1)} %get-tuple-element.118.refs_4_), channel_id=1, source_target_pairs={{2,0},{4,2},{6,4},{7,6},{5,7},{3,5},{1,3},{0,1},{10,8},{12,10},{14... | collective-permute-start | bytes 786440 | tf_op jit(solution)/shard_map/left/ppermute | solution.py:220
  82.0 9.5 %collective-permute-start.27 = (bf16[32,4096]{1,0:T(8,128)(2,1)S(1)}, bf16[32,4096]{1,0:T(8,128)(2,1)S(1)}, u32[]{:S(2)}, u32[]{:S(2)}) collective-permute-start(bf16[32,4096]{1,0:T(8,128)(2,1)S(1)} %get-tuple-element.117.refs_5_), channel_id=1, source_target_pairs={{0,2},{2,4},{4,6},{6,7},{7,5},{5,3},{3,1},{1,0},{8,10},{10,12},{12... | collective-permute-start | bytes 786440 | tf_op jit(solution)/shard_map/right/ppermute | solution.py:216
  87.4 9.7 %collective-permute-start.25 = (bf16[32,4096]{1,0:T(8,128)(2,1)S(1)}, bf16[32,4096]{1,0:T(8,128)(2,1)S(1)}, u32[]{:S(2)}, u32[]{:S(2)}) collective-permute-start(bf16[32,4096]{1,0:T(8,128)(2,1)S(1)} %add_convert_fusion.refs_3_), channel_id=1, source_target_pairs={{0,2},{2,4},{4,6},{6,7},{7,5},{5,3},{3,1},{1,0},{8,10},{10,12},{12... | collective-permute-start | bytes 786440 | tf_op jit(solution)/shard_map/right/ppermute | solution.py:216
  87.9 9.3 %collective-permute-start.24 = (bf16[32,4096]{1,0:T(8,128)(2,1)S(1)}, bf16[32,4096]{1,0:T(8,128)(2,1)S(1)}, u32[]{:S(2)}, u32[]{:S(2)}) collective-permute-start(bf16[32,4096]{1,0:T(8,128)(2,1)S(1)} %add_convert_fusion.1.refs_2_), channel_id=1, source_target_pairs={{2,0},{4,2},{6,4},{7,6},{5,7},{3,5},{1,3},{0,1},{10,8},{12,10},{14... | collective-permute-start | bytes 786440 | tf_op jit(solution)/shard_map/left/ppermute | solution.py:220
  91.6 11.1 %collective-permute-start.30 = (bf16[32,4096]{1,0:T(8,128)(2,1)S(1)}, bf16[32,4096]{1,0:T(8,128)(2,1)S(1)}, u32[]{:S(2)}, u32[]{:S(2)}) collective-permute-start(bf16[32,4096]{1,0:T(8,128)(2,1)S(1)} %get-tuple-element.114.refs_2_), channel_id=1, source_target_pairs={{2,0},{4,2},{6,4},{7,6},{5,7},{3,5},{1,3},{0,1},{10,8},{12,10},{14... | collective-permute-start | bytes 786440 | tf_op jit(solution)/shard_map/left/ppermute | solution.py:220
  93.3 9.5 %collective-permute-start.31 = (bf16[32,4096]{1,0:T(8,128)(2,1)S(1)}, bf16[32,4096]{1,0:T(8,128)(2,1)S(1)}, u32[]{:S(2)}, u32[]{:S(2)}) collective-permute-start(bf16[32,4096]{1,0:T(8,128)(2,1)S(1)} %get-tuple-element.113.refs_3_), channel_id=1, source_target_pairs={{0,2},{2,4},{4,6},{6,7},{7,5},{5,3},{3,1},{1,0},{8,10},{10,12},{12... | collective-permute-start | bytes 786440 | tf_op jit(solution)/shard_map/right/ppermute | solution.py:216
  97.2 8.7 %collective-permute-start.28 = (bf16[32,4096]{1,0:T(8,128)(2,1)S(1)}, bf16[32,4096]{1,0:T(8,128)(2,1)S(1)}, u32[]{:S(2)}, u32[]{:S(2)}) collective-permute-start(bf16[32,4096]{1,0:T(8,128)(2,1)S(1)} %get-tuple-element.116.refs_2_), channel_id=1, source_target_pairs={{2,0},{4,2},{6,4},{7,6},{5,7},{3,5},{1,3},{0,1},{10,8},{12,10},{14... | collective-permute-start | bytes 786440 | tf_op jit(solution)/shard_map/left/ppermute | solution.py:220
  98.9 8.4 %collective-permute-start.29 = (bf16[32,4096]{1,0:T(8,128)(2,1)S(1)}, bf16[32,4096]{1,0:T(8,128)(2,1)S(1)}, u32[]{:S(2)}, u32[]{:S(2)}) collective-permute-start(bf16[32,4096]{1,0:T(8,128)(2,1)S(1)} %get-tuple-element.115.refs_3_), channel_id=1, source_target_pairs={{0,2},{2,4},{4,6},{6,7},{7,5},{5,3},{3,1},{1,0},{8,10},{10,12},{12... | collective-permute-start | bytes 786440 | tf_op jit(solution)/shard_map/right/ppermute | solution.py:216
  107.4 7.2 %collective-permute-start.32 = (bf16[32,4096]{1,0:T(8,128)(2,1)S(1)}, bf16[32,4096]{1,0:T(8,128)(2,1)S(1)}, u32[]{:S(2)}, u32[]{:S(2)}) collective-permute-start(bf16[32,4096]{1,0:T(8,128)(2,1)S(1)} %get-tuple-element.112), channel_id=1, source_target_pairs={{2,0},{4,2},{6,4},{7,6},{5,7},{3,5},{1,3},{0,1},{10,8},{12,10},{14... | collective-permute-start | bytes 786440 | tf_op jit(solution)/shard_map/left/ppermute | solution.py:220
  109.0 6.9 %collective-permute-start.33 = (bf16[32,4096]{1,0:T(8,128)(2,1)S(1)}, bf16[32,4096]{1,0:T(8,128)(2,1)S(1)}, u32[]{:S(2)}, u32[]{:S(2)}) collective-permute-start(bf16[32,4096]{1,0:T(8,128)(2,1)S(1)} %get-tuple-element.111), channel_id=1, source_target_pairs={{0,2},{2,4},{4,6},{6,7},{7,5},{5,3},{3,1},{1,0},{8,10},{10,12},{12... | collective-permute-start | bytes 786440 | tf_op jit(solution)/shard_map/right/ppermute | solution.py:216

commit v8 on v7

--- a/solution.py
+++ b/solution.py
@@ -23,7 +23,7 @@
     return pltpu.with_memory_space_constraint(x, pltpu.VMEM)
 
 
-GATE, KERNEL = 22_000_000_000, 5_500_000_000
+GATE, KERNEL = 22_000_000_000, 1_100_000_000
 
 
 def params(vmem, work=0):
@@ -84,7 +84,7 @@
     )(part, *map(in_hbm, weights), *after)
 
 
-def gate_up(pieces, weights, after, load=None):
+def gate_up(pieces, weights, after, load=None, side=0):
     if any(p.shape[0] % 16 for p in pieces):
         pieces = [jnp.concatenate(pieces, axis=0)]
     m, k = sum(p.shape[0] for p in pieces), pieces[0].shape[1]
@@ -97,8 +97,8 @@
     if load is not None:
         wide = load.shape[1] // 2
         extra = [in_hbm(load)]
-        shapes += [pltpu.VMEM((load.shape[0], wide), load.dtype)] * 2
-        scratch += [pltpu.SemaphoreType.DMA((2, 8))]
+        shapes += [pltpu.VMEM((load.shape[0], wide), load.dtype)]
+        scratch += [pltpu.SemaphoreType.DMA((1, 8))]
 
     def body(*refs):
         weight_refs = refs[count : count + len(weights)]
@@ -107,7 +107,7 @@
         copies = []
         if load is not None:
             source = refs[count + len(weights)]
-            copies = fetches([(source, 0), (source, wide)], outs[halves:], refs[-1])
+            copies = fetches([(source, side * wide)], outs[halves:], refs[-1])
         for copy in copies:
             copy.start()
         at = 0
@@ -133,7 +133,7 @@
         out_specs=[VMEM] * len(shapes),
         out_shape=shapes,
         scratch_shapes=scratch,
-        **params(6 << 20, KERNEL),
+        **params(3 << 20, KERNEL),
     )(*pieces, *map(in_vmem, weights), *extra, *after)
 
 
@@ -155,7 +155,7 @@
         in_specs=[VMEM, VMEM],
         out_specs=VMEM,
         out_shape=jax.ShapeDtypeStruct((m, w), BF16),
-        **params(4 << 20),
+        **params(2 << 20),
     )(ours, theirs)
 
 
@@ -200,7 +200,7 @@
             jax.ShapeDtypeStruct((size, 2 * n), dtype) for _, size, dtype in outs
         ],
         scratch_shapes=[pltpu.VMEM((m, 2 * w), BF16)],
-        **params(6 << 20),
+        **params(3 << 20),
     )(part, *[h for pair in halves for h in pair], *map(in_vmem, weights), *after)
 
 
@@ -233,83 +233,88 @@
         keep, give = core.reshape(1), (1 - core).reshape(1)
 
         a, b = tokens[:cut], tokens[cut:]
-        far_r, far_l = right(a, "far_r1"), left(b, "far_l1")
-        near_r, near_l = right(b, "near_r1"), left(a, "near_l1")
-        wide = bring([gate_weight, up_weight], give, [])
-        blocks, groups, sums, got = [[tokens]], [], [], []
+        far_r, far_l = right(a, "farR1"), left(b, "farL1")
+        wide = bring([gate_weight], give, [])
+        near_r, near_l = right(b, "nearR1"), left(a, "nearL1")
+        wide += bring([up_weight], give, wide)
+        waiting = {("own", 0): tokens}
+        groups, theirs, ours = [], [], []
         after = wide[-1:]
         for d in range(1, half):
             far_r, far_l = gate(far_r, far_l, after=after, work=GATE)
-            held_r, held_l = far_r, far_l
-            far_r = right(far_r, f"far_r{d + 1}")
-            far_l = left(far_l, f"far_l{d + 1}")
+            held = {("far_r", d): far_r, ("far_l", d): far_l}
+            after = [far_r]
+            far_r, far_l = right(far_r, f"farR{d + 1}"), left(far_l, f"farL{d + 1}")
             if d == 1:
-                wide += bring([gate_weight, up_weight], keep, [held_r])
-                near_r, near_l = gate(near_r, near_l, after=wide[-1:], work=GATE)
+                wide += bring([gate_weight, up_weight], keep, after)
+                done = wide[-1:]
             else:
-                groups.append(blocks[0] + blocks[1] if d == 2 else blocks[d - 1])
-                theirs, ours = gate_up(groups[-1], wide, [held_r])
-                near_r, near_l, theirs, ours, *got = gate(
-                    near_r, near_l, theirs, ours, *got, work=GATE
-                )
-                sums.append(ours)
-                if d < half - 1:
-                    got.append(other(theirs, f"swap{d}"))
-            blocks.append([held_r, near_r, near_l, held_l])
+                if d > 2:
+                    waiting |= held
+                out = gate_up(list(waiting.values()), wide, after)
+                groups.append(list(waiting))
+                theirs.append(out[0])
+                ours.append(out[1])
+                done, waiting = out[:1], {}
+            if d <= 2:
+                waiting |= held
+            near_r, near_l = gate(near_r, near_l, after=done, work=GATE)
+            waiting |= {("near_r", d): near_r, ("near_l", d): near_l}
+            after = [near_r]
             if d < half - 1:
-                after = [near_r]
-                near_r = right(near_r, f"near_r{d + 1}")
-                near_l = left(near_l, f"near_l{d + 1}")
-        far_r, far_l, theirs, *got = gate(far_r, far_l, theirs, *got, after=[near_r])
-        got.append(other(theirs, "swap_last"))
-        last = [far_r, far_l, *blocks[-1]]
+                near_r = right(near_r, f"nearR{d + 1}")
+                near_l = left(near_l, f"nearL{d + 1}")
+        far_r, far_l, *theirs = gate(far_r, far_l, *theirs, after=after)
+        got = [other(x) for x in theirs]
+        waiting |= {("far_r", half): far_r, ("far_l", half): far_l}
 
         def hide(ours, got):
             h = gated(ours, got)
             return h, other(h)
 
-        (theirs,) = gate_up(last, wide[:2], [])
-        last_got = other(theirs)
-        ours, *weight = gate_up(last, wide[2:], [theirs], down_weight)
-        last = hide(ours, last_got)
-        near = [hide(*pair) for pair in zip(sums, got)]
-        at = [(i * cut, cut) for i in range(6)]
-        outs = [(*at[3], BF16), (*at[4], BF16), (*at[0], BF16), (*at[1], BF16)]
-        outs += [(*at[2], F32), (*at[5], F32)]
-        b_l, b_r, a_l, a_r, next_l, next_r = down([last], weight, keep, outs, [])
-
+        last = list(waiting.values())
+        last_theirs, low = gate_up(last, wide[:2], [], down_weight, 0)
+        last_got = other(last_theirs)
+        last_ours, high = gate_up(last, wide[2:], [last_theirs], down_weight, 1)
+        weight = [low, high]
+        last = hide(last_ours, last_got)
+        outs = [(i * cut, cut, BF16) for i in range(4)]
+        b_l, b_r, a_l, a_r = down([last], weight, keep, outs, [])
+        hidden = [hide(*pair) for pair in zip(ours, got)]
+
+        def put_down(which, after):
+            size = sum(h.shape[0] for h, _ in hidden[which])
+            outs = [(0, size, F32)]
+            (rest,) = down(hidden[which], weight, keep, outs, after)
+            at = 0
+            for key in sum(groups[which], []):
+                part[key] = rest[at : at + (rows if key[0] == "own" else cut)]
+                at += part[key].shape[0]
+            return rest
+
+        part = {}
         b_l, b_r = left(b_l), right(b_r)
         a_l, a_r = left(a_l), right(a_r)
-        (rest,) = down(near[-1:], weight, keep, [(0, 2 * rows, F32)], [next_l])
-        parts = {half - 2: [rest[i * cut : (i + 1) * cut] for i in range(4)]}
-        after = [rest]
-        for d in range(half - 2, -1, -1):
+        after = [put_down(slice(-1, None), [])]
+        for d in range(half - 1, 0, -1):
             b_l, b_r = gate(b_l, b_r, after=after)
-            if d > 0:
-                _, left_b, right_a, _ = parts[d]
-                b_l, b_r = add(left_b, b_l), add(right_a, b_r)
+            if d > 1:
+                b_l = add(part["near_r", d - 1], b_l)
+                b_r = add(part["near_l", d - 1], b_r)
                 after = [b_l, b_r]
                 b_l, b_r = left(b_l), right(b_r)
             else:
                 after = [b_l, b_r]
-            if d == half - 2:
-                size = rows * (2 * half - 5)
-                (rest,) = down(near[:-1], weight, keep, [(0, size, F32)], after)
-                for e in range(1, half - 2):
-                    first = rows * (2 * e - 1)
-                    parts[e] = [
-                        rest[first + i * cut : first + (i + 1) * cut] for i in range(4)
-                    ]
-                after = [rest]
+            if d == half - 1:
+                after = [put_down(slice(0, -1), after)]
             a_l, a_r = gate(a_l, a_r, after=after)
-            a_l, a_r = add(next_l, a_l), add(next_r, a_r)
+            a_l, a_r = add(part["far_r", d], a_l), add(part["far_l", d], a_r)
             after = [a_l, a_r]
             a_l, a_r = left(a_l), right(a_r)
-            if d > 0:
-                next_l, _, _, next_r = parts[d]
         a_l, a_r = gate(a_l, a_r)
-        total_a = rest[:cut] + a_l.astype(F32) + b_r.astype(F32)
-        total_b = rest[cut:rows] + a_r.astype(F32) + b_l.astype(F32)
+        own = part["own", 0]
+        total_a = own[:cut] + a_l.astype(F32) + b_r.astype(F32)
+        total_b = own[cut:] + a_r.astype(F32) + b_l.astype(F32)
         return jnp.concatenate([total_a, total_b], axis=0).astype(BF16)
 
     return shards

time: 117 us -> 108 us (0.923)
  waiting for transfers between devices: 33.3 us -> 22.2 us
    ppermute x14, waiting for transfers between devices: 19.2 us -> 4.41 us  [right(): return lax.ppermute(x, 'gy', to_right)]
    ppermute x14, starting transfers between devices: 22.6 us -> 11.4 us  [left(): return lax.ppermute(x, 'gy', to_left)]
    ppermute x14, starting transfers between devices: 7.32 us -> 18.5 us  [right(): return lax.ppermute(x, 'gy', to_right)]
    ppermute x14, waiting for transfers between devices: 13.2 us -> 17.1 us  [left(): return lax.ppermute(x, 'gy', to_left)]
    pallas_call x2 -> x3, Pallas kernels: 11.9 us -> 12.9 us  [bring(): pl.pallas_call(body, name='bring', in_specs=[SMEM] + [ANY] * (count + len...]
  transfers between devices with their start and end apart: 34 -> 34, of which waited for: 14 -> 14; matrix products, arithmetic and copies ran while one was open for 0% -> 0% of each run, Pallas kernels for 39% -> 47%
where the time goes in v8:
time: 108 us
  Pallas kernels  50.4 us (47%)
  starting transfers between devices  31.2 us (29%)
  waiting for transfers between devices  22.2 us (21%)
  local copies, waits for them, and re-layouts  1.86 us (2%)
  other arithmetic  1.53 us (1%)
    pallas_call x4, Pallas kernels, gate_up(): pl.pallas_call(body, name='gate_up', in_specs=[VMEM] * (count + len(weigh...  23.4 us
    ppermute x14, starting transfers between devices, right(): return lax.ppermute(x, 'gy', to_right)  18.5 us
    ppermute x14, waiting for transfers between devices, left(): return lax.ppermute(x, 'gy', to_left)  17.1 us
    pallas_call x3, Pallas kernels, down(): pl.pallas_call(body, name='down', in_specs=[SMEM] + [VMEM] * (2 * count +...  13.3 us
    pallas_call x3, Pallas kernels, bring(): pl.pallas_call(body, name='bring', in_specs=[SMEM] + [ANY] * (count + len...  12.9 us
    ppermute x14, starting transfers between devices, left(): return lax.ppermute(x, 'gy', to_left)  11.4 us
    ppermute x14, waiting for transfers between devices, right(): return lax.ppermute(x, 'gy', to_right)  4.41 us
  transfers between devices with their start and end apart: 34, of which 14 were waited for; matrix products, arithmetic and copies ran while one was open for 0% of the time, Pallas kernels for 47%

profile of v8, /device:TPU:0, one launch (start us, length us, event | category | flops | bytes accessed | tf_op | source)
XLA Modules:
  0.0 107.5 jit_solution(3548903967467262386)
XLA Ops:
  0.0 1.9 %fusion.14 = (bf16[32,4096]{1,0:T(8,128)(2,1)}, bf16[32,4096]{1,0:T(8,128)(2,1)}) fusion(bf16[64,4096]{1,0:T(8,128)(2,1)} %refs_0_.7), kind=kLoop, calls=%fused_computation.27 | loop fusion | bytes 1048576 | tf_op jit(solution)/shard_map/slice | solution.py:235
  1.9 3.0 %collective-permute-start = (bf16[32,4096]{1,0:T(8,128)(2,1)}, bf16[32,4096]{1,0:T(8,128)(2,1)}, u32[]{:S(2)}, u32[]{:S(2)}) collective-permute-start(bf16[32,4096]{1,0:T(8,128)(2,1)} %get-tuple-element.106), channel_id=1, source_target_pairs={{0,2},{2,4},{4,6},{6,7},{7,5},{5,3},{3,1},{1,0},{8,10},{10,12},{12... | collective-permute-start | bytes 786440 | tf_op jit(solution)/shard_map/farR1/ppermute | solution.py:216
  4.9 2.0 %collective-permute-start.2 = (bf16[32,4096]{1,0:T(8,128)(2,1)}, bf16[32,4096]{1,0:T(8,128)(2,1)}, u32[]{:S(2)}, u32[]{:S(2)}) collective-permute-start(bf16[32,4096]{1,0:T(8,128)(2,1)} %get-tuple-element.105), channel_id=1, source_target_pairs={{0,2},{2,4},{4,6},{6,7},{7,5},{5,3},{3,1},{1,0},{8,10},{10,12},{12... | collective-permute-start | bytes 786440 | tf_op jit(solution)/shard_map/nearR1/ppermute | solution.py:216
  6.9 3.5 %bring.3.refs_1_.refs_5_.refs_6_.refs_4_ = bf16[4096,1024]{1,0:T(8,128)(2,1)S(1)} custom-call(s32[1]{0:T(128)} %bitcast.1.part_ref, bf16[4096,2048]{1,0:T(8,128)(2,1)} %refs_0_.6), custom_call_target="tpu_custom_call" | custom-call | flops 1100000000 | tf_op jit(solution)/shard_map/bring/pallas_call | solution.py:76
  10.4 3.5 %bring.4.refs_2_.refs_6_.refs_7_.refs_5_ = bf16[4096,1024]{1,0:T(8,128)(2,1)S(1)} custom-call(s32[1]{0:T(128)} %bitcast.1.part_ref, bf16[4096,2048]{1,0:T(8,128)(2,1)} %refs_1_.1, bf16[4096,1024]{1,0:T(8,128)(2,1)S(1)} %bring.3.refs_1_.refs_5_.refs_6_.refs_4_), custom_call_target="tpu_custom_call" | custom-call | flops 1100000000 | tf_op jit(solution)/shard_map/bring/pallas_call | solution.py:76
  13.9 0.5 collective-permute-done.1.refs_1_
  14.4 1.6 %collective-permute-start.4 = (bf16[32,4096]{1,0:T(8,128)(2,1)}, bf16[32,4096]{1,0:T(8,128)(2,1)S(1)}, u32[]{:S(2)}, u32[]{:S(2)}) collective-permute-start(bf16[32,4096]{1,0:T(8,128)(2,1)} %get-tuple-element.49.refs_2_.refs_1_), channel_id=1, source_target_pairs={{0,2},{2,4},{4,6},{6,7},{7,5},{5,3},{3,1},{1,0},{8,10},{10,12},{12... | collective-permute-start | bytes 786440 | tf_op jit(solution)/shard_map/farR2/ppermute | solution.py:216
  16.0 0.4 collective-permute-start.5
  16.5 5.9 %bring.5 = (bf16[4096,1024]{1,0:T(8,128)(2,1)S(1)}, bf16[4096,1024]{1,0:T(8,128)(2,1)S(1)}) custom-call(s32[1]{0:T(128)} %bitcast.part_ref, bf16[4096,2048]{1,0:T(8,128)(2,1)} %refs_0_.6, bf16[4096,2048]{1,0:T(8,128)(2,1)} %refs_1_.1, bf16[32,4096]{1,0:T(8,128)(2,1)} %get-tuple-element.49.refs_2_.refs_1_), custom_call_target="tpu_custom_call" | custom-call | flops 1100000000 | tf_op jit(solution)/shard_map/bring/pallas_call | solution.py:76
  22.4 1.6 %collective-permute-start.8 = (bf16[32,4096]{1,0:T(8,128)(2,1)}, bf16[32,4096]{1,0:T(8,128)(2,1)S(1)}, u32[]{:S(2)}, u32[]{:S(2)}) collective-permute-start(bf16[32,4096]{1,0:T(8,128)(2,1)} %get-tuple-element.52.refs_2_.refs_3_), channel_id=1, source_target_pairs={{0,2},{2,4},{4,6},{6,7},{7,5},{5,3},{3,1},{1,0},{8,10},{10,12},{12... | collective-permute-start | bytes 786440 | tf_op jit(solution)/shard_map/nearR2/ppermute | solution.py:216
  24.1 0.4 collective-permute-start.9
  24.5 1.6 %collective-permute-start.6 = (bf16[32,4096]{1,0:T(8,128)(2,1)S(1)}, bf16[32,4096]{1,0:T(8,128)(2,1)S(1)}, u32[]{:S(2)}, u32[]{:S(2)}) collective-permute-start(bf16[32,4096]{1,0:T(8,128)(2,1)S(1)} %get-tuple-element.55.refs_9_.refs_0_), channel_id=1, source_target_pairs={{0,2},{2,4},{4,6},{6,7},{7,5},{5,3},{3,1},{1,0},{8,10},{10,12},{12... | collective-permute-start | bytes 786440 | tf_op jit(solution)/shard_map/farR3/ppermute | solution.py:216
  26.1 0.4 collective-permute-start.7
  26.6 8.8 %gate_up.4 = (f32[2,192,1024]{2,1,0:T(8,128)S(1)}, f32[2,192,1024]{2,1,0:T(8,128)S(1)}) custom-call(bf16[64,4096]{1,0:T(8,128)(2,1)S(1)} %copy-done, bf16[32,4096]{1,0:T(8,128)(2,1)} %get-tuple-element.49.refs_2_.refs_1_, bf16[32,4096]{1,0:T(8,128)(2,1)} %get-tuple-element.50.refs_2_, bf16[32,4096]{1,0:T(8,128)(2,1)} %get-tuple-element.52.refs_2_.refs_3_, ...), custom_call_target="tpu_custom_call" | custom-call | flops 1100000000 | tf_op jit(solution)/shard_map/gate_up/pallas_call | solution.py:129
  35.4 1.6 %collective-permute-start.12 = (bf16[32,4096]{1,0:T(8,128)(2,1)S(1)}, bf16[32,4096]{1,0:T(8,128)(2,1)S(1)}, u32[]{:S(2)}, u32[]{:S(2)}) collective-permute-start(bf16[32,4096]{1,0:T(8,128)(2,1)S(1)} %get-tuple-element.59.refs_2_), channel_id=1, source_target_pairs={{0,2},{2,4},{4,6},{6,7},{7,5},{5,3},{3,1},{1,0},{8,10},{10,12},{12... | collective-permute-start | bytes 786440 | tf_op jit(solution)/shard_map/nearR3/ppermute | solution.py:216
  37.0 0.5 collective-permute-start.13
  37.5 1.6 %collective-permute-start.10 = (bf16[32,4096]{1,0:T(8,128)(2,1)S(1)}, bf16[32,4096]{1,0:T(8,128)(2,1)S(1)}, u32[]{:S(2)}, u32[]{:S(2)}) collective-permute-start(bf16[32,4096]{1,0:T(8,128)(2,1)S(1)} %get-tuple-element.60.refs_4_.refs_10_), channel_id=1, source_target_pairs={{0,2},{2,4},{4,6},{6,7},{7,5},{5,3},{3,1},{1,0},{8,10},{10,12},{12... | collective-permute-start | bytes 786440 | tf_op jit(solution)/shard_map/farR4/ppermute | solution.py:216
  39.0 0.5 collective-permute-start.11
  39.5 7.6 %gate_up.5 = (f32[2,192,1024]{2,1,0:T(8,128)S(1)}, f32[2,192,1024]{2,1,0:T(8,128)S(1)}) custom-call(bf16[32,4096]{1,0:T(8,128)(2,1)S(1)} %get-tuple-element.55.refs_9_.refs_0_, bf16[32,4096]{1,0:T(8,128)(2,1)S(1)} %get-tuple-element.57.refs_1_, bf16[32,4096]{1,0:T(8,128)(2,1)S(1)} %get-tuple-element.59.refs_2_, ...), custom_call_target="tpu_custom_call" | custom-call | flops 1100000000 | tf_op jit(solution)/shard_map/gate_up/pallas_call | solution.py:129
  47.2 1.1 %collective-permute-done.11.refs_1_ = bf16[32,4096]{1,0:T(8,128)(2,1)S(1)} collective-permute-done((bf16[32,4096]{1,0:T(8,128)(2,1)S(1)}, bf16[32,4096]{1,0:T(8,128)(2,1)S(1)}, u32[]{:S(2)}, u32[]{:S(2)}) %collective-permute-start.11) | collective-permute-done | bytes 262176 | tf_op jit(solution)/shard_map/farL4/ppermute | solution.py:220
  48.3 3.5 %gate_up.6 = (f32[2,128,1024]{2,1,0:T(8,128)S(1)}, bf16[2048,2048]{1,0:T(8,128)(2,1)S(1)}) custom-call(bf16[32,4096]{1,0:T(8,128)(2,1)S(1)} %get-tuple-element.64.refs_4_.refs_0_, bf16[32,4096]{1,0:T(8,128)(2,1)S(1)} %get-tuple-element.66.refs_1_, bf16[32,4096]{1,0:T(8,128)(2,1)S(1)} %get-tuple-element.67.refs_2_, ...), custom_call_target="tpu_custom_call" | custom-call | flops 1100000000 | tf_op jit(solution)/shard_map/gate_up/pallas_call | solution.py:129
  51.8 0.6 collective-permute-start.18
  52.4 3.5 %gate_up.7 = (f32[2,128,1024]{2,1,0:T(8,128)S(1)}, bf16[2048,2048]{1,0:T(8,128)(2,1)S(1)}) custom-call(bf16[32,4096]{1,0:T(8,128)(2,1)S(1)} %get-tuple-element.64.refs_4_.refs_0_, bf16[32,4096]{1,0:T(8,128)(2,1)S(1)} %get-tuple-element.66.refs_1_, bf16[32,4096]{1,0:T(8,128)(2,1)S(1)} %get-tuple-element.67.refs_2_, ...), custom_call_target="tpu_custom_call" | custom-call | flops 1100000000 | tf_op jit(solution)/shard_map/gate_up/pallas_call | solution.py:129
  56.2 0.5 collective-permute-start.19
  57.1 0.7 collective-permute-done.19.refs_1_
  57.8 3.7 %down.4 = (bf16[32,4096]{1,0:T(8,128)(2,1)S(1)}, bf16[32,4096]{1,0:T(8,128)(2,1)S(1)}, bf16[32,4096]{1,0:T(8,128)(2,1)S(1)}, bf16[32,4096]{1,0:T(8,128)(2,1)S(1)}) custom-call(s32[1]{0:T(128)} %bitcast.part_ref, bf16[128,1024]{1,0:T(8,128)(2,1)S(1)} %gated.5.refs_0_, bf16[128,1024]{1,0:T(8,128)(2,1)S(1)} %collective-permute-done.19.refs_1_, ...), custom_call_target="tpu_custom_call" | custom-call | tf_op jit(solution)/shard_map/down/pallas_call | solution.py:194
  61.5 0.5 collective-permute-start.20
  62.1 1.6 %collective-permute-start.21 = (bf16[32,4096]{1,0:T(8,128)(2,1)S(1)}, bf16[32,4096]{1,0:T(8,128)(2,1)S(1)}, u32[]{:S(2)}, u32[]{:S(2)}) collective-permute-start(bf16[32,4096]{1,0:T(8,128)(2,1)S(1)} %get-tuple-element.76), channel_id=1, source_target_pairs={{0,2},{2,4},{4,6},{6,7},{7,5},{5,3},{3,1},{1,0},{8,10},{10,12},{12... | collective-permute-start | bytes 786440 | tf_op jit(solution)/shard_map/right/ppermute | solution.py:216
  63.6 0.5 collective-permute-start.22
  64.1 1.6 %collective-permute-start.23 = (bf16[32,4096]{1,0:T(8,128)(2,1)S(1)}, bf16[32,4096]{1,0:T(8,128)(2,1)S(1)}, u32[]{:S(2)}, u32[]{:S(2)}) collective-permute-start(bf16[32,4096]{1,0:T(8,128)(2,1)S(1)} %get-tuple-element.80), channel_id=1, source_target_pairs={{0,2},{2,4},{4,6},{6,7},{7,5},{5,3},{3,1},{1,0},{8,10},{10,12},{12... | collective-permute-start | bytes 786440 | tf_op jit(solution)/shard_map/right/ppermute | solution.py:216
  66.1 4.8 %down.3.refs_2_ = f32[192,4096]{1,0:T(8,128)S(1)} custom-call(s32[1]{0:T(128)} %bitcast.part_ref, bf16[192,1024]{1,0:T(8,128)(2,1)S(1)} %gated.4.refs_0_, bf16[192,1024]{1,0:T(8,128)(2,1)S(1)} %collective-permute-done.17.refs_1_, bf16[2048,2048]{1,0:T(8,128)(2,1)S(1)} %get-tuple-element.69.refs_2_, bf16[2048,2048]{1,0:T(8,128)(2,1)S(1)} %get-tuple-element.71.refs_3_), custom_call_target="tpu_custom_call" | custom-call | tf_op jit(solution)/shard_map/down/pallas_call | solution.py:194
  71.4 1.6 %collective-permute-start.26 = (bf16[32,4096]{1,0:T(8,128)(2,1)S(1)}, bf16[32,4096]{1,0:T(8,128)(2,1)S(1)}, u32[]{:S(2)}, u32[]{:S(2)}) collective-permute-start(bf16[32,4096]{1,0:T(8,128)(2,1)S(1)} %get-tuple-element.104.refs_4_), channel_id=1, source_target_pairs={{2,0},{4,2},{6,4},{7,6},{5,7},{3,5},{1,3},{0,1},{10,8},{12,10},{14... | collective-permute-start | bytes 786440 | tf_op jit(solution)/shard_map/left/ppermute | solution.py:220
  73.0 0.5 collective-permute-start.27
  73.4 4.8 %down.5.refs_2_ = f32[192,4096]{1,0:T(8,128)S(1)} custom-call(s32[1]{0:T(128)} %bitcast.part_ref, bf16[192,1024]{1,0:T(8,128)(2,1)S(1)} %gated.3.refs_0_, bf16[192,1024]{1,0:T(8,128)(2,1)S(1)} %collective-permute-done.15.refs_1_, bf16[2048,2048]{1,0:T(8,128)(2,1)S(1)} %get-tuple-element.69.refs_2_, bf16[2048,2048]{1,0:T(8,128)(2,1)S(1)} %get-tuple-element.71.refs_3_, ...), custom_call_target="tpu_custom_call" | custom-call | tf_op jit(solution)/shard_map/down/pallas_call | solution.py:194
  78.4 1.6 %collective-permute-start.24 = (bf16[32,4096]{1,0:T(8,128)(2,1)S(1)}, bf16[32,4096]{1,0:T(8,128)(2,1)S(1)}, u32[]{:S(2)}, u32[]{:S(2)}) collective-permute-start(bf16[32,4096]{1,0:T(8,128)(2,1)S(1)} %get-tuple-element.102.refs_2_), channel_id=1, source_target_pairs={{2,0},{4,2},{6,4},{7,6},{5,7},{3,5},{1,3},{0,1},{10,8},{12,10},{14... | collective-permute-start | bytes 786440 | tf_op jit(solution)/shard_map/left/ppermute | solution.py:220
  80.0 0.5 collective-permute-start.25
  80.5 1.5 %collective-permute-done.26.refs_0_ = bf16[32,4096]{1,0:T(8,128)(2,1)S(1)} collective-permute-done((bf16[32,4096]{1,0:T(8,128)(2,1)S(1)}, bf16[32,4096]{1,0:T(8,128)(2,1)S(1)}, u32[]{:S(2)}, u32[]{:S(2)}) %collective-permute-start.26) | collective-permute-done | bytes 262176 | tf_op jit(solution)/shard_map/left/ppermute | solution.py:220
  82.4 1.6 %collective-permute-start.30 = (bf16[32,4096]{1,0:T(8,128)(2,1)S(1)}, bf16[32,4096]{1,0:T(8,128)(2,1)S(1)}, u32[]{:S(2)}, u32[]{:S(2)}) collective-permute-start(bf16[32,4096]{1,0:T(8,128)(2,1)S(1)} %get-tuple-element.100.refs_2_), channel_id=1, source_target_pairs={{2,0},{4,2},{6,4},{7,6},{5,7},{3,5},{1,3},{0,1},{10,8},{12,10},{14... | collective-permute-start | bytes 786440 | tf_op jit(solution)/shard_map/left/ppermute | solution.py:220
  84.5 3.2 %collective-permute-done.24.refs_0_ = bf16[32,4096]{1,0:T(8,128)(2,1)S(1)} collective-permute-done((bf16[32,4096]{1,0:T(8,128)(2,1)S(1)}, bf16[32,4096]{1,0:T(8,128)(2,1)S(1)}, u32[]{:S(2)}, u32[]{:S(2)}) %collective-permute-start.24) | collective-permute-done | bytes 262176 | tf_op jit(solution)/shard_map/left/ppermute | solution.py:220
  87.7 1.6 %collective-permute-done.25.refs_1_ = bf16[32,4096]{1,0:T(8,128)(2,1)S(1)} collective-permute-done((bf16[32,4096]{1,0:T(8,128)(2,1)S(1)}, bf16[32,4096]{1,0:T(8,128)(2,1)S(1)}, u32[]{:S(2)}, u32[]{:S(2)}) %collective-permute-start.25) | collective-permute-done | bytes 262176 | tf_op jit(solution)/shard_map/right/ppermute | solution.py:216
  89.4 1.6 %collective-permute-start.28 = (bf16[32,4096]{1,0:T(8,128)(2,1)S(1)}, bf16[32,4096]{1,0:T(8,128)(2,1)S(1)}, u32[]{:S(2)}, u32[]{:S(2)}) collective-permute-start(bf16[32,4096]{1,0:T(8,128)(2,1)S(1)} %get-tuple-element.98.refs_2_), channel_id=1, source_target_pairs={{2,0},{4,2},{6,4},{7,6},{5,7},{3,5},{1,3},{0,1},{10,8},{12,10},{14... | collective-permute-start | bytes 786440 | tf_op jit(solution)/shard_map/left/ppermute | solution.py:220
  91.5 1.8 %collective-permute-done.30.refs_0_ = bf16[32,4096]{1,0:T(8,128)(2,1)S(1)} collective-permute-done((bf16[32,4096]{1,0:T(8,128)(2,1)S(1)}, bf16[32,4096]{1,0:T(8,128)(2,1)S(1)}, u32[]{:S(2)}, u32[]{:S(2)}) %collective-permute-start.30) | collective-permute-done | bytes 262176 | tf_op jit(solution)/shard_map/left/ppermute | solution.py:220
  93.3 1.6 %collective-permute-done.31.refs_1_ = bf16[32,4096]{1,0:T(8,128)(2,1)S(1)} collective-permute-done((bf16[32,4096]{1,0:T(8,128)(2,1)S(1)}, bf16[32,4096]{1,0:T(8,128)(2,1)S(1)}, u32[]{:S(2)}, u32[]{:S(2)}) %collective-permute-start.31) | collective-permute-done | bytes 262176 | tf_op jit(solution)/shard_map/right/ppermute | solution.py:216
  94.9 3.4 %collective-permute-done.28.refs_0_ = bf16[32,4096]{1,0:T(8,128)(2,1)S(1)} collective-permute-done((bf16[32,4096]{1,0:T(8,128)(2,1)S(1)}, bf16[32,4096]{1,0:T(8,128)(2,1)S(1)}, u32[]{:S(2)}, u32[]{:S(2)}) %collective-permute-start.28) | collective-permute-done | bytes 262176 | tf_op jit(solution)/shard_map/left/ppermute | solution.py:220
  98.5 1.6 %collective-permute-start.32 = (bf16[32,4096]{1,0:T(8,128)(2,1)S(1)}, bf16[32,4096]{1,0:T(8,128)(2,1)S(1)}, u32[]{:S(2)}, u32[]{:S(2)}) collective-permute-start(bf16[32,4096]{1,0:T(8,128)(2,1)S(1)} %get-tuple-element.96), channel_id=1, source_target_pairs={{2,0},{4,2},{6,4},{7,6},{5,7},{3,5},{1,3},{0,1},{10,8},{12,10},{14... | collective-permute-start | bytes 786440 | tf_op jit(solution)/shard_map/left/ppermute | solution.py:220
  100.1 0.5 collective-permute-start.33
  100.6 5.5 %collective-permute-done.32.refs_0_ = bf16[32,4096]{1,0:T(8,128)(2,1)S(1)} collective-permute-done((bf16[32,4096]{1,0:T(8,128)(2,1)S(1)}, bf16[32,4096]{1,0:T(8,128)(2,1)S(1)}, u32[]{:S(2)}, u32[]{:S(2)}) %collective-permute-start.32) | collective-permute-done | bytes 262176 | tf_op jit(solution)/shard_map/left/ppermute | solution.py:220
  106.7 0.8 pad_maximum_fusion
  (57 shorter events, 4.1 us)
Async XLA Ops:
  1.9 12.0 %collective-permute-start = (bf16[32,4096]{1,0:T(8,128)(2,1)}, bf16[32,4096]{1,0:T(8,128)(2,1)}, u32[]{:S(2)}, u32[]{:S(2)}) collective-permute-start(bf16[32,4096]{1,0:T(8,128)(2,1)} %get-tuple-element.106), channel_id=1, source_target_pairs={{0,2},{2,4},{4,6},{6,7},{7,5},{5,3},{3,1},{1,0},{8,10},{10,12},{12... | collective-permute-start | bytes 786440 | tf_op jit(solution)/shard_map/farR1/ppermute | solution.py:216
  4.9 9.5 %collective-permute-start.1 = (bf16[32,4096]{1,0:T(8,128)(2,1)}, bf16[32,4096]{1,0:T(8,128)(2,1)}, u32[]{:S(2)}, u32[]{:S(2)}) collective-permute-start(bf16[32,4096]{1,0:T(8,128)(2,1)} %get-tuple-element.105), channel_id=1, source_target_pairs={{2,0},{4,2},{6,4},{7,6},{5,7},{3,5},{1,3},{0,1},{10,8},{12,10},{14... | collective-permute-start | bytes 786440 | tf_op jit(solution)/shard_map/farL1/ppermute | solution.py:220
  4.9 17.5 %collective-permute-start.2 = (bf16[32,4096]{1,0:T(8,128)(2,1)}, bf16[32,4096]{1,0:T(8,128)(2,1)}, u32[]{:S(2)}, u32[]{:S(2)}) collective-permute-start(bf16[32,4096]{1,0:T(8,128)(2,1)} %get-tuple-element.105), channel_id=1, source_target_pairs={{0,2},{2,4},{4,6},{6,7},{7,5},{5,3},{3,1},{1,0},{8,10},{10,12},{12... | collective-permute-start | bytes 786440 | tf_op jit(solution)/shard_map/nearR1/ppermute | solution.py:216
  6.9 15.5 %collective-permute-start.3 = (bf16[32,4096]{1,0:T(8,128)(2,1)}, bf16[32,4096]{1,0:T(8,128)(2,1)}, u32[]{:S(2)}, u32[]{:S(2)}) collective-permute-start(bf16[32,4096]{1,0:T(8,128)(2,1)} %get-tuple-element.106), channel_id=1, source_target_pairs={{2,0},{4,2},{6,4},{7,6},{5,7},{3,5},{1,3},{0,1},{10,8},{12,10},{14... | collective-permute-start | bytes 786440 | tf_op jit(solution)/shard_map/nearL1/ppermute | solution.py:220
  14.4 10.1 %collective-permute-start.4 = (bf16[32,4096]{1,0:T(8,128)(2,1)}, bf16[32,4096]{1,0:T(8,128)(2,1)S(1)}, u32[]{:S(2)}, u32[]{:S(2)}) collective-permute-start(bf16[32,4096]{1,0:T(8,128)(2,1)} %get-tuple-element.49.refs_2_.refs_1_), channel_id=1, source_target_pairs={{0,2},{2,4},{4,6},{6,7},{7,5},{5,3},{3,1},{1,0},{8,10},{10,12},{12... | collective-permute-start | bytes 786440 | tf_op jit(solution)/shard_map/farR2/ppermute | solution.py:216
  16.0 8.5 %collective-permute-start.5 = (bf16[32,4096]{1,0:T(8,128)(2,1)}, bf16[32,4096]{1,0:T(8,128)(2,1)S(1)}, u32[]{:S(2)}, u32[]{:S(2)}) collective-permute-start(bf16[32,4096]{1,0:T(8,128)(2,1)} %get-tuple-element.50.refs_2_), channel_id=1, source_target_pairs={{2,0},{4,2},{6,4},{7,6},{5,7},{3,5},{1,3},{0,1},{10,8},{12,10},{14... | collective-permute-start | bytes 786440 | tf_op jit(solution)/shard_map/farL2/ppermute | solution.py:220
  22.4 12.9 %collective-permute-start.8 = (bf16[32,4096]{1,0:T(8,128)(2,1)}, bf16[32,4096]{1,0:T(8,128)(2,1)S(1)}, u32[]{:S(2)}, u32[]{:S(2)}) collective-permute-start(bf16[32,4096]{1,0:T(8,128)(2,1)} %get-tuple-element.52.refs_2_.refs_3_), channel_id=1, source_target_pairs={{0,2},{2,4},{4,6},{6,7},{7,5},{5,3},{3,1},{1,0},{8,10},{10,12},{12... | collective-permute-start | bytes 786440 | tf_op jit(solution)/shard_map/nearR2/ppermute | solution.py:216
  24.1 2.5 %copy-start = (bf16[64,4096]{1,0:T(8,128)(2,1)S(1)}, bf16[64,4096]{1,0:T(8,128)(2,1)}, u32[]{:S(2)}) copy-start(bf16[64,4096]{1,0:T(8,128)(2,1)} %refs_0_.7) | copy-start | bytes 1572868
  24.1 11.3 %collective-permute-start.9 = (bf16[32,4096]{1,0:T(8,128)(2,1)}, bf16[32,4096]{1,0:T(8,128)(2,1)S(1)}, u32[]{:S(2)}, u32[]{:S(2)}) collective-permute-start(bf16[32,4096]{1,0:T(8,128)(2,1)} %get-tuple-element.53.refs_4_), channel_id=1, source_target_pairs={{2,0},{4,2},{6,4},{7,6},{5,7},{3,5},{1,3},{0,1},{10,8},{12,10},{14... | collective-permute-start | bytes 786440 | tf_op jit(solution)/shard_map/nearL2/ppermute | solution.py:220
  24.5 12.9 %collective-permute-start.6 = (bf16[32,4096]{1,0:T(8,128)(2,1)S(1)}, bf16[32,4096]{1,0:T(8,128)(2,1)S(1)}, u32[]{:S(2)}, u32[]{:S(2)}) collective-permute-start(bf16[32,4096]{1,0:T(8,128)(2,1)S(1)} %get-tuple-element.55.refs_9_.refs_0_), channel_id=1, source_target_pairs={{0,2},{2,4},{4,6},{6,7},{7,5},{5,3},{3,1},{1,0},{8,10},{10,12},{12... | collective-permute-start | bytes 786440 | tf_op jit(solution)/shard_map/farR3/ppermute | solution.py:216
  26.1 11.4 %collective-permute-start.7 = (bf16[32,4096]{1,0:T(8,128)(2,1)S(1)}, bf16[32,4096]{1,0:T(8,128)(2,1)S(1)}, u32[]{:S(2)}, u32[]{:S(2)}) collective-permute-start(bf16[32,4096]{1,0:T(8,128)(2,1)S(1)} %get-tuple-element.57.refs_1_), channel_id=1, source_target_pairs={{2,0},{4,2},{6,4},{7,6},{5,7},{3,5},{1,3},{0,1},{10,8},{12,10},{14... | collective-permute-start | bytes 786440 | tf_op jit(solution)/shard_map/farL3/ppermute | solution.py:220
  35.4 11.7 %collective-permute-start.12 = (bf16[32,4096]{1,0:T(8,128)(2,1)S(1)}, bf16[32,4096]{1,0:T(8,128)(2,1)S(1)}, u32[]{:S(2)}, u32[]{:S(2)}) collective-permute-start(bf16[32,4096]{1,0:T(8,128)(2,1)S(1)} %get-tuple-element.59.refs_2_), channel_id=1, source_target_pairs={{0,2},{2,4},{4,6},{6,7},{7,5},{5,3},{3,1},{1,0},{8,10},{10,12},{12... | collective-permute-start | bytes 786440 | tf_op jit(solution)/shard_map/nearR3/ppermute | solution.py:216
  37.0 10.1 %collective-permute-start.13 = (bf16[32,4096]{1,0:T(8,128)(2,1)S(1)}, bf16[32,4096]{1,0:T(8,128)(2,1)S(1)}, u32[]{:S(2)}, u32[]{:S(2)}) collective-permute-start(bf16[32,4096]{1,0:T(8,128)(2,1)S(1)} %get-tuple-element.62.refs_3_), channel_id=1, source_target_pairs={{2,0},{4,2},{6,4},{7,6},{5,7},{3,5},{1,3},{0,1},{10,8},{12,10},{14... | collective-permute-start | bytes 786440 | tf_op jit(solution)/shard_map/nearL3/ppermute | solution.py:220
  37.5 9.7 %collective-permute-start.10 = (bf16[32,4096]{1,0:T(8,128)(2,1)S(1)}, bf16[32,4096]{1,0:T(8,128)(2,1)S(1)}, u32[]{:S(2)}, u32[]{:S(2)}) collective-permute-start(bf16[32,4096]{1,0:T(8,128)(2,1)S(1)} %get-tuple-element.60.refs_4_.refs_10_), channel_id=1, source_target_pairs={{0,2},{2,4},{4,6},{6,7},{7,5},{5,3},{3,1},{1,0},{8,10},{10,12},{12... | collective-permute-start | bytes 786440 | tf_op jit(solution)/shard_map/farR4/ppermute | solution.py:216
  39.0 9.2 %collective-permute-start.11 = (bf16[32,4096]{1,0:T(8,128)(2,1)S(1)}, bf16[32,4096]{1,0:T(8,128)(2,1)S(1)}, u32[]{:S(2)}, u32[]{:S(2)}) collective-permute-start(bf16[32,4096]{1,0:T(8,128)(2,1)S(1)} %get-tuple-element.61.refs_5_), channel_id=1, source_target_pairs={{2,0},{4,2},{6,4},{7,6},{5,7},{3,5},{1,3},{0,1},{10,8},{12,10},{14... | collective-permute-start | bytes 786440 | tf_op jit(solution)/shard_map/farL4/ppermute | solution.py:220
  48.3 8.4 %collective-permute-start.16 = (f32[2,192,1024]{2,1,0:T(8,128)S(1)}, f32[2,192,1024]{2,1,0:T(8,128)S(1)}, u32[]{:S(2)}, u32[]{:S(2)}) collective-permute-start(f32[2,192,1024]{2,1,0:T(8,128)S(1)} %get-tuple-element.73), channel_id=1, source_target_pairs={{0,8},{8,0},{1,9},{9,1},{2,10},{10,2},{3,11},{11,3},{4,12},{12,4},... | collective-permute-start | bytes 4718600 | tf_op jit(solution)/shard_map/swap/ppermute | solution.py:224
  51.8 4.1 %collective-permute-start.18 = (f32[2,128,1024]{2,1,0:T(8,128)S(1)}, f32[2,128,1024]{2,1,0:T(8,128)S(1)}, u32[]{:S(2)}, u32[]{:S(2)}) collective-permute-start(f32[2,128,1024]{2,1,0:T(8,128)S(1)} %get-tuple-element.70.refs_7_), channel_id=1, source_target_pairs={{0,8},{8,0},{1,9},{9,1},{2,10},{10,2},{3,11},{11,3},{4,12},{12,4},... | collective-permute-start | bytes 3145736 | tf_op jit(solution)/shard_map/swap/ppermute | solution.py:224
  52.3 11.7 %collective-permute-start.14 = (f32[2,192,1024]{2,1,0:T(8,128)S(1)}, f32[2,192,1024]{2,1,0:T(8,128)S(1)}, u32[]{:S(2)}, u32[]{:S(2)}) collective-permute-start(f32[2,192,1024]{2,1,0:T(8,128)S(1)} %get-tuple-element.65), channel_id=1, source_target_pairs={{0,8},{8,0},{1,9},{9,1},{2,10},{10,2},{3,11},{11,3},{4,12},{12,4},... | collective-permute-start | bytes 4718600 | tf_op jit(solution)/shard_map/swap/ppermute | solution.py:224
  56.2 1.7 %collective-permute-start.19 = (bf16[128,1024]{1,0:T(8,128)(2,1)S(1)}, bf16[128,1024]{1,0:T(8,128)(2,1)S(1)}, u32[]{:S(2)}, u32[]{:S(2)}) collective-permute-start(bf16[128,1024]{1,0:T(8,128)(2,1)S(1)} %gated.5.refs_0_), channel_id=1, source_target_pairs={{0,8},{8,0},{1,9},{9,1},{2,10},{10,2},{3,11},{11,3},{4,12},{12,4},... | collective-permute-start | bytes 786440 | tf_op jit(solution)/shard_map/swap/ppermute | solution.py:224
  57.0 9.0 %collective-permute-start.17 = (bf16[192,1024]{1,0:T(8,128)(2,1)S(1)}, bf16[192,1024]{1,0:T(8,128)(2,1)S(1)}, u32[]{:S(2)}, u32[]{:S(2)}) collective-permute-start(bf16[192,1024]{1,0:T(8,128)(2,1)S(1)} %gated.4.refs_0_), channel_id=1, source_target_pairs={{0,8},{8,0},{1,9},{9,1},{2,10},{10,2},{3,11},{11,3},{4,12},{12,4},... | collective-permute-start | bytes 1179656 | tf_op jit(solution)/shard_map/swap/ppermute | solution.py:224
  61.5 9.3 %collective-permute-start.20 = (bf16[32,4096]{1,0:T(8,128)(2,1)S(1)}, bf16[32,4096]{1,0:T(8,128)(2,1)S(1)}, u32[]{:S(2)}, u32[]{:S(2)}) collective-permute-start(bf16[32,4096]{1,0:T(8,128)(2,1)S(1)} %get-tuple-element.75), channel_id=1, source_target_pairs={{2,0},{4,2},{6,4},{7,6},{5,7},{3,5},{1,3},{0,1},{10,8},{12,10},{14... | collective-permute-start | bytes 786440 | tf_op jit(solution)/shard_map/left/ppermute | solution.py:220
  62.1 9.2 %collective-permute-start.21 = (bf16[32,4096]{1,0:T(8,128)(2,1)S(1)}, bf16[32,4096]{1,0:T(8,128)(2,1)S(1)}, u32[]{:S(2)}, u32[]{:S(2)}) collective-permute-start(bf16[32,4096]{1,0:T(8,128)(2,1)S(1)} %get-tuple-element.76), channel_id=1, source_target_pairs={{0,2},{2,4},{4,6},{6,7},{7,5},{5,3},{3,1},{1,0},{8,10},{10,12},{12... | collective-permute-start | bytes 786440 | tf_op jit(solution)/shard_map/right/ppermute | solution.py:216
  63.6 14.6 %collective-permute-start.22 = (bf16[32,4096]{1,0:T(8,128)(2,1)S(1)}, bf16[32,4096]{1,0:T(8,128)(2,1)S(1)}, u32[]{:S(2)}, u32[]{:S(2)}) collective-permute-start(bf16[32,4096]{1,0:T(8,128)(2,1)S(1)} %get-tuple-element.79), channel_id=1, source_target_pairs={{2,0},{4,2},{6,4},{7,6},{5,7},{3,5},{1,3},{0,1},{10,8},{12,10},{14... | collective-permute-start | bytes 786440 | tf_op jit(solution)/shard_map/left/ppermute | solution.py:220
  64.1 14.2 %collective-permute-start.23 = (bf16[32,4096]{1,0:T(8,128)(2,1)S(1)}, bf16[32,4096]{1,0:T(8,128)(2,1)S(1)}, u32[]{:S(2)}, u32[]{:S(2)}) collective-permute-start(bf16[32,4096]{1,0:T(8,128)(2,1)S(1)} %get-tuple-element.80), channel_id=1, source_target_pairs={{0,2},{2,4},{4,6},{6,7},{7,5},{5,3},{3,1},{1,0},{8,10},{10,12},{12... | collective-permute-start | bytes 786440 | tf_op jit(solution)/shard_map/right/ppermute | solution.py:216
  66.0 7.5 %collective-permute-start.15 = (bf16[192,1024]{1,0:T(8,128)(2,1)S(1)}, bf16[192,1024]{1,0:T(8,128)(2,1)S(1)}, u32[]{:S(2)}, u32[]{:S(2)}) collective-permute-start(bf16[192,1024]{1,0:T(8,128)(2,1)S(1)} %gated.3.refs_0_), channel_id=1, source_target_pairs={{0,8},{8,0},{1,9},{9,1},{2,10},{10,2},{3,11},{11,3},{4,12},{12,4},... | collective-permute-start | bytes 1179656 | tf_op jit(solution)/shard_map/swap/ppermute | solution.py:224
  71.4 10.6 %collective-permute-start.26 = (bf16[32,4096]{1,0:T(8,128)(2,1)S(1)}, bf16[32,4096]{1,0:T(8,128)(2,1)S(1)}, u32[]{:S(2)}, u32[]{:S(2)}) collective-permute-start(bf16[32,4096]{1,0:T(8,128)(2,1)S(1)} %get-tuple-element.104.refs_4_), channel_id=1, source_target_pairs={{2,0},{4,2},{6,4},{7,6},{5,7},{3,5},{1,3},{0,1},{10,8},{12,10},{14... | collective-permute-start | bytes 786440 | tf_op jit(solution)/shard_map/left/ppermute | solution.py:220
  73.0 9.3 %collective-permute-start.27 = (bf16[32,4096]{1,0:T(8,128)(2,1)S(1)}, bf16[32,4096]{1,0:T(8,128)(2,1)S(1)}, u32[]{:S(2)}, u32[]{:S(2)}) collective-permute-start(bf16[32,4096]{1,0:T(8,128)(2,1)S(1)} %get-tuple-element.103.refs_5_), channel_id=1, source_target_pairs={{0,2},{2,4},{4,6},{6,7},{7,5},{5,3},{3,1},{1,0},{8,10},{10,12},{12... | collective-permute-start | bytes 786440 | tf_op jit(solution)/shard_map/right/ppermute | solution.py:216
  78.4 9.3 %collective-permute-start.24 = (bf16[32,4096]{1,0:T(8,128)(2,1)S(1)}, bf16[32,4096]{1,0:T(8,128)(2,1)S(1)}, u32[]{:S(2)}, u32[]{:S(2)}) collective-permute-start(bf16[32,4096]{1,0:T(8,128)(2,1)S(1)} %get-tuple-element.102.refs_2_), channel_id=1, source_target_pairs={{2,0},{4,2},{6,4},{7,6},{5,7},{3,5},{1,3},{0,1},{10,8},{12,10},{14... | collective-permute-start | bytes 786440 | tf_op jit(solution)/shard_map/left/ppermute | solution.py:220
  80.0 9.2 %collective-permute-start.25 = (bf16[32,4096]{1,0:T(8,128)(2,1)S(1)}, bf16[32,4096]{1,0:T(8,128)(2,1)S(1)}, u32[]{:S(2)}, u32[]{:S(2)}) collective-permute-start(bf16[32,4096]{1,0:T(8,128)(2,1)S(1)} %get-tuple-element.101.refs_3_), channel_id=1, source_target_pairs={{0,2},{2,4},{4,6},{6,7},{7,5},{5,3},{3,1},{1,0},{8,10},{10,12},{12... | collective-permute-start | bytes 786440 | tf_op jit(solution)/shard_map/right/ppermute | solution.py:216
  82.4 10.9 %collective-permute-start.30 = (bf16[32,4096]{1,0:T(8,128)(2,1)S(1)}, bf16[32,4096]{1,0:T(8,128)(2,1)S(1)}, u32[]{:S(2)}, u32[]{:S(2)}) collective-permute-start(bf16[32,4096]{1,0:T(8,128)(2,1)S(1)} %get-tuple-element.100.refs_2_), channel_id=1, source_target_pairs={{2,0},{4,2},{6,4},{7,6},{5,7},{3,5},{1,3},{0,1},{10,8},{12,10},{14... | collective-permute-start | bytes 786440 | tf_op jit(solution)/shard_map/left/ppermute | solution.py:220
  84.0 10.8 %collective-permute-start.31 = (bf16[32,4096]{1,0:T(8,128)(2,1)S(1)}, bf16[32,4096]{1,0:T(8,128)(2,1)S(1)}, u32[]{:S(2)}, u32[]{:S(2)}) collective-permute-start(bf16[32,4096]{1,0:T(8,128)(2,1)S(1)} %get-tuple-element.99.refs_3_), channel_id=1, source_target_pairs={{0,2},{2,4},{4,6},{6,7},{7,5},{5,3},{3,1},{1,0},{8,10},{10,12},{12... | collective-permute-start | bytes 786440 | tf_op jit(solution)/shard_map/right/ppermute | solution.py:216
  89.4 8.9 %collective-permute-start.28 = (bf16[32,4096]{1,0:T(8,128)(2,1)S(1)}, bf16[32,4096]{1,0:T(8,128)(2,1)S(1)}, u32[]{:S(2)}, u32[]{:S(2)}) collective-permute-start(bf16[32,4096]{1,0:T(8,128)(2,1)S(1)} %get-tuple-element.98.refs_2_), channel_id=1, source_target_pairs={{2,0},{4,2},{6,4},{7,6},{5,7},{3,5},{1,3},{0,1},{10,8},{12,10},{14... | collective-permute-start | bytes 786440 | tf_op jit(solution)/shard_map/left/ppermute | solution.py:220
  91.0 7.4 %collective-permute-start.29 = (bf16[32,4096]{1,0:T(8,128)(2,1)S(1)}, bf16[32,4096]{1,0:T(8,128)(2,1)S(1)}, u32[]{:S(2)}, u32[]{:S(2)}) collective-permute-start(bf16[32,4096]{1,0:T(8,128)(2,1)S(1)} %get-tuple-element.97.refs_3_), channel_id=1, source_target_pairs={{0,2},{2,4},{4,6},{6,7},{7,5},{5,3},{3,1},{1,0},{8,10},{10,12},{12... | collective-permute-start | bytes 786440 | tf_op jit(solution)/shard_map/right/ppermute | solution.py:216
  98.5 7.6 %collective-permute-start.32 = (bf16[32,4096]{1,0:T(8,128)(2,1)S(1)}, bf16[32,4096]{1,0:T(8,128)(2,1)S(1)}, u32[]{:S(2)}, u32[]{:S(2)}) collective-permute-start(bf16[32,4096]{1,0:T(8,128)(2,1)S(1)} %get-tuple-element.96), channel_id=1, source_target_pairs={{2,0},{4,2},{6,4},{7,6},{5,7},{3,5},{1,3},{0,1},{10,8},{12,10},{14... | collective-permute-start | bytes 786440 | tf_op jit(solution)/shard_map/left/ppermute | solution.py:220
  100.1 6.4 %collective-permute-start.33 = (bf16[32,4096]{1,0:T(8,128)(2,1)S(1)}, bf16[32,4096]{1,0:T(8,128)(2,1)S(1)}, u32[]{:S(2)}, u32[]{:S(2)}) collective-permute-start(bf16[32,4096]{1,0:T(8,128)(2,1)S(1)} %get-tuple-element.95), channel_id=1, source_target_pairs={{0,2},{2,4},{4,6},{6,7},{7,5},{5,3},{3,1},{1,0},{8,10},{10,12},{12... | collective-permute-start | bytes 786440 | tf_op jit(solution)/shard_map/right/ppermute | solution.py:216

commit v9 on v8

--- a/solution.py
+++ b/solution.py
@@ -237,7 +237,7 @@
         wide = bring([gate_weight], give, [])
         near_r, near_l = right(b, "nearR1"), left(a, "nearL1")
         wide += bring([up_weight], give, wide)
-        waiting = {("own", 0): tokens}
+        waiting = {("own", "a"): a, ("own", "b"): b}
         groups, theirs, ours = [], [], []
         after = wide[-1:]
         for d in range(1, half):
@@ -245,17 +245,19 @@
             held = {("far_r", d): far_r, ("far_l", d): far_l}
             after = [far_r]
             far_r, far_l = right(far_r, f"farR{d + 1}"), left(far_l, f"farL{d + 1}")
+            if d > 2:
+                waiting |= held
             if d == 1:
                 wide += bring([gate_weight, up_weight], keep, after)
                 done = wide[-1:]
             else:
-                if d > 2:
-                    waiting |= held
-                out = gate_up(list(waiting.values()), wide, after)
                 groups.append(list(waiting))
+                rows_now, waiting = list(waiting.values()), {}
+                both = True
+                out = gate_up(rows_now, wide if both else wide[:2], after)
                 theirs.append(out[0])
-                ours.append(out[1])
-                done, waiting = out[:1], {}
+                ours += out[1:]
+                done = out[:1]
             if d <= 2:
                 waiting |= held
             near_r, near_l = gate(near_r, near_l, after=done, work=GATE)
@@ -264,8 +266,10 @@
             if d < half - 1:
                 near_r = right(near_r, f"nearR{d + 1}")
                 near_l = left(near_l, f"nearL{d + 1}")
+                if d > 1 and not both:
+                    ours += gate_up(rows_now, wide[2:], after)
+                    after = ours[-1:]
         far_r, far_l, *theirs = gate(far_r, far_l, *theirs, after=after)
-        got = [other(x) for x in theirs]
         waiting |= {("far_r", half): far_r, ("far_l", half): far_l}
 
         def hide(ours, got):
@@ -275,6 +279,7 @@
         last = list(waiting.values())
         last_theirs, low = gate_up(last, wide[:2], [], down_weight, 0)
         last_got = other(last_theirs)
+        got = [other(x) for x in theirs]
         last_ours, high = gate_up(last, wide[2:], [last_theirs], down_weight, 1)
         weight = [low, high]
         last = hide(last_ours, last_got)
@@ -288,33 +293,30 @@
             (rest,) = down(hidden[which], weight, keep, outs, after)
             at = 0
             for key in sum(groups[which], []):
-                part[key] = rest[at : at + (rows if key[0] == "own" else cut)]
-                at += part[key].shape[0]
+                part[key] = rest[at : at + cut]
+                at += cut
             return rest
 
         part = {}
+        a_l, a_r = left(a_l), right(a_r)
         b_l, b_r = left(b_l), right(b_r)
-        a_l, a_r = left(a_l), right(a_r)
         after = [put_down(slice(-1, None), [])]
         for d in range(half - 1, 0, -1):
+            a_l, a_r = gate(a_l, a_r, after=after)
+            a_l, a_r = add(part["far_r", d], a_l), add(part["far_l", d], a_r)
+            after = [a_l, a_r]
+            a_l, a_r = left(a_l), right(a_r)
             b_l, b_r = gate(b_l, b_r, after=after)
             if d > 1:
                 b_l = add(part["near_r", d - 1], b_l)
                 b_r = add(part["near_l", d - 1], b_r)
                 after = [b_l, b_r]
                 b_l, b_r = left(b_l), right(b_r)
-            else:
-                after = [b_l, b_r]
             if d == half - 1:
                 after = [put_down(slice(0, -1), after)]
-            a_l, a_r = gate(a_l, a_r, after=after)
-            a_l, a_r = add(part["far_r", d], a_l), add(part["far_l", d], a_r)
-            after = [a_l, a_r]
-            a_l, a_r = left(a_l), right(a_r)
-        a_l, a_r = gate(a_l, a_r)
-        own = part["own", 0]
-        total_a = own[:cut] + a_l.astype(F32) + b_r.astype(F32)
-        total_b = own[cut:] + a_r.astype(F32) + b_l.astype(F32)
+        a_l, a_r = gate(a_l, a_r, after=[b_l])
+        total_a = part["own", "a"] + a_l.astype(F32) + b_r.astype(F32)
+        total_b = part["own", "b"] + a_r.astype(F32) + b_l.astype(F32)
         return jnp.concatenate([total_a, total_b], axis=0).astype(BF16)
 
     return shards

time: 108 us -> 105 us (0.972)
  waiting for transfers between devices: 22.2 us -> 19.9 us
    ppermute x14, waiting for transfers between devices: 17.1 us -> 14.6 us  [left(): return lax.ppermute(x, 'gy', to_left)]
  transfers between devices with their start and end apart: 34 -> 34, of which waited for: 14 -> 14; matrix products, arithmetic and copies ran while one was open for 0% -> 0% of each run, Pallas kernels for 47% -> 48%
where the time goes in v9:
time: 105 us
  Pallas kernels  50.5 us (48%)
  starting transfers between devices  31.2 us (30%)
  waiting for transfers between devices  19.9 us (19%)
  local copies, waits for them, and re-layouts  1.86 us (2%)
  other arithmetic  1.5 us (1%)
    pallas_call x4, Pallas kernels, gate_up(): pl.pallas_call(body, name='gate_up', in_specs=[VMEM] * (count + len(weigh...  23.5 us
    ppermute x14, starting transfers between devices, right(): return lax.ppermute(x, 'gy', to_right)  18.8 us
    ppermute x14, waiting for transfers between devices, left(): return lax.ppermute(x, 'gy', to_left)  14.6 us
    pallas_call x3, Pallas kernels, down(): pl.pallas_call(body, name='down', in_specs=[SMEM] + [VMEM] * (2 * count +...  13.3 us
    pallas_call x3, Pallas kernels, bring(): pl.pallas_call(body, name='bring', in_specs=[SMEM] + [ANY] * (count + len...  12.9 us
    ppermute x14, starting transfers between devices, left(): return lax.ppermute(x, 'gy', to_left)  11 us
    ppermute x14, waiting for transfers between devices, right(): return lax.ppermute(x, 'gy', to_right)  4.58 us
  transfers between devices with their start and end apart: 34, of which 14 were waited for; matrix products, arithmetic and copies ran while one was open for 0% of the time, Pallas kernels for 48%

profile of v9, /device:TPU:0, one launch (start us, length us, event | category | flops | bytes accessed | tf_op | source)
XLA Modules:
  0.0 105.2 jit_solution(9768385688705581010)
XLA Ops:
  0.0 1.9 %fusion.14 = (bf16[32,4096]{1,0:T(8,128)(2,1)}, bf16[32,4096]{1,0:T(8,128)(2,1)}) fusion(bf16[64,4096]{1,0:T(8,128)(2,1)} %param.4), kind=kLoop, calls=%fused_computation.27 | loop fusion | bytes 1048576 | tf_op jit(solution)/shard_map/slice | solution.py:235
  1.9 3.0 %collective-permute-start = (bf16[32,4096]{1,0:T(8,128)(2,1)}, bf16[32,4096]{1,0:T(8,128)(2,1)}, u32[]{:S(2)}, u32[]{:S(2)}) collective-permute-start(bf16[32,4096]{1,0:T(8,128)(2,1)} %get-tuple-element.106.refs_0_), channel_id=1, source_target_pairs={{0,2},{2,4},{4,6},{6,7},{7,5},{5,3},{3,1},{1,0},{8,10},{10,12},{12... | collective-permute-start | bytes 786440 | tf_op jit(solution)/shard_map/farR1/ppermute | solution.py:216
  4.9 2.0 %collective-permute-start.2 = (bf16[32,4096]{1,0:T(8,128)(2,1)}, bf16[32,4096]{1,0:T(8,128)(2,1)}, u32[]{:S(2)}, u32[]{:S(2)}) collective-permute-start(bf16[32,4096]{1,0:T(8,128)(2,1)} %get-tuple-element.105.refs_1_), channel_id=1, source_target_pairs={{0,2},{2,4},{4,6},{6,7},{7,5},{5,3},{3,1},{1,0},{8,10},{10,12},{12... | collective-permute-start | bytes 786440 | tf_op jit(solution)/shard_map/nearR1/ppermute | solution.py:216
  6.9 3.5 %bring.3.refs_1_.refs_6_.refs_4_ = bf16[4096,1024]{1,0:T(8,128)(2,1)S(1)} custom-call(s32[1]{0:T(128)} %bitcast.1.part_ref, bf16[4096,2048]{1,0:T(8,128)(2,1)} %refs_0_.5), custom_call_target="tpu_custom_call" | custom-call | flops 1100000000 | tf_op jit(solution)/shard_map/bring/pallas_call | solution.py:76
  10.4 3.5 %bring.4.refs_2_.refs_7_.refs_5_ = bf16[4096,1024]{1,0:T(8,128)(2,1)S(1)} custom-call(s32[1]{0:T(128)} %bitcast.1.part_ref, bf16[4096,2048]{1,0:T(8,128)(2,1)} %refs_1_.1, bf16[4096,1024]{1,0:T(8,128)(2,1)S(1)} %bring.3.refs_1_.refs_6_.refs_4_), custom_call_target="tpu_custom_call" | custom-call | flops 1100000000 | tf_op jit(solution)/shard_map/bring/pallas_call | solution.py:76
  13.9 0.5 collective-permute-done.1.refs_1_
  14.4 1.6 %collective-permute-start.4 = (bf16[32,4096]{1,0:T(8,128)(2,1)}, bf16[32,4096]{1,0:T(8,128)(2,1)S(1)}, u32[]{:S(2)}, u32[]{:S(2)}) collective-permute-start(bf16[32,4096]{1,0:T(8,128)(2,1)} %get-tuple-element.49.refs_2_), channel_id=1, source_target_pairs={{0,2},{2,4},{4,6},{6,7},{7,5},{5,3},{3,1},{1,0},{8,10},{10,12},{12... | collective-permute-start | bytes 786440 | tf_op jit(solution)/shard_map/farR2/ppermute | solution.py:216
  16.0 0.4 collective-permute-start.5
  16.5 5.9 %bring.5 = (bf16[4096,1024]{1,0:T(8,128)(2,1)S(1)}, bf16[4096,1024]{1,0:T(8,128)(2,1)S(1)}) custom-call(s32[1]{0:T(128)} %bitcast.part_ref, bf16[4096,2048]{1,0:T(8,128)(2,1)} %refs_0_.5, bf16[4096,2048]{1,0:T(8,128)(2,1)} %refs_1_.1, bf16[32,4096]{1,0:T(8,128)(2,1)} %get-tuple-element.49.refs_2_), custom_call_target="tpu_custom_call" | custom-call | flops 1100000000 | tf_op jit(solution)/shard_map/bring/pallas_call | solution.py:76
  22.4 1.6 %collective-permute-start.8 = (bf16[32,4096]{1,0:T(8,128)(2,1)}, bf16[32,4096]{1,0:T(8,128)(2,1)S(1)}, u32[]{:S(2)}, u32[]{:S(2)}) collective-permute-start(bf16[32,4096]{1,0:T(8,128)(2,1)} %get-tuple-element.52.refs_2_.refs_4_), channel_id=1, source_target_pairs={{0,2},{2,4},{4,6},{6,7},{7,5},{5,3},{3,1},{1,0},{8,10},{10,12},{12... | collective-permute-start | bytes 786440 | tf_op jit(solution)/shard_map/nearR2/ppermute | solution.py:216
  24.1 0.4 collective-permute-start.9
  24.5 1.6 %collective-permute-start.6 = (bf16[32,4096]{1,0:T(8,128)(2,1)S(1)}, bf16[32,4096]{1,0:T(8,128)(2,1)S(1)}, u32[]{:S(2)}, u32[]{:S(2)}) collective-permute-start(bf16[32,4096]{1,0:T(8,128)(2,1)S(1)} %get-tuple-element.55.refs_10_.refs_0_), channel_id=1, source_target_pairs={{0,2},{2,4},{4,6},{6,7},{7,5},{5,3},{3,1},{1,0},{8,10},{10,12},{12... | collective-permute-start | bytes 786440 | tf_op jit(solution)/shard_map/farR3/ppermute | solution.py:216
  26.6 8.9 %gate_up.4 = (f32[2,192,1024]{2,1,0:T(8,128)S(1)}, f32[2,192,1024]{2,1,0:T(8,128)S(1)}) custom-call(bf16[32,4096]{1,0:T(8,128)(2,1)} %get-tuple-element.106.refs_0_, bf16[32,4096]{1,0:T(8,128)(2,1)} %get-tuple-element.105.refs_1_, bf16[32,4096]{1,0:T(8,128)(2,1)} %get-tuple-element.49.refs_2_, bf16[32,4096]{1,0:T(8,128)(2,1)} %get-tuple-element.50.refs_3_, ...), custom_call_target="tpu_custom_call" | custom-call | flops 1100000000 | tf_op jit(solution)/shard_map/gate_up/pallas_call | solution.py:129
  35.5 1.7 %collective-permute-start.12 = (bf16[32,4096]{1,0:T(8,128)(2,1)S(1)}, bf16[32,4096]{1,0:T(8,128)(2,1)S(1)}, u32[]{:S(2)}, u32[]{:S(2)}) collective-permute-start(bf16[32,4096]{1,0:T(8,128)(2,1)S(1)} %get-tuple-element.59.refs_2_), channel_id=1, source_target_pairs={{0,2},{2,4},{4,6},{6,7},{7,5},{5,3},{3,1},{1,0},{8,10},{10,12},{12... | collective-permute-start | bytes 786440 | tf_op jit(solution)/shard_map/nearR3/ppermute | solution.py:216
  37.6 1.6 %collective-permute-start.10 = (bf16[32,4096]{1,0:T(8,128)(2,1)S(1)}, bf16[32,4096]{1,0:T(8,128)(2,1)S(1)}, u32[]{:S(2)}, u32[]{:S(2)}) collective-permute-start(bf16[32,4096]{1,0:T(8,128)(2,1)S(1)} %get-tuple-element.60.refs_4_.refs_10_), channel_id=1, source_target_pairs={{0,2},{2,4},{4,6},{6,7},{7,5},{5,3},{3,1},{1,0},{8,10},{10,12},{12... | collective-permute-start | bytes 786440 | tf_op jit(solution)/shard_map/farR4/ppermute | solution.py:216
  39.6 7.6 %gate_up.5 = (f32[2,192,1024]{2,1,0:T(8,128)S(1)}, f32[2,192,1024]{2,1,0:T(8,128)S(1)}) custom-call(bf16[32,4096]{1,0:T(8,128)(2,1)S(1)} %get-tuple-element.55.refs_10_.refs_0_, bf16[32,4096]{1,0:T(8,128)(2,1)S(1)} %get-tuple-element.57.refs_1_, bf16[32,4096]{1,0:T(8,128)(2,1)S(1)} %get-tuple-element.59.refs_2_, ...), custom_call_target="tpu_custom_call" | custom-call | flops 1100000000 | tf_op jit(solution)/shard_map/gate_up/pallas_call | solution.py:129
  47.3 1.2 %collective-permute-done.11.refs_1_ = bf16[32,4096]{1,0:T(8,128)(2,1)S(1)} collective-permute-done((bf16[32,4096]{1,0:T(8,128)(2,1)S(1)}, bf16[32,4096]{1,0:T(8,128)(2,1)S(1)}, u32[]{:S(2)}, u32[]{:S(2)}) %collective-permute-start.11) | collective-permute-done | bytes 262176 | tf_op jit(solution)/shard_map/farL4/ppermute | solution.py:220
  48.5 3.5 %gate_up.6 = (f32[2,128,1024]{2,1,0:T(8,128)S(1)}, bf16[2048,2048]{1,0:T(8,128)(2,1)S(1)}) custom-call(bf16[32,4096]{1,0:T(8,128)(2,1)S(1)} %get-tuple-element.64.refs_4_.refs_0_, bf16[32,4096]{1,0:T(8,128)(2,1)S(1)} %get-tuple-element.66.refs_1_, bf16[32,4096]{1,0:T(8,128)(2,1)S(1)} %get-tuple-element.67.refs_2_, ...), custom_call_target="tpu_custom_call" | custom-call | flops 1100000000 | tf_op jit(solution)/shard_map/gate_up/pallas_call | solution.py:129
  52.0 0.6 collective-permute-start.18
  52.6 3.5 %gate_up.7 = (f32[2,128,1024]{2,1,0:T(8,128)S(1)}, bf16[2048,2048]{1,0:T(8,128)(2,1)S(1)}) custom-call(bf16[32,4096]{1,0:T(8,128)(2,1)S(1)} %get-tuple-element.64.refs_4_.refs_0_, bf16[32,4096]{1,0:T(8,128)(2,1)S(1)} %get-tuple-element.66.refs_1_, bf16[32,4096]{1,0:T(8,128)(2,1)S(1)} %get-tuple-element.67.refs_2_, ...), custom_call_target="tpu_custom_call" | custom-call | flops 1100000000 | tf_op jit(solution)/shard_map/gate_up/pallas_call | solution.py:129
  56.4 0.5 collective-permute-start.19
  57.3 0.7 collective-permute-done.19.refs_1_
  58.0 3.7 %down.4 = (bf16[32,4096]{1,0:T(8,128)(2,1)S(1)}, bf16[32,4096]{1,0:T(8,128)(2,1)S(1)}, bf16[32,4096]{1,0:T(8,128)(2,1)S(1)}, bf16[32,4096]{1,0:T(8,128)(2,1)S(1)}) custom-call(s32[1]{0:T(128)} %bitcast.part_ref, bf16[128,1024]{1,0:T(8,128)(2,1)S(1)} %gated.5.refs_0_, bf16[128,1024]{1,0:T(8,128)(2,1)S(1)} %collective-permute-done.19.refs_1_, ...), custom_call_target="tpu_custom_call" | custom-call | tf_op jit(solution)/shard_map/down/pallas_call | solution.py:194
  61.7 0.5 collective-permute-start.22
  62.2 1.6 %collective-permute-start.23 = (bf16[32,4096]{1,0:T(8,128)(2,1)S(1)}, bf16[32,4096]{1,0:T(8,128)(2,1)S(1)}, u32[]{:S(2)}, u32[]{:S(2)}) collective-permute-start(bf16[32,4096]{1,0:T(8,128)(2,1)S(1)} %get-tuple-element.78), channel_id=1, source_target_pairs={{0,2},{2,4},{4,6},{6,7},{7,5},{5,3},{3,1},{1,0},{8,10},{10,12},{12... | collective-permute-start | bytes 786440 | tf_op jit(solution)/shard_map/right/ppermute | solution.py:216
  64.3 1.6 %collective-permute-start.21 = (bf16[32,4096]{1,0:T(8,128)(2,1)S(1)}, bf16[32,4096]{1,0:T(8,128)(2,1)S(1)}, u32[]{:S(2)}, u32[]{:S(2)}) collective-permute-start(bf16[32,4096]{1,0:T(8,128)(2,1)S(1)} %get-tuple-element.76), channel_id=1, source_target_pairs={{0,2},{2,4},{4,6},{6,7},{7,5},{5,3},{3,1},{1,0},{8,10},{10,12},{12... | collective-permute-start | bytes 786440 | tf_op jit(solution)/shard_map/right/ppermute | solution.py:216
  66.3 4.8 %down.3.refs_2_ = f32[192,4096]{1,0:T(8,128)S(1)} custom-call(s32[1]{0:T(128)} %bitcast.part_ref, bf16[192,1024]{1,0:T(8,128)(2,1)S(1)} %gated.4.refs_0_, bf16[192,1024]{1,0:T(8,128)(2,1)S(1)} %collective-permute-done.17.refs_1_, bf16[2048,2048]{1,0:T(8,128)(2,1)S(1)} %get-tuple-element.69.refs_2_, bf16[2048,2048]{1,0:T(8,128)(2,1)S(1)} %get-tuple-element.71.refs_3_), custom_call_target="tpu_custom_call" | custom-call | tf_op jit(solution)/shard_map/down/pallas_call | solution.py:194
  71.5 1.6 %collective-permute-start.24 = (bf16[32,4096]{1,0:T(8,128)(2,1)S(1)}, bf16[32,4096]{1,0:T(8,128)(2,1)S(1)}, u32[]{:S(2)}, u32[]{:S(2)}) collective-permute-start(bf16[32,4096]{1,0:T(8,128)(2,1)S(1)} %get-tuple-element.104.refs_2_), channel_id=1, source_target_pairs={{2,0},{4,2},{6,4},{7,6},{5,7},{3,5},{1,3},{0,1},{10,8},{12,10},{14... | collective-permute-start | bytes 786440 | tf_op jit(solution)/shard_map/left/ppermute | solution.py:220
  73.1 0.5 collective-permute-start.25
  73.6 3.0 %collective-permute-done.20.refs_0_ = bf16[32,4096]{1,0:T(8,128)(2,1)S(1)} collective-permute-done((bf16[32,4096]{1,0:T(8,128)(2,1)S(1)}, bf16[32,4096]{1,0:T(8,128)(2,1)S(1)}, u32[]{:S(2)}, u32[]{:S(2)}) %collective-permute-start.20) | collective-permute-done | bytes 262176 | tf_op jit(solution)/shard_map/left/ppermute | solution.py:220
  76.6 0.5 collective-permute-done.21.refs_1_
  77.1 1.6 %collective-permute-start.28 = (bf16[32,4096]{1,0:T(8,128)(2,1)S(1)}, bf16[32,4096]{1,0:T(8,128)(2,1)S(1)}, u32[]{:S(2)}, u32[]{:S(2)}) collective-permute-start(bf16[32,4096]{1,0:T(8,128)(2,1)S(1)} %get-tuple-element.102.refs_4_), channel_id=1, source_target_pairs={{2,0},{4,2},{6,4},{7,6},{5,7},{3,5},{1,3},{0,1},{10,8},{12,10},{14... | collective-permute-start | bytes 786440 | tf_op jit(solution)/shard_map/left/ppermute | solution.py:220
  78.7 0.5 collective-permute-start.29
  79.2 4.8 %down.5.refs_2_ = f32[192,4096]{1,0:T(8,128)S(1)} custom-call(s32[1]{0:T(128)} %bitcast.part_ref, bf16[192,1024]{1,0:T(8,128)(2,1)S(1)} %gated.3.refs_0_, bf16[192,1024]{1,0:T(8,128)(2,1)S(1)} %collective-permute-done.15.refs_1_, bf16[2048,2048]{1,0:T(8,128)(2,1)S(1)} %get-tuple-element.69.refs_2_, bf16[2048,2048]{1,0:T(8,128)(2,1)S(1)} %get-tuple-element.71.refs_3_, ...), custom_call_target="tpu_custom_call" | custom-call | tf_op jit(solution)/shard_map/down/pallas_call | solution.py:194
  84.2 1.6 %collective-permute-start.26 = (bf16[32,4096]{1,0:T(8,128)(2,1)S(1)}, bf16[32,4096]{1,0:T(8,128)(2,1)S(1)}, u32[]{:S(2)}, u32[]{:S(2)}) collective-permute-start(bf16[32,4096]{1,0:T(8,128)(2,1)S(1)} %get-tuple-element.100.refs_2_), channel_id=1, source_target_pairs={{2,0},{4,2},{6,4},{7,6},{5,7},{3,5},{1,3},{0,1},{10,8},{12,10},{14... | collective-permute-start | bytes 786440 | tf_op jit(solution)/shard_map/left/ppermute | solution.py:220
  85.7 0.5 collective-permute-start.27
  86.2 1.5 %collective-permute-done.28.refs_0_ = bf16[32,4096]{1,0:T(8,128)(2,1)S(1)} collective-permute-done((bf16[32,4096]{1,0:T(8,128)(2,1)S(1)}, bf16[32,4096]{1,0:T(8,128)(2,1)S(1)}, u32[]{:S(2)}, u32[]{:S(2)}) %collective-permute-start.28) | collective-permute-done | bytes 262176 | tf_op jit(solution)/shard_map/left/ppermute | solution.py:220
  87.8 0.5 collective-permute-done.29.refs_1_
  88.3 1.6 %collective-permute-start.32 = (bf16[32,4096]{1,0:T(8,128)(2,1)S(1)}, bf16[32,4096]{1,0:T(8,128)(2,1)S(1)}, u32[]{:S(2)}, u32[]{:S(2)}) collective-permute-start(bf16[32,4096]{1,0:T(8,128)(2,1)S(1)} %get-tuple-element.98.refs_2_), channel_id=1, source_target_pairs={{2,0},{4,2},{6,4},{7,6},{5,7},{3,5},{1,3},{0,1},{10,8},{12,10},{14... | collective-permute-start | bytes 786440 | tf_op jit(solution)/shard_map/left/ppermute | solution.py:220
  89.9 0.5 collective-permute-start.33
  90.4 3.0 %collective-permute-done.26.refs_0_ = bf16[32,4096]{1,0:T(8,128)(2,1)S(1)} collective-permute-done((bf16[32,4096]{1,0:T(8,128)(2,1)S(1)}, bf16[32,4096]{1,0:T(8,128)(2,1)S(1)}, u32[]{:S(2)}, u32[]{:S(2)}) %collective-permute-start.26) | collective-permute-done | bytes 262176 | tf_op jit(solution)/shard_map/left/ppermute | solution.py:220
  93.4 1.6 %collective-permute-done.27.refs_1_ = bf16[32,4096]{1,0:T(8,128)(2,1)S(1)} collective-permute-done((bf16[32,4096]{1,0:T(8,128)(2,1)S(1)}, bf16[32,4096]{1,0:T(8,128)(2,1)S(1)}, u32[]{:S(2)}, u32[]{:S(2)}) %collective-permute-start.27) | collective-permute-done | bytes 262176 | tf_op jit(solution)/shard_map/right/ppermute | solution.py:216
  95.1 1.6 %collective-permute-start.30 = (bf16[32,4096]{1,0:T(8,128)(2,1)S(1)}, bf16[32,4096]{1,0:T(8,128)(2,1)S(1)}, u32[]{:S(2)}, u32[]{:S(2)}) collective-permute-start(bf16[32,4096]{1,0:T(8,128)(2,1)S(1)} %get-tuple-element.96.refs_2_), channel_id=1, source_target_pairs={{2,0},{4,2},{6,4},{7,6},{5,7},{3,5},{1,3},{0,1},{10,8},{12,10},{14... | collective-permute-start | bytes 786440 | tf_op jit(solution)/shard_map/left/ppermute | solution.py:220
  96.7 0.5 collective-permute-start.31
  97.2 1.9 %collective-permute-done.32.refs_0_ = bf16[32,4096]{1,0:T(8,128)(2,1)S(1)} collective-permute-done((bf16[32,4096]{1,0:T(8,128)(2,1)S(1)}, bf16[32,4096]{1,0:T(8,128)(2,1)S(1)}, u32[]{:S(2)}, u32[]{:S(2)}) %collective-permute-start.32) | collective-permute-done | bytes 262176 | tf_op jit(solution)/shard_map/left/ppermute | solution.py:220
  99.0 1.6 %collective-permute-done.33.refs_1_ = bf16[32,4096]{1,0:T(8,128)(2,1)S(1)} collective-permute-done((bf16[32,4096]{1,0:T(8,128)(2,1)S(1)}, bf16[32,4096]{1,0:T(8,128)(2,1)S(1)}, u32[]{:S(2)}, u32[]{:S(2)}) %collective-permute-start.33) | collective-permute-done | bytes 262176 | tf_op jit(solution)/shard_map/right/ppermute | solution.py:216
  100.6 3.5 %collective-permute-done.30.refs_0_ = bf16[32,4096]{1,0:T(8,128)(2,1)S(1)} collective-permute-done((bf16[32,4096]{1,0:T(8,128)(2,1)S(1)}, bf16[32,4096]{1,0:T(8,128)(2,1)S(1)}, u32[]{:S(2)}, u32[]{:S(2)}) %collective-permute-start.30) | collective-permute-done | bytes 262176 | tf_op jit(solution)/shard_map/left/ppermute | solution.py:220
  104.4 0.8 pad_maximum_fusion
  (55 shorter events, 4.1 us)
Async XLA Ops:
  1.9 12.0 %collective-permute-start = (bf16[32,4096]{1,0:T(8,128)(2,1)}, bf16[32,4096]{1,0:T(8,128)(2,1)}, u32[]{:S(2)}, u32[]{:S(2)}) collective-permute-start(bf16[32,4096]{1,0:T(8,128)(2,1)} %get-tuple-element.106.refs_0_), channel_id=1, source_target_pairs={{0,2},{2,4},{4,6},{6,7},{7,5},{5,3},{3,1},{1,0},{8,10},{10,12},{12... | collective-permute-start | bytes 786440 | tf_op jit(solution)/shard_map/farR1/ppermute | solution.py:216
  4.9 9.5 %collective-permute-start.1 = (bf16[32,4096]{1,0:T(8,128)(2,1)}, bf16[32,4096]{1,0:T(8,128)(2,1)}, u32[]{:S(2)}, u32[]{:S(2)}) collective-permute-start(bf16[32,4096]{1,0:T(8,128)(2,1)} %get-tuple-element.105.refs_1_), channel_id=1, source_target_pairs={{2,0},{4,2},{6,4},{7,6},{5,7},{3,5},{1,3},{0,1},{10,8},{12,10},{14... | collective-permute-start | bytes 786440 | tf_op jit(solution)/shard_map/farL1/ppermute | solution.py:220
  4.9 17.5 %collective-permute-start.2 = (bf16[32,4096]{1,0:T(8,128)(2,1)}, bf16[32,4096]{1,0:T(8,128)(2,1)}, u32[]{:S(2)}, u32[]{:S(2)}) collective-permute-start(bf16[32,4096]{1,0:T(8,128)(2,1)} %get-tuple-element.105.refs_1_), channel_id=1, source_target_pairs={{0,2},{2,4},{4,6},{6,7},{7,5},{5,3},{3,1},{1,0},{8,10},{10,12},{12... | collective-permute-start | bytes 786440 | tf_op jit(solution)/shard_map/nearR1/ppermute | solution.py:216
  6.9 15.5 %collective-permute-start.3 = (bf16[32,4096]{1,0:T(8,128)(2,1)}, bf16[32,4096]{1,0:T(8,128)(2,1)}, u32[]{:S(2)}, u32[]{:S(2)}) collective-permute-start(bf16[32,4096]{1,0:T(8,128)(2,1)} %get-tuple-element.106.refs_0_), channel_id=1, source_target_pairs={{2,0},{4,2},{6,4},{7,6},{5,7},{3,5},{1,3},{0,1},{10,8},{12,10},{14... | collective-permute-start | bytes 786440 | tf_op jit(solution)/shard_map/nearL1/ppermute | solution.py:220
  14.4 10.1 %collective-permute-start.4 = (bf16[32,4096]{1,0:T(8,128)(2,1)}, bf16[32,4096]{1,0:T(8,128)(2,1)S(1)}, u32[]{:S(2)}, u32[]{:S(2)}) collective-permute-start(bf16[32,4096]{1,0:T(8,128)(2,1)} %get-tuple-element.49.refs_2_), channel_id=1, source_target_pairs={{0,2},{2,4},{4,6},{6,7},{7,5},{5,3},{3,1},{1,0},{8,10},{10,12},{12... | collective-permute-start | bytes 786440 | tf_op jit(solution)/shard_map/farR2/ppermute | solution.py:216
  16.0 8.5 %collective-permute-start.5 = (bf16[32,4096]{1,0:T(8,128)(2,1)}, bf16[32,4096]{1,0:T(8,128)(2,1)S(1)}, u32[]{:S(2)}, u32[]{:S(2)}) collective-permute-start(bf16[32,4096]{1,0:T(8,128)(2,1)} %get-tuple-element.50.refs_3_), channel_id=1, source_target_pairs={{2,0},{4,2},{6,4},{7,6},{5,7},{3,5},{1,3},{0,1},{10,8},{12,10},{14... | collective-permute-start | bytes 786440 | tf_op jit(solution)/shard_map/farL2/ppermute | solution.py:220
  22.4 13.1 %collective-permute-start.8 = (bf16[32,4096]{1,0:T(8,128)(2,1)}, bf16[32,4096]{1,0:T(8,128)(2,1)S(1)}, u32[]{:S(2)}, u32[]{:S(2)}) collective-permute-start(bf16[32,4096]{1,0:T(8,128)(2,1)} %get-tuple-element.52.refs_2_.refs_4_), channel_id=1, source_target_pairs={{0,2},{2,4},{4,6},{6,7},{7,5},{5,3},{3,1},{1,0},{8,10},{10,12},{12... | collective-permute-start | bytes 786440 | tf_op jit(solution)/shard_map/nearR2/ppermute | solution.py:216
  24.1 11.4 %collective-permute-start.9 = (bf16[32,4096]{1,0:T(8,128)(2,1)}, bf16[32,4096]{1,0:T(8,128)(2,1)S(1)}, u32[]{:S(2)}, u32[]{:S(2)}) collective-permute-start(bf16[32,4096]{1,0:T(8,128)(2,1)} %get-tuple-element.53.refs_5_), channel_id=1, source_target_pairs={{2,0},{4,2},{6,4},{7,6},{5,7},{3,5},{1,3},{0,1},{10,8},{12,10},{14... | collective-permute-start | bytes 786440 | tf_op jit(solution)/shard_map/nearL2/ppermute | solution.py:220
  24.5 13.1 %collective-permute-start.6 = (bf16[32,4096]{1,0:T(8,128)(2,1)S(1)}, bf16[32,4096]{1,0:T(8,128)(2,1)S(1)}, u32[]{:S(2)}, u32[]{:S(2)}) collective-permute-start(bf16[32,4096]{1,0:T(8,128)(2,1)S(1)} %get-tuple-element.55.refs_10_.refs_0_), channel_id=1, source_target_pairs={{0,2},{2,4},{4,6},{6,7},{7,5},{5,3},{3,1},{1,0},{8,10},{10,12},{12... | collective-permute-start | bytes 786440 | tf_op jit(solution)/shard_map/farR3/ppermute | solution.py:216
  26.1 11.5 %collective-permute-start.7 = (bf16[32,4096]{1,0:T(8,128)(2,1)S(1)}, bf16[32,4096]{1,0:T(8,128)(2,1)S(1)}, u32[]{:S(2)}, u32[]{:S(2)}) collective-permute-start(bf16[32,4096]{1,0:T(8,128)(2,1)S(1)} %get-tuple-element.57.refs_1_), channel_id=1, source_target_pairs={{2,0},{4,2},{6,4},{7,6},{5,7},{3,5},{1,3},{0,1},{10,8},{12,10},{14... | collective-permute-start | bytes 786440 | tf_op jit(solution)/shard_map/farL3/ppermute | solution.py:220
  35.5 11.7 %collective-permute-start.12 = (bf16[32,4096]{1,0:T(8,128)(2,1)S(1)}, bf16[32,4096]{1,0:T(8,128)(2,1)S(1)}, u32[]{:S(2)}, u32[]{:S(2)}) collective-permute-start(bf16[32,4096]{1,0:T(8,128)(2,1)S(1)} %get-tuple-element.59.refs_2_), channel_id=1, source_target_pairs={{0,2},{2,4},{4,6},{6,7},{7,5},{5,3},{3,1},{1,0},{8,10},{10,12},{12... | collective-permute-start | bytes 786440 | tf_op jit(solution)/shard_map/nearR3/ppermute | solution.py:216
  37.2 10.1 %collective-permute-start.13 = (bf16[32,4096]{1,0:T(8,128)(2,1)S(1)}, bf16[32,4096]{1,0:T(8,128)(2,1)S(1)}, u32[]{:S(2)}, u32[]{:S(2)}) collective-permute-start(bf16[32,4096]{1,0:T(8,128)(2,1)S(1)} %get-tuple-element.62.refs_3_), channel_id=1, source_target_pairs={{2,0},{4,2},{6,4},{7,6},{5,7},{3,5},{1,3},{0,1},{10,8},{12,10},{14... | collective-permute-start | bytes 786440 | tf_op jit(solution)/shard_map/nearL3/ppermute | solution.py:220
  37.6 9.7 %collective-permute-start.10 = (bf16[32,4096]{1,0:T(8,128)(2,1)S(1)}, bf16[32,4096]{1,0:T(8,128)(2,1)S(1)}, u32[]{:S(2)}, u32[]{:S(2)}) collective-permute-start(bf16[32,4096]{1,0:T(8,128)(2,1)S(1)} %get-tuple-element.60.refs_4_.refs_10_), channel_id=1, source_target_pairs={{0,2},{2,4},{4,6},{6,7},{7,5},{5,3},{3,1},{1,0},{8,10},{10,12},{12... | collective-permute-start | bytes 786440 | tf_op jit(solution)/shard_map/farR4/ppermute | solution.py:216
  39.2 9.3 %collective-permute-start.11 = (bf16[32,4096]{1,0:T(8,128)(2,1)S(1)}, bf16[32,4096]{1,0:T(8,128)(2,1)S(1)}, u32[]{:S(2)}, u32[]{:S(2)}) collective-permute-start(bf16[32,4096]{1,0:T(8,128)(2,1)S(1)} %get-tuple-element.61.refs_5_), channel_id=1, source_target_pairs={{2,0},{4,2},{6,4},{7,6},{5,7},{3,5},{1,3},{0,1},{10,8},{12,10},{14... | collective-permute-start | bytes 786440 | tf_op jit(solution)/shard_map/farL4/ppermute | solution.py:220
  48.5 8.4 %collective-permute-start.16 = (f32[2,192,1024]{2,1,0:T(8,128)S(1)}, f32[2,192,1024]{2,1,0:T(8,128)S(1)}, u32[]{:S(2)}, u32[]{:S(2)}) collective-permute-start(f32[2,192,1024]{2,1,0:T(8,128)S(1)} %get-tuple-element.73), channel_id=1, source_target_pairs={{0,8},{8,0},{1,9},{9,1},{2,10},{10,2},{3,11},{11,3},{4,12},{12,4},... | collective-permute-start | bytes 4718600 | tf_op jit(solution)/shard_map/swap/ppermute | solution.py:224
  52.0 4.1 %collective-permute-start.18 = (f32[2,128,1024]{2,1,0:T(8,128)S(1)}, f32[2,128,1024]{2,1,0:T(8,128)S(1)}, u32[]{:S(2)}, u32[]{:S(2)}) collective-permute-start(f32[2,128,1024]{2,1,0:T(8,128)S(1)} %get-tuple-element.70.refs_7_), channel_id=1, source_target_pairs={{0,8},{8,0},{1,9},{9,1},{2,10},{10,2},{3,11},{11,3},{4,12},{12,4},... | collective-permute-start | bytes 3145736 | tf_op jit(solution)/shard_map/swap/ppermute | solution.py:224
  52.5 11.7 %collective-permute-start.14 = (f32[2,192,1024]{2,1,0:T(8,128)S(1)}, f32[2,192,1024]{2,1,0:T(8,128)S(1)}, u32[]{:S(2)}, u32[]{:S(2)}) collective-permute-start(f32[2,192,1024]{2,1,0:T(8,128)S(1)} %get-tuple-element.65), channel_id=1, source_target_pairs={{0,8},{8,0},{1,9},{9,1},{2,10},{10,2},{3,11},{11,3},{4,12},{12,4},... | collective-permute-start | bytes 4718600 | tf_op jit(solution)/shard_map/swap/ppermute | solution.py:224
  56.4 1.7 %collective-permute-start.19 = (bf16[128,1024]{1,0:T(8,128)(2,1)S(1)}, bf16[128,1024]{1,0:T(8,128)(2,1)S(1)}, u32[]{:S(2)}, u32[]{:S(2)}) collective-permute-start(bf16[128,1024]{1,0:T(8,128)(2,1)S(1)} %gated.5.refs_0_), channel_id=1, source_target_pairs={{0,8},{8,0},{1,9},{9,1},{2,10},{10,2},{3,11},{11,3},{4,12},{12,4},... | collective-permute-start | bytes 786440 | tf_op jit(solution)/shard_map/swap/ppermute | solution.py:224
  57.2 9.0 %collective-permute-start.17 = (bf16[192,1024]{1,0:T(8,128)(2,1)S(1)}, bf16[192,1024]{1,0:T(8,128)(2,1)S(1)}, u32[]{:S(2)}, u32[]{:S(2)}) collective-permute-start(bf16[192,1024]{1,0:T(8,128)(2,1)S(1)} %gated.4.refs_0_), channel_id=1, source_target_pairs={{0,8},{8,0},{1,9},{9,1},{2,10},{10,2},{3,11},{11,3},{4,12},{12,4},... | collective-permute-start | bytes 1179656 | tf_op jit(solution)/shard_map/swap/ppermute | solution.py:224
  61.7 9.3 %collective-permute-start.22 = (bf16[32,4096]{1,0:T(8,128)(2,1)S(1)}, bf16[32,4096]{1,0:T(8,128)(2,1)S(1)}, u32[]{:S(2)}, u32[]{:S(2)}) collective-permute-start(bf16[32,4096]{1,0:T(8,128)(2,1)S(1)} %get-tuple-element.77), channel_id=1, source_target_pairs={{2,0},{4,2},{6,4},{7,6},{5,7},{3,5},{1,3},{0,1},{10,8},{12,10},{14... | collective-permute-start | bytes 786440 | tf_op jit(solution)/shard_map/left/ppermute | solution.py:220
  62.2 9.2 %collective-permute-start.23 = (bf16[32,4096]{1,0:T(8,128)(2,1)S(1)}, bf16[32,4096]{1,0:T(8,128)(2,1)S(1)}, u32[]{:S(2)}, u32[]{:S(2)}) collective-permute-start(bf16[32,4096]{1,0:T(8,128)(2,1)S(1)} %get-tuple-element.78), channel_id=1, source_target_pairs={{0,2},{2,4},{4,6},{6,7},{7,5},{5,3},{3,1},{1,0},{8,10},{10,12},{12... | collective-permute-start | bytes 786440 | tf_op jit(solution)/shard_map/right/ppermute | solution.py:216
  63.8 12.7 %collective-permute-start.20 = (bf16[32,4096]{1,0:T(8,128)(2,1)S(1)}, bf16[32,4096]{1,0:T(8,128)(2,1)S(1)}, u32[]{:S(2)}, u32[]{:S(2)}) collective-permute-start(bf16[32,4096]{1,0:T(8,128)(2,1)S(1)} %get-tuple-element.75), channel_id=1, source_target_pairs={{2,0},{4,2},{6,4},{7,6},{5,7},{3,5},{1,3},{0,1},{10,8},{12,10},{14... | collective-permute-start | bytes 786440 | tf_op jit(solution)/shard_map/left/ppermute | solution.py:220
  64.3 12.8 %collective-permute-start.21 = (bf16[32,4096]{1,0:T(8,128)(2,1)S(1)}, bf16[32,4096]{1,0:T(8,128)(2,1)S(1)}, u32[]{:S(2)}, u32[]{:S(2)}) collective-permute-start(bf16[32,4096]{1,0:T(8,128)(2,1)S(1)} %get-tuple-element.76), channel_id=1, source_target_pairs={{0,2},{2,4},{4,6},{6,7},{7,5},{5,3},{3,1},{1,0},{8,10},{10,12},{12... | collective-permute-start | bytes 786440 | tf_op jit(solution)/shard_map/right/ppermute | solution.py:216
  66.2 13.0 %collective-permute-start.15 = (bf16[192,1024]{1,0:T(8,128)(2,1)S(1)}, bf16[192,1024]{1,0:T(8,128)(2,1)S(1)}, u32[]{:S(2)}, u32[]{:S(2)}) collective-permute-start(bf16[192,1024]{1,0:T(8,128)(2,1)S(1)} %gated.3.refs_0_), channel_id=1, source_target_pairs={{0,8},{8,0},{1,9},{9,1},{2,10},{10,2},{3,11},{11,3},{4,12},{12,4},... | collective-permute-start | bytes 1179656 | tf_op jit(solution)/shard_map/swap/ppermute | solution.py:224
  71.5 12.5 %collective-permute-start.24 = (bf16[32,4096]{1,0:T(8,128)(2,1)S(1)}, bf16[32,4096]{1,0:T(8,128)(2,1)S(1)}, u32[]{:S(2)}, u32[]{:S(2)}) collective-permute-start(bf16[32,4096]{1,0:T(8,128)(2,1)S(1)} %get-tuple-element.104.refs_2_), channel_id=1, source_target_pairs={{2,0},{4,2},{6,4},{7,6},{5,7},{3,5},{1,3},{0,1},{10,8},{12,10},{14... | collective-permute-start | bytes 786440 | tf_op jit(solution)/shard_map/left/ppermute | solution.py:220
  73.1 11.0 %collective-permute-start.25 = (bf16[32,4096]{1,0:T(8,128)(2,1)S(1)}, bf16[32,4096]{1,0:T(8,128)(2,1)S(1)}, u32[]{:S(2)}, u32[]{:S(2)}) collective-permute-start(bf16[32,4096]{1,0:T(8,128)(2,1)S(1)} %get-tuple-element.103.refs_3_), channel_id=1, source_target_pairs={{0,2},{2,4},{4,6},{6,7},{7,5},{5,3},{3,1},{1,0},{8,10},{10,12},{12... | collective-permute-start | bytes 786440 | tf_op jit(solution)/shard_map/right/ppermute | solution.py:216
  77.1 10.6 %collective-permute-start.28 = (bf16[32,4096]{1,0:T(8,128)(2,1)S(1)}, bf16[32,4096]{1,0:T(8,128)(2,1)S(1)}, u32[]{:S(2)}, u32[]{:S(2)}) collective-permute-start(bf16[32,4096]{1,0:T(8,128)(2,1)S(1)} %get-tuple-element.102.refs_4_), channel_id=1, source_target_pairs={{2,0},{4,2},{6,4},{7,6},{5,7},{3,5},{1,3},{0,1},{10,8},{12,10},{14... | collective-permute-start | bytes 786440 | tf_op jit(solution)/shard_map/left/ppermute | solution.py:220
  78.7 9.5 %collective-permute-start.29 = (bf16[32,4096]{1,0:T(8,128)(2,1)S(1)}, bf16[32,4096]{1,0:T(8,128)(2,1)S(1)}, u32[]{:S(2)}, u32[]{:S(2)}) collective-permute-start(bf16[32,4096]{1,0:T(8,128)(2,1)S(1)} %get-tuple-element.101.refs_5_), channel_id=1, source_target_pairs={{0,2},{2,4},{4,6},{6,7},{7,5},{5,3},{3,1},{1,0},{8,10},{10,12},{12... | collective-permute-start | bytes 786440 | tf_op jit(solution)/shard_map/right/ppermute | solution.py:216
  84.2 9.2 %collective-permute-start.26 = (bf16[32,4096]{1,0:T(8,128)(2,1)S(1)}, bf16[32,4096]{1,0:T(8,128)(2,1)S(1)}, u32[]{:S(2)}, u32[]{:S(2)}) collective-permute-start(bf16[32,4096]{1,0:T(8,128)(2,1)S(1)} %get-tuple-element.100.refs_2_), channel_id=1, source_target_pairs={{2,0},{4,2},{6,4},{7,6},{5,7},{3,5},{1,3},{0,1},{10,8},{12,10},{14... | collective-permute-start | bytes 786440 | tf_op jit(solution)/shard_map/left/ppermute | solution.py:220
  85.7 9.2 %collective-permute-start.27 = (bf16[32,4096]{1,0:T(8,128)(2,1)S(1)}, bf16[32,4096]{1,0:T(8,128)(2,1)S(1)}, u32[]{:S(2)}, u32[]{:S(2)}) collective-permute-start(bf16[32,4096]{1,0:T(8,128)(2,1)S(1)} %get-tuple-element.99.refs_3_), channel_id=1, source_target_pairs={{0,2},{2,4},{4,6},{6,7},{7,5},{5,3},{3,1},{1,0},{8,10},{10,12},{12... | collective-permute-start | bytes 786440 | tf_op jit(solution)/shard_map/right/ppermute | solution.py:216
  88.3 10.7 %collective-permute-start.32 = (bf16[32,4096]{1,0:T(8,128)(2,1)S(1)}, bf16[32,4096]{1,0:T(8,128)(2,1)S(1)}, u32[]{:S(2)}, u32[]{:S(2)}) collective-permute-start(bf16[32,4096]{1,0:T(8,128)(2,1)S(1)} %get-tuple-element.98.refs_2_), channel_id=1, source_target_pairs={{2,0},{4,2},{6,4},{7,6},{5,7},{3,5},{1,3},{0,1},{10,8},{12,10},{14... | collective-permute-start | bytes 786440 | tf_op jit(solution)/shard_map/left/ppermute | solution.py:220
  89.9 10.7 %collective-permute-start.33 = (bf16[32,4096]{1,0:T(8,128)(2,1)S(1)}, bf16[32,4096]{1,0:T(8,128)(2,1)S(1)}, u32[]{:S(2)}, u32[]{:S(2)}) collective-permute-start(bf16[32,4096]{1,0:T(8,128)(2,1)S(1)} %get-tuple-element.97.refs_3_), channel_id=1, source_target_pairs={{0,2},{2,4},{4,6},{6,7},{7,5},{5,3},{3,1},{1,0},{8,10},{10,12},{12... | collective-permute-start | bytes 786440 | tf_op jit(solution)/shard_map/right/ppermute | solution.py:216
  95.1 9.0 %collective-permute-start.30 = (bf16[32,4096]{1,0:T(8,128)(2,1)S(1)}, bf16[32,4096]{1,0:T(8,128)(2,1)S(1)}, u32[]{:S(2)}, u32[]{:S(2)}) collective-permute-start(bf16[32,4096]{1,0:T(8,128)(2,1)S(1)} %get-tuple-element.96.refs_2_), channel_id=1, source_target_pairs={{2,0},{4,2},{6,4},{7,6},{5,7},{3,5},{1,3},{0,1},{10,8},{12,10},{14... | collective-permute-start | bytes 786440 | tf_op jit(solution)/shard_map/left/ppermute | solution.py:220
  96.7 7.5 %collective-permute-start.31 = (bf16[32,4096]{1,0:T(8,128)(2,1)S(1)}, bf16[32,4096]{1,0:T(8,128)(2,1)S(1)}, u32[]{:S(2)}, u32[]{:S(2)}) collective-permute-start(bf16[32,4096]{1,0:T(8,128)(2,1)S(1)} %get-tuple-element.95.refs_3_), channel_id=1, source_target_pairs={{0,2},{2,4},{4,6},{6,7},{7,5},{5,3},{3,1},{1,0},{8,10},{10,12},{12... | collective-permute-start | bytes 786440 | tf_op jit(solution)/shard_map/right/ppermute | solution.py:216

commit v10 on v9

--- a/solution.py
+++ b/solution.py
@@ -7,7 +7,6 @@
 
 F32, BF16 = jnp.float32, jnp.bfloat16
 ANY = pl.BlockSpec(memory_space=pl.ANY)
-SMEM = pl.BlockSpec(memory_space=pltpu.SMEM)
 VMEM = pl.BlockSpec(memory_space=pltpu.VMEM)
 
 
@@ -60,13 +59,17 @@
     return copies
 
 
-def bring(weights, part, after):
+def half_of(mine, w):
+    core = lax.axis_index("gx")
+    return pl.multiple_of((core if mine else 1 - core) * w, w)
+
+
+def bring(weights, mine, after):
     k, w = weights[0].shape[0], weights[0].shape[1] // 2
     count = len(weights)
 
-    def body(part_ref, *refs):
-        start = pl.multiple_of(part_ref[0] * w, w)
-        sources = [(ref, start) for ref in refs[:count]]
+    def body(*refs):
+        sources = [(ref, half_of(mine, w)) for ref in refs[:count]]
         copies = fetches(sources, refs[-1 - count : -1], refs[-1])
         for copy in copies:
             copy.start()
@@ -76,38 +79,40 @@
     return pl.pallas_call(
         body,
         name="bring",
-        in_specs=[SMEM] + [ANY] * (count + len(after)),
+        in_specs=[ANY] * (count + len(after)),
         out_specs=[VMEM] * count,
         out_shape=[pltpu.VMEM((k, w), weights[0].dtype)] * count,
         scratch_shapes=[pltpu.SemaphoreType.DMA((count, 8))],
         **params(1 << 18, KERNEL),
-    )(part, *map(in_hbm, weights), *after)
-
-
-def gate_up(pieces, weights, after, load=None, side=0):
+    )(*map(in_hbm, weights), *after)
+
+
+def gate_up(pieces, weights, after, load=()):
     if any(p.shape[0] % 16 for p in pieces):
         pieces = [jnp.concatenate(pieces, axis=0)]
     m, k = sum(p.shape[0] for p in pieces), pieces[0].shape[1]
     w = weights[0].shape[1]
-    tile = min(w, 256)
+    tile = min(w, 512)
     count, halves = len(pieces), len(weights) // 2
     shapes = [jax.ShapeDtypeStruct((2, m, w), F32)] * halves
     scratch = [pltpu.VMEM((m, k), BF16)]
-    extra = []
-    if load is not None:
-        wide = load.shape[1] // 2
-        extra = [in_hbm(load)]
-        shapes += [pltpu.VMEM((load.shape[0], wide), load.dtype)]
-        scratch += [pltpu.SemaphoreType.DMA((1, 8))]
+    for x, _ in load:
+        shapes.append(pltpu.VMEM((x.shape[0], x.shape[1] // 2), x.dtype))
+    if load:
+        scratch.append(pltpu.SemaphoreType.DMA((len(load), 8)))
 
     def body(*refs):
         weight_refs = refs[count : count + len(weights)]
         outs = refs[-len(shapes) - len(scratch) : -len(scratch)]
         out_refs, x_ref = outs[:halves], refs[-len(scratch)]
         copies = []
-        if load is not None:
-            source = refs[count + len(weights)]
-            copies = fetches([(source, side * wide)], outs[halves:], refs[-1])
+        if load:
+            sources = refs[count + len(weights) :]
+            starts = [
+                half_of(True, w) if which == "own" else which * (x.shape[1] // 2)
+                for x, which in load
+            ]
+            copies = fetches(list(zip(sources, starts)), outs[halves:], refs[-1])
         for copy in copies:
             copy.start()
         at = 0
@@ -129,12 +134,12 @@
     return pl.pallas_call(
         body,
         name="gate_up",
-        in_specs=[VMEM] * (count + len(weights)) + [ANY] * (len(extra) + len(after)),
+        in_specs=[VMEM] * (count + len(weights)) + [ANY] * (len(load) + len(after)),
         out_specs=[VMEM] * len(shapes),
         out_shape=shapes,
         scratch_shapes=scratch,
         **params(3 << 20, KERNEL),
-    )(*pieces, *map(in_vmem, weights), *extra, *after)
+    )(*pieces, *map(in_vmem, weights), *[in_hbm(x) for x, _ in load], *after)
 
 
 def gated(ours, theirs):
@@ -159,7 +164,7 @@
     )(ours, theirs)
 
 
-def down(halves, weights, part, outs, after):
+def down(halves, weights, outs, after):
     m = sum(h.shape[0] for h, _ in halves)
     w = halves[0][0].shape[1]
     n = weights[0].shape[1]
@@ -168,16 +173,15 @@
         halves = [tuple(jnp.concatenate(hs, axis=0) for hs in zip(*halves))]
     count = len(halves)
 
-    def body(part_ref, *refs):
+    def body(*refs):
         weight_refs, h_ref = refs[2 * count : 2 * count + 2], refs[-1]
         out_refs = refs[-1 - len(outs) : -1]
         at = 0
         for i in range(count):
             rows = slice(at, at + refs[2 * i].shape[0])
             at = rows.stop
-            first = pl.multiple_of(part_ref[0] * w, w)
-            h_ref[rows, pl.ds(first, w)] = refs[2 * i][...]
-            h_ref[rows, pl.ds(pl.multiple_of(w - first, w), w)] = refs[2 * i + 1][...]
+            h_ref[rows, pl.ds(half_of(True, w), w)] = refs[2 * i][...]
+            h_ref[rows, pl.ds(half_of(False, w), w)] = refs[2 * i + 1][...]
 
         for i, d_ref in enumerate(weight_refs):
 
@@ -194,14 +198,14 @@
     return pl.pallas_call(
         body,
         name="down",
-        in_specs=[SMEM] + [VMEM] * (2 * count + 2) + [ANY] * len(after),
+        in_specs=[VMEM] * (2 * count + 2) + [ANY] * len(after),
         out_specs=[VMEM] * len(outs),
         out_shape=[
             jax.ShapeDtypeStruct((size, 2 * n), dtype) for _, size, dtype in outs
         ],
         scratch_shapes=[pltpu.VMEM((m, 2 * w), BF16)],
         **params(3 << 20),
-    )(part, *[h for pair in halves for h in pair], *map(in_vmem, weights), *after)
+    )(*[h for pair in halves for h in pair], *map(in_vmem, weights), *after)
 
 
 def make_shards(n):
@@ -229,15 +233,12 @@
     def shards(tokens, gate_weight, up_weight, down_weight):
         rows = tokens.shape[0]
         cut = rows // 2
-        core = lax.axis_index("gx").astype(jnp.int32)
-        keep, give = core.reshape(1), (1 - core).reshape(1)
 
         a, b = tokens[:cut], tokens[cut:]
         far_r, far_l = right(a, "farR1"), left(b, "farL1")
-        wide = bring([gate_weight], give, [])
+        wide = bring([gate_weight], False, [])
         near_r, near_l = right(b, "nearR1"), left(a, "nearL1")
-        wide += bring([up_weight], give, wide)
-        waiting = {("own", "a"): a, ("own", "b"): b}
+        wide += bring([up_weight], False, wide)
         groups, theirs, ours = [], [], []
         after = wide[-1:]
         for d in range(1, half):
@@ -245,30 +246,33 @@
             held = {("far_r", d): far_r, ("far_l", d): far_l}
             after = [far_r]
             far_r, far_l = right(far_r, f"farR{d + 1}"), left(far_l, f"farL{d + 1}")
-            if d > 2:
+            if d == 1:
+                waiting = {("own", "a"): a, ("own", "b"): b} | held
+                done = after
+            elif d == 2:
+                ours += gate_up(rows_now, wide[2:], after)
+                waiting, done = held, ours[-1:]
+            else:
                 waiting |= held
-            if d == 1:
-                wide += bring([gate_weight, up_weight], keep, after)
-                done = wide[-1:]
-            else:
                 groups.append(list(waiting))
-                rows_now, waiting = list(waiting.values()), {}
-                both = True
-                out = gate_up(rows_now, wide if both else wide[:2], after)
+                out = gate_up(list(waiting.values()), wide, after)
                 theirs.append(out[0])
-                ours += out[1:]
-                done = out[:1]
-            if d <= 2:
-                waiting |= held
+                ours.append(out[1])
+                waiting, done = {}, out[:1]
             near_r, near_l = gate(near_r, near_l, after=done, work=GATE)
             waiting |= {("near_r", d): near_r, ("near_l", d): near_l}
             after = [near_r]
             if d < half - 1:
                 near_r = right(near_r, f"nearR{d + 1}")
                 near_l = left(near_l, f"nearL{d + 1}")
-                if d > 1 and not both:
-                    ours += gate_up(rows_now, wide[2:], after)
-                    after = ours[-1:]
+            if d == 1:
+                groups.append(list(waiting))
+                rows_now = list(waiting.values())
+                load = [(gate_weight, "own"), (up_weight, "own")]
+                out = gate_up(rows_now, wide, after, load)
+                theirs.append(out[0])
+                wide += out[1:]
+                after = out[:1]
         far_r, far_l, *theirs = gate(far_r, far_l, *theirs, after=after)
         waiting |= {("far_r", half): far_r, ("far_l", half): far_l}
 
@@ -277,20 +281,20 @@
             return h, other(h)
 
         last = list(waiting.values())
-        last_theirs, low = gate_up(last, wide[:2], [], down_weight, 0)
+        last_theirs, low = gate_up(last, wide[:2], [], [(down_weight, 0)])
         last_got = other(last_theirs)
         got = [other(x) for x in theirs]
-        last_ours, high = gate_up(last, wide[2:], [last_theirs], down_weight, 1)
+        last_ours, high = gate_up(last, wide[2:], [last_theirs], [(down_weight, 1)])
         weight = [low, high]
         last = hide(last_ours, last_got)
         outs = [(i * cut, cut, BF16) for i in range(4)]
-        b_l, b_r, a_l, a_r = down([last], weight, keep, outs, [])
+        b_l, b_r, a_l, a_r = down([last], weight, outs, [])
         hidden = [hide(*pair) for pair in zip(ours, got)]
 
         def put_down(which, after):
             size = sum(h.shape[0] for h, _ in hidden[which])
             outs = [(0, size, F32)]
-            (rest,) = down(hidden[which], weight, keep, outs, after)
+            (rest,) = down(hidden[which], weight, outs, after)
             at = 0
             for key in sum(groups[which], []):
                 part[key] = rest[at : at + cut]

time: 105 us -> 103 us (0.981)
  Pallas kernels: 50.5 us -> 44.8 us
  waiting for transfers between devices: 19.9 us -> 23.9 us
    pallas_call x6 -> x5, Pallas kernels: 26.2 us -> 20.3 us  [the longest x3 13.3 us: down(): pl.pallas_call(body, name='down', in_specs=[VMEM] * (2 * count + 2) + [AN...]
    ppermute x14, waiting for transfers between devices: 14.6 us -> 17.8 us  [left(): return lax.ppermute(x, 'gy', to_left)]
    ppermute x14, starting transfers between devices: 18.8 us -> 20.3 us  [right(): return lax.ppermute(x, 'gy', to_right)]
    ppermute x14, starting transfers between devices: 11 us -> 9.55 us  [left(): return lax.ppermute(x, 'gy', to_left)]
    pallas_call x4 -> x5, Pallas kernels: 23.5 us -> 23.7 us  [gate_up(): pl.pallas_call(body, name='gate_up', in_specs=[VMEM] * (count + len(weigh...]
  transfers between devices with their start and end apart: 34 -> 34, of which waited for: 14 -> 17; matrix products, arithmetic and copies ran while one was open for 0% -> 0% of each run, Pallas kernels for 48% -> 44%
where the time goes in v10:
time: 103 us
  Pallas kernels  44.8 us (43%)
  starting transfers between devices  31.2 us (30%)
  waiting for transfers between devices  23.9 us (23%)
  other arithmetic  1.44 us (1%)
  local copies, waits for them, and re-layouts  1.06 us (1%)
    pallas_call x5, Pallas kernels, gate_up(): pl.pallas_call(body, name='gate_up', in_specs=[VMEM] * (count + len(weigh...  23.7 us
    ppermute x14, starting transfers between devices, right(): return lax.ppermute(x, 'gy', to_right)  20.3 us
    ppermute x14, waiting for transfers between devices, left(): return lax.ppermute(x, 'gy', to_left)  17.8 us
    pallas_call x3, Pallas kernels, down(): pl.pallas_call(body, name='down', in_specs=[VMEM] * (2 * count + 2) + [AN...  13.3 us
    ppermute x14, starting transfers between devices, left(): return lax.ppermute(x, 'gy', to_left)  9.55 us
    pallas_call x2, Pallas kernels, bring(): pl.pallas_call(body, name='bring', in_specs=[ANY] * (count + len(after)),...  6.96 us
    ppermute x14, waiting for transfers between devices, right(): return lax.ppermute(x, 'gy', to_right)  5.38 us
  transfers between devices with their start and end apart: 34, of which 17 were waited for; matrix products, arithmetic and copies ran while one was open for 0% of the time, Pallas kernels for 44%

profile of v10, /device:TPU:0, one launch (start us, length us, event | category | flops | bytes accessed | tf_op | source)
XLA Modules:
  0.0 102.7 jit_solution(2640020311248931608)
XLA Ops:
  0.0 1.1 %fusion.14 = (bf16[32,4096]{1,0:T(8,128)(2,1)S(1)}, bf16[32,4096]{1,0:T(8,128)(2,1)S(1)}) fusion(bf16[64,4096]{1,0:T(8,128)(2,1)} %param.4), kind=kLoop, calls=%fused_computation.27 | loop fusion | bytes 1048576 | tf_op jit(solution)/shard_map/slice | solution.py:237
  1.1 3.1 %collective-permute-start = (bf16[32,4096]{1,0:T(8,128)(2,1)S(1)}, bf16[32,4096]{1,0:T(8,128)(2,1)S(1)}, u32[]{:S(2)}, u32[]{:S(2)}) collective-permute-start(bf16[32,4096]{1,0:T(8,128)(2,1)S(1)} %get-tuple-element.104.refs_0_), channel_id=1, source_target_pairs={{0,2},{2,4},{4,6},{6,7},{7,5},{5,3},{3,1},{1,0},{8,10},{10,12},{12... | collective-permute-start | bytes 786440 | tf_op jit(solution)/shard_map/farR1/ppermute | solution.py:220
  4.2 2.0 %collective-permute-start.2 = (bf16[32,4096]{1,0:T(8,128)(2,1)S(1)}, bf16[32,4096]{1,0:T(8,128)(2,1)S(1)}, u32[]{:S(2)}, u32[]{:S(2)}) collective-permute-start(bf16[32,4096]{1,0:T(8,128)(2,1)S(1)} %get-tuple-element.103.refs_1_), channel_id=1, source_target_pairs={{0,2},{2,4},{4,6},{6,7},{7,5},{5,3},{3,1},{1,0},{8,10},{10,12},{12... | collective-permute-start | bytes 786440 | tf_op jit(solution)/shard_map/nearR1/ppermute | solution.py:220
  6.2 3.5 %bring.2.refs_1_.refs_6_.refs_4_ = bf16[4096,1024]{1,0:T(8,128)(2,1)S(1)} custom-call(bf16[4096,2048]{1,0:T(8,128)(2,1)} %refs_8_.1), custom_call_target="tpu_custom_call" | custom-call | flops 1100000000 | tf_op jit(solution)/shard_map/bring/pallas_call | solution.py:79
  9.7 3.5 %bring.3.refs_2_.refs_7_.refs_5_ = bf16[4096,1024]{1,0:T(8,128)(2,1)S(1)} custom-call(bf16[4096,2048]{1,0:T(8,128)(2,1)} %refs_9_.1, bf16[4096,1024]{1,0:T(8,128)(2,1)S(1)} %bring.2.refs_1_.refs_6_.refs_4_), custom_call_target="tpu_custom_call" | custom-call | flops 1100000000 | tf_op jit(solution)/shard_map/bring/pallas_call | solution.py:79
  13.4 1.9 %collective-permute-start.4 = (bf16[32,4096]{1,0:T(8,128)(2,1)S(1)}, bf16[32,4096]{1,0:T(8,128)(2,1)S(1)}, u32[]{:S(2)}, u32[]{:S(2)}) collective-permute-start(bf16[32,4096]{1,0:T(8,128)(2,1)S(1)} %get-tuple-element.48.refs_2_), channel_id=1, source_target_pairs={{0,2},{2,4},{4,6},{6,7},{7,5},{5,3},{3,1},{1,0},{8,10},{10,12},{12... | collective-permute-start | bytes 786440 | tf_op jit(solution)/shard_map/farR2/ppermute | solution.py:220
  15.4 1.4 %collective-permute-done.2.refs_0_ = bf16[32,4096]{1,0:T(8,128)(2,1)S(1)} collective-permute-done((bf16[32,4096]{1,0:T(8,128)(2,1)S(1)}, bf16[32,4096]{1,0:T(8,128)(2,1)S(1)}, u32[]{:S(2)}, u32[]{:S(2)}) %collective-permute-start.2) | collective-permute-done | bytes 262176 | tf_op jit(solution)/shard_map/nearR1/ppermute | solution.py:220
  16.8 1.9 %collective-permute-done.3.refs_1_ = bf16[32,4096]{1,0:T(8,128)(2,1)S(1)} collective-permute-done((bf16[32,4096]{1,0:T(8,128)(2,1)S(1)}, bf16[32,4096]{1,0:T(8,128)(2,1)S(1)}, u32[]{:S(2)}, u32[]{:S(2)}) %collective-permute-start.3) | collective-permute-done | bytes 262176 | tf_op jit(solution)/shard_map/nearL1/ppermute | solution.py:224
  18.7 1.6 %collective-permute-start.8 = (bf16[32,4096]{1,0:T(8,128)(2,1)S(1)}, bf16[32,4096]{1,0:T(8,128)(2,1)S(1)}, u32[]{:S(2)}, u32[]{:S(2)}) collective-permute-start(bf16[32,4096]{1,0:T(8,128)(2,1)S(1)} %get-tuple-element.50.refs_4_.refs_10_), channel_id=1, source_target_pairs={{0,2},{2,4},{4,6},{6,7},{7,5},{5,3},{3,1},{1,0},{8,10},{10,12},{12... | collective-permute-start | bytes 786440 | tf_op jit(solution)/shard_map/nearR2/ppermute | solution.py:220
  20.3 0.4 collective-permute-start.9
  20.7 5.9 %gate_up.5 = (f32[2,192,1024]{2,1,0:T(8,128)S(1)}, bf16[4096,1024]{1,0:T(8,128)(2,1)S(1)}, bf16[4096,1024]{1,0:T(8,128)(2,1)S(1)}) custom-call(bf16[32,4096]{1,0:T(8,128)(2,1)S(1)} %get-tuple-element.104.refs_0_, bf16[32,4096]{1,0:T(8,128)(2,1)S(1)} %get-tuple-element.103.refs_1_, bf16[32,4096]{1,0:T(8,128)(2,1)S(1)} %get-tuple-element.48.refs_2_, ...), custom_call_target="tpu_custom_call" | custom-call | flops 1100000000 | tf_op jit(solution)/shard_map/gate_up/pallas_call | solution.py:134
  26.7 1.6 %collective-permute-start.6 = (bf16[32,4096]{1,0:T(8,128)(2,1)S(1)}, bf16[32,4096]{1,0:T(8,128)(2,1)S(1)}, u32[]{:S(2)}, u32[]{:S(2)}) collective-permute-start(bf16[32,4096]{1,0:T(8,128)(2,1)S(1)} %get-tuple-element.55.refs_8_.refs_0_), channel_id=1, source_target_pairs={{0,2},{2,4},{4,6},{6,7},{7,5},{5,3},{3,1},{1,0},{8,10},{10,12},{12... | collective-permute-start | bytes 786440 | tf_op jit(solution)/shard_map/farR3/ppermute | solution.py:220
  28.8 3.7 %gate_up.6.refs_2_.a_ref = f32[2,192,1024]{2,1,0:T(8,128)S(1)} custom-call(bf16[32,4096]{1,0:T(8,128)(2,1)S(1)} %get-tuple-element.104.refs_0_, bf16[32,4096]{1,0:T(8,128)(2,1)S(1)} %get-tuple-element.103.refs_1_, bf16[32,4096]{1,0:T(8,128)(2,1)S(1)} %get-tuple-element.48.refs_2_, bf16[32,4096]{1,0:T(8,128)(2,1)S(1)} %get-tuple-element.49.refs_3_, ...), custom_call_target="tpu_custom_call" | custom-call | flops 1100000000 | tf_op jit(solution)/shard_map/gate_up/pallas_call | solution.py:134
  32.6 1.6 %collective-permute-start.12 = (bf16[32,4096]{1,0:T(8,128)(2,1)S(1)}, bf16[32,4096]{1,0:T(8,128)(2,1)S(1)}, u32[]{:S(2)}, u32[]{:S(2)}) collective-permute-start(bf16[32,4096]{1,0:T(8,128)(2,1)S(1)} %get-tuple-element.57.refs_2_), channel_id=1, source_target_pairs={{0,2},{2,4},{4,6},{6,7},{7,5},{5,3},{3,1},{1,0},{8,10},{10,12},{12... | collective-permute-start | bytes 786440 | tf_op jit(solution)/shard_map/nearR3/ppermute | solution.py:220
  34.7 1.9 %collective-permute-done.7.refs_1_ = bf16[32,4096]{1,0:T(8,128)(2,1)S(1)} collective-permute-done((bf16[32,4096]{1,0:T(8,128)(2,1)S(1)}, bf16[32,4096]{1,0:T(8,128)(2,1)S(1)}, u32[]{:S(2)}, u32[]{:S(2)}) %collective-permute-start.7) | collective-permute-done | bytes 262176 | tf_op jit(solution)/shard_map/farL3/ppermute | solution.py:224
  36.6 1.6 %collective-permute-start.10 = (bf16[32,4096]{1,0:T(8,128)(2,1)S(1)}, bf16[32,4096]{1,0:T(8,128)(2,1)S(1)}, u32[]{:S(2)}, u32[]{:S(2)}) collective-permute-start(bf16[32,4096]{1,0:T(8,128)(2,1)S(1)} %get-tuple-element.58.refs_4_.refs_10_), channel_id=1, source_target_pairs={{0,2},{2,4},{4,6},{6,7},{7,5},{5,3},{3,1},{1,0},{8,10},{10,12},{12... | collective-permute-start | bytes 786440 | tf_op jit(solution)/shard_map/farR4/ppermute | solution.py:220
  38.1 0.5 collective-permute-start.11
  38.6 7.0 %gate_up.7 = (f32[2,192,1024]{2,1,0:T(8,128)S(1)}, f32[2,192,1024]{2,1,0:T(8,128)S(1)}) custom-call(bf16[32,4096]{1,0:T(8,128)(2,1)S(1)} %get-tuple-element.55.refs_8_.refs_0_, bf16[32,4096]{1,0:T(8,128)(2,1)S(1)} %get-tuple-element.56.refs_1_, bf16[32,4096]{1,0:T(8,128)(2,1)S(1)} %get-tuple-element.57.refs_2_, ...), custom_call_target="tpu_custom_call" | custom-call | flops 1100000000 | tf_op jit(solution)/shard_map/gate_up/pallas_call | solution.py:134
  46.0 3.5 %gate_up.8 = (f32[2,128,1024]{2,1,0:T(8,128)S(1)}, bf16[2048,2048]{1,0:T(8,128)(2,1)S(1)}) custom-call(bf16[32,4096]{1,0:T(8,128)(2,1)S(1)} %get-tuple-element.62.refs_4_.refs_0_, bf16[32,4096]{1,0:T(8,128)(2,1)S(1)} %get-tuple-element.64.refs_1_, bf16[32,4096]{1,0:T(8,128)(2,1)S(1)} %get-tuple-element.65.refs_2_, ...), custom_call_target="tpu_custom_call" | custom-call | flops 1100000000 | tf_op jit(solution)/shard_map/gate_up/pallas_call | solution.py:134
  49.4 0.6 collective-permute-start.18
  50.1 3.5 %gate_up.9 = (f32[2,128,1024]{2,1,0:T(8,128)S(1)}, bf16[2048,2048]{1,0:T(8,128)(2,1)S(1)}) custom-call(bf16[32,4096]{1,0:T(8,128)(2,1)S(1)} %get-tuple-element.62.refs_4_.refs_0_, bf16[32,4096]{1,0:T(8,128)(2,1)S(1)} %get-tuple-element.64.refs_1_, bf16[32,4096]{1,0:T(8,128)(2,1)S(1)} %get-tuple-element.65.refs_2_, ...), custom_call_target="tpu_custom_call" | custom-call | flops 1100000000 | tf_op jit(solution)/shard_map/gate_up/pallas_call | solution.py:134
  53.8 0.5 collective-permute-start.19
  54.8 0.7 collective-permute-done.19.refs_1_
  55.5 3.7 %down.4 = (bf16[32,4096]{1,0:T(8,128)(2,1)S(1)}, bf16[32,4096]{1,0:T(8,128)(2,1)S(1)}, bf16[32,4096]{1,0:T(8,128)(2,1)S(1)}, bf16[32,4096]{1,0:T(8,128)(2,1)S(1)}) custom-call(bf16[128,1024]{1,0:T(8,128)(2,1)S(1)} %gated.5.refs_0_, bf16[128,1024]{1,0:T(8,128)(2,1)S(1)} %collective-permute-done.19.refs_1_, bf16[2048,2048]{1,0:T(8,128)(2,1)S(1)} %get-tuple-element.67.refs_2_, ...), custom_call_target="tpu_custom_call" | custom-call | tf_op jit(solution)/shard_map/down/pallas_call | solution.py:198
  59.2 0.5 collective-permute-start.22
  59.7 1.6 %collective-permute-start.23 = (bf16[32,4096]{1,0:T(8,128)(2,1)S(1)}, bf16[32,4096]{1,0:T(8,128)(2,1)S(1)}, u32[]{:S(2)}, u32[]{:S(2)}) collective-permute-start(bf16[32,4096]{1,0:T(8,128)(2,1)S(1)} %get-tuple-element.76), channel_id=1, source_target_pairs={{0,2},{2,4},{4,6},{6,7},{7,5},{5,3},{3,1},{1,0},{8,10},{10,12},{12... | collective-permute-start | bytes 786440 | tf_op jit(solution)/shard_map/right/ppermute | solution.py:220
  61.8 1.6 %collective-permute-start.21 = (bf16[32,4096]{1,0:T(8,128)(2,1)S(1)}, bf16[32,4096]{1,0:T(8,128)(2,1)S(1)}, u32[]{:S(2)}, u32[]{:S(2)}) collective-permute-start(bf16[32,4096]{1,0:T(8,128)(2,1)S(1)} %get-tuple-element.74), channel_id=1, source_target_pairs={{0,2},{2,4},{4,6},{6,7},{7,5},{5,3},{3,1},{1,0},{8,10},{10,12},{12... | collective-permute-start | bytes 786440 | tf_op jit(solution)/shard_map/right/ppermute | solution.py:220
  63.8 4.8 %down.3.refs_2_ = f32[192,4096]{1,0:T(8,128)S(1)} custom-call(bf16[192,1024]{1,0:T(8,128)(2,1)S(1)} %gated.4.refs_0_, bf16[192,1024]{1,0:T(8,128)(2,1)S(1)} %collective-permute-done.17.refs_1_, bf16[2048,2048]{1,0:T(8,128)(2,1)S(1)} %get-tuple-element.67.refs_2_, bf16[2048,2048]{1,0:T(8,128)(2,1)S(1)} %get-tuple-element.69.refs_3_), custom_call_target="tpu_custom_call" | custom-call | tf_op jit(solution)/shard_map/down/pallas_call | solution.py:198
  69.0 1.2 %collective-permute-start.24 = (bf16[32,4096]{1,0:T(8,128)(2,1)S(1)}, bf16[32,4096]{1,0:T(8,128)(2,1)S(1)}, u32[]{:S(2)}, u32[]{:S(2)}) collective-permute-start(bf16[32,4096]{1,0:T(8,128)(2,1)S(1)} %get-tuple-element.102.refs_2_), channel_id=1, source_target_pairs={{2,0},{4,2},{6,4},{7,6},{5,7},{3,5},{1,3},{0,1},{10,8},{12,10},{14... | collective-permute-start | bytes 786440 | tf_op jit(solution)/shard_map/left/ppermute | solution.py:224
  70.2 0.8 collective-permute-start.25
  71.1 3.0 %collective-permute-done.20.refs_0_ = bf16[32,4096]{1,0:T(8,128)(2,1)S(1)} collective-permute-done((bf16[32,4096]{1,0:T(8,128)(2,1)S(1)}, bf16[32,4096]{1,0:T(8,128)(2,1)S(1)}, u32[]{:S(2)}, u32[]{:S(2)}) %collective-permute-start.20) | collective-permute-done | bytes 262176 | tf_op jit(solution)/shard_map/left/ppermute | solution.py:224
  74.0 0.5 collective-permute-done.21.refs_1_
  74.6 1.2 %collective-permute-start.28 = (bf16[32,4096]{1,0:T(8,128)(2,1)S(1)}, bf16[32,4096]{1,0:T(8,128)(2,1)S(1)}, u32[]{:S(2)}, u32[]{:S(2)}) collective-permute-start(bf16[32,4096]{1,0:T(8,128)(2,1)S(1)} %get-tuple-element.100.refs_4_), channel_id=1, source_target_pairs={{2,0},{4,2},{6,4},{7,6},{5,7},{3,5},{1,3},{0,1},{10,8},{12,10},{14... | collective-permute-start | bytes 786440 | tf_op jit(solution)/shard_map/left/ppermute | solution.py:224
  75.8 0.8 collective-permute-start.29
  76.7 4.8 %down.5.refs_2_ = f32[192,4096]{1,0:T(8,128)S(1)} custom-call(bf16[192,1024]{1,0:T(8,128)(2,1)S(1)} %gated.3.refs_0_, bf16[192,1024]{1,0:T(8,128)(2,1)S(1)} %collective-permute-done.15.refs_1_, bf16[2048,2048]{1,0:T(8,128)(2,1)S(1)} %get-tuple-element.67.refs_2_, bf16[2048,2048]{1,0:T(8,128)(2,1)S(1)} %get-tuple-element.69.refs_3_, ...), custom_call_target="tpu_custom_call" | custom-call | tf_op jit(solution)/shard_map/down/pallas_call | solution.py:198
  81.6 1.2 %collective-permute-start.26 = (bf16[32,4096]{1,0:T(8,128)(2,1)S(1)}, bf16[32,4096]{1,0:T(8,128)(2,1)S(1)}, u32[]{:S(2)}, u32[]{:S(2)}) collective-permute-start(bf16[32,4096]{1,0:T(8,128)(2,1)S(1)} %get-tuple-element.98.refs_2_), channel_id=1, source_target_pairs={{2,0},{4,2},{6,4},{7,6},{5,7},{3,5},{1,3},{0,1},{10,8},{12,10},{14... | collective-permute-start | bytes 786440 | tf_op jit(solution)/shard_map/left/ppermute | solution.py:224
  82.9 0.9 collective-permute-start.27
  83.7 1.6 %collective-permute-done.28.refs_0_ = bf16[32,4096]{1,0:T(8,128)(2,1)S(1)} collective-permute-done((bf16[32,4096]{1,0:T(8,128)(2,1)S(1)}, bf16[32,4096]{1,0:T(8,128)(2,1)S(1)}, u32[]{:S(2)}, u32[]{:S(2)}) %collective-permute-start.28) | collective-permute-done | bytes 262176 | tf_op jit(solution)/shard_map/left/ppermute | solution.py:224
  85.3 0.5 collective-permute-done.29.refs_1_
  85.9 1.2 %collective-permute-start.32 = (bf16[32,4096]{1,0:T(8,128)(2,1)S(1)}, bf16[32,4096]{1,0:T(8,128)(2,1)S(1)}, u32[]{:S(2)}, u32[]{:S(2)}) collective-permute-start(bf16[32,4096]{1,0:T(8,128)(2,1)S(1)} %get-tuple-element.96.refs_2_), channel_id=1, source_target_pairs={{2,0},{4,2},{6,4},{7,6},{5,7},{3,5},{1,3},{0,1},{10,8},{12,10},{14... | collective-permute-start | bytes 786440 | tf_op jit(solution)/shard_map/left/ppermute | solution.py:224
  87.1 0.8 collective-permute-start.33
  87.9 3.0 %collective-permute-done.26.refs_0_ = bf16[32,4096]{1,0:T(8,128)(2,1)S(1)} collective-permute-done((bf16[32,4096]{1,0:T(8,128)(2,1)S(1)}, bf16[32,4096]{1,0:T(8,128)(2,1)S(1)}, u32[]{:S(2)}, u32[]{:S(2)}) %collective-permute-start.26) | collective-permute-done | bytes 262176 | tf_op jit(solution)/shard_map/left/ppermute | solution.py:224
  90.9 1.2 %collective-permute-done.27.refs_1_ = bf16[32,4096]{1,0:T(8,128)(2,1)S(1)} collective-permute-done((bf16[32,4096]{1,0:T(8,128)(2,1)S(1)}, bf16[32,4096]{1,0:T(8,128)(2,1)S(1)}, u32[]{:S(2)}, u32[]{:S(2)}) %collective-permute-start.27) | collective-permute-done | bytes 262176 | tf_op jit(solution)/shard_map/right/ppermute | solution.py:220
  92.2 1.7 %collective-permute-start.30 = (bf16[32,4096]{1,0:T(8,128)(2,1)S(1)}, bf16[32,4096]{1,0:T(8,128)(2,1)S(1)}, u32[]{:S(2)}, u32[]{:S(2)}) collective-permute-start(bf16[32,4096]{1,0:T(8,128)(2,1)S(1)} %get-tuple-element.94.refs_2_), channel_id=1, source_target_pairs={{2,0},{4,2},{6,4},{7,6},{5,7},{3,5},{1,3},{0,1},{10,8},{12,10},{14... | collective-permute-start | bytes 786440 | tf_op jit(solution)/shard_map/left/ppermute | solution.py:224
  94.3 2.2 %collective-permute-done.32.refs_0_ = bf16[32,4096]{1,0:T(8,128)(2,1)S(1)} collective-permute-done((bf16[32,4096]{1,0:T(8,128)(2,1)S(1)}, bf16[32,4096]{1,0:T(8,128)(2,1)S(1)}, u32[]{:S(2)}, u32[]{:S(2)}) %collective-permute-start.32) | collective-permute-done | bytes 262176 | tf_op jit(solution)/shard_map/left/ppermute | solution.py:224
  96.5 1.2 %collective-permute-done.33.refs_1_ = bf16[32,4096]{1,0:T(8,128)(2,1)S(1)} collective-permute-done((bf16[32,4096]{1,0:T(8,128)(2,1)S(1)}, bf16[32,4096]{1,0:T(8,128)(2,1)S(1)}, u32[]{:S(2)}, u32[]{:S(2)}) %collective-permute-start.33) | collective-permute-done | bytes 262176 | tf_op jit(solution)/shard_map/right/ppermute | solution.py:220
  97.7 3.8 %collective-permute-done.30.refs_0_ = bf16[32,4096]{1,0:T(8,128)(2,1)S(1)} collective-permute-done((bf16[32,4096]{1,0:T(8,128)(2,1)S(1)}, bf16[32,4096]{1,0:T(8,128)(2,1)S(1)}, u32[]{:S(2)}, u32[]{:S(2)}) %collective-permute-start.30) | collective-permute-done | bytes 262176 | tf_op jit(solution)/shard_map/left/ppermute | solution.py:224
  101.9 0.8 pad_maximum_fusion
  (55 shorter events, 4.7 us)
Async XLA Ops:
  1.1 12.1 %collective-permute-start = (bf16[32,4096]{1,0:T(8,128)(2,1)S(1)}, bf16[32,4096]{1,0:T(8,128)(2,1)S(1)}, u32[]{:S(2)}, u32[]{:S(2)}) collective-permute-start(bf16[32,4096]{1,0:T(8,128)(2,1)S(1)} %get-tuple-element.104.refs_0_), channel_id=1, source_target_pairs={{0,2},{2,4},{4,6},{6,7},{7,5},{5,3},{3,1},{1,0},{8,10},{10,12},{12... | collective-permute-start | bytes 786440 | tf_op jit(solution)/shard_map/farR1/ppermute | solution.py:220
  4.1 9.2 %collective-permute-start.1 = (bf16[32,4096]{1,0:T(8,128)(2,1)S(1)}, bf16[32,4096]{1,0:T(8,128)(2,1)S(1)}, u32[]{:S(2)}, u32[]{:S(2)}) collective-permute-start(bf16[32,4096]{1,0:T(8,128)(2,1)S(1)} %get-tuple-element.103.refs_1_), channel_id=1, source_target_pairs={{2,0},{4,2},{6,4},{7,6},{5,7},{3,5},{1,3},{0,1},{10,8},{12,10},{14... | collective-permute-start | bytes 786440 | tf_op jit(solution)/shard_map/farL1/ppermute | solution.py:224
  4.2 12.7 %collective-permute-start.2 = (bf16[32,4096]{1,0:T(8,128)(2,1)S(1)}, bf16[32,4096]{1,0:T(8,128)(2,1)S(1)}, u32[]{:S(2)}, u32[]{:S(2)}) collective-permute-start(bf16[32,4096]{1,0:T(8,128)(2,1)S(1)} %get-tuple-element.103.refs_1_), channel_id=1, source_target_pairs={{0,2},{2,4},{4,6},{6,7},{7,5},{5,3},{3,1},{1,0},{8,10},{10,12},{12... | collective-permute-start | bytes 786440 | tf_op jit(solution)/shard_map/nearR1/ppermute | solution.py:220
  6.2 12.5 %collective-permute-start.3 = (bf16[32,4096]{1,0:T(8,128)(2,1)S(1)}, bf16[32,4096]{1,0:T(8,128)(2,1)S(1)}, u32[]{:S(2)}, u32[]{:S(2)}) collective-permute-start(bf16[32,4096]{1,0:T(8,128)(2,1)S(1)} %get-tuple-element.104.refs_0_), channel_id=1, source_target_pairs={{2,0},{4,2},{6,4},{7,6},{5,7},{3,5},{1,3},{0,1},{10,8},{12,10},{14... | collective-permute-start | bytes 786440 | tf_op jit(solution)/shard_map/nearL1/ppermute | solution.py:224
  13.4 13.3 %collective-permute-start.4 = (bf16[32,4096]{1,0:T(8,128)(2,1)S(1)}, bf16[32,4096]{1,0:T(8,128)(2,1)S(1)}, u32[]{:S(2)}, u32[]{:S(2)}) collective-permute-start(bf16[32,4096]{1,0:T(8,128)(2,1)S(1)} %get-tuple-element.48.refs_2_), channel_id=1, source_target_pairs={{0,2},{2,4},{4,6},{6,7},{7,5},{5,3},{3,1},{1,0},{8,10},{10,12},{12... | collective-permute-start | bytes 786440 | tf_op jit(solution)/shard_map/farR2/ppermute | solution.py:220
  15.3 11.4 %collective-permute-start.5 = (bf16[32,4096]{1,0:T(8,128)(2,1)S(1)}, bf16[32,4096]{1,0:T(8,128)(2,1)S(1)}, u32[]{:S(2)}, u32[]{:S(2)}) collective-permute-start(bf16[32,4096]{1,0:T(8,128)(2,1)S(1)} %get-tuple-element.49.refs_3_), channel_id=1, source_target_pairs={{2,0},{4,2},{6,4},{7,6},{5,7},{3,5},{1,3},{0,1},{10,8},{12,10},{14... | collective-permute-start | bytes 786440 | tf_op jit(solution)/shard_map/farL2/ppermute | solution.py:224
  18.7 13.9 %collective-permute-start.8 = (bf16[32,4096]{1,0:T(8,128)(2,1)S(1)}, bf16[32,4096]{1,0:T(8,128)(2,1)S(1)}, u32[]{:S(2)}, u32[]{:S(2)}) collective-permute-start(bf16[32,4096]{1,0:T(8,128)(2,1)S(1)} %get-tuple-element.50.refs_4_.refs_10_), channel_id=1, source_target_pairs={{0,2},{2,4},{4,6},{6,7},{7,5},{5,3},{3,1},{1,0},{8,10},{10,12},{12... | collective-permute-start | bytes 786440 | tf_op jit(solution)/shard_map/nearR2/ppermute | solution.py:220
  20.3 12.3 %collective-permute-start.9 = (bf16[32,4096]{1,0:T(8,128)(2,1)S(1)}, bf16[32,4096]{1,0:T(8,128)(2,1)S(1)}, u32[]{:S(2)}, u32[]{:S(2)}) collective-permute-start(bf16[32,4096]{1,0:T(8,128)(2,1)S(1)} %get-tuple-element.51.refs_5_), channel_id=1, source_target_pairs={{2,0},{4,2},{6,4},{7,6},{5,7},{3,5},{1,3},{0,1},{10,8},{12,10},{14... | collective-permute-start | bytes 786440 | tf_op jit(solution)/shard_map/nearL2/ppermute | solution.py:224
  26.7 7.9 %collective-permute-start.6 = (bf16[32,4096]{1,0:T(8,128)(2,1)S(1)}, bf16[32,4096]{1,0:T(8,128)(2,1)S(1)}, u32[]{:S(2)}, u32[]{:S(2)}) collective-permute-start(bf16[32,4096]{1,0:T(8,128)(2,1)S(1)} %get-tuple-element.55.refs_8_.refs_0_), channel_id=1, source_target_pairs={{0,2},{2,4},{4,6},{6,7},{7,5},{5,3},{3,1},{1,0},{8,10},{10,12},{12... | collective-permute-start | bytes 786440 | tf_op jit(solution)/shard_map/farR3/ppermute | solution.py:220
  28.3 8.2 %collective-permute-start.7 = (bf16[32,4096]{1,0:T(8,128)(2,1)S(1)}, bf16[32,4096]{1,0:T(8,128)(2,1)S(1)}, u32[]{:S(2)}, u32[]{:S(2)}) collective-permute-start(bf16[32,4096]{1,0:T(8,128)(2,1)S(1)} %get-tuple-element.56.refs_1_), channel_id=1, source_target_pairs={{2,0},{4,2},{6,4},{7,6},{5,7},{3,5},{1,3},{0,1},{10,8},{12,10},{14... | collective-permute-start | bytes 786440 | tf_op jit(solution)/shard_map/farL3/ppermute | solution.py:224
  32.6 13.1 %collective-permute-start.12 = (bf16[32,4096]{1,0:T(8,128)(2,1)S(1)}, bf16[32,4096]{1,0:T(8,128)(2,1)S(1)}, u32[]{:S(2)}, u32[]{:S(2)}) collective-permute-start(bf16[32,4096]{1,0:T(8,128)(2,1)S(1)} %get-tuple-element.57.refs_2_), channel_id=1, source_target_pairs={{0,2},{2,4},{4,6},{6,7},{7,5},{5,3},{3,1},{1,0},{8,10},{10,12},{12... | collective-permute-start | bytes 786440 | tf_op jit(solution)/shard_map/nearR3/ppermute | solution.py:220
  34.2 11.4 %collective-permute-start.13 = (bf16[32,4096]{1,0:T(8,128)(2,1)S(1)}, bf16[32,4096]{1,0:T(8,128)(2,1)S(1)}, u32[]{:S(2)}, u32[]{:S(2)}) collective-permute-start(bf16[32,4096]{1,0:T(8,128)(2,1)S(1)} %get-tuple-element.60.refs_3_), channel_id=1, source_target_pairs={{2,0},{4,2},{6,4},{7,6},{5,7},{3,5},{1,3},{0,1},{10,8},{12,10},{14... | collective-permute-start | bytes 786440 | tf_op jit(solution)/shard_map/nearL3/ppermute | solution.py:224
  36.6 9.1 %collective-permute-start.10 = (bf16[32,4096]{1,0:T(8,128)(2,1)S(1)}, bf16[32,4096]{1,0:T(8,128)(2,1)S(1)}, u32[]{:S(2)}, u32[]{:S(2)}) collective-permute-start(bf16[32,4096]{1,0:T(8,128)(2,1)S(1)} %get-tuple-element.58.refs_4_.refs_10_), channel_id=1, source_target_pairs={{0,2},{2,4},{4,6},{6,7},{7,5},{5,3},{3,1},{1,0},{8,10},{10,12},{12... | collective-permute-start | bytes 786440 | tf_op jit(solution)/shard_map/farR4/ppermute | solution.py:220
  38.1 7.8 %collective-permute-start.11 = (bf16[32,4096]{1,0:T(8,128)(2,1)S(1)}, bf16[32,4096]{1,0:T(8,128)(2,1)S(1)}, u32[]{:S(2)}, u32[]{:S(2)}) collective-permute-start(bf16[32,4096]{1,0:T(8,128)(2,1)S(1)} %get-tuple-element.59.refs_5_), channel_id=1, source_target_pairs={{2,0},{4,2},{6,4},{7,6},{5,7},{3,5},{1,3},{0,1},{10,8},{12,10},{14... | collective-permute-start | bytes 786440 | tf_op jit(solution)/shard_map/farL4/ppermute | solution.py:224
  46.0 8.4 %collective-permute-start.16 = (f32[2,192,1024]{2,1,0:T(8,128)S(1)}, f32[2,192,1024]{2,1,0:T(8,128)S(1)}, u32[]{:S(2)}, u32[]{:S(2)}) collective-permute-start(f32[2,192,1024]{2,1,0:T(8,128)S(1)} %get-tuple-element.71), channel_id=1, source_target_pairs={{0,8},{8,0},{1,9},{9,1},{2,10},{10,2},{3,11},{11,3},{4,12},{12,4},... | collective-permute-start | bytes 4718600 | tf_op jit(solution)/shard_map/swap/ppermute | solution.py:228
  49.4 4.1 %collective-permute-start.18 = (f32[2,128,1024]{2,1,0:T(8,128)S(1)}, f32[2,128,1024]{2,1,0:T(8,128)S(1)}, u32[]{:S(2)}, u32[]{:S(2)}) collective-permute-start(f32[2,128,1024]{2,1,0:T(8,128)S(1)} %get-tuple-element.68.refs_7_), channel_id=1, source_target_pairs={{0,8},{8,0},{1,9},{9,1},{2,10},{10,2},{3,11},{11,3},{4,12},{12,4},... | collective-permute-start | bytes 3145736 | tf_op jit(solution)/shard_map/swap/ppermute | solution.py:228
  50.0 11.8 %collective-permute-start.14 = (f32[2,192,1024]{2,1,0:T(8,128)S(1)}, f32[2,192,1024]{2,1,0:T(8,128)S(1)}, u32[]{:S(2)}, u32[]{:S(2)}) collective-permute-start(f32[2,192,1024]{2,1,0:T(8,128)S(1)} %get-tuple-element.63), channel_id=1, source_target_pairs={{0,8},{8,0},{1,9},{9,1},{2,10},{10,2},{3,11},{11,3},{4,12},{12,4},... | collective-permute-start | bytes 4718600 | tf_op jit(solution)/shard_map/swap/ppermute | solution.py:228
  53.8 1.7 %collective-permute-start.19 = (bf16[128,1024]{1,0:T(8,128)(2,1)S(1)}, bf16[128,1024]{1,0:T(8,128)(2,1)S(1)}, u32[]{:S(2)}, u32[]{:S(2)}) collective-permute-start(bf16[128,1024]{1,0:T(8,128)(2,1)S(1)} %gated.5.refs_0_), channel_id=1, source_target_pairs={{0,8},{8,0},{1,9},{9,1},{2,10},{10,2},{3,11},{11,3},{4,12},{12,4},... | collective-permute-start | bytes 786440 | tf_op jit(solution)/shard_map/swap/ppermute | solution.py:228
  54.7 9.0 %collective-permute-start.17 = (bf16[192,1024]{1,0:T(8,128)(2,1)S(1)}, bf16[192,1024]{1,0:T(8,128)(2,1)S(1)}, u32[]{:S(2)}, u32[]{:S(2)}) collective-permute-start(bf16[192,1024]{1,0:T(8,128)(2,1)S(1)} %gated.4.refs_0_), channel_id=1, source_target_pairs={{0,8},{8,0},{1,9},{9,1},{2,10},{10,2},{3,11},{11,3},{4,12},{12,4},... | collective-permute-start | bytes 1179656 | tf_op jit(solution)/shard_map/swap/ppermute | solution.py:228
  59.2 9.3 %collective-permute-start.22 = (bf16[32,4096]{1,0:T(8,128)(2,1)S(1)}, bf16[32,4096]{1,0:T(8,128)(2,1)S(1)}, u32[]{:S(2)}, u32[]{:S(2)}) collective-permute-start(bf16[32,4096]{1,0:T(8,128)(2,1)S(1)} %get-tuple-element.75), channel_id=1, source_target_pairs={{2,0},{4,2},{6,4},{7,6},{5,7},{3,5},{1,3},{0,1},{10,8},{12,10},{14... | collective-permute-start | bytes 786440 | tf_op jit(solution)/shard_map/left/ppermute | solution.py:224
  59.7 9.2 %collective-permute-start.23 = (bf16[32,4096]{1,0:T(8,128)(2,1)S(1)}, bf16[32,4096]{1,0:T(8,128)(2,1)S(1)}, u32[]{:S(2)}, u32[]{:S(2)}) collective-permute-start(bf16[32,4096]{1,0:T(8,128)(2,1)S(1)} %get-tuple-element.76), channel_id=1, source_target_pairs={{0,2},{2,4},{4,6},{6,7},{7,5},{5,3},{3,1},{1,0},{8,10},{10,12},{12... | collective-permute-start | bytes 786440 | tf_op jit(solution)/shard_map/right/ppermute | solution.py:220
  61.3 12.7 %collective-permute-start.20 = (bf16[32,4096]{1,0:T(8,128)(2,1)S(1)}, bf16[32,4096]{1,0:T(8,128)(2,1)S(1)}, u32[]{:S(2)}, u32[]{:S(2)}) collective-permute-start(bf16[32,4096]{1,0:T(8,128)(2,1)S(1)} %get-tuple-element.73), channel_id=1, source_target_pairs={{2,0},{4,2},{6,4},{7,6},{5,7},{3,5},{1,3},{0,1},{10,8},{12,10},{14... | collective-permute-start | bytes 786440 | tf_op jit(solution)/shard_map/left/ppermute | solution.py:224
  61.8 12.7 %collective-permute-start.21 = (bf16[32,4096]{1,0:T(8,128)(2,1)S(1)}, bf16[32,4096]{1,0:T(8,128)(2,1)S(1)}, u32[]{:S(2)}, u32[]{:S(2)}) collective-permute-start(bf16[32,4096]{1,0:T(8,128)(2,1)S(1)} %get-tuple-element.74), channel_id=1, source_target_pairs={{0,2},{2,4},{4,6},{6,7},{7,5},{5,3},{3,1},{1,0},{8,10},{10,12},{12... | collective-permute-start | bytes 786440 | tf_op jit(solution)/shard_map/right/ppermute | solution.py:220
  63.7 13.0 %collective-permute-start.15 = (bf16[192,1024]{1,0:T(8,128)(2,1)S(1)}, bf16[192,1024]{1,0:T(8,128)(2,1)S(1)}, u32[]{:S(2)}, u32[]{:S(2)}) collective-permute-start(bf16[192,1024]{1,0:T(8,128)(2,1)S(1)} %gated.3.refs_0_), channel_id=1, source_target_pairs={{0,8},{8,0},{1,9},{9,1},{2,10},{10,2},{3,11},{11,3},{4,12},{12,4},... | collective-permute-start | bytes 1179656 | tf_op jit(solution)/shard_map/swap/ppermute | solution.py:228
  69.0 12.5 %collective-permute-start.24 = (bf16[32,4096]{1,0:T(8,128)(2,1)S(1)}, bf16[32,4096]{1,0:T(8,128)(2,1)S(1)}, u32[]{:S(2)}, u32[]{:S(2)}) collective-permute-start(bf16[32,4096]{1,0:T(8,128)(2,1)S(1)} %get-tuple-element.102.refs_2_), channel_id=1, source_target_pairs={{2,0},{4,2},{6,4},{7,6},{5,7},{3,5},{1,3},{0,1},{10,8},{12,10},{14... | collective-permute-start | bytes 786440 | tf_op jit(solution)/shard_map/left/ppermute | solution.py:224
  70.2 11.3 %collective-permute-start.25 = (bf16[32,4096]{1,0:T(8,128)(2,1)S(1)}, bf16[32,4096]{1,0:T(8,128)(2,1)S(1)}, u32[]{:S(2)}, u32[]{:S(2)}) collective-permute-start(bf16[32,4096]{1,0:T(8,128)(2,1)S(1)} %get-tuple-element.101.refs_3_), channel_id=1, source_target_pairs={{0,2},{2,4},{4,6},{6,7},{7,5},{5,3},{3,1},{1,0},{8,10},{10,12},{12... | collective-permute-start | bytes 786440 | tf_op jit(solution)/shard_map/right/ppermute | solution.py:220
  74.6 10.7 %collective-permute-start.28 = (bf16[32,4096]{1,0:T(8,128)(2,1)S(1)}, bf16[32,4096]{1,0:T(8,128)(2,1)S(1)}, u32[]{:S(2)}, u32[]{:S(2)}) collective-permute-start(bf16[32,4096]{1,0:T(8,128)(2,1)S(1)} %get-tuple-element.100.refs_4_), channel_id=1, source_target_pairs={{2,0},{4,2},{6,4},{7,6},{5,7},{3,5},{1,3},{0,1},{10,8},{12,10},{14... | collective-permute-start | bytes 786440 | tf_op jit(solution)/shard_map/left/ppermute | solution.py:224
  75.8 9.9 %collective-permute-start.29 = (bf16[32,4096]{1,0:T(8,128)(2,1)S(1)}, bf16[32,4096]{1,0:T(8,128)(2,1)S(1)}, u32[]{:S(2)}, u32[]{:S(2)}) collective-permute-start(bf16[32,4096]{1,0:T(8,128)(2,1)S(1)} %get-tuple-element.99.refs_5_), channel_id=1, source_target_pairs={{0,2},{2,4},{4,6},{6,7},{7,5},{5,3},{3,1},{1,0},{8,10},{10,12},{12... | collective-permute-start | bytes 786440 | tf_op jit(solution)/shard_map/right/ppermute | solution.py:220
  81.6 9.2 %collective-permute-start.26 = (bf16[32,4096]{1,0:T(8,128)(2,1)S(1)}, bf16[32,4096]{1,0:T(8,128)(2,1)S(1)}, u32[]{:S(2)}, u32[]{:S(2)}) collective-permute-start(bf16[32,4096]{1,0:T(8,128)(2,1)S(1)} %get-tuple-element.98.refs_2_), channel_id=1, source_target_pairs={{2,0},{4,2},{6,4},{7,6},{5,7},{3,5},{1,3},{0,1},{10,8},{12,10},{14... | collective-permute-start | bytes 786440 | tf_op jit(solution)/shard_map/left/ppermute | solution.py:224
  82.9 9.2 %collective-permute-start.27 = (bf16[32,4096]{1,0:T(8,128)(2,1)S(1)}, bf16[32,4096]{1,0:T(8,128)(2,1)S(1)}, u32[]{:S(2)}, u32[]{:S(2)}) collective-permute-start(bf16[32,4096]{1,0:T(8,128)(2,1)S(1)} %get-tuple-element.97.refs_3_), channel_id=1, source_target_pairs={{0,2},{2,4},{4,6},{6,7},{7,5},{5,3},{3,1},{1,0},{8,10},{10,12},{12... | collective-permute-start | bytes 786440 | tf_op jit(solution)/shard_map/right/ppermute | solution.py:220
  85.9 10.7 %collective-permute-start.32 = (bf16[32,4096]{1,0:T(8,128)(2,1)S(1)}, bf16[32,4096]{1,0:T(8,128)(2,1)S(1)}, u32[]{:S(2)}, u32[]{:S(2)}) collective-permute-start(bf16[32,4096]{1,0:T(8,128)(2,1)S(1)} %get-tuple-element.96.refs_2_), channel_id=1, source_target_pairs={{2,0},{4,2},{6,4},{7,6},{5,7},{3,5},{1,3},{0,1},{10,8},{12,10},{14... | collective-permute-start | bytes 786440 | tf_op jit(solution)/shard_map/left/ppermute | solution.py:224
  87.1 10.6 %collective-permute-start.33 = (bf16[32,4096]{1,0:T(8,128)(2,1)S(1)}, bf16[32,4096]{1,0:T(8,128)(2,1)S(1)}, u32[]{:S(2)}, u32[]{:S(2)}) collective-permute-start(bf16[32,4096]{1,0:T(8,128)(2,1)S(1)} %get-tuple-element.95.refs_3_), channel_id=1, source_target_pairs={{0,2},{2,4},{4,6},{6,7},{7,5},{5,3},{3,1},{1,0},{8,10},{10,12},{12... | collective-permute-start | bytes 786440 | tf_op jit(solution)/shard_map/right/ppermute | solution.py:220
  92.2 9.4 %collective-permute-start.30 = (bf16[32,4096]{1,0:T(8,128)(2,1)S(1)}, bf16[32,4096]{1,0:T(8,128)(2,1)S(1)}, u32[]{:S(2)}, u32[]{:S(2)}) collective-permute-start(bf16[32,4096]{1,0:T(8,128)(2,1)S(1)} %get-tuple-element.94.refs_2_), channel_id=1, source_target_pairs={{2,0},{4,2},{6,4},{7,6},{5,7},{3,5},{1,3},{0,1},{10,8},{12,10},{14... | collective-permute-start | bytes 786440 | tf_op jit(solution)/shard_map/left/ppermute | solution.py:224
  93.9 7.8 %collective-permute-start.31 = (bf16[32,4096]{1,0:T(8,128)(2,1)S(1)}, bf16[32,4096]{1,0:T(8,128)(2,1)S(1)}, u32[]{:S(2)}, u32[]{:S(2)}) collective-permute-start(bf16[32,4096]{1,0:T(8,128)(2,1)S(1)} %get-tuple-element.93.refs_3_), channel_id=1, source_target_pairs={{0,2},{2,4},{4,6},{6,7},{7,5},{5,3},{3,1},{1,0},{8,10},{10,12},{12... | collective-permute-start | bytes 786440 | tf_op jit(solution)/shard_map/right/ppermute | solution.py:220

commit v11 on v10

--- a/solution.py
+++ b/solution.py
@@ -92,7 +92,7 @@
         pieces = [jnp.concatenate(pieces, axis=0)]
     m, k = sum(p.shape[0] for p in pieces), pieces[0].shape[1]
     w = weights[0].shape[1]
-    tile = min(w, 512)
+    tile = min(w, 1024)
     count, halves = len(pieces), len(weights) // 2
     shapes = [jax.ShapeDtypeStruct((2, m, w), F32)] * halves
     scratch = [pltpu.VMEM((m, k), BF16)]
@@ -168,7 +168,7 @@
     m = sum(h.shape[0] for h, _ in halves)
     w = halves[0][0].shape[1]
     n = weights[0].shape[1]
-    tile = 512
+    tile = 1024
     if any(h.shape[0] % 16 for h, _ in halves):
         halves = [tuple(jnp.concatenate(hs, axis=0) for hs in zip(*halves))]
     count = len(halves)
@@ -206,6 +206,27 @@
         scratch_shapes=[pltpu.VMEM((m, 2 * w), BF16)],
         **params(3 << 20),
     )(*[h for pair in halves for h in pair], *map(in_vmem, weights), *after)
+
+
+def finish(*parts):
+    m, n = parts[0].shape
+
+    def body(*refs):
+        o_ref = refs[-1]
+        for i in range(2):
+            own, first, second = refs[3 * i : 3 * i + 3]
+            total = own[...] + first[...].astype(F32) + second[...].astype(F32)
+            o_ref[i * m : (i + 1) * m] = total.astype(BF16)
+
+    return pl.pallas_call(
+        body,
+        name="finish",
+        grid=(4,),
+        in_specs=[pl.BlockSpec((m, n // 4), lambda j: (0, j))] * 6,
+        out_specs=pl.BlockSpec((2 * m, n // 4), lambda j: (0, j)),
+        out_shape=jax.ShapeDtypeStruct((2 * m, n), BF16),
+        **params(4 << 20),
+    )(*parts)
 
 
 def make_shards(n):
@@ -319,9 +340,7 @@
             if d == half - 1:
                 after = [put_down(slice(0, -1), after)]
         a_l, a_r = gate(a_l, a_r, after=[b_l])
-        total_a = part["own", "a"] + a_l.astype(F32) + b_r.astype(F32)
-        total_b = part["own", "b"] + a_r.astype(F32) + b_l.astype(F32)
-        return jnp.concatenate([total_a, total_b], axis=0).astype(BF16)
+        return finish(part["own", "a"], a_l, b_r, part["own", "b"], a_r, b_l)
 
     return shards
 

time: 103 us -> 109 us (1.058)
  Pallas kernels: 44.8 us -> 49.3 us
  waiting for transfers between devices: 23.9 us -> 26 us
    pallas_call x5, Pallas kernels: 23.7 us -> 28.8 us  [gate_up(): pl.pallas_call(body, name='gate_up', in_specs=[VMEM] * (count + len(weigh...]
    ppermute x14, starting transfers between devices: 20.3 us -> 24.9 us  [right(): return lax.ppermute(x, 'gy', to_right)]
    ppermute x14, starting transfers between devices: 9.55 us -> 4.98 us  [left(): return lax.ppermute(x, 'gy', to_left)]
    ppermute x14, waiting for transfers between devices: 17.8 us -> 20.6 us  [left(): return lax.ppermute(x, 'gy', to_left)]
    pallas_call x3, Pallas kernels: 13.3 us -> 11 us  [down(): pl.pallas_call(body, name='down', in_specs=[VMEM] * (2 * count + 2) + [AN...]
    pallas_call x0 -> x1, Pallas kernels: none -> 1.61 us  [finish(): pl.pallas_call(body, name='finish', grid=(4,), in_specs=[pl.BlockSpec((m,...]
  transfers between devices with their start and end apart: 34 -> 34, of which waited for: 17 -> 19; matrix products, arithmetic and copies ran while one was open for 0% -> 0% of each run, Pallas kernels for 44% -> 44%
where the time goes in v11:
time: 109 us; the launch traced here: 108 us
  Pallas kernels  49.3 us (45%)
  starting transfers between devices  31.2 us (29%)
  waiting for transfers between devices  26 us (24%)
    pallas_call x5, Pallas kernels, gate_up(): pl.pallas_call(body, name='gate_up', in_specs=[VMEM] * (count + len(weigh...  28.8 us
    ppermute x14, starting transfers between devices, right(): return lax.ppermute(x, 'gy', to_right)  24.9 us
    ppermute x14, waiting for transfers between devices, left(): return lax.ppermute(x, 'gy', to_left)  20.6 us
    pallas_call x3, Pallas kernels, down(): pl.pallas_call(body, name='down', in_specs=[VMEM] * (2 * count + 2) + [AN...  11 us
    pallas_call x2, Pallas kernels, bring(): pl.pallas_call(body, name='bring', in_specs=[ANY] * (count + len(after)),...  6.96 us
    ppermute x14, starting transfers between devices, left(): return lax.ppermute(x, 'gy', to_left)  4.98 us
    ppermute x14, waiting for transfers between devices, right(): return lax.ppermute(x, 'gy', to_right)  4.69 us
  transfers between devices with their start and end apart: 34, of which 19 were waited for; matrix products, arithmetic and copies ran while one was open for 0% of the time, Pallas kernels for 44%

profile of v11, /device:TPU:0, one launch (start us, length us, event | category | flops | bytes accessed | tf_op | source)
XLA Modules:
  0.0 108.4 jit_solution(6781759705527509594)
XLA Ops:
  0.0 1.1 fusion.11
  1.1 3.1 %collective-permute-start = (bf16[32,4096]{1,0:T(8,128)(2,1)S(1)}, bf16[32,4096]{1,0:T(8,128)(2,1)S(1)}, u32[]{:S(2)}, u32[]{:S(2)}) collective-permute-start(bf16[32,4096]{1,0:T(8,128)(2,1)S(1)} %get-tuple-element.104.refs_0_), channel_id=1, source_target_pairs={{0,2},{2,4},{4,6},{6,7},{7,5},{5,3},{3,1},{1,0},{8,10},{10,12},{12... | collective-permute-start | bytes 786440 | tf_op jit(solution)/shard_map/farR1/ppermute | solution.py:241
  4.2 2.0 %collective-permute-start.2 = (bf16[32,4096]{1,0:T(8,128)(2,1)S(1)}, bf16[32,4096]{1,0:T(8,128)(2,1)S(1)}, u32[]{:S(2)}, u32[]{:S(2)}) collective-permute-start(bf16[32,4096]{1,0:T(8,128)(2,1)S(1)} %get-tuple-element.103.refs_1_), channel_id=1, source_target_pairs={{0,2},{2,4},{4,6},{6,7},{7,5},{5,3},{3,1},{1,0},{8,10},{10,12},{12... | collective-permute-start | bytes 786440 | tf_op jit(solution)/shard_map/nearR1/ppermute | solution.py:241
  6.2 3.5 %bring.2.refs_1_.refs_6_.refs_4_ = bf16[4096,1024]{1,0:T(8,128)(2,1)S(1)} custom-call(bf16[4096,2048]{1,0:T(8,128)(2,1)} %refs_8_.1), custom_call_target="tpu_custom_call" | custom-call | flops 1100000000 | tf_op jit(solution)/shard_map/bring/pallas_call | solution.py:79
  9.7 3.5 %bring.3.refs_2_.refs_7_.refs_5_ = bf16[4096,1024]{1,0:T(8,128)(2,1)S(1)} custom-call(bf16[4096,2048]{1,0:T(8,128)(2,1)} %refs_9_.1, bf16[4096,1024]{1,0:T(8,128)(2,1)S(1)} %bring.2.refs_1_.refs_6_.refs_4_), custom_call_target="tpu_custom_call" | custom-call | flops 1100000000 | tf_op jit(solution)/shard_map/bring/pallas_call | solution.py:79
  13.4 1.9 %collective-permute-start.4 = (bf16[32,4096]{1,0:T(8,128)(2,1)S(1)}, bf16[32,4096]{1,0:T(8,128)(2,1)S(1)}, u32[]{:S(2)}, u32[]{:S(2)}) collective-permute-start(bf16[32,4096]{1,0:T(8,128)(2,1)S(1)} %get-tuple-element.48.refs_2_), channel_id=1, source_target_pairs={{0,2},{2,4},{4,6},{6,7},{7,5},{5,3},{3,1},{1,0},{8,10},{10,12},{12... | collective-permute-start | bytes 786440 | tf_op jit(solution)/shard_map/farR2/ppermute | solution.py:241
  15.4 1.4 %collective-permute-done.2.refs_0_ = bf16[32,4096]{1,0:T(8,128)(2,1)S(1)} collective-permute-done((bf16[32,4096]{1,0:T(8,128)(2,1)S(1)}, bf16[32,4096]{1,0:T(8,128)(2,1)S(1)}, u32[]{:S(2)}, u32[]{:S(2)}) %collective-permute-start.2) | collective-permute-done | bytes 262176 | tf_op jit(solution)/shard_map/nearR1/ppermute | solution.py:241
  16.8 1.9 %collective-permute-done.3.refs_1_ = bf16[32,4096]{1,0:T(8,128)(2,1)S(1)} collective-permute-done((bf16[32,4096]{1,0:T(8,128)(2,1)S(1)}, bf16[32,4096]{1,0:T(8,128)(2,1)S(1)}, u32[]{:S(2)}, u32[]{:S(2)}) %collective-permute-start.3) | collective-permute-done | bytes 262176 | tf_op jit(solution)/shard_map/nearL1/ppermute | solution.py:245
  18.7 1.6 %collective-permute-start.8 = (bf16[32,4096]{1,0:T(8,128)(2,1)S(1)}, bf16[32,4096]{1,0:T(8,128)(2,1)S(1)}, u32[]{:S(2)}, u32[]{:S(2)}) collective-permute-start(bf16[32,4096]{1,0:T(8,128)(2,1)S(1)} %get-tuple-element.50.refs_4_.refs_10_), channel_id=1, source_target_pairs={{0,2},{2,4},{4,6},{6,7},{7,5},{5,3},{3,1},{1,0},{8,10},{10,12},{12... | collective-permute-start | bytes 786440 | tf_op jit(solution)/shard_map/nearR2/ppermute | solution.py:241
  20.7 9.2 %gate_up.5 = (f32[2,192,1024]{2,1,0:T(8,128)S(1)}, bf16[4096,1024]{1,0:T(8,128)(2,1)S(1)}, bf16[4096,1024]{1,0:T(8,128)(2,1)S(1)}) custom-call(bf16[32,4096]{1,0:T(8,128)(2,1)S(1)} %get-tuple-element.104.refs_0_, bf16[32,4096]{1,0:T(8,128)(2,1)S(1)} %get-tuple-element.103.refs_1_, bf16[32,4096]{1,0:T(8,128)(2,1)S(1)} %get-tuple-element.48.refs_2_, ...), custom_call_target="tpu_custom_call" | custom-call | flops 1100000000 | tf_op jit(solution)/shard_map/gate_up/pallas_call | solution.py:134
  29.9 1.6 %collective-permute-start.6 = (bf16[32,4096]{1,0:T(8,128)(2,1)S(1)}, bf16[32,4096]{1,0:T(8,128)(2,1)S(1)}, u32[]{:S(2)}, u32[]{:S(2)}) collective-permute-start(bf16[32,4096]{1,0:T(8,128)(2,1)S(1)} %get-tuple-element.55.refs_8_.refs_0_), channel_id=1, source_target_pairs={{0,2},{2,4},{4,6},{6,7},{7,5},{5,3},{3,1},{1,0},{8,10},{10,12},{12... | collective-permute-start | bytes 786440 | tf_op jit(solution)/shard_map/farR3/ppermute | solution.py:241
  31.6 0.5 collective-permute-start.7
  32.0 3.4 %gate_up.6.refs_2_.a_ref = f32[2,192,1024]{2,1,0:T(8,128)S(1)} custom-call(bf16[32,4096]{1,0:T(8,128)(2,1)S(1)} %get-tuple-element.104.refs_0_, bf16[32,4096]{1,0:T(8,128)(2,1)S(1)} %get-tuple-element.103.refs_1_, bf16[32,4096]{1,0:T(8,128)(2,1)S(1)} %get-tuple-element.48.refs_2_, bf16[32,4096]{1,0:T(8,128)(2,1)S(1)} %get-tuple-element.49.refs_3_, ...), custom_call_target="tpu_custom_call" | custom-call | flops 1100000000 | tf_op jit(solution)/shard_map/gate_up/pallas_call | solution.py:134
  35.5 1.6 %collective-permute-start.12 = (bf16[32,4096]{1,0:T(8,128)(2,1)S(1)}, bf16[32,4096]{1,0:T(8,128)(2,1)S(1)}, u32[]{:S(2)}, u32[]{:S(2)}) collective-permute-start(bf16[32,4096]{1,0:T(8,128)(2,1)S(1)} %get-tuple-element.57.refs_2_), channel_id=1, source_target_pairs={{0,2},{2,4},{4,6},{6,7},{7,5},{5,3},{3,1},{1,0},{8,10},{10,12},{12... | collective-permute-start | bytes 786440 | tf_op jit(solution)/shard_map/nearR3/ppermute | solution.py:241
  37.1 0.5 collective-permute-start.13
  37.6 0.7 collective-permute-done.6.refs_0_
  38.3 1.9 %collective-permute-done.7.refs_1_ = bf16[32,4096]{1,0:T(8,128)(2,1)S(1)} collective-permute-done((bf16[32,4096]{1,0:T(8,128)(2,1)S(1)}, bf16[32,4096]{1,0:T(8,128)(2,1)S(1)}, u32[]{:S(2)}, u32[]{:S(2)}) %collective-permute-start.7) | collective-permute-done | bytes 262176 | tf_op jit(solution)/shard_map/farL3/ppermute | solution.py:245
  40.2 1.6 %collective-permute-start.10 = (bf16[32,4096]{1,0:T(8,128)(2,1)S(1)}, bf16[32,4096]{1,0:T(8,128)(2,1)S(1)}, u32[]{:S(2)}, u32[]{:S(2)}) collective-permute-start(bf16[32,4096]{1,0:T(8,128)(2,1)S(1)} %get-tuple-element.58.refs_4_.refs_10_), channel_id=1, source_target_pairs={{0,2},{2,4},{4,6},{6,7},{7,5},{5,3},{3,1},{1,0},{8,10},{10,12},{12... | collective-permute-start | bytes 786440 | tf_op jit(solution)/shard_map/farR4/ppermute | solution.py:241
  42.2 6.7 %gate_up.7 = (f32[2,192,1024]{2,1,0:T(8,128)S(1)}, f32[2,192,1024]{2,1,0:T(8,128)S(1)}) custom-call(bf16[32,4096]{1,0:T(8,128)(2,1)S(1)} %get-tuple-element.55.refs_8_.refs_0_, bf16[32,4096]{1,0:T(8,128)(2,1)S(1)} %get-tuple-element.56.refs_1_, bf16[32,4096]{1,0:T(8,128)(2,1)S(1)} %get-tuple-element.57.refs_2_, ...), custom_call_target="tpu_custom_call" | custom-call | flops 1100000000 | tf_op jit(solution)/shard_map/gate_up/pallas_call | solution.py:134
  49.2 4.8 %gate_up.8 = (f32[2,128,1024]{2,1,0:T(8,128)S(1)}, bf16[2048,2048]{1,0:T(8,128)(2,1)S(1)}) custom-call(bf16[32,4096]{1,0:T(8,128)(2,1)S(1)} %get-tuple-element.62.refs_4_.refs_0_, bf16[32,4096]{1,0:T(8,128)(2,1)S(1)} %get-tuple-element.64.refs_1_, bf16[32,4096]{1,0:T(8,128)(2,1)S(1)} %get-tuple-element.65.refs_2_, ...), custom_call_target="tpu_custom_call" | custom-call | flops 1100000000 | tf_op jit(solution)/shard_map/gate_up/pallas_call | solution.py:134
  54.0 0.6 collective-permute-start.18
  54.6 4.8 %gate_up.9 = (f32[2,128,1024]{2,1,0:T(8,128)S(1)}, bf16[2048,2048]{1,0:T(8,128)(2,1)S(1)}) custom-call(bf16[32,4096]{1,0:T(8,128)(2,1)S(1)} %get-tuple-element.62.refs_4_.refs_0_, bf16[32,4096]{1,0:T(8,128)(2,1)S(1)} %get-tuple-element.64.refs_1_, bf16[32,4096]{1,0:T(8,128)(2,1)S(1)} %get-tuple-element.65.refs_2_, ...), custom_call_target="tpu_custom_call" | custom-call | flops 1100000000 | tf_op jit(solution)/shard_map/gate_up/pallas_call | solution.py:134
  59.7 0.5 collective-permute-start.19
  60.7 0.7 collective-permute-done.19.refs_1_
  61.4 2.9 %down.4 = (bf16[32,4096]{1,0:T(8,128)(2,1)S(1)}, bf16[32,4096]{1,0:T(8,128)(2,1)S(1)}, bf16[32,4096]{1,0:T(8,128)(2,1)S(1)}, bf16[32,4096]{1,0:T(8,128)(2,1)S(1)}) custom-call(bf16[128,1024]{1,0:T(8,128)(2,1)S(1)} %gated.5.refs_0_, bf16[128,1024]{1,0:T(8,128)(2,1)S(1)} %collective-permute-done.19.refs_1_, bf16[2048,2048]{1,0:T(8,128)(2,1)S(1)} %get-tuple-element.67.refs_2_, ...), custom_call_target="tpu_custom_call" | custom-call | tf_op jit(solution)/shard_map/down/pallas_call | solution.py:198
  64.3 0.5 collective-permute-start.22
  64.8 1.6 %collective-permute-start.23 = (bf16[32,4096]{1,0:T(8,128)(2,1)S(1)}, bf16[32,4096]{1,0:T(8,128)(2,1)S(1)}, u32[]{:S(2)}, u32[]{:S(2)}) collective-permute-start(bf16[32,4096]{1,0:T(8,128)(2,1)S(1)} %get-tuple-element.76), channel_id=1, source_target_pairs={{0,2},{2,4},{4,6},{6,7},{7,5},{5,3},{3,1},{1,0},{8,10},{10,12},{12... | collective-permute-start | bytes 786440 | tf_op jit(solution)/shard_map/right/ppermute | solution.py:241
  66.9 1.6 %collective-permute-start.21 = (bf16[32,4096]{1,0:T(8,128)(2,1)S(1)}, bf16[32,4096]{1,0:T(8,128)(2,1)S(1)}, u32[]{:S(2)}, u32[]{:S(2)}) collective-permute-start(bf16[32,4096]{1,0:T(8,128)(2,1)S(1)} %get-tuple-element.74), channel_id=1, source_target_pairs={{0,2},{2,4},{4,6},{6,7},{7,5},{5,3},{3,1},{1,0},{8,10},{10,12},{12... | collective-permute-start | bytes 786440 | tf_op jit(solution)/shard_map/right/ppermute | solution.py:241
  68.9 4.1 %down.3.refs_2_ = f32[192,4096]{1,0:T(8,128)S(1)} custom-call(bf16[192,1024]{1,0:T(8,128)(2,1)S(1)} %gated.4.refs_0_, bf16[192,1024]{1,0:T(8,128)(2,1)S(1)} %collective-permute-done.17.refs_1_, bf16[2048,2048]{1,0:T(8,128)(2,1)S(1)} %get-tuple-element.67.refs_2_, bf16[2048,2048]{1,0:T(8,128)(2,1)S(1)} %get-tuple-element.69.refs_3_), custom_call_target="tpu_custom_call" | custom-call | tf_op jit(solution)/shard_map/down/pallas_call | solution.py:198
  72.9 0.6 collective-permute-done.22.refs_0_
  73.5 0.5 collective-permute-done.23.refs_1_
  74.4 1.8 %collective-permute-start.25 = (bf16[32,4096]{1,0:T(8,128)(2,1)S(1)}, bf16[32,4096]{1,0:T(8,128)(2,1)S(1)}, u32[]{:S(2)}, u32[]{:S(2)}) collective-permute-start(bf16[32,4096]{1,0:T(8,128)(2,1)S(1)} %get-tuple-element.101.refs_3_), channel_id=1, source_target_pairs={{0,2},{2,4},{4,6},{6,7},{7,5},{5,3},{3,1},{1,0},{8,10},{10,12},{12... | collective-permute-start | bytes 786440 | tf_op jit(solution)/shard_map/right/ppermute | solution.py:241
  76.2 3.0 %collective-permute-done.20.refs_0_ = bf16[32,4096]{1,0:T(8,128)(2,1)S(1)} collective-permute-done((bf16[32,4096]{1,0:T(8,128)(2,1)S(1)}, bf16[32,4096]{1,0:T(8,128)(2,1)S(1)}, u32[]{:S(2)}, u32[]{:S(2)}) %collective-permute-start.20) | collective-permute-done | bytes 262176 | tf_op jit(solution)/shard_map/left/ppermute | solution.py:245
  79.1 0.5 collective-permute-done.21.refs_1_
  80.0 1.8 %collective-permute-start.29 = (bf16[32,4096]{1,0:T(8,128)(2,1)S(1)}, bf16[32,4096]{1,0:T(8,128)(2,1)S(1)}, u32[]{:S(2)}, u32[]{:S(2)}) collective-permute-start(bf16[32,4096]{1,0:T(8,128)(2,1)S(1)} %get-tuple-element.99.refs_5_), channel_id=1, source_target_pairs={{0,2},{2,4},{4,6},{6,7},{7,5},{5,3},{3,1},{1,0},{8,10},{10,12},{12... | collective-permute-start | bytes 786440 | tf_op jit(solution)/shard_map/right/ppermute | solution.py:241
  81.8 4.0 %down.5.refs_2_ = f32[192,4096]{1,0:T(8,128)S(1)} custom-call(bf16[192,1024]{1,0:T(8,128)(2,1)S(1)} %gated.3.refs_0_, bf16[192,1024]{1,0:T(8,128)(2,1)S(1)} %collective-permute-done.15.refs_1_, bf16[2048,2048]{1,0:T(8,128)(2,1)S(1)} %get-tuple-element.67.refs_2_, bf16[2048,2048]{1,0:T(8,128)(2,1)S(1)} %get-tuple-element.69.refs_3_, ...), custom_call_target="tpu_custom_call" | custom-call | tf_op jit(solution)/shard_map/down/pallas_call | solution.py:198
  86.3 1.8 %collective-permute-start.27 = (bf16[32,4096]{1,0:T(8,128)(2,1)S(1)}, bf16[32,4096]{1,0:T(8,128)(2,1)S(1)}, u32[]{:S(2)}, u32[]{:S(2)}) collective-permute-start(bf16[32,4096]{1,0:T(8,128)(2,1)S(1)} %get-tuple-element.97.refs_3_), channel_id=1, source_target_pairs={{0,2},{2,4},{4,6},{6,7},{7,5},{5,3},{3,1},{1,0},{8,10},{10,12},{12... | collective-permute-start | bytes 786440 | tf_op jit(solution)/shard_map/right/ppermute | solution.py:241
  88.0 2.3 %collective-permute-done.28.refs_0_ = bf16[32,4096]{1,0:T(8,128)(2,1)S(1)} collective-permute-done((bf16[32,4096]{1,0:T(8,128)(2,1)S(1)}, bf16[32,4096]{1,0:T(8,128)(2,1)S(1)}, u32[]{:S(2)}, u32[]{:S(2)}) %collective-permute-start.28) | collective-permute-done | bytes 262176 | tf_op jit(solution)/shard_map/left/ppermute | solution.py:245
  90.4 0.5 collective-permute-done.29.refs_1_
  91.3 1.8 %collective-permute-start.33 = (bf16[32,4096]{1,0:T(8,128)(2,1)S(1)}, bf16[32,4096]{1,0:T(8,128)(2,1)S(1)}, u32[]{:S(2)}, u32[]{:S(2)}) collective-permute-start(bf16[32,4096]{1,0:T(8,128)(2,1)S(1)} %get-tuple-element.95.refs_3_), channel_id=1, source_target_pairs={{0,2},{2,4},{4,6},{6,7},{7,5},{5,3},{3,1},{1,0},{8,10},{10,12},{12... | collective-permute-start | bytes 786440 | tf_op jit(solution)/shard_map/right/ppermute | solution.py:241
  93.0 3.0 %collective-permute-done.26.refs_0_ = bf16[32,4096]{1,0:T(8,128)(2,1)S(1)} collective-permute-done((bf16[32,4096]{1,0:T(8,128)(2,1)S(1)}, bf16[32,4096]{1,0:T(8,128)(2,1)S(1)}, u32[]{:S(2)}, u32[]{:S(2)}) %collective-permute-start.26) | collective-permute-done | bytes 262176 | tf_op jit(solution)/shard_map/left/ppermute | solution.py:245
  96.0 0.5 collective-permute-done.27.refs_1_
  96.7 0.8 collective-permute-start.30
  97.5 1.3 %collective-permute-start.31 = (bf16[32,4096]{1,0:T(8,128)(2,1)S(1)}, bf16[32,4096]{1,0:T(8,128)(2,1)S(1)}, u32[]{:S(2)}, u32[]{:S(2)}) collective-permute-start(bf16[32,4096]{1,0:T(8,128)(2,1)S(1)} %get-tuple-element.92.refs_3_), channel_id=1, source_target_pairs={{0,2},{2,4},{4,6},{6,7},{7,5},{5,3},{3,1},{1,0},{8,10},{10,12},{12... | collective-permute-start | bytes 786440 | tf_op jit(solution)/shard_map/right/ppermute | solution.py:241
  98.7 2.9 %collective-permute-done.32.refs_0_ = bf16[32,4096]{1,0:T(8,128)(2,1)S(1)} collective-permute-done((bf16[32,4096]{1,0:T(8,128)(2,1)S(1)}, bf16[32,4096]{1,0:T(8,128)(2,1)S(1)}, u32[]{:S(2)}, u32[]{:S(2)}) %collective-permute-start.32) | collective-permute-done | bytes 262176 | tf_op jit(solution)/shard_map/left/ppermute | solution.py:245
  101.6 0.5 collective-permute-done.33.refs_1_
  102.1 4.6 %collective-permute-done.30.refs_0_ = bf16[32,4096]{1,0:T(8,128)(2,1)S(1)} collective-permute-done((bf16[32,4096]{1,0:T(8,128)(2,1)S(1)}, bf16[32,4096]{1,0:T(8,128)(2,1)S(1)}, u32[]{:S(2)}, u32[]{:S(2)}) %collective-permute-start.30) | collective-permute-done | bytes 262176 | tf_op jit(solution)/shard_map/left/ppermute | solution.py:245
  106.8 1.6 %finish.1 = bf16[64,4096]{1,0:T(8,128)(2,1)} custom-call(f32[32,4096]{1,0:T(8,128)S(1)} %get-tuple-element.94.refs_0_, bf16[32,4096]{1,0:T(8,128)(2,1)S(1)} %get-tuple-element.88.refs_1_, bf16[32,4096]{1,0:T(8,128)(2,1)S(1)} %get-tuple-element.89.refs_2_, f32[32,4096]{1,0:T(8,128)S(1)} %get-tuple-element.91.refs_3_, ...), custom_call_target="tpu_custom_call" | custom-call | tf_op jit(solution)/shard_map/finish/pallas_call | solution.py:221
  (54 shorter events, 5.1 us)
Async XLA Ops:
  1.1 12.1 %collective-permute-start = (bf16[32,4096]{1,0:T(8,128)(2,1)S(1)}, bf16[32,4096]{1,0:T(8,128)(2,1)S(1)}, u32[]{:S(2)}, u32[]{:S(2)}) collective-permute-start(bf16[32,4096]{1,0:T(8,128)(2,1)S(1)} %get-tuple-element.104.refs_0_), channel_id=1, source_target_pairs={{0,2},{2,4},{4,6},{6,7},{7,5},{5,3},{3,1},{1,0},{8,10},{10,12},{12... | collective-permute-start | bytes 786440 | tf_op jit(solution)/shard_map/farR1/ppermute | solution.py:241
  4.1 9.2 %collective-permute-start.1 = (bf16[32,4096]{1,0:T(8,128)(2,1)S(1)}, bf16[32,4096]{1,0:T(8,128)(2,1)S(1)}, u32[]{:S(2)}, u32[]{:S(2)}) collective-permute-start(bf16[32,4096]{1,0:T(8,128)(2,1)S(1)} %get-tuple-element.103.refs_1_), channel_id=1, source_target_pairs={{2,0},{4,2},{6,4},{7,6},{5,7},{3,5},{1,3},{0,1},{10,8},{12,10},{14... | collective-permute-start | bytes 786440 | tf_op jit(solution)/shard_map/farL1/ppermute | solution.py:245
  4.2 12.7 %collective-permute-start.2 = (bf16[32,4096]{1,0:T(8,128)(2,1)S(1)}, bf16[32,4096]{1,0:T(8,128)(2,1)S(1)}, u32[]{:S(2)}, u32[]{:S(2)}) collective-permute-start(bf16[32,4096]{1,0:T(8,128)(2,1)S(1)} %get-tuple-element.103.refs_1_), channel_id=1, source_target_pairs={{0,2},{2,4},{4,6},{6,7},{7,5},{5,3},{3,1},{1,0},{8,10},{10,12},{12... | collective-permute-start | bytes 786440 | tf_op jit(solution)/shard_map/nearR1/ppermute | solution.py:241
  6.2 12.5 %collective-permute-start.3 = (bf16[32,4096]{1,0:T(8,128)(2,1)S(1)}, bf16[32,4096]{1,0:T(8,128)(2,1)S(1)}, u32[]{:S(2)}, u32[]{:S(2)}) collective-permute-start(bf16[32,4096]{1,0:T(8,128)(2,1)S(1)} %get-tuple-element.104.refs_0_), channel_id=1, source_target_pairs={{2,0},{4,2},{6,4},{7,6},{5,7},{3,5},{1,3},{0,1},{10,8},{12,10},{14... | collective-permute-start | bytes 786440 | tf_op jit(solution)/shard_map/nearL1/ppermute | solution.py:245
  13.4 16.5 %collective-permute-start.4 = (bf16[32,4096]{1,0:T(8,128)(2,1)S(1)}, bf16[32,4096]{1,0:T(8,128)(2,1)S(1)}, u32[]{:S(2)}, u32[]{:S(2)}) collective-permute-start(bf16[32,4096]{1,0:T(8,128)(2,1)S(1)} %get-tuple-element.48.refs_2_), channel_id=1, source_target_pairs={{0,2},{2,4},{4,6},{6,7},{7,5},{5,3},{3,1},{1,0},{8,10},{10,12},{12... | collective-permute-start | bytes 786440 | tf_op jit(solution)/shard_map/farR2/ppermute | solution.py:241
  15.3 14.7 %collective-permute-start.5 = (bf16[32,4096]{1,0:T(8,128)(2,1)S(1)}, bf16[32,4096]{1,0:T(8,128)(2,1)S(1)}, u32[]{:S(2)}, u32[]{:S(2)}) collective-permute-start(bf16[32,4096]{1,0:T(8,128)(2,1)S(1)} %get-tuple-element.49.refs_3_), channel_id=1, source_target_pairs={{2,0},{4,2},{6,4},{7,6},{5,7},{3,5},{1,3},{0,1},{10,8},{12,10},{14... | collective-permute-start | bytes 786440 | tf_op jit(solution)/shard_map/farL2/ppermute | solution.py:245
  18.7 16.7 %collective-permute-start.8 = (bf16[32,4096]{1,0:T(8,128)(2,1)S(1)}, bf16[32,4096]{1,0:T(8,128)(2,1)S(1)}, u32[]{:S(2)}, u32[]{:S(2)}) collective-permute-start(bf16[32,4096]{1,0:T(8,128)(2,1)S(1)} %get-tuple-element.50.refs_4_.refs_10_), channel_id=1, source_target_pairs={{0,2},{2,4},{4,6},{6,7},{7,5},{5,3},{3,1},{1,0},{8,10},{10,12},{12... | collective-permute-start | bytes 786440 | tf_op jit(solution)/shard_map/nearR2/ppermute | solution.py:241
  20.3 15.2 %collective-permute-start.9 = (bf16[32,4096]{1,0:T(8,128)(2,1)S(1)}, bf16[32,4096]{1,0:T(8,128)(2,1)S(1)}, u32[]{:S(2)}, u32[]{:S(2)}) collective-permute-start(bf16[32,4096]{1,0:T(8,128)(2,1)S(1)} %get-tuple-element.51.refs_5_), channel_id=1, source_target_pairs={{2,0},{4,2},{6,4},{7,6},{5,7},{3,5},{1,3},{0,1},{10,8},{12,10},{14... | collective-permute-start | bytes 786440 | tf_op jit(solution)/shard_map/nearL2/ppermute | solution.py:245
  29.9 8.3 %collective-permute-start.6 = (bf16[32,4096]{1,0:T(8,128)(2,1)S(1)}, bf16[32,4096]{1,0:T(8,128)(2,1)S(1)}, u32[]{:S(2)}, u32[]{:S(2)}) collective-permute-start(bf16[32,4096]{1,0:T(8,128)(2,1)S(1)} %get-tuple-element.55.refs_8_.refs_0_), channel_id=1, source_target_pairs={{0,2},{2,4},{4,6},{6,7},{7,5},{5,3},{3,1},{1,0},{8,10},{10,12},{12... | collective-permute-start | bytes 786440 | tf_op jit(solution)/shard_map/farR3/ppermute | solution.py:241
  31.6 8.6 %collective-permute-start.7 = (bf16[32,4096]{1,0:T(8,128)(2,1)S(1)}, bf16[32,4096]{1,0:T(8,128)(2,1)S(1)}, u32[]{:S(2)}, u32[]{:S(2)}) collective-permute-start(bf16[32,4096]{1,0:T(8,128)(2,1)S(1)} %get-tuple-element.56.refs_1_), channel_id=1, source_target_pairs={{2,0},{4,2},{6,4},{7,6},{5,7},{3,5},{1,3},{0,1},{10,8},{12,10},{14... | collective-permute-start | bytes 786440 | tf_op jit(solution)/shard_map/farL3/ppermute | solution.py:245
  35.5 13.4 %collective-permute-start.12 = (bf16[32,4096]{1,0:T(8,128)(2,1)S(1)}, bf16[32,4096]{1,0:T(8,128)(2,1)S(1)}, u32[]{:S(2)}, u32[]{:S(2)}) collective-permute-start(bf16[32,4096]{1,0:T(8,128)(2,1)S(1)} %get-tuple-element.57.refs_2_), channel_id=1, source_target_pairs={{0,2},{2,4},{4,6},{6,7},{7,5},{5,3},{3,1},{1,0},{8,10},{10,12},{12... | collective-permute-start | bytes 786440 | tf_op jit(solution)/shard_map/nearR3/ppermute | solution.py:241
  37.1 11.8 %collective-permute-start.13 = (bf16[32,4096]{1,0:T(8,128)(2,1)S(1)}, bf16[32,4096]{1,0:T(8,128)(2,1)S(1)}, u32[]{:S(2)}, u32[]{:S(2)}) collective-permute-start(bf16[32,4096]{1,0:T(8,128)(2,1)S(1)} %get-tuple-element.60.refs_3_), channel_id=1, source_target_pairs={{2,0},{4,2},{6,4},{7,6},{5,7},{3,5},{1,3},{0,1},{10,8},{12,10},{14... | collective-permute-start | bytes 786440 | tf_op jit(solution)/shard_map/nearL3/ppermute | solution.py:245
  40.2 8.7 %collective-permute-start.10 = (bf16[32,4096]{1,0:T(8,128)(2,1)S(1)}, bf16[32,4096]{1,0:T(8,128)(2,1)S(1)}, u32[]{:S(2)}, u32[]{:S(2)}) collective-permute-start(bf16[32,4096]{1,0:T(8,128)(2,1)S(1)} %get-tuple-element.58.refs_4_.refs_10_), channel_id=1, source_target_pairs={{0,2},{2,4},{4,6},{6,7},{7,5},{5,3},{3,1},{1,0},{8,10},{10,12},{12... | collective-permute-start | bytes 786440 | tf_op jit(solution)/shard_map/farR4/ppermute | solution.py:241
  41.7 7.4 %collective-permute-start.11 = (bf16[32,4096]{1,0:T(8,128)(2,1)S(1)}, bf16[32,4096]{1,0:T(8,128)(2,1)S(1)}, u32[]{:S(2)}, u32[]{:S(2)}) collective-permute-start(bf16[32,4096]{1,0:T(8,128)(2,1)S(1)} %get-tuple-element.59.refs_5_), channel_id=1, source_target_pairs={{2,0},{4,2},{6,4},{7,6},{5,7},{3,5},{1,3},{0,1},{10,8},{12,10},{14... | collective-permute-start | bytes 786440 | tf_op jit(solution)/shard_map/farL4/ppermute | solution.py:245
  49.2 11.1 %collective-permute-start.16 = (f32[2,192,1024]{2,1,0:T(8,128)S(1)}, f32[2,192,1024]{2,1,0:T(8,128)S(1)}, u32[]{:S(2)}, u32[]{:S(2)}) collective-permute-start(f32[2,192,1024]{2,1,0:T(8,128)S(1)} %get-tuple-element.71), channel_id=1, source_target_pairs={{0,8},{8,0},{1,9},{9,1},{2,10},{10,2},{3,11},{11,3},{4,12},{12,4},... | collective-permute-start | bytes 4718600 | tf_op jit(solution)/shard_map/swap/ppermute | solution.py:249
  54.0 5.5 %collective-permute-start.18 = (f32[2,128,1024]{2,1,0:T(8,128)S(1)}, f32[2,128,1024]{2,1,0:T(8,128)S(1)}, u32[]{:S(2)}, u32[]{:S(2)}) collective-permute-start(f32[2,128,1024]{2,1,0:T(8,128)S(1)} %get-tuple-element.68.refs_7_), channel_id=1, source_target_pairs={{0,8},{8,0},{1,9},{9,1},{2,10},{10,2},{3,11},{11,3},{4,12},{12,4},... | collective-permute-start | bytes 3145736 | tf_op jit(solution)/shard_map/swap/ppermute | solution.py:249
  54.6 12.3 %collective-permute-start.14 = (f32[2,192,1024]{2,1,0:T(8,128)S(1)}, f32[2,192,1024]{2,1,0:T(8,128)S(1)}, u32[]{:S(2)}, u32[]{:S(2)}) collective-permute-start(f32[2,192,1024]{2,1,0:T(8,128)S(1)} %get-tuple-element.63), channel_id=1, source_target_pairs={{0,8},{8,0},{1,9},{9,1},{2,10},{10,2},{3,11},{11,3},{4,12},{12,4},... | collective-permute-start | bytes 4718600 | tf_op jit(solution)/shard_map/swap/ppermute | solution.py:249
  59.7 1.7 %collective-permute-start.19 = (bf16[128,1024]{1,0:T(8,128)(2,1)S(1)}, bf16[128,1024]{1,0:T(8,128)(2,1)S(1)}, u32[]{:S(2)}, u32[]{:S(2)}) collective-permute-start(bf16[128,1024]{1,0:T(8,128)(2,1)S(1)} %gated.5.refs_0_), channel_id=1, source_target_pairs={{0,8},{8,0},{1,9},{9,1},{2,10},{10,2},{3,11},{11,3},{4,12},{12,4},... | collective-permute-start | bytes 786440 | tf_op jit(solution)/shard_map/swap/ppermute | solution.py:249
  60.5 8.2 %collective-permute-start.17 = (bf16[192,1024]{1,0:T(8,128)(2,1)S(1)}, bf16[192,1024]{1,0:T(8,128)(2,1)S(1)}, u32[]{:S(2)}, u32[]{:S(2)}) collective-permute-start(bf16[192,1024]{1,0:T(8,128)(2,1)S(1)} %gated.4.refs_0_), channel_id=1, source_target_pairs={{0,8},{8,0},{1,9},{9,1},{2,10},{10,2},{3,11},{11,3},{4,12},{12,4},... | collective-permute-start | bytes 1179656 | tf_op jit(solution)/shard_map/swap/ppermute | solution.py:249
  64.3 9.2 %collective-permute-start.22 = (bf16[32,4096]{1,0:T(8,128)(2,1)S(1)}, bf16[32,4096]{1,0:T(8,128)(2,1)S(1)}, u32[]{:S(2)}, u32[]{:S(2)}) collective-permute-start(bf16[32,4096]{1,0:T(8,128)(2,1)S(1)} %get-tuple-element.75), channel_id=1, source_target_pairs={{2,0},{4,2},{6,4},{7,6},{5,7},{3,5},{1,3},{0,1},{10,8},{12,10},{14... | collective-permute-start | bytes 786440 | tf_op jit(solution)/shard_map/left/ppermute | solution.py:245
  64.8 9.2 %collective-permute-start.23 = (bf16[32,4096]{1,0:T(8,128)(2,1)S(1)}, bf16[32,4096]{1,0:T(8,128)(2,1)S(1)}, u32[]{:S(2)}, u32[]{:S(2)}) collective-permute-start(bf16[32,4096]{1,0:T(8,128)(2,1)S(1)} %get-tuple-element.76), channel_id=1, source_target_pairs={{0,2},{2,4},{4,6},{6,7},{7,5},{5,3},{3,1},{1,0},{8,10},{10,12},{12... | collective-permute-start | bytes 786440 | tf_op jit(solution)/shard_map/right/ppermute | solution.py:241
  66.4 12.7 %collective-permute-start.20 = (bf16[32,4096]{1,0:T(8,128)(2,1)S(1)}, bf16[32,4096]{1,0:T(8,128)(2,1)S(1)}, u32[]{:S(2)}, u32[]{:S(2)}) collective-permute-start(bf16[32,4096]{1,0:T(8,128)(2,1)S(1)} %get-tuple-element.73), channel_id=1, source_target_pairs={{2,0},{4,2},{6,4},{7,6},{5,7},{3,5},{1,3},{0,1},{10,8},{12,10},{14... | collective-permute-start | bytes 786440 | tf_op jit(solution)/shard_map/left/ppermute | solution.py:245
  66.9 12.8 %collective-permute-start.21 = (bf16[32,4096]{1,0:T(8,128)(2,1)S(1)}, bf16[32,4096]{1,0:T(8,128)(2,1)S(1)}, u32[]{:S(2)}, u32[]{:S(2)}) collective-permute-start(bf16[32,4096]{1,0:T(8,128)(2,1)S(1)} %get-tuple-element.74), channel_id=1, source_target_pairs={{0,2},{2,4},{4,6},{6,7},{7,5},{5,3},{3,1},{1,0},{8,10},{10,12},{12... | collective-permute-start | bytes 786440 | tf_op jit(solution)/shard_map/right/ppermute | solution.py:241
  68.8 13.0 %collective-permute-start.15 = (bf16[192,1024]{1,0:T(8,128)(2,1)S(1)}, bf16[192,1024]{1,0:T(8,128)(2,1)S(1)}, u32[]{:S(2)}, u32[]{:S(2)}) collective-permute-start(bf16[192,1024]{1,0:T(8,128)(2,1)S(1)} %gated.3.refs_0_), channel_id=1, source_target_pairs={{0,8},{8,0},{1,9},{9,1},{2,10},{10,2},{3,11},{11,3},{4,12},{12,4},... | collective-permute-start | bytes 1179656 | tf_op jit(solution)/shard_map/swap/ppermute | solution.py:249
  74.1 11.7 %collective-permute-start.24 = (bf16[32,4096]{1,0:T(8,128)(2,1)S(1)}, bf16[32,4096]{1,0:T(8,128)(2,1)S(1)}, u32[]{:S(2)}, u32[]{:S(2)}) collective-permute-start(bf16[32,4096]{1,0:T(8,128)(2,1)S(1)} %get-tuple-element.102.refs_2_), channel_id=1, source_target_pairs={{2,0},{4,2},{6,4},{7,6},{5,7},{3,5},{1,3},{0,1},{10,8},{12,10},{14... | collective-permute-start | bytes 786440 | tf_op jit(solution)/shard_map/left/ppermute | solution.py:245
  74.4 11.4 %collective-permute-start.25 = (bf16[32,4096]{1,0:T(8,128)(2,1)S(1)}, bf16[32,4096]{1,0:T(8,128)(2,1)S(1)}, u32[]{:S(2)}, u32[]{:S(2)}) collective-permute-start(bf16[32,4096]{1,0:T(8,128)(2,1)S(1)} %get-tuple-element.101.refs_3_), channel_id=1, source_target_pairs={{0,2},{2,4},{4,6},{6,7},{7,5},{5,3},{3,1},{1,0},{8,10},{10,12},{12... | collective-permute-start | bytes 786440 | tf_op jit(solution)/shard_map/right/ppermute | solution.py:241
  79.7 10.7 %collective-permute-start.28 = (bf16[32,4096]{1,0:T(8,128)(2,1)S(1)}, bf16[32,4096]{1,0:T(8,128)(2,1)S(1)}, u32[]{:S(2)}, u32[]{:S(2)}) collective-permute-start(bf16[32,4096]{1,0:T(8,128)(2,1)S(1)} %get-tuple-element.100.refs_4_), channel_id=1, source_target_pairs={{2,0},{4,2},{6,4},{7,6},{5,7},{3,5},{1,3},{0,1},{10,8},{12,10},{14... | collective-permute-start | bytes 786440 | tf_op jit(solution)/shard_map/left/ppermute | solution.py:245
  80.0 10.8 %collective-permute-start.29 = (bf16[32,4096]{1,0:T(8,128)(2,1)S(1)}, bf16[32,4096]{1,0:T(8,128)(2,1)S(1)}, u32[]{:S(2)}, u32[]{:S(2)}) collective-permute-start(bf16[32,4096]{1,0:T(8,128)(2,1)S(1)} %get-tuple-element.99.refs_5_), channel_id=1, source_target_pairs={{0,2},{2,4},{4,6},{6,7},{7,5},{5,3},{3,1},{1,0},{8,10},{10,12},{12... | collective-permute-start | bytes 786440 | tf_op jit(solution)/shard_map/right/ppermute | solution.py:241
  86.0 10.0 %collective-permute-start.26 = (bf16[32,4096]{1,0:T(8,128)(2,1)S(1)}, bf16[32,4096]{1,0:T(8,128)(2,1)S(1)}, u32[]{:S(2)}, u32[]{:S(2)}) collective-permute-start(bf16[32,4096]{1,0:T(8,128)(2,1)S(1)} %get-tuple-element.98.refs_2_), channel_id=1, source_target_pairs={{2,0},{4,2},{6,4},{7,6},{5,7},{3,5},{1,3},{0,1},{10,8},{12,10},{14... | collective-permute-start | bytes 786440 | tf_op jit(solution)/shard_map/left/ppermute | solution.py:245
  86.3 10.2 %collective-permute-start.27 = (bf16[32,4096]{1,0:T(8,128)(2,1)S(1)}, bf16[32,4096]{1,0:T(8,128)(2,1)S(1)}, u32[]{:S(2)}, u32[]{:S(2)}) collective-permute-start(bf16[32,4096]{1,0:T(8,128)(2,1)S(1)} %get-tuple-element.97.refs_3_), channel_id=1, source_target_pairs={{0,2},{2,4},{4,6},{6,7},{7,5},{5,3},{3,1},{1,0},{8,10},{10,12},{12... | collective-permute-start | bytes 786440 | tf_op jit(solution)/shard_map/right/ppermute | solution.py:241
  90.9 10.7 %collective-permute-start.32 = (bf16[32,4096]{1,0:T(8,128)(2,1)S(1)}, bf16[32,4096]{1,0:T(8,128)(2,1)S(1)}, u32[]{:S(2)}, u32[]{:S(2)}) collective-permute-start(bf16[32,4096]{1,0:T(8,128)(2,1)S(1)} %get-tuple-element.96.refs_2_), channel_id=1, source_target_pairs={{2,0},{4,2},{6,4},{7,6},{5,7},{3,5},{1,3},{0,1},{10,8},{12,10},{14... | collective-permute-start | bytes 786440 | tf_op jit(solution)/shard_map/left/ppermute | solution.py:245
  91.3 10.8 %collective-permute-start.33 = (bf16[32,4096]{1,0:T(8,128)(2,1)S(1)}, bf16[32,4096]{1,0:T(8,128)(2,1)S(1)}, u32[]{:S(2)}, u32[]{:S(2)}) collective-permute-start(bf16[32,4096]{1,0:T(8,128)(2,1)S(1)} %get-tuple-element.95.refs_3_), channel_id=1, source_target_pairs={{0,2},{2,4},{4,6},{6,7},{7,5},{5,3},{3,1},{1,0},{8,10},{10,12},{12... | collective-permute-start | bytes 786440 | tf_op jit(solution)/shard_map/right/ppermute | solution.py:241
  96.7 10.0 %collective-permute-start.30 = (bf16[32,4096]{1,0:T(8,128)(2,1)S(1)}, bf16[32,4096]{1,0:T(8,128)(2,1)S(1)}, u32[]{:S(2)}, u32[]{:S(2)}) collective-permute-start(bf16[32,4096]{1,0:T(8,128)(2,1)S(1)} %get-tuple-element.93.refs_2_), channel_id=1, source_target_pairs={{2,0},{4,2},{6,4},{7,6},{5,7},{3,5},{1,3},{0,1},{10,8},{12,10},{14... | collective-permute-start | bytes 786440 | tf_op jit(solution)/shard_map/left/ppermute | solution.py:245
  97.5 9.4 %collective-permute-start.31 = (bf16[32,4096]{1,0:T(8,128)(2,1)S(1)}, bf16[32,4096]{1,0:T(8,128)(2,1)S(1)}, u32[]{:S(2)}, u32[]{:S(2)}) collective-permute-start(bf16[32,4096]{1,0:T(8,128)(2,1)S(1)} %get-tuple-element.92.refs_3_), channel_id=1, source_target_pairs={{0,2},{2,4},{4,6},{6,7},{7,5},{5,3},{3,1},{1,0},{8,10},{10,12},{12... | collective-permute-start | bytes 786440 | tf_op jit(solution)/shard_map/right/ppermute | solution.py:241

commit v12 on v10

--- a/solution.py
+++ b/solution.py
@@ -92,7 +92,7 @@
         pieces = [jnp.concatenate(pieces, axis=0)]
     m, k = sum(p.shape[0] for p in pieces), pieces[0].shape[1]
     w = weights[0].shape[1]
-    tile = min(w, 512)
+    tile = min(w, 512 if load else 1024)
     count, halves = len(pieces), len(weights) // 2
     shapes = [jax.ShapeDtypeStruct((2, m, w), F32)] * halves
     scratch = [pltpu.VMEM((m, k), BF16)]
@@ -168,7 +168,7 @@
     m = sum(h.shape[0] for h, _ in halves)
     w = halves[0][0].shape[1]
     n = weights[0].shape[1]
-    tile = 512
+    tile = 1024
     if any(h.shape[0] % 16 for h, _ in halves):
         halves = [tuple(jnp.concatenate(hs, axis=0) for hs in zip(*halves))]
     count = len(halves)

time: 103 us -> 102 us (level)
  Pallas kernels: 44.8 us -> 41.8 us
  waiting for transfers between devices: 23.9 us -> 25.9 us
    pallas_call x3, Pallas kernels: 13.3 us -> 11 us  [down(): pl.pallas_call(body, name='down', in_specs=[VMEM] * (2 * count + 2) + [AN...]
    ppermute x14, waiting for transfers between devices: 17.8 us -> 20 us  [left(): return lax.ppermute(x, 'gy', to_left)]
  transfers between devices with their start and end apart: 34 -> 34, of which waited for: 17 -> 19; matrix products, arithmetic and copies ran while one was open for 0% -> 0% of each run, Pallas kernels for 44% -> 41%
where the time goes in v12:
time: 102 us
  Pallas kernels  41.8 us (41%)
  starting transfers between devices  31.4 us (31%)
  waiting for transfers between devices  25.9 us (25%)
  other arithmetic  1.44 us (1%)
  local copies, waits for them, and re-layouts  1.06 us (1%)
    pallas_call x5, Pallas kernels, gate_up(): pl.pallas_call(body, name='gate_up', in_specs=[VMEM] * (count + len(weigh...  23 us
    ppermute x14, starting transfers between devices, right(): return lax.ppermute(x, 'gy', to_right)  20.4 us
    ppermute x14, waiting for transfers between devices, left(): return lax.ppermute(x, 'gy', to_left)  20 us
    pallas_call x3, Pallas kernels, down(): pl.pallas_call(body, name='down', in_specs=[VMEM] * (2 * count + 2) + [AN...  11 us
    ppermute x14, starting transfers between devices, left(): return lax.ppermute(x, 'gy', to_left)  9.72 us
    pallas_call x2, Pallas kernels, bring(): pl.pallas_call(body, name='bring', in_specs=[ANY] * (count + len(after)),...  6.96 us
    ppermute x14, waiting for transfers between devices, right(): return lax.ppermute(x, 'gy', to_right)  5.19 us
  transfers between devices with their start and end apart: 34, of which 19 were waited for; matrix products, arithmetic and copies ran while one was open for 0% of the time, Pallas kernels for 41%

profile of v12, /device:TPU:0, one launch (start us, length us, event | category | flops | bytes accessed | tf_op | source)
XLA Modules:
  0.0 102.0 jit_solution(7719637815780707136)
XLA Ops:
  0.0 1.1 %fusion.14 = (bf16[32,4096]{1,0:T(8,128)(2,1)S(1)}, bf16[32,4096]{1,0:T(8,128)(2,1)S(1)}) fusion(bf16[64,4096]{1,0:T(8,128)(2,1)} %param.4), kind=kLoop, calls=%fused_computation.27 | loop fusion | bytes 1048576 | tf_op jit(solution)/shard_map/slice | solution.py:237
  1.1 3.1 %collective-permute-start = (bf16[32,4096]{1,0:T(8,128)(2,1)S(1)}, bf16[32,4096]{1,0:T(8,128)(2,1)S(1)}, u32[]{:S(2)}, u32[]{:S(2)}) collective-permute-start(bf16[32,4096]{1,0:T(8,128)(2,1)S(1)} %get-tuple-element.104.refs_0_), channel_id=1, source_target_pairs={{0,2},{2,4},{4,6},{6,7},{7,5},{5,3},{3,1},{1,0},{8,10},{10,12},{12... | collective-permute-start | bytes 786440 | tf_op jit(solution)/shard_map/farR1/ppermute | solution.py:220
  4.2 2.0 %collective-permute-start.2 = (bf16[32,4096]{1,0:T(8,128)(2,1)S(1)}, bf16[32,4096]{1,0:T(8,128)(2,1)S(1)}, u32[]{:S(2)}, u32[]{:S(2)}) collective-permute-start(bf16[32,4096]{1,0:T(8,128)(2,1)S(1)} %get-tuple-element.103.refs_1_), channel_id=1, source_target_pairs={{0,2},{2,4},{4,6},{6,7},{7,5},{5,3},{3,1},{1,0},{8,10},{10,12},{12... | collective-permute-start | bytes 786440 | tf_op jit(solution)/shard_map/nearR1/ppermute | solution.py:220
  6.2 3.5 %bring.2.refs_1_.refs_6_.refs_4_ = bf16[4096,1024]{1,0:T(8,128)(2,1)S(1)} custom-call(bf16[4096,2048]{1,0:T(8,128)(2,1)} %refs_8_.1), custom_call_target="tpu_custom_call" | custom-call | flops 1100000000 | tf_op jit(solution)/shard_map/bring/pallas_call | solution.py:79
  9.7 3.5 %bring.3.refs_2_.refs_7_.refs_5_ = bf16[4096,1024]{1,0:T(8,128)(2,1)S(1)} custom-call(bf16[4096,2048]{1,0:T(8,128)(2,1)} %refs_9_.1, bf16[4096,1024]{1,0:T(8,128)(2,1)S(1)} %bring.2.refs_1_.refs_6_.refs_4_), custom_call_target="tpu_custom_call" | custom-call | flops 1100000000 | tf_op jit(solution)/shard_map/bring/pallas_call | solution.py:79
  13.4 1.9 %collective-permute-start.4 = (bf16[32,4096]{1,0:T(8,128)(2,1)S(1)}, bf16[32,4096]{1,0:T(8,128)(2,1)S(1)}, u32[]{:S(2)}, u32[]{:S(2)}) collective-permute-start(bf16[32,4096]{1,0:T(8,128)(2,1)S(1)} %get-tuple-element.48.refs_2_), channel_id=1, source_target_pairs={{0,2},{2,4},{4,6},{6,7},{7,5},{5,3},{3,1},{1,0},{8,10},{10,12},{12... | collective-permute-start | bytes 786440 | tf_op jit(solution)/shard_map/farR2/ppermute | solution.py:220
  15.4 1.4 %collective-permute-done.2.refs_0_ = bf16[32,4096]{1,0:T(8,128)(2,1)S(1)} collective-permute-done((bf16[32,4096]{1,0:T(8,128)(2,1)S(1)}, bf16[32,4096]{1,0:T(8,128)(2,1)S(1)}, u32[]{:S(2)}, u32[]{:S(2)}) %collective-permute-start.2) | collective-permute-done | bytes 262176 | tf_op jit(solution)/shard_map/nearR1/ppermute | solution.py:220
  16.8 1.9 %collective-permute-done.3.refs_1_ = bf16[32,4096]{1,0:T(8,128)(2,1)S(1)} collective-permute-done((bf16[32,4096]{1,0:T(8,128)(2,1)S(1)}, bf16[32,4096]{1,0:T(8,128)(2,1)S(1)}, u32[]{:S(2)}, u32[]{:S(2)}) %collective-permute-start.3) | collective-permute-done | bytes 262176 | tf_op jit(solution)/shard_map/nearL1/ppermute | solution.py:224
  18.7 1.6 %collective-permute-start.8 = (bf16[32,4096]{1,0:T(8,128)(2,1)S(1)}, bf16[32,4096]{1,0:T(8,128)(2,1)S(1)}, u32[]{:S(2)}, u32[]{:S(2)}) collective-permute-start(bf16[32,4096]{1,0:T(8,128)(2,1)S(1)} %get-tuple-element.50.refs_4_.refs_10_), channel_id=1, source_target_pairs={{0,2},{2,4},{4,6},{6,7},{7,5},{5,3},{3,1},{1,0},{8,10},{10,12},{12... | collective-permute-start | bytes 786440 | tf_op jit(solution)/shard_map/nearR2/ppermute | solution.py:220
  20.7 5.9 %gate_up.5 = (f32[2,192,1024]{2,1,0:T(8,128)S(1)}, bf16[4096,1024]{1,0:T(8,128)(2,1)S(1)}, bf16[4096,1024]{1,0:T(8,128)(2,1)S(1)}) custom-call(bf16[32,4096]{1,0:T(8,128)(2,1)S(1)} %get-tuple-element.104.refs_0_, bf16[32,4096]{1,0:T(8,128)(2,1)S(1)} %get-tuple-element.103.refs_1_, bf16[32,4096]{1,0:T(8,128)(2,1)S(1)} %get-tuple-element.48.refs_2_, ...), custom_call_target="tpu_custom_call" | custom-call | flops 1100000000 | tf_op jit(solution)/shard_map/gate_up/pallas_call | solution.py:134
  26.7 1.6 %collective-permute-start.6 = (bf16[32,4096]{1,0:T(8,128)(2,1)S(1)}, bf16[32,4096]{1,0:T(8,128)(2,1)S(1)}, u32[]{:S(2)}, u32[]{:S(2)}) collective-permute-start(bf16[32,4096]{1,0:T(8,128)(2,1)S(1)} %get-tuple-element.55.refs_8_.refs_0_), channel_id=1, source_target_pairs={{0,2},{2,4},{4,6},{6,7},{7,5},{5,3},{3,1},{1,0},{8,10},{10,12},{12... | collective-permute-start | bytes 786440 | tf_op jit(solution)/shard_map/farR3/ppermute | solution.py:220
  28.8 3.4 %gate_up.6.refs_2_.a_ref = f32[2,192,1024]{2,1,0:T(8,128)S(1)} custom-call(bf16[32,4096]{1,0:T(8,128)(2,1)S(1)} %get-tuple-element.104.refs_0_, bf16[32,4096]{1,0:T(8,128)(2,1)S(1)} %get-tuple-element.103.refs_1_, bf16[32,4096]{1,0:T(8,128)(2,1)S(1)} %get-tuple-element.48.refs_2_, bf16[32,4096]{1,0:T(8,128)(2,1)S(1)} %get-tuple-element.49.refs_3_, ...), custom_call_target="tpu_custom_call" | custom-call | flops 1100000000 | tf_op jit(solution)/shard_map/gate_up/pallas_call | solution.py:134
  32.2 1.6 %collective-permute-start.12 = (bf16[32,4096]{1,0:T(8,128)(2,1)S(1)}, bf16[32,4096]{1,0:T(8,128)(2,1)S(1)}, u32[]{:S(2)}, u32[]{:S(2)}) collective-permute-start(bf16[32,4096]{1,0:T(8,128)(2,1)S(1)} %get-tuple-element.57.refs_2_), channel_id=1, source_target_pairs={{0,2},{2,4},{4,6},{6,7},{7,5},{5,3},{3,1},{1,0},{8,10},{10,12},{12... | collective-permute-start | bytes 786440 | tf_op jit(solution)/shard_map/nearR3/ppermute | solution.py:220
  34.3 0.7 collective-permute-done.6.refs_0_
  35.1 1.9 %collective-permute-done.7.refs_1_ = bf16[32,4096]{1,0:T(8,128)(2,1)S(1)} collective-permute-done((bf16[32,4096]{1,0:T(8,128)(2,1)S(1)}, bf16[32,4096]{1,0:T(8,128)(2,1)S(1)}, u32[]{:S(2)}, u32[]{:S(2)}) %collective-permute-start.7) | collective-permute-done | bytes 262176 | tf_op jit(solution)/shard_map/farL3/ppermute | solution.py:224
  36.9 1.6 %collective-permute-start.10 = (bf16[32,4096]{1,0:T(8,128)(2,1)S(1)}, bf16[32,4096]{1,0:T(8,128)(2,1)S(1)}, u32[]{:S(2)}, u32[]{:S(2)}) collective-permute-start(bf16[32,4096]{1,0:T(8,128)(2,1)S(1)} %get-tuple-element.58.refs_4_.refs_10_), channel_id=1, source_target_pairs={{0,2},{2,4},{4,6},{6,7},{7,5},{5,3},{3,1},{1,0},{8,10},{10,12},{12... | collective-permute-start | bytes 786440 | tf_op jit(solution)/shard_map/farR4/ppermute | solution.py:220
  39.0 6.7 %gate_up.7 = (f32[2,192,1024]{2,1,0:T(8,128)S(1)}, f32[2,192,1024]{2,1,0:T(8,128)S(1)}) custom-call(bf16[32,4096]{1,0:T(8,128)(2,1)S(1)} %get-tuple-element.55.refs_8_.refs_0_, bf16[32,4096]{1,0:T(8,128)(2,1)S(1)} %get-tuple-element.56.refs_1_, bf16[32,4096]{1,0:T(8,128)(2,1)S(1)} %get-tuple-element.57.refs_2_, ...), custom_call_target="tpu_custom_call" | custom-call | flops 1100000000 | tf_op jit(solution)/shard_map/gate_up/pallas_call | solution.py:134
  46.0 3.5 %gate_up.8 = (f32[2,128,1024]{2,1,0:T(8,128)S(1)}, bf16[2048,2048]{1,0:T(8,128)(2,1)S(1)}) custom-call(bf16[32,4096]{1,0:T(8,128)(2,1)S(1)} %get-tuple-element.62.refs_4_.refs_0_, bf16[32,4096]{1,0:T(8,128)(2,1)S(1)} %get-tuple-element.64.refs_1_, bf16[32,4096]{1,0:T(8,128)(2,1)S(1)} %get-tuple-element.65.refs_2_, ...), custom_call_target="tpu_custom_call" | custom-call | flops 1100000000 | tf_op jit(solution)/shard_map/gate_up/pallas_call | solution.py:134
  49.4 0.6 collective-permute-start.18
  50.1 3.5 %gate_up.9 = (f32[2,128,1024]{2,1,0:T(8,128)S(1)}, bf16[2048,2048]{1,0:T(8,128)(2,1)S(1)}) custom-call(bf16[32,4096]{1,0:T(8,128)(2,1)S(1)} %get-tuple-element.62.refs_4_.refs_0_, bf16[32,4096]{1,0:T(8,128)(2,1)S(1)} %get-tuple-element.64.refs_1_, bf16[32,4096]{1,0:T(8,128)(2,1)S(1)} %get-tuple-element.65.refs_2_, ...), custom_call_target="tpu_custom_call" | custom-call | flops 1100000000 | tf_op jit(solution)/shard_map/gate_up/pallas_call | solution.py:134
  53.8 0.5 collective-permute-start.19
  54.8 0.7 collective-permute-done.19.refs_1_
  55.5 2.9 %down.4 = (bf16[32,4096]{1,0:T(8,128)(2,1)S(1)}, bf16[32,4096]{1,0:T(8,128)(2,1)S(1)}, bf16[32,4096]{1,0:T(8,128)(2,1)S(1)}, bf16[32,4096]{1,0:T(8,128)(2,1)S(1)}) custom-call(bf16[128,1024]{1,0:T(8,128)(2,1)S(1)} %gated.5.refs_0_, bf16[128,1024]{1,0:T(8,128)(2,1)S(1)} %collective-permute-done.19.refs_1_, bf16[2048,2048]{1,0:T(8,128)(2,1)S(1)} %get-tuple-element.67.refs_2_, ...), custom_call_target="tpu_custom_call" | custom-call | tf_op jit(solution)/shard_map/down/pallas_call | solution.py:198
  58.4 0.5 collective-permute-start.22
  59.0 1.6 %collective-permute-start.23 = (bf16[32,4096]{1,0:T(8,128)(2,1)S(1)}, bf16[32,4096]{1,0:T(8,128)(2,1)S(1)}, u32[]{:S(2)}, u32[]{:S(2)}) collective-permute-start(bf16[32,4096]{1,0:T(8,128)(2,1)S(1)} %get-tuple-element.76), channel_id=1, source_target_pairs={{0,2},{2,4},{4,6},{6,7},{7,5},{5,3},{3,1},{1,0},{8,10},{10,12},{12... | collective-permute-start | bytes 786440 | tf_op jit(solution)/shard_map/right/ppermute | solution.py:220
  61.0 1.6 %collective-permute-start.21 = (bf16[32,4096]{1,0:T(8,128)(2,1)S(1)}, bf16[32,4096]{1,0:T(8,128)(2,1)S(1)}, u32[]{:S(2)}, u32[]{:S(2)}) collective-permute-start(bf16[32,4096]{1,0:T(8,128)(2,1)S(1)} %get-tuple-element.74), channel_id=1, source_target_pairs={{0,2},{2,4},{4,6},{6,7},{7,5},{5,3},{3,1},{1,0},{8,10},{10,12},{12... | collective-permute-start | bytes 786440 | tf_op jit(solution)/shard_map/right/ppermute | solution.py:220
  63.0 4.0 %down.3.refs_2_ = f32[192,4096]{1,0:T(8,128)S(1)} custom-call(bf16[192,1024]{1,0:T(8,128)(2,1)S(1)} %gated.4.refs_0_, bf16[192,1024]{1,0:T(8,128)(2,1)S(1)} %collective-permute-done.17.refs_1_, bf16[2048,2048]{1,0:T(8,128)(2,1)S(1)} %get-tuple-element.67.refs_2_, bf16[2048,2048]{1,0:T(8,128)(2,1)S(1)} %get-tuple-element.69.refs_3_), custom_call_target="tpu_custom_call" | custom-call | tf_op jit(solution)/shard_map/down/pallas_call | solution.py:198
  67.0 0.6 collective-permute-done.22.refs_0_
  67.6 0.5 collective-permute-done.23.refs_1_
  68.2 1.2 %collective-permute-start.24 = (bf16[32,4096]{1,0:T(8,128)(2,1)S(1)}, bf16[32,4096]{1,0:T(8,128)(2,1)S(1)}, u32[]{:S(2)}, u32[]{:S(2)}) collective-permute-start(bf16[32,4096]{1,0:T(8,128)(2,1)S(1)} %get-tuple-element.102.refs_2_), channel_id=1, source_target_pairs={{2,0},{4,2},{6,4},{7,6},{5,7},{3,5},{1,3},{0,1},{10,8},{12,10},{14... | collective-permute-start | bytes 786440 | tf_op jit(solution)/shard_map/left/ppermute | solution.py:224
  69.5 0.8 collective-permute-start.25
  70.3 3.0 %collective-permute-done.20.refs_0_ = bf16[32,4096]{1,0:T(8,128)(2,1)S(1)} collective-permute-done((bf16[32,4096]{1,0:T(8,128)(2,1)S(1)}, bf16[32,4096]{1,0:T(8,128)(2,1)S(1)}, u32[]{:S(2)}, u32[]{:S(2)}) %collective-permute-start.20) | collective-permute-done | bytes 262176 | tf_op jit(solution)/shard_map/left/ppermute | solution.py:224
  73.3 0.5 collective-permute-done.21.refs_1_
  73.8 1.5 %collective-permute-start.28 = (bf16[32,4096]{1,0:T(8,128)(2,1)S(1)}, bf16[32,4096]{1,0:T(8,128)(2,1)S(1)}, u32[]{:S(2)}, u32[]{:S(2)}) collective-permute-start(bf16[32,4096]{1,0:T(8,128)(2,1)S(1)} %get-tuple-element.100.refs_4_), channel_id=1, source_target_pairs={{2,0},{4,2},{6,4},{7,6},{5,7},{3,5},{1,3},{0,1},{10,8},{12,10},{14... | collective-permute-start | bytes 786440 | tf_op jit(solution)/shard_map/left/ppermute | solution.py:224
  75.3 0.8 collective-permute-start.29
  76.1 4.0 %down.5.refs_2_ = f32[192,4096]{1,0:T(8,128)S(1)} custom-call(bf16[192,1024]{1,0:T(8,128)(2,1)S(1)} %gated.3.refs_0_, bf16[192,1024]{1,0:T(8,128)(2,1)S(1)} %collective-permute-done.15.refs_1_, bf16[2048,2048]{1,0:T(8,128)(2,1)S(1)} %get-tuple-element.67.refs_2_, bf16[2048,2048]{1,0:T(8,128)(2,1)S(1)} %get-tuple-element.69.refs_3_, ...), custom_call_target="tpu_custom_call" | custom-call | tf_op jit(solution)/shard_map/down/pallas_call | solution.py:198
  80.3 1.3 %collective-permute-start.26 = (bf16[32,4096]{1,0:T(8,128)(2,1)S(1)}, bf16[32,4096]{1,0:T(8,128)(2,1)S(1)}, u32[]{:S(2)}, u32[]{:S(2)}) collective-permute-start(bf16[32,4096]{1,0:T(8,128)(2,1)S(1)} %get-tuple-element.98.refs_2_), channel_id=1, source_target_pairs={{2,0},{4,2},{6,4},{7,6},{5,7},{3,5},{1,3},{0,1},{10,8},{12,10},{14... | collective-permute-start | bytes 786440 | tf_op jit(solution)/shard_map/left/ppermute | solution.py:224
  81.6 0.8 collective-permute-start.27
  82.4 2.1 %collective-permute-done.28.refs_0_ = bf16[32,4096]{1,0:T(8,128)(2,1)S(1)} collective-permute-done((bf16[32,4096]{1,0:T(8,128)(2,1)S(1)}, bf16[32,4096]{1,0:T(8,128)(2,1)S(1)}, u32[]{:S(2)}, u32[]{:S(2)}) %collective-permute-start.28) | collective-permute-done | bytes 262176 | tf_op jit(solution)/shard_map/left/ppermute | solution.py:224
  85.1 1.2 %collective-permute-start.32 = (bf16[32,4096]{1,0:T(8,128)(2,1)S(1)}, bf16[32,4096]{1,0:T(8,128)(2,1)S(1)}, u32[]{:S(2)}, u32[]{:S(2)}) collective-permute-start(bf16[32,4096]{1,0:T(8,128)(2,1)S(1)} %get-tuple-element.96.refs_2_), channel_id=1, source_target_pairs={{2,0},{4,2},{6,4},{7,6},{5,7},{3,5},{1,3},{0,1},{10,8},{12,10},{14... | collective-permute-start | bytes 786440 | tf_op jit(solution)/shard_map/left/ppermute | solution.py:224
  86.3 0.8 collective-permute-start.33
  87.2 3.0 %collective-permute-done.26.refs_0_ = bf16[32,4096]{1,0:T(8,128)(2,1)S(1)} collective-permute-done((bf16[32,4096]{1,0:T(8,128)(2,1)S(1)}, bf16[32,4096]{1,0:T(8,128)(2,1)S(1)}, u32[]{:S(2)}, u32[]{:S(2)}) %collective-permute-start.26) | collective-permute-done | bytes 262176 | tf_op jit(solution)/shard_map/left/ppermute | solution.py:224
  90.1 0.7 collective-permute-done.27.refs_1_
  90.9 1.6 %collective-permute-start.30 = (bf16[32,4096]{1,0:T(8,128)(2,1)S(1)}, bf16[32,4096]{1,0:T(8,128)(2,1)S(1)}, u32[]{:S(2)}, u32[]{:S(2)}) collective-permute-start(bf16[32,4096]{1,0:T(8,128)(2,1)S(1)} %get-tuple-element.94.refs_2_), channel_id=1, source_target_pairs={{2,0},{4,2},{6,4},{7,6},{5,7},{3,5},{1,3},{0,1},{10,8},{12,10},{14... | collective-permute-start | bytes 786440 | tf_op jit(solution)/shard_map/left/ppermute | solution.py:224
  93.0 2.8 %collective-permute-done.32.refs_0_ = bf16[32,4096]{1,0:T(8,128)(2,1)S(1)} collective-permute-done((bf16[32,4096]{1,0:T(8,128)(2,1)S(1)}, bf16[32,4096]{1,0:T(8,128)(2,1)S(1)}, u32[]{:S(2)}, u32[]{:S(2)}) %collective-permute-start.32) | collective-permute-done | bytes 262176 | tf_op jit(solution)/shard_map/left/ppermute | solution.py:224
  95.7 0.7 collective-permute-done.33.refs_1_
  96.4 4.4 %collective-permute-done.30.refs_0_ = bf16[32,4096]{1,0:T(8,128)(2,1)S(1)} collective-permute-done((bf16[32,4096]{1,0:T(8,128)(2,1)S(1)}, bf16[32,4096]{1,0:T(8,128)(2,1)S(1)}, u32[]{:S(2)}, u32[]{:S(2)}) %collective-permute-start.30) | collective-permute-done | bytes 262176 | tf_op jit(solution)/shard_map/left/ppermute | solution.py:224
  101.1 0.8 pad_maximum_fusion
  (55 shorter events, 5.8 us)
Async XLA Ops:
  1.1 12.1 %collective-permute-start = (bf16[32,4096]{1,0:T(8,128)(2,1)S(1)}, bf16[32,4096]{1,0:T(8,128)(2,1)S(1)}, u32[]{:S(2)}, u32[]{:S(2)}) collective-permute-start(bf16[32,4096]{1,0:T(8,128)(2,1)S(1)} %get-tuple-element.104.refs_0_), channel_id=1, source_target_pairs={{0,2},{2,4},{4,6},{6,7},{7,5},{5,3},{3,1},{1,0},{8,10},{10,12},{12... | collective-permute-start | bytes 786440 | tf_op jit(solution)/shard_map/farR1/ppermute | solution.py:220
  4.1 9.2 %collective-permute-start.1 = (bf16[32,4096]{1,0:T(8,128)(2,1)S(1)}, bf16[32,4096]{1,0:T(8,128)(2,1)S(1)}, u32[]{:S(2)}, u32[]{:S(2)}) collective-permute-start(bf16[32,4096]{1,0:T(8,128)(2,1)S(1)} %get-tuple-element.103.refs_1_), channel_id=1, source_target_pairs={{2,0},{4,2},{6,4},{7,6},{5,7},{3,5},{1,3},{0,1},{10,8},{12,10},{14... | collective-permute-start | bytes 786440 | tf_op jit(solution)/shard_map/farL1/ppermute | solution.py:224
  4.2 12.7 %collective-permute-start.2 = (bf16[32,4096]{1,0:T(8,128)(2,1)S(1)}, bf16[32,4096]{1,0:T(8,128)(2,1)S(1)}, u32[]{:S(2)}, u32[]{:S(2)}) collective-permute-start(bf16[32,4096]{1,0:T(8,128)(2,1)S(1)} %get-tuple-element.103.refs_1_), channel_id=1, source_target_pairs={{0,2},{2,4},{4,6},{6,7},{7,5},{5,3},{3,1},{1,0},{8,10},{10,12},{12... | collective-permute-start | bytes 786440 | tf_op jit(solution)/shard_map/nearR1/ppermute | solution.py:220
  6.2 12.5 %collective-permute-start.3 = (bf16[32,4096]{1,0:T(8,128)(2,1)S(1)}, bf16[32,4096]{1,0:T(8,128)(2,1)S(1)}, u32[]{:S(2)}, u32[]{:S(2)}) collective-permute-start(bf16[32,4096]{1,0:T(8,128)(2,1)S(1)} %get-tuple-element.104.refs_0_), channel_id=1, source_target_pairs={{2,0},{4,2},{6,4},{7,6},{5,7},{3,5},{1,3},{0,1},{10,8},{12,10},{14... | collective-permute-start | bytes 786440 | tf_op jit(solution)/shard_map/nearL1/ppermute | solution.py:224
  13.4 13.3 %collective-permute-start.4 = (bf16[32,4096]{1,0:T(8,128)(2,1)S(1)}, bf16[32,4096]{1,0:T(8,128)(2,1)S(1)}, u32[]{:S(2)}, u32[]{:S(2)}) collective-permute-start(bf16[32,4096]{1,0:T(8,128)(2,1)S(1)} %get-tuple-element.48.refs_2_), channel_id=1, source_target_pairs={{0,2},{2,4},{4,6},{6,7},{7,5},{5,3},{3,1},{1,0},{8,10},{10,12},{12... | collective-permute-start | bytes 786440 | tf_op jit(solution)/shard_map/farR2/ppermute | solution.py:220
  15.3 11.4 %collective-permute-start.5 = (bf16[32,4096]{1,0:T(8,128)(2,1)S(1)}, bf16[32,4096]{1,0:T(8,128)(2,1)S(1)}, u32[]{:S(2)}, u32[]{:S(2)}) collective-permute-start(bf16[32,4096]{1,0:T(8,128)(2,1)S(1)} %get-tuple-element.49.refs_3_), channel_id=1, source_target_pairs={{2,0},{4,2},{6,4},{7,6},{5,7},{3,5},{1,3},{0,1},{10,8},{12,10},{14... | collective-permute-start | bytes 786440 | tf_op jit(solution)/shard_map/farL2/ppermute | solution.py:224
  18.7 13.5 %collective-permute-start.8 = (bf16[32,4096]{1,0:T(8,128)(2,1)S(1)}, bf16[32,4096]{1,0:T(8,128)(2,1)S(1)}, u32[]{:S(2)}, u32[]{:S(2)}) collective-permute-start(bf16[32,4096]{1,0:T(8,128)(2,1)S(1)} %get-tuple-element.50.refs_4_.refs_10_), channel_id=1, source_target_pairs={{0,2},{2,4},{4,6},{6,7},{7,5},{5,3},{3,1},{1,0},{8,10},{10,12},{12... | collective-permute-start | bytes 786440 | tf_op jit(solution)/shard_map/nearR2/ppermute | solution.py:220
  20.3 11.9 %collective-permute-start.9 = (bf16[32,4096]{1,0:T(8,128)(2,1)S(1)}, bf16[32,4096]{1,0:T(8,128)(2,1)S(1)}, u32[]{:S(2)}, u32[]{:S(2)}) collective-permute-start(bf16[32,4096]{1,0:T(8,128)(2,1)S(1)} %get-tuple-element.51.refs_5_), channel_id=1, source_target_pairs={{2,0},{4,2},{6,4},{7,6},{5,7},{3,5},{1,3},{0,1},{10,8},{12,10},{14... | collective-permute-start | bytes 786440 | tf_op jit(solution)/shard_map/nearL2/ppermute | solution.py:224
  26.7 8.3 %collective-permute-start.6 = (bf16[32,4096]{1,0:T(8,128)(2,1)S(1)}, bf16[32,4096]{1,0:T(8,128)(2,1)S(1)}, u32[]{:S(2)}, u32[]{:S(2)}) collective-permute-start(bf16[32,4096]{1,0:T(8,128)(2,1)S(1)} %get-tuple-element.55.refs_8_.refs_0_), channel_id=1, source_target_pairs={{0,2},{2,4},{4,6},{6,7},{7,5},{5,3},{3,1},{1,0},{8,10},{10,12},{12... | collective-permute-start | bytes 786440 | tf_op jit(solution)/shard_map/farR3/ppermute | solution.py:220
  28.3 8.6 %collective-permute-start.7 = (bf16[32,4096]{1,0:T(8,128)(2,1)S(1)}, bf16[32,4096]{1,0:T(8,128)(2,1)S(1)}, u32[]{:S(2)}, u32[]{:S(2)}) collective-permute-start(bf16[32,4096]{1,0:T(8,128)(2,1)S(1)} %get-tuple-element.56.refs_1_), channel_id=1, source_target_pairs={{2,0},{4,2},{6,4},{7,6},{5,7},{3,5},{1,3},{0,1},{10,8},{12,10},{14... | collective-permute-start | bytes 786440 | tf_op jit(solution)/shard_map/farL3/ppermute | solution.py:224
  32.2 13.4 %collective-permute-start.12 = (bf16[32,4096]{1,0:T(8,128)(2,1)S(1)}, bf16[32,4096]{1,0:T(8,128)(2,1)S(1)}, u32[]{:S(2)}, u32[]{:S(2)}) collective-permute-start(bf16[32,4096]{1,0:T(8,128)(2,1)S(1)} %get-tuple-element.57.refs_2_), channel_id=1, source_target_pairs={{0,2},{2,4},{4,6},{6,7},{7,5},{5,3},{3,1},{1,0},{8,10},{10,12},{12... | collective-permute-start | bytes 786440 | tf_op jit(solution)/shard_map/nearR3/ppermute | solution.py:220
  33.9 11.8 %collective-permute-start.13 = (bf16[32,4096]{1,0:T(8,128)(2,1)S(1)}, bf16[32,4096]{1,0:T(8,128)(2,1)S(1)}, u32[]{:S(2)}, u32[]{:S(2)}) collective-permute-start(bf16[32,4096]{1,0:T(8,128)(2,1)S(1)} %get-tuple-element.60.refs_3_), channel_id=1, source_target_pairs={{2,0},{4,2},{6,4},{7,6},{5,7},{3,5},{1,3},{0,1},{10,8},{12,10},{14... | collective-permute-start | bytes 786440 | tf_op jit(solution)/shard_map/nearL3/ppermute | solution.py:224
  36.9 8.7 %collective-permute-start.10 = (bf16[32,4096]{1,0:T(8,128)(2,1)S(1)}, bf16[32,4096]{1,0:T(8,128)(2,1)S(1)}, u32[]{:S(2)}, u32[]{:S(2)}) collective-permute-start(bf16[32,4096]{1,0:T(8,128)(2,1)S(1)} %get-tuple-element.58.refs_4_.refs_10_), channel_id=1, source_target_pairs={{0,2},{2,4},{4,6},{6,7},{7,5},{5,3},{3,1},{1,0},{8,10},{10,12},{12... | collective-permute-start | bytes 786440 | tf_op jit(solution)/shard_map/farR4/ppermute | solution.py:220
  38.5 7.4 %collective-permute-start.11 = (bf16[32,4096]{1,0:T(8,128)(2,1)S(1)}, bf16[32,4096]{1,0:T(8,128)(2,1)S(1)}, u32[]{:S(2)}, u32[]{:S(2)}) collective-permute-start(bf16[32,4096]{1,0:T(8,128)(2,1)S(1)} %get-tuple-element.59.refs_5_), channel_id=1, source_target_pairs={{2,0},{4,2},{6,4},{7,6},{5,7},{3,5},{1,3},{0,1},{10,8},{12,10},{14... | collective-permute-start | bytes 786440 | tf_op jit(solution)/shard_map/farL4/ppermute | solution.py:224
  46.0 8.4 %collective-permute-start.16 = (f32[2,192,1024]{2,1,0:T(8,128)S(1)}, f32[2,192,1024]{2,1,0:T(8,128)S(1)}, u32[]{:S(2)}, u32[]{:S(2)}) collective-permute-start(f32[2,192,1024]{2,1,0:T(8,128)S(1)} %get-tuple-element.71), channel_id=1, source_target_pairs={{0,8},{8,0},{1,9},{9,1},{2,10},{10,2},{3,11},{11,3},{4,12},{12,4},... | collective-permute-start | bytes 4718600 | tf_op jit(solution)/shard_map/swap/ppermute | solution.py:228
  49.4 4.1 %collective-permute-start.18 = (f32[2,128,1024]{2,1,0:T(8,128)S(1)}, f32[2,128,1024]{2,1,0:T(8,128)S(1)}, u32[]{:S(2)}, u32[]{:S(2)}) collective-permute-start(f32[2,128,1024]{2,1,0:T(8,128)S(1)} %get-tuple-element.68.refs_7_), channel_id=1, source_target_pairs={{0,8},{8,0},{1,9},{9,1},{2,10},{10,2},{3,11},{11,3},{4,12},{12,4},... | collective-permute-start | bytes 3145736 | tf_op jit(solution)/shard_map/swap/ppermute | solution.py:228
  50.0 11.0 %collective-permute-start.14 = (f32[2,192,1024]{2,1,0:T(8,128)S(1)}, f32[2,192,1024]{2,1,0:T(8,128)S(1)}, u32[]{:S(2)}, u32[]{:S(2)}) collective-permute-start(f32[2,192,1024]{2,1,0:T(8,128)S(1)} %get-tuple-element.63), channel_id=1, source_target_pairs={{0,8},{8,0},{1,9},{9,1},{2,10},{10,2},{3,11},{11,3},{4,12},{12,4},... | collective-permute-start | bytes 4718600 | tf_op jit(solution)/shard_map/swap/ppermute | solution.py:228
  53.8 1.7 %collective-permute-start.19 = (bf16[128,1024]{1,0:T(8,128)(2,1)S(1)}, bf16[128,1024]{1,0:T(8,128)(2,1)S(1)}, u32[]{:S(2)}, u32[]{:S(2)}) collective-permute-start(bf16[128,1024]{1,0:T(8,128)(2,1)S(1)} %gated.5.refs_0_), channel_id=1, source_target_pairs={{0,8},{8,0},{1,9},{9,1},{2,10},{10,2},{3,11},{11,3},{4,12},{12,4},... | collective-permute-start | bytes 786440 | tf_op jit(solution)/shard_map/swap/ppermute | solution.py:228
  54.7 8.2 %collective-permute-start.17 = (bf16[192,1024]{1,0:T(8,128)(2,1)S(1)}, bf16[192,1024]{1,0:T(8,128)(2,1)S(1)}, u32[]{:S(2)}, u32[]{:S(2)}) collective-permute-start(bf16[192,1024]{1,0:T(8,128)(2,1)S(1)} %gated.4.refs_0_), channel_id=1, source_target_pairs={{0,8},{8,0},{1,9},{9,1},{2,10},{10,2},{3,11},{11,3},{4,12},{12,4},... | collective-permute-start | bytes 1179656 | tf_op jit(solution)/shard_map/swap/ppermute | solution.py:228
  58.4 9.2 %collective-permute-start.22 = (bf16[32,4096]{1,0:T(8,128)(2,1)S(1)}, bf16[32,4096]{1,0:T(8,128)(2,1)S(1)}, u32[]{:S(2)}, u32[]{:S(2)}) collective-permute-start(bf16[32,4096]{1,0:T(8,128)(2,1)S(1)} %get-tuple-element.75), channel_id=1, source_target_pairs={{2,0},{4,2},{6,4},{7,6},{5,7},{3,5},{1,3},{0,1},{10,8},{12,10},{14... | collective-permute-start | bytes 786440 | tf_op jit(solution)/shard_map/left/ppermute | solution.py:224
  59.0 9.2 %collective-permute-start.23 = (bf16[32,4096]{1,0:T(8,128)(2,1)S(1)}, bf16[32,4096]{1,0:T(8,128)(2,1)S(1)}, u32[]{:S(2)}, u32[]{:S(2)}) collective-permute-start(bf16[32,4096]{1,0:T(8,128)(2,1)S(1)} %get-tuple-element.76), channel_id=1, source_target_pairs={{0,2},{2,4},{4,6},{6,7},{7,5},{5,3},{3,1},{1,0},{8,10},{10,12},{12... | collective-permute-start | bytes 786440 | tf_op jit(solution)/shard_map/right/ppermute | solution.py:220
  60.5 12.7 %collective-permute-start.20 = (bf16[32,4096]{1,0:T(8,128)(2,1)S(1)}, bf16[32,4096]{1,0:T(8,128)(2,1)S(1)}, u32[]{:S(2)}, u32[]{:S(2)}) collective-permute-start(bf16[32,4096]{1,0:T(8,128)(2,1)S(1)} %get-tuple-element.73), channel_id=1, source_target_pairs={{2,0},{4,2},{6,4},{7,6},{5,7},{3,5},{1,3},{0,1},{10,8},{12,10},{14... | collective-permute-start | bytes 786440 | tf_op jit(solution)/shard_map/left/ppermute | solution.py:224
  61.0 12.7 %collective-permute-start.21 = (bf16[32,4096]{1,0:T(8,128)(2,1)S(1)}, bf16[32,4096]{1,0:T(8,128)(2,1)S(1)}, u32[]{:S(2)}, u32[]{:S(2)}) collective-permute-start(bf16[32,4096]{1,0:T(8,128)(2,1)S(1)} %get-tuple-element.74), channel_id=1, source_target_pairs={{0,2},{2,4},{4,6},{6,7},{7,5},{5,3},{3,1},{1,0},{8,10},{10,12},{12... | collective-permute-start | bytes 786440 | tf_op jit(solution)/shard_map/right/ppermute | solution.py:220
  62.9 13.2 %collective-permute-start.15 = (bf16[192,1024]{1,0:T(8,128)(2,1)S(1)}, bf16[192,1024]{1,0:T(8,128)(2,1)S(1)}, u32[]{:S(2)}, u32[]{:S(2)}) collective-permute-start(bf16[192,1024]{1,0:T(8,128)(2,1)S(1)} %gated.3.refs_0_), channel_id=1, source_target_pairs={{0,8},{8,0},{1,9},{9,1},{2,10},{10,2},{3,11},{11,3},{4,12},{12,4},... | collective-permute-start | bytes 1179656 | tf_op jit(solution)/shard_map/swap/ppermute | solution.py:228
  68.2 12.0 %collective-permute-start.24 = (bf16[32,4096]{1,0:T(8,128)(2,1)S(1)}, bf16[32,4096]{1,0:T(8,128)(2,1)S(1)}, u32[]{:S(2)}, u32[]{:S(2)}) collective-permute-start(bf16[32,4096]{1,0:T(8,128)(2,1)S(1)} %get-tuple-element.102.refs_2_), channel_id=1, source_target_pairs={{2,0},{4,2},{6,4},{7,6},{5,7},{3,5},{1,3},{0,1},{10,8},{12,10},{14... | collective-permute-start | bytes 786440 | tf_op jit(solution)/shard_map/left/ppermute | solution.py:224
  69.5 10.7 %collective-permute-start.25 = (bf16[32,4096]{1,0:T(8,128)(2,1)S(1)}, bf16[32,4096]{1,0:T(8,128)(2,1)S(1)}, u32[]{:S(2)}, u32[]{:S(2)}) collective-permute-start(bf16[32,4096]{1,0:T(8,128)(2,1)S(1)} %get-tuple-element.101.refs_3_), channel_id=1, source_target_pairs={{0,2},{2,4},{4,6},{6,7},{7,5},{5,3},{3,1},{1,0},{8,10},{10,12},{12... | collective-permute-start | bytes 786440 | tf_op jit(solution)/shard_map/right/ppermute | solution.py:220
  73.8 10.7 %collective-permute-start.28 = (bf16[32,4096]{1,0:T(8,128)(2,1)S(1)}, bf16[32,4096]{1,0:T(8,128)(2,1)S(1)}, u32[]{:S(2)}, u32[]{:S(2)}) collective-permute-start(bf16[32,4096]{1,0:T(8,128)(2,1)S(1)} %get-tuple-element.100.refs_4_), channel_id=1, source_target_pairs={{2,0},{4,2},{6,4},{7,6},{5,7},{3,5},{1,3},{0,1},{10,8},{12,10},{14... | collective-permute-start | bytes 786440 | tf_op jit(solution)/shard_map/left/ppermute | solution.py:224
  75.3 9.7 %collective-permute-start.29 = (bf16[32,4096]{1,0:T(8,128)(2,1)S(1)}, bf16[32,4096]{1,0:T(8,128)(2,1)S(1)}, u32[]{:S(2)}, u32[]{:S(2)}) collective-permute-start(bf16[32,4096]{1,0:T(8,128)(2,1)S(1)} %get-tuple-element.99.refs_5_), channel_id=1, source_target_pairs={{0,2},{2,4},{4,6},{6,7},{7,5},{5,3},{3,1},{1,0},{8,10},{10,12},{12... | collective-permute-start | bytes 786440 | tf_op jit(solution)/shard_map/right/ppermute | solution.py:220
  80.3 9.8 %collective-permute-start.26 = (bf16[32,4096]{1,0:T(8,128)(2,1)S(1)}, bf16[32,4096]{1,0:T(8,128)(2,1)S(1)}, u32[]{:S(2)}, u32[]{:S(2)}) collective-permute-start(bf16[32,4096]{1,0:T(8,128)(2,1)S(1)} %get-tuple-element.98.refs_2_), channel_id=1, source_target_pairs={{2,0},{4,2},{6,4},{7,6},{5,7},{3,5},{1,3},{0,1},{10,8},{12,10},{14... | collective-permute-start | bytes 786440 | tf_op jit(solution)/shard_map/left/ppermute | solution.py:224
  81.6 9.2 %collective-permute-start.27 = (bf16[32,4096]{1,0:T(8,128)(2,1)S(1)}, bf16[32,4096]{1,0:T(8,128)(2,1)S(1)}, u32[]{:S(2)}, u32[]{:S(2)}) collective-permute-start(bf16[32,4096]{1,0:T(8,128)(2,1)S(1)} %get-tuple-element.97.refs_3_), channel_id=1, source_target_pairs={{0,2},{2,4},{4,6},{6,7},{7,5},{5,3},{3,1},{1,0},{8,10},{10,12},{12... | collective-permute-start | bytes 786440 | tf_op jit(solution)/shard_map/right/ppermute | solution.py:220
  85.1 10.7 %collective-permute-start.32 = (bf16[32,4096]{1,0:T(8,128)(2,1)S(1)}, bf16[32,4096]{1,0:T(8,128)(2,1)S(1)}, u32[]{:S(2)}, u32[]{:S(2)}) collective-permute-start(bf16[32,4096]{1,0:T(8,128)(2,1)S(1)} %get-tuple-element.96.refs_2_), channel_id=1, source_target_pairs={{2,0},{4,2},{6,4},{7,6},{5,7},{3,5},{1,3},{0,1},{10,8},{12,10},{14... | collective-permute-start | bytes 786440 | tf_op jit(solution)/shard_map/left/ppermute | solution.py:224
  86.3 10.1 %collective-permute-start.33 = (bf16[32,4096]{1,0:T(8,128)(2,1)S(1)}, bf16[32,4096]{1,0:T(8,128)(2,1)S(1)}, u32[]{:S(2)}, u32[]{:S(2)}) collective-permute-start(bf16[32,4096]{1,0:T(8,128)(2,1)S(1)} %get-tuple-element.95.refs_3_), channel_id=1, source_target_pairs={{0,2},{2,4},{4,6},{6,7},{7,5},{5,3},{3,1},{1,0},{8,10},{10,12},{12... | collective-permute-start | bytes 786440 | tf_op jit(solution)/shard_map/right/ppermute | solution.py:220
  90.9 9.9 %collective-permute-start.30 = (bf16[32,4096]{1,0:T(8,128)(2,1)S(1)}, bf16[32,4096]{1,0:T(8,128)(2,1)S(1)}, u32[]{:S(2)}, u32[]{:S(2)}) collective-permute-start(bf16[32,4096]{1,0:T(8,128)(2,1)S(1)} %get-tuple-element.94.refs_2_), channel_id=1, source_target_pairs={{2,0},{4,2},{6,4},{7,6},{5,7},{3,5},{1,3},{0,1},{10,8},{12,10},{14... | collective-permute-start | bytes 786440 | tf_op jit(solution)/shard_map/left/ppermute | solution.py:224
  92.5 8.4 %collective-permute-start.31 = (bf16[32,4096]{1,0:T(8,128)(2,1)S(1)}, bf16[32,4096]{1,0:T(8,128)(2,1)S(1)}, u32[]{:S(2)}, u32[]{:S(2)}) collective-permute-start(bf16[32,4096]{1,0:T(8,128)(2,1)S(1)} %get-tuple-element.93.refs_3_), channel_id=1, source_target_pairs={{0,2},{2,4},{4,6},{6,7},{7,5},{5,3},{3,1},{1,0},{8,10},{10,12},{12... | collective-permute-start | bytes 786440 | tf_op jit(solution)/shard_map/right/ppermute | solution.py:220

commit v13 on v12

--- a/solution.py
+++ b/solution.py
@@ -96,8 +96,8 @@
     count, halves = len(pieces), len(weights) // 2
     shapes = [jax.ShapeDtypeStruct((2, m, w), F32)] * halves
     scratch = [pltpu.VMEM((m, k), BF16)]
-    for x, _ in load:
-        shapes.append(pltpu.VMEM((x.shape[0], x.shape[1] // 2), x.dtype))
+    for x, cols, _ in load:
+        shapes.append(pltpu.VMEM((x.shape[0], cols), x.dtype))
     if load:
         scratch.append(pltpu.SemaphoreType.DMA((len(load), 8)))
 
@@ -108,10 +108,7 @@
         copies = []
         if load:
             sources = refs[count + len(weights) :]
-            starts = [
-                half_of(True, w) if which == "own" else which * (x.shape[1] // 2)
-                for x, which in load
-            ]
+            starts = [half_of(True, w) if at is None else at for _, _, at in load]
             copies = fetches(list(zip(sources, starts)), outs[halves:], refs[-1])
         for copy in copies:
             copy.start()
@@ -139,7 +136,7 @@
         out_shape=shapes,
         scratch_shapes=scratch,
         **params(3 << 20, KERNEL),
-    )(*pieces, *map(in_vmem, weights), *[in_hbm(x) for x, _ in load], *after)
+    )(*pieces, *map(in_vmem, weights), *[in_hbm(x) for x, _, _ in load], *after)
 
 
 def gated(ours, theirs):
@@ -165,17 +162,22 @@
 
 
 def down(halves, weights, outs, after):
+    *weights, whole = weights
     m = sum(h.shape[0] for h, _ in halves)
     w = halves[0][0].shape[1]
-    n = weights[0].shape[1]
-    tile = 1024
+    n, wide = whole.shape[1], weights[0].shape[1]
+    rest = n - 2 * wide
+    tile = wide // 2
     if any(h.shape[0] % 16 for h, _ in halves):
         halves = [tuple(jnp.concatenate(hs, axis=0) for hs in zip(*halves))]
     count = len(halves)
 
     def body(*refs):
-        weight_refs, h_ref = refs[2 * count : 2 * count + 2], refs[-1]
-        out_refs = refs[-1 - len(outs) : -1]
+        weight_refs, source = refs[2 * count : 2 * count + 2], refs[2 * count + 2]
+        out_refs, (h_ref, rest_ref, sems) = refs[-3 - len(outs) : -3], refs[-3:]
+        copies = fetches([(source, 2 * wide)], [rest_ref], sems)
+        for copy in copies:
+            copy.start()
         at = 0
         for i in range(count):
             rows = slice(at, at + refs[2 * i].shape[0])
@@ -183,29 +185,40 @@
             h_ref[rows, pl.ds(half_of(True, w), w)] = refs[2 * i][...]
             h_ref[rows, pl.ds(half_of(False, w), w)] = refs[2 * i + 1][...]
 
+        def multiply(columns, cols):
+            out = jnp.dot(h_ref[...], columns, preferred_element_type=F32)
+            for (at, size, dtype), ref in zip(outs, out_refs):
+                ref[:, cols] = out[at : at + size].astype(dtype)
+
         for i, d_ref in enumerate(weight_refs):
 
-            @pl.loop(0, n // tile)
+            @pl.loop(0, 2)
             def _(j):
                 here = pl.multiple_of(j * tile, tile)
-                out = jnp.dot(
-                    h_ref[...], d_ref[:, pl.ds(here, tile)], preferred_element_type=F32
-                )
-                cols = pl.ds(i * n + here, tile)
-                for (at, size, dtype), ref in zip(outs, out_refs):
-                    ref[:, cols] = out[at : at + size].astype(dtype)
+                multiply(d_ref[:, pl.ds(here, tile)], pl.ds(i * wide + here, tile))
+
+        for copy in copies:
+            copy.wait()
+        multiply(rest_ref[...], pl.ds(2 * wide, rest))
 
     return pl.pallas_call(
         body,
         name="down",
-        in_specs=[VMEM] * (2 * count + 2) + [ANY] * len(after),
+        in_specs=[VMEM] * (2 * count + 2) + [ANY] * (1 + len(after)),
         out_specs=[VMEM] * len(outs),
-        out_shape=[
-            jax.ShapeDtypeStruct((size, 2 * n), dtype) for _, size, dtype in outs
+        out_shape=[jax.ShapeDtypeStruct((size, n), dtype) for _, size, dtype in outs],
+        scratch_shapes=[
+            pltpu.VMEM((m, 2 * w), BF16),
+            pltpu.VMEM((2 * w, rest), BF16),
+            pltpu.SemaphoreType.DMA((1, 8)),
         ],
-        scratch_shapes=[pltpu.VMEM((m, 2 * w), BF16)],
-        **params(3 << 20),
-    )(*[h for pair in halves for h in pair], *map(in_vmem, weights), *after)
+        **params(8 << 20),
+    )(
+        *[h for pair in halves for h in pair],
+        *map(in_vmem, weights),
+        in_hbm(whole),
+        *after,
+    )
 
 
 def make_shards(n):
@@ -268,7 +281,7 @@
             if d == 1:
                 groups.append(list(waiting))
                 rows_now = list(waiting.values())
-                load = [(gate_weight, "own"), (up_weight, "own")]
+                load = [(x, x.shape[1] // 2, None) for x in (gate_weight, up_weight)]
                 out = gate_up(rows_now, wide, after, load)
                 theirs.append(out[0])
                 wide += out[1:]
@@ -281,11 +294,14 @@
             return h, other(h)
 
         last = list(waiting.values())
-        last_theirs, low = gate_up(last, wide[:2], [], [(down_weight, 0)])
+        part_cols = down_weight.shape[1] * 3 // 8
+        load = [(down_weight, part_cols, 0)]
+        last_theirs, low = gate_up(last, wide[:2], [], load)
         last_got = other(last_theirs)
         got = [other(x) for x in theirs]
-        last_ours, high = gate_up(last, wide[2:], [last_theirs], [(down_weight, 1)])
-        weight = [low, high]
+        load = [(down_weight, part_cols, part_cols)]
+        last_ours, high = gate_up(last, wide[2:], [last_theirs], load)
+        weight = [low, high, down_weight]
         last = hide(last_ours, last_got)
         outs = [(i * cut, cut, BF16) for i in range(4)]
         b_l, b_r, a_l, a_r = down([last], weight, outs, [])

time: 102 us -> 101 us (level)
    pallas_call x5, Pallas kernels: 23 us -> 21.8 us  [gate_up(): pl.pallas_call(body, name='gate_up', in_specs=[VMEM] * (count + len(weigh...]
where the time goes in v13:
time: 101 us
  Pallas kernels  41.6 us (41%)
  starting transfers between devices  31.2 us (31%)
  waiting for transfers between devices  25.5 us (25%)
  other arithmetic  1.44 us (1%)
  local copies, waits for them, and re-layouts  1.06 us (1%)
    pallas_call x5, Pallas kernels, gate_up(): pl.pallas_call(body, name='gate_up', in_specs=[VMEM] * (count + len(weigh...  21.8 us
    ppermute x14, starting transfers between devices, right(): return lax.ppermute(x, 'gy', to_right)  20.4 us
    ppermute x14, waiting for transfers between devices, left(): return lax.ppermute(x, 'gy', to_left)  19.3 us
    pallas_call x3, Pallas kernels, down(): pl.pallas_call(body, name='down', in_specs=[VMEM] * (2 * count + 2) + [AN...  12 us
    ppermute x14, starting transfers between devices, left(): return lax.ppermute(x, 'gy', to_left)  9.48 us
    pallas_call x2, Pallas kernels, bring(): pl.pallas_call(body, name='bring', in_specs=[ANY] * (count + len(after)),...  6.96 us
    ppermute x14, waiting for transfers between devices, right(): return lax.ppermute(x, 'gy', to_right)  5.42 us
  transfers between devices with their start and end apart: 34, of which 19 were waited for; matrix products, arithmetic and copies ran while one was open for 0% of the time, Pallas kernels for 41%

profile of v13, /device:TPU:0, one launch (start us, length us, event | category | flops | bytes accessed | tf_op | source)
XLA Modules:
  0.0 101.1 jit_solution(3355323215012869844)
XLA Ops:
  0.0 1.1 %fusion.14 = (bf16[32,4096]{1,0:T(8,128)(2,1)S(1)}, bf16[32,4096]{1,0:T(8,128)(2,1)S(1)}) fusion(bf16[64,4096]{1,0:T(8,128)(2,1)} %param.4), kind=kLoop, calls=%fused_computation.27 | loop fusion | bytes 1048576 | tf_op jit(solution)/shard_map/slice | solution.py:250
  1.1 3.1 %collective-permute-start = (bf16[32,4096]{1,0:T(8,128)(2,1)S(1)}, bf16[32,4096]{1,0:T(8,128)(2,1)S(1)}, u32[]{:S(2)}, u32[]{:S(2)}) collective-permute-start(bf16[32,4096]{1,0:T(8,128)(2,1)S(1)} %get-tuple-element.104.refs_0_), channel_id=1, source_target_pairs={{0,2},{2,4},{4,6},{6,7},{7,5},{5,3},{3,1},{1,0},{8,10},{10,12},{12... | collective-permute-start | bytes 786440 | tf_op jit(solution)/shard_map/farR1/ppermute | solution.py:233
  4.2 2.0 %collective-permute-start.2 = (bf16[32,4096]{1,0:T(8,128)(2,1)S(1)}, bf16[32,4096]{1,0:T(8,128)(2,1)S(1)}, u32[]{:S(2)}, u32[]{:S(2)}) collective-permute-start(bf16[32,4096]{1,0:T(8,128)(2,1)S(1)} %get-tuple-element.103.refs_1_), channel_id=1, source_target_pairs={{0,2},{2,4},{4,6},{6,7},{7,5},{5,3},{3,1},{1,0},{8,10},{10,12},{12... | collective-permute-start | bytes 786440 | tf_op jit(solution)/shard_map/nearR1/ppermute | solution.py:233
  6.2 3.5 %bring.2.refs_1_.refs_6_.refs_4_ = bf16[4096,1024]{1,0:T(8,128)(2,1)S(1)} custom-call(bf16[4096,2048]{1,0:T(8,128)(2,1)} %refs_8_.1), custom_call_target="tpu_custom_call" | custom-call | flops 1100000000 | tf_op jit(solution)/shard_map/bring/pallas_call | solution.py:79
  9.7 3.5 %bring.3.refs_2_.refs_7_.refs_5_ = bf16[4096,1024]{1,0:T(8,128)(2,1)S(1)} custom-call(bf16[4096,2048]{1,0:T(8,128)(2,1)} %refs_9_.1, bf16[4096,1024]{1,0:T(8,128)(2,1)S(1)} %bring.2.refs_1_.refs_6_.refs_4_), custom_call_target="tpu_custom_call" | custom-call | flops 1100000000 | tf_op jit(solution)/shard_map/bring/pallas_call | solution.py:79
  13.4 1.9 %collective-permute-start.4 = (bf16[32,4096]{1,0:T(8,128)(2,1)S(1)}, bf16[32,4096]{1,0:T(8,128)(2,1)S(1)}, u32[]{:S(2)}, u32[]{:S(2)}) collective-permute-start(bf16[32,4096]{1,0:T(8,128)(2,1)S(1)} %get-tuple-element.48.refs_2_), channel_id=1, source_target_pairs={{0,2},{2,4},{4,6},{6,7},{7,5},{5,3},{3,1},{1,0},{8,10},{10,12},{12... | collective-permute-start | bytes 786440 | tf_op jit(solution)/shard_map/farR2/ppermute | solution.py:233
  15.4 1.4 %collective-permute-done.2.refs_0_ = bf16[32,4096]{1,0:T(8,128)(2,1)S(1)} collective-permute-done((bf16[32,4096]{1,0:T(8,128)(2,1)S(1)}, bf16[32,4096]{1,0:T(8,128)(2,1)S(1)}, u32[]{:S(2)}, u32[]{:S(2)}) %collective-permute-start.2) | collective-permute-done | bytes 262176 | tf_op jit(solution)/shard_map/nearR1/ppermute | solution.py:233
  16.8 1.9 %collective-permute-done.3.refs_1_ = bf16[32,4096]{1,0:T(8,128)(2,1)S(1)} collective-permute-done((bf16[32,4096]{1,0:T(8,128)(2,1)S(1)}, bf16[32,4096]{1,0:T(8,128)(2,1)S(1)}, u32[]{:S(2)}, u32[]{:S(2)}) %collective-permute-start.3) | collective-permute-done | bytes 262176 | tf_op jit(solution)/shard_map/nearL1/ppermute | solution.py:237
  18.7 1.6 %collective-permute-start.8 = (bf16[32,4096]{1,0:T(8,128)(2,1)S(1)}, bf16[32,4096]{1,0:T(8,128)(2,1)S(1)}, u32[]{:S(2)}, u32[]{:S(2)}) collective-permute-start(bf16[32,4096]{1,0:T(8,128)(2,1)S(1)} %get-tuple-element.50.refs_4_.refs_10_), channel_id=1, source_target_pairs={{0,2},{2,4},{4,6},{6,7},{7,5},{5,3},{3,1},{1,0},{8,10},{10,12},{12... | collective-permute-start | bytes 786440 | tf_op jit(solution)/shard_map/nearR2/ppermute | solution.py:233
  20.7 5.9 %gate_up.5 = (f32[2,192,1024]{2,1,0:T(8,128)S(1)}, bf16[4096,1024]{1,0:T(8,128)(2,1)S(1)}, bf16[4096,1024]{1,0:T(8,128)(2,1)S(1)}) custom-call(bf16[32,4096]{1,0:T(8,128)(2,1)S(1)} %get-tuple-element.104.refs_0_, bf16[32,4096]{1,0:T(8,128)(2,1)S(1)} %get-tuple-element.103.refs_1_, bf16[32,4096]{1,0:T(8,128)(2,1)S(1)} %get-tuple-element.48.refs_2_, ...), custom_call_target="tpu_custom_call" | custom-call | flops 1100000000 | tf_op jit(solution)/shard_map/gate_up/pallas_call | solution.py:131
  26.7 1.6 %collective-permute-start.6 = (bf16[32,4096]{1,0:T(8,128)(2,1)S(1)}, bf16[32,4096]{1,0:T(8,128)(2,1)S(1)}, u32[]{:S(2)}, u32[]{:S(2)}) collective-permute-start(bf16[32,4096]{1,0:T(8,128)(2,1)S(1)} %get-tuple-element.55.refs_8_.refs_0_), channel_id=1, source_target_pairs={{0,2},{2,4},{4,6},{6,7},{7,5},{5,3},{3,1},{1,0},{8,10},{10,12},{12... | collective-permute-start | bytes 786440 | tf_op jit(solution)/shard_map/farR3/ppermute | solution.py:233
  28.8 3.4 %gate_up.6.refs_2_.a_ref = f32[2,192,1024]{2,1,0:T(8,128)S(1)} custom-call(bf16[32,4096]{1,0:T(8,128)(2,1)S(1)} %get-tuple-element.104.refs_0_, bf16[32,4096]{1,0:T(8,128)(2,1)S(1)} %get-tuple-element.103.refs_1_, bf16[32,4096]{1,0:T(8,128)(2,1)S(1)} %get-tuple-element.48.refs_2_, bf16[32,4096]{1,0:T(8,128)(2,1)S(1)} %get-tuple-element.49.refs_3_, ...), custom_call_target="tpu_custom_call" | custom-call | flops 1100000000 | tf_op jit(solution)/shard_map/gate_up/pallas_call | solution.py:131
  32.2 1.6 %collective-permute-start.12 = (bf16[32,4096]{1,0:T(8,128)(2,1)S(1)}, bf16[32,4096]{1,0:T(8,128)(2,1)S(1)}, u32[]{:S(2)}, u32[]{:S(2)}) collective-permute-start(bf16[32,4096]{1,0:T(8,128)(2,1)S(1)} %get-tuple-element.57.refs_2_), channel_id=1, source_target_pairs={{0,2},{2,4},{4,6},{6,7},{7,5},{5,3},{3,1},{1,0},{8,10},{10,12},{12... | collective-permute-start | bytes 786440 | tf_op jit(solution)/shard_map/nearR3/ppermute | solution.py:233
  34.3 0.7 collective-permute-done.6.refs_0_
  35.1 1.9 %collective-permute-done.7.refs_1_ = bf16[32,4096]{1,0:T(8,128)(2,1)S(1)} collective-permute-done((bf16[32,4096]{1,0:T(8,128)(2,1)S(1)}, bf16[32,4096]{1,0:T(8,128)(2,1)S(1)}, u32[]{:S(2)}, u32[]{:S(2)}) %collective-permute-start.7) | collective-permute-done | bytes 262176 | tf_op jit(solution)/shard_map/farL3/ppermute | solution.py:237
  36.9 1.6 %collective-permute-start.10 = (bf16[32,4096]{1,0:T(8,128)(2,1)S(1)}, bf16[32,4096]{1,0:T(8,128)(2,1)S(1)}, u32[]{:S(2)}, u32[]{:S(2)}) collective-permute-start(bf16[32,4096]{1,0:T(8,128)(2,1)S(1)} %get-tuple-element.58.refs_4_.refs_10_), channel_id=1, source_target_pairs={{0,2},{2,4},{4,6},{6,7},{7,5},{5,3},{3,1},{1,0},{8,10},{10,12},{12... | collective-permute-start | bytes 786440 | tf_op jit(solution)/shard_map/farR4/ppermute | solution.py:233
  39.0 6.7 %gate_up.7 = (f32[2,192,1024]{2,1,0:T(8,128)S(1)}, f32[2,192,1024]{2,1,0:T(8,128)S(1)}) custom-call(bf16[32,4096]{1,0:T(8,128)(2,1)S(1)} %get-tuple-element.55.refs_8_.refs_0_, bf16[32,4096]{1,0:T(8,128)(2,1)S(1)} %get-tuple-element.56.refs_1_, bf16[32,4096]{1,0:T(8,128)(2,1)S(1)} %get-tuple-element.57.refs_2_, ...), custom_call_target="tpu_custom_call" | custom-call | flops 1100000000 | tf_op jit(solution)/shard_map/gate_up/pallas_call | solution.py:131
  46.0 2.9 %gate_up.8 = (f32[2,128,1024]{2,1,0:T(8,128)S(1)}, bf16[2048,1536]{1,0:T(8,128)(2,1)S(1)}) custom-call(bf16[32,4096]{1,0:T(8,128)(2,1)S(1)} %get-tuple-element.62.refs_4_.refs_0_, bf16[32,4096]{1,0:T(8,128)(2,1)S(1)} %get-tuple-element.64.refs_1_, bf16[32,4096]{1,0:T(8,128)(2,1)S(1)} %get-tuple-element.65.refs_2_, ...), custom_call_target="tpu_custom_call" | custom-call | flops 1100000000 | tf_op jit(solution)/shard_map/gate_up/pallas_call | solution.py:131
  48.8 0.6 collective-permute-start.18
  49.5 2.9 %gate_up.9 = (f32[2,128,1024]{2,1,0:T(8,128)S(1)}, bf16[2048,1536]{1,0:T(8,128)(2,1)S(1)}) custom-call(bf16[32,4096]{1,0:T(8,128)(2,1)S(1)} %get-tuple-element.62.refs_4_.refs_0_, bf16[32,4096]{1,0:T(8,128)(2,1)S(1)} %get-tuple-element.64.refs_1_, bf16[32,4096]{1,0:T(8,128)(2,1)S(1)} %get-tuple-element.65.refs_2_, ...), custom_call_target="tpu_custom_call" | custom-call | flops 1100000000 | tf_op jit(solution)/shard_map/gate_up/pallas_call | solution.py:131
  52.6 0.5 collective-permute-start.19
  53.6 0.7 collective-permute-done.19.refs_1_
  54.3 3.2 %down.4 = (bf16[32,4096]{1,0:T(8,128)(2,1)S(1)}, bf16[32,4096]{1,0:T(8,128)(2,1)S(1)}, bf16[32,4096]{1,0:T(8,128)(2,1)S(1)}, bf16[32,4096]{1,0:T(8,128)(2,1)S(1)}) custom-call(bf16[128,1024]{1,0:T(8,128)(2,1)S(1)} %gated.5.refs_0_, bf16[128,1024]{1,0:T(8,128)(2,1)S(1)} %collective-permute-done.19.refs_1_, bf16[2048,1536]{1,0:T(8,128)(2,1)S(1)} %get-tuple-element.67.refs_2_, ...), custom_call_target="tpu_custom_call" | custom-call | tf_op jit(solution)/shard_map/down/pallas_call | solution.py:204
  57.6 0.5 collective-permute-start.22
  58.1 1.6 %collective-permute-start.23 = (bf16[32,4096]{1,0:T(8,128)(2,1)S(1)}, bf16[32,4096]{1,0:T(8,128)(2,1)S(1)}, u32[]{:S(2)}, u32[]{:S(2)}) collective-permute-start(bf16[32,4096]{1,0:T(8,128)(2,1)S(1)} %get-tuple-element.76), channel_id=1, source_target_pairs={{0,2},{2,4},{4,6},{6,7},{7,5},{5,3},{3,1},{1,0},{8,10},{10,12},{12... | collective-permute-start | bytes 786440 | tf_op jit(solution)/shard_map/right/ppermute | solution.py:233
  60.1 1.6 %collective-permute-start.21 = (bf16[32,4096]{1,0:T(8,128)(2,1)S(1)}, bf16[32,4096]{1,0:T(8,128)(2,1)S(1)}, u32[]{:S(2)}, u32[]{:S(2)}) collective-permute-start(bf16[32,4096]{1,0:T(8,128)(2,1)S(1)} %get-tuple-element.74), channel_id=1, source_target_pairs={{0,2},{2,4},{4,6},{6,7},{7,5},{5,3},{3,1},{1,0},{8,10},{10,12},{12... | collective-permute-start | bytes 786440 | tf_op jit(solution)/shard_map/right/ppermute | solution.py:233
  62.1 4.4 %down.3.refs_2_ = f32[192,4096]{1,0:T(8,128)S(1)} custom-call(bf16[192,1024]{1,0:T(8,128)(2,1)S(1)} %gated.4.refs_0_, bf16[192,1024]{1,0:T(8,128)(2,1)S(1)} %collective-permute-done.17.refs_1_, bf16[2048,1536]{1,0:T(8,128)(2,1)S(1)} %get-tuple-element.67.refs_2_, bf16[2048,1536]{1,0:T(8,128)(2,1)S(1)} %get-tuple-element.69.refs_3_, bf16[2048,4096]{1,0:T(8,128)(2,1)} %refs_4_.5), custom_call_target="tpu_custom_call" | custom-call | tf_op jit(solution)/shard_map/down/pallas_call | solution.py:204
  66.8 0.5 collective-permute-done.23.refs_1_
  67.3 1.2 %collective-permute-start.24 = (bf16[32,4096]{1,0:T(8,128)(2,1)S(1)}, bf16[32,4096]{1,0:T(8,128)(2,1)S(1)}, u32[]{:S(2)}, u32[]{:S(2)}) collective-permute-start(bf16[32,4096]{1,0:T(8,128)(2,1)S(1)} %get-tuple-element.102.refs_2_), channel_id=1, source_target_pairs={{2,0},{4,2},{6,4},{7,6},{5,7},{3,5},{1,3},{0,1},{10,8},{12,10},{14... | collective-permute-start | bytes 786440 | tf_op jit(solution)/shard_map/left/ppermute | solution.py:237
  68.6 0.8 collective-permute-start.25
  69.4 3.0 %collective-permute-done.20.refs_0_ = bf16[32,4096]{1,0:T(8,128)(2,1)S(1)} collective-permute-done((bf16[32,4096]{1,0:T(8,128)(2,1)S(1)}, bf16[32,4096]{1,0:T(8,128)(2,1)S(1)}, u32[]{:S(2)}, u32[]{:S(2)}) %collective-permute-start.20) | collective-permute-done | bytes 262176 | tf_op jit(solution)/shard_map/left/ppermute | solution.py:237
  72.4 0.5 collective-permute-done.21.refs_1_
  73.0 1.2 %collective-permute-start.28 = (bf16[32,4096]{1,0:T(8,128)(2,1)S(1)}, bf16[32,4096]{1,0:T(8,128)(2,1)S(1)}, u32[]{:S(2)}, u32[]{:S(2)}) collective-permute-start(bf16[32,4096]{1,0:T(8,128)(2,1)S(1)} %get-tuple-element.100.refs_5_), channel_id=1, source_target_pairs={{2,0},{4,2},{6,4},{7,6},{5,7},{3,5},{1,3},{0,1},{10,8},{12,10},{14... | collective-permute-start | bytes 786440 | tf_op jit(solution)/shard_map/left/ppermute | solution.py:237
  74.2 0.8 collective-permute-start.29
  75.0 4.4 %down.5.refs_2_ = f32[192,4096]{1,0:T(8,128)S(1)} custom-call(bf16[192,1024]{1,0:T(8,128)(2,1)S(1)} %gated.3.refs_0_, bf16[192,1024]{1,0:T(8,128)(2,1)S(1)} %collective-permute-done.15.refs_1_, bf16[2048,1536]{1,0:T(8,128)(2,1)S(1)} %get-tuple-element.67.refs_2_, bf16[2048,1536]{1,0:T(8,128)(2,1)S(1)} %get-tuple-element.69.refs_3_, ...), custom_call_target="tpu_custom_call" | custom-call | tf_op jit(solution)/shard_map/down/pallas_call | solution.py:204
  79.6 1.2 %collective-permute-start.26 = (bf16[32,4096]{1,0:T(8,128)(2,1)S(1)}, bf16[32,4096]{1,0:T(8,128)(2,1)S(1)}, u32[]{:S(2)}, u32[]{:S(2)}) collective-permute-start(bf16[32,4096]{1,0:T(8,128)(2,1)S(1)} %get-tuple-element.98.refs_2_), channel_id=1, source_target_pairs={{2,0},{4,2},{6,4},{7,6},{5,7},{3,5},{1,3},{0,1},{10,8},{12,10},{14... | collective-permute-start | bytes 786440 | tf_op jit(solution)/shard_map/left/ppermute | solution.py:237
  80.8 0.8 collective-permute-start.27
  81.6 2.0 %collective-permute-done.28.refs_0_ = bf16[32,4096]{1,0:T(8,128)(2,1)S(1)} collective-permute-done((bf16[32,4096]{1,0:T(8,128)(2,1)S(1)}, bf16[32,4096]{1,0:T(8,128)(2,1)S(1)}, u32[]{:S(2)}, u32[]{:S(2)}) %collective-permute-start.28) | collective-permute-done | bytes 262176 | tf_op jit(solution)/shard_map/left/ppermute | solution.py:237
  83.6 0.5 collective-permute-done.29.refs_1_
  84.2 1.2 %collective-permute-start.32 = (bf16[32,4096]{1,0:T(8,128)(2,1)S(1)}, bf16[32,4096]{1,0:T(8,128)(2,1)S(1)}, u32[]{:S(2)}, u32[]{:S(2)}) collective-permute-start(bf16[32,4096]{1,0:T(8,128)(2,1)S(1)} %get-tuple-element.96.refs_2_), channel_id=1, source_target_pairs={{2,0},{4,2},{6,4},{7,6},{5,7},{3,5},{1,3},{0,1},{10,8},{12,10},{14... | collective-permute-start | bytes 786440 | tf_op jit(solution)/shard_map/left/ppermute | solution.py:237
  85.4 0.8 collective-permute-start.33
  86.3 3.0 %collective-permute-done.26.refs_0_ = bf16[32,4096]{1,0:T(8,128)(2,1)S(1)} collective-permute-done((bf16[32,4096]{1,0:T(8,128)(2,1)S(1)}, bf16[32,4096]{1,0:T(8,128)(2,1)S(1)}, u32[]{:S(2)}, u32[]{:S(2)}) %collective-permute-start.26) | collective-permute-done | bytes 262176 | tf_op jit(solution)/shard_map/left/ppermute | solution.py:237
  89.2 0.8 collective-permute-done.27.refs_1_
  90.1 1.6 %collective-permute-start.30 = (bf16[32,4096]{1,0:T(8,128)(2,1)S(1)}, bf16[32,4096]{1,0:T(8,128)(2,1)S(1)}, u32[]{:S(2)}, u32[]{:S(2)}) collective-permute-start(bf16[32,4096]{1,0:T(8,128)(2,1)S(1)} %get-tuple-element.94.refs_2_), channel_id=1, source_target_pairs={{2,0},{4,2},{6,4},{7,6},{5,7},{3,5},{1,3},{0,1},{10,8},{12,10},{14... | collective-permute-start | bytes 786440 | tf_op jit(solution)/shard_map/left/ppermute | solution.py:237
  92.2 2.6 %collective-permute-done.32.refs_0_ = bf16[32,4096]{1,0:T(8,128)(2,1)S(1)} collective-permute-done((bf16[32,4096]{1,0:T(8,128)(2,1)S(1)}, bf16[32,4096]{1,0:T(8,128)(2,1)S(1)}, u32[]{:S(2)}, u32[]{:S(2)}) %collective-permute-start.32) | collective-permute-done | bytes 262176 | tf_op jit(solution)/shard_map/left/ppermute | solution.py:237
  94.9 0.8 collective-permute-done.33.refs_1_
  95.7 4.3 %collective-permute-done.30.refs_0_ = bf16[32,4096]{1,0:T(8,128)(2,1)S(1)} collective-permute-done((bf16[32,4096]{1,0:T(8,128)(2,1)S(1)}, bf16[32,4096]{1,0:T(8,128)(2,1)S(1)}, u32[]{:S(2)}, u32[]{:S(2)}) %collective-permute-start.30) | collective-permute-done | bytes 262176 | tf_op jit(solution)/shard_map/left/ppermute | solution.py:237
  100.3 0.8 pad_maximum_fusion
  (55 shorter events, 5.6 us)
Async XLA Ops:
  1.1 12.1 %collective-permute-start = (bf16[32,4096]{1,0:T(8,128)(2,1)S(1)}, bf16[32,4096]{1,0:T(8,128)(2,1)S(1)}, u32[]{:S(2)}, u32[]{:S(2)}) collective-permute-start(bf16[32,4096]{1,0:T(8,128)(2,1)S(1)} %get-tuple-element.104.refs_0_), channel_id=1, source_target_pairs={{0,2},{2,4},{4,6},{6,7},{7,5},{5,3},{3,1},{1,0},{8,10},{10,12},{12... | collective-permute-start | bytes 786440 | tf_op jit(solution)/shard_map/farR1/ppermute | solution.py:233
  4.1 9.2 %collective-permute-start.1 = (bf16[32,4096]{1,0:T(8,128)(2,1)S(1)}, bf16[32,4096]{1,0:T(8,128)(2,1)S(1)}, u32[]{:S(2)}, u32[]{:S(2)}) collective-permute-start(bf16[32,4096]{1,0:T(8,128)(2,1)S(1)} %get-tuple-element.103.refs_1_), channel_id=1, source_target_pairs={{2,0},{4,2},{6,4},{7,6},{5,7},{3,5},{1,3},{0,1},{10,8},{12,10},{14... | collective-permute-start | bytes 786440 | tf_op jit(solution)/shard_map/farL1/ppermute | solution.py:237
  4.2 12.7 %collective-permute-start.2 = (bf16[32,4096]{1,0:T(8,128)(2,1)S(1)}, bf16[32,4096]{1,0:T(8,128)(2,1)S(1)}, u32[]{:S(2)}, u32[]{:S(2)}) collective-permute-start(bf16[32,4096]{1,0:T(8,128)(2,1)S(1)} %get-tuple-element.103.refs_1_), channel_id=1, source_target_pairs={{0,2},{2,4},{4,6},{6,7},{7,5},{5,3},{3,1},{1,0},{8,10},{10,12},{12... | collective-permute-start | bytes 786440 | tf_op jit(solution)/shard_map/nearR1/ppermute | solution.py:233
  6.2 12.5 %collective-permute-start.3 = (bf16[32,4096]{1,0:T(8,128)(2,1)S(1)}, bf16[32,4096]{1,0:T(8,128)(2,1)S(1)}, u32[]{:S(2)}, u32[]{:S(2)}) collective-permute-start(bf16[32,4096]{1,0:T(8,128)(2,1)S(1)} %get-tuple-element.104.refs_0_), channel_id=1, source_target_pairs={{2,0},{4,2},{6,4},{7,6},{5,7},{3,5},{1,3},{0,1},{10,8},{12,10},{14... | collective-permute-start | bytes 786440 | tf_op jit(solution)/shard_map/nearL1/ppermute | solution.py:237
  13.4 13.3 %collective-permute-start.4 = (bf16[32,4096]{1,0:T(8,128)(2,1)S(1)}, bf16[32,4096]{1,0:T(8,128)(2,1)S(1)}, u32[]{:S(2)}, u32[]{:S(2)}) collective-permute-start(bf16[32,4096]{1,0:T(8,128)(2,1)S(1)} %get-tuple-element.48.refs_2_), channel_id=1, source_target_pairs={{0,2},{2,4},{4,6},{6,7},{7,5},{5,3},{3,1},{1,0},{8,10},{10,12},{12... | collective-permute-start | bytes 786440 | tf_op jit(solution)/shard_map/farR2/ppermute | solution.py:233
  15.3 11.4 %collective-permute-start.5 = (bf16[32,4096]{1,0:T(8,128)(2,1)S(1)}, bf16[32,4096]{1,0:T(8,128)(2,1)S(1)}, u32[]{:S(2)}, u32[]{:S(2)}) collective-permute-start(bf16[32,4096]{1,0:T(8,128)(2,1)S(1)} %get-tuple-element.49.refs_3_), channel_id=1, source_target_pairs={{2,0},{4,2},{6,4},{7,6},{5,7},{3,5},{1,3},{0,1},{10,8},{12,10},{14... | collective-permute-start | bytes 786440 | tf_op jit(solution)/shard_map/farL2/ppermute | solution.py:237
  18.7 13.5 %collective-permute-start.8 = (bf16[32,4096]{1,0:T(8,128)(2,1)S(1)}, bf16[32,4096]{1,0:T(8,128)(2,1)S(1)}, u32[]{:S(2)}, u32[]{:S(2)}) collective-permute-start(bf16[32,4096]{1,0:T(8,128)(2,1)S(1)} %get-tuple-element.50.refs_4_.refs_10_), channel_id=1, source_target_pairs={{0,2},{2,4},{4,6},{6,7},{7,5},{5,3},{3,1},{1,0},{8,10},{10,12},{12... | collective-permute-start | bytes 786440 | tf_op jit(solution)/shard_map/nearR2/ppermute | solution.py:233
  20.3 11.9 %collective-permute-start.9 = (bf16[32,4096]{1,0:T(8,128)(2,1)S(1)}, bf16[32,4096]{1,0:T(8,128)(2,1)S(1)}, u32[]{:S(2)}, u32[]{:S(2)}) collective-permute-start(bf16[32,4096]{1,0:T(8,128)(2,1)S(1)} %get-tuple-element.51.refs_5_), channel_id=1, source_target_pairs={{2,0},{4,2},{6,4},{7,6},{5,7},{3,5},{1,3},{0,1},{10,8},{12,10},{14... | collective-permute-start | bytes 786440 | tf_op jit(solution)/shard_map/nearL2/ppermute | solution.py:237
  26.7 8.3 %collective-permute-start.6 = (bf16[32,4096]{1,0:T(8,128)(2,1)S(1)}, bf16[32,4096]{1,0:T(8,128)(2,1)S(1)}, u32[]{:S(2)}, u32[]{:S(2)}) collective-permute-start(bf16[32,4096]{1,0:T(8,128)(2,1)S(1)} %get-tuple-element.55.refs_8_.refs_0_), channel_id=1, source_target_pairs={{0,2},{2,4},{4,6},{6,7},{7,5},{5,3},{3,1},{1,0},{8,10},{10,12},{12... | collective-permute-start | bytes 786440 | tf_op jit(solution)/shard_map/farR3/ppermute | solution.py:233
  28.3 8.6 %collective-permute-start.7 = (bf16[32,4096]{1,0:T(8,128)(2,1)S(1)}, bf16[32,4096]{1,0:T(8,128)(2,1)S(1)}, u32[]{:S(2)}, u32[]{:S(2)}) collective-permute-start(bf16[32,4096]{1,0:T(8,128)(2,1)S(1)} %get-tuple-element.56.refs_1_), channel_id=1, source_target_pairs={{2,0},{4,2},{6,4},{7,6},{5,7},{3,5},{1,3},{0,1},{10,8},{12,10},{14... | collective-permute-start | bytes 786440 | tf_op jit(solution)/shard_map/farL3/ppermute | solution.py:237
  32.2 13.4 %collective-permute-start.12 = (bf16[32,4096]{1,0:T(8,128)(2,1)S(1)}, bf16[32,4096]{1,0:T(8,128)(2,1)S(1)}, u32[]{:S(2)}, u32[]{:S(2)}) collective-permute-start(bf16[32,4096]{1,0:T(8,128)(2,1)S(1)} %get-tuple-element.57.refs_2_), channel_id=1, source_target_pairs={{0,2},{2,4},{4,6},{6,7},{7,5},{5,3},{3,1},{1,0},{8,10},{10,12},{12... | collective-permute-start | bytes 786440 | tf_op jit(solution)/shard_map/nearR3/ppermute | solution.py:233
  33.9 11.8 %collective-permute-start.13 = (bf16[32,4096]{1,0:T(8,128)(2,1)S(1)}, bf16[32,4096]{1,0:T(8,128)(2,1)S(1)}, u32[]{:S(2)}, u32[]{:S(2)}) collective-permute-start(bf16[32,4096]{1,0:T(8,128)(2,1)S(1)} %get-tuple-element.60.refs_3_), channel_id=1, source_target_pairs={{2,0},{4,2},{6,4},{7,6},{5,7},{3,5},{1,3},{0,1},{10,8},{12,10},{14... | collective-permute-start | bytes 786440 | tf_op jit(solution)/shard_map/nearL3/ppermute | solution.py:237
  36.9 8.7 %collective-permute-start.10 = (bf16[32,4096]{1,0:T(8,128)(2,1)S(1)}, bf16[32,4096]{1,0:T(8,128)(2,1)S(1)}, u32[]{:S(2)}, u32[]{:S(2)}) collective-permute-start(bf16[32,4096]{1,0:T(8,128)(2,1)S(1)} %get-tuple-element.58.refs_4_.refs_10_), channel_id=1, source_target_pairs={{0,2},{2,4},{4,6},{6,7},{7,5},{5,3},{3,1},{1,0},{8,10},{10,12},{12... | collective-permute-start | bytes 786440 | tf_op jit(solution)/shard_map/farR4/ppermute | solution.py:233
  38.5 7.4 %collective-permute-start.11 = (bf16[32,4096]{1,0:T(8,128)(2,1)S(1)}, bf16[32,4096]{1,0:T(8,128)(2,1)S(1)}, u32[]{:S(2)}, u32[]{:S(2)}) collective-permute-start(bf16[32,4096]{1,0:T(8,128)(2,1)S(1)} %get-tuple-element.59.refs_5_), channel_id=1, source_target_pairs={{2,0},{4,2},{6,4},{7,6},{5,7},{3,5},{1,3},{0,1},{10,8},{12,10},{14... | collective-permute-start | bytes 786440 | tf_op jit(solution)/shard_map/farL4/ppermute | solution.py:237
  46.0 7.2 %collective-permute-start.16 = (f32[2,192,1024]{2,1,0:T(8,128)S(1)}, f32[2,192,1024]{2,1,0:T(8,128)S(1)}, u32[]{:S(2)}, u32[]{:S(2)}) collective-permute-start(f32[2,192,1024]{2,1,0:T(8,128)S(1)} %get-tuple-element.71), channel_id=1, source_target_pairs={{0,8},{8,0},{1,9},{9,1},{2,10},{10,2},{3,11},{11,3},{4,12},{12,4},... | collective-permute-start | bytes 4718600 | tf_op jit(solution)/shard_map/swap/ppermute | solution.py:241
  48.8 3.5 %collective-permute-start.18 = (f32[2,128,1024]{2,1,0:T(8,128)S(1)}, f32[2,128,1024]{2,1,0:T(8,128)S(1)}, u32[]{:S(2)}, u32[]{:S(2)}) collective-permute-start(f32[2,128,1024]{2,1,0:T(8,128)S(1)} %get-tuple-element.68.refs_7_), channel_id=1, source_target_pairs={{0,8},{8,0},{1,9},{9,1},{2,10},{10,2},{3,11},{11,3},{4,12},{12,4},... | collective-permute-start | bytes 3145736 | tf_op jit(solution)/shard_map/swap/ppermute | solution.py:241
  49.4 10.7 %collective-permute-start.14 = (f32[2,192,1024]{2,1,0:T(8,128)S(1)}, f32[2,192,1024]{2,1,0:T(8,128)S(1)}, u32[]{:S(2)}, u32[]{:S(2)}) collective-permute-start(f32[2,192,1024]{2,1,0:T(8,128)S(1)} %get-tuple-element.63), channel_id=1, source_target_pairs={{0,8},{8,0},{1,9},{9,1},{2,10},{10,2},{3,11},{11,3},{4,12},{12,4},... | collective-permute-start | bytes 4718600 | tf_op jit(solution)/shard_map/swap/ppermute | solution.py:241
  52.6 1.7 %collective-permute-start.19 = (bf16[128,1024]{1,0:T(8,128)(2,1)S(1)}, bf16[128,1024]{1,0:T(8,128)(2,1)S(1)}, u32[]{:S(2)}, u32[]{:S(2)}) collective-permute-start(bf16[128,1024]{1,0:T(8,128)(2,1)S(1)} %gated.5.refs_0_), channel_id=1, source_target_pairs={{0,8},{8,0},{1,9},{9,1},{2,10},{10,2},{3,11},{11,3},{4,12},{12,4},... | collective-permute-start | bytes 786440 | tf_op jit(solution)/shard_map/swap/ppermute | solution.py:241
  53.5 8.6 %collective-permute-start.17 = (bf16[192,1024]{1,0:T(8,128)(2,1)S(1)}, bf16[192,1024]{1,0:T(8,128)(2,1)S(1)}, u32[]{:S(2)}, u32[]{:S(2)}) collective-permute-start(bf16[192,1024]{1,0:T(8,128)(2,1)S(1)} %gated.4.refs_0_), channel_id=1, source_target_pairs={{0,8},{8,0},{1,9},{9,1},{2,10},{10,2},{3,11},{11,3},{4,12},{12,4},... | collective-permute-start | bytes 1179656 | tf_op jit(solution)/shard_map/swap/ppermute | solution.py:241
  57.6 9.2 %collective-permute-start.22 = (bf16[32,4096]{1,0:T(8,128)(2,1)S(1)}, bf16[32,4096]{1,0:T(8,128)(2,1)S(1)}, u32[]{:S(2)}, u32[]{:S(2)}) collective-permute-start(bf16[32,4096]{1,0:T(8,128)(2,1)S(1)} %get-tuple-element.75), channel_id=1, source_target_pairs={{2,0},{4,2},{6,4},{7,6},{5,7},{3,5},{1,3},{0,1},{10,8},{12,10},{14... | collective-permute-start | bytes 786440 | tf_op jit(solution)/shard_map/left/ppermute | solution.py:237
  58.1 9.2 %collective-permute-start.23 = (bf16[32,4096]{1,0:T(8,128)(2,1)S(1)}, bf16[32,4096]{1,0:T(8,128)(2,1)S(1)}, u32[]{:S(2)}, u32[]{:S(2)}) collective-permute-start(bf16[32,4096]{1,0:T(8,128)(2,1)S(1)} %get-tuple-element.76), channel_id=1, source_target_pairs={{0,2},{2,4},{4,6},{6,7},{7,5},{5,3},{3,1},{1,0},{8,10},{10,12},{12... | collective-permute-start | bytes 786440 | tf_op jit(solution)/shard_map/right/ppermute | solution.py:233
  59.7 12.7 %collective-permute-start.20 = (bf16[32,4096]{1,0:T(8,128)(2,1)S(1)}, bf16[32,4096]{1,0:T(8,128)(2,1)S(1)}, u32[]{:S(2)}, u32[]{:S(2)}) collective-permute-start(bf16[32,4096]{1,0:T(8,128)(2,1)S(1)} %get-tuple-element.73), channel_id=1, source_target_pairs={{2,0},{4,2},{6,4},{7,6},{5,7},{3,5},{1,3},{0,1},{10,8},{12,10},{14... | collective-permute-start | bytes 786440 | tf_op jit(solution)/shard_map/left/ppermute | solution.py:237
  60.1 12.7 %collective-permute-start.21 = (bf16[32,4096]{1,0:T(8,128)(2,1)S(1)}, bf16[32,4096]{1,0:T(8,128)(2,1)S(1)}, u32[]{:S(2)}, u32[]{:S(2)}) collective-permute-start(bf16[32,4096]{1,0:T(8,128)(2,1)S(1)} %get-tuple-element.74), channel_id=1, source_target_pairs={{0,2},{2,4},{4,6},{6,7},{7,5},{5,3},{3,1},{1,0},{8,10},{10,12},{12... | collective-permute-start | bytes 786440 | tf_op jit(solution)/shard_map/right/ppermute | solution.py:233
  62.0 13.0 %collective-permute-start.15 = (bf16[192,1024]{1,0:T(8,128)(2,1)S(1)}, bf16[192,1024]{1,0:T(8,128)(2,1)S(1)}, u32[]{:S(2)}, u32[]{:S(2)}) collective-permute-start(bf16[192,1024]{1,0:T(8,128)(2,1)S(1)} %gated.3.refs_0_), channel_id=1, source_target_pairs={{0,8},{8,0},{1,9},{9,1},{2,10},{10,2},{3,11},{11,3},{4,12},{12,4},... | collective-permute-start | bytes 1179656 | tf_op jit(solution)/shard_map/swap/ppermute | solution.py:241
  67.3 12.1 %collective-permute-start.24 = (bf16[32,4096]{1,0:T(8,128)(2,1)S(1)}, bf16[32,4096]{1,0:T(8,128)(2,1)S(1)}, u32[]{:S(2)}, u32[]{:S(2)}) collective-permute-start(bf16[32,4096]{1,0:T(8,128)(2,1)S(1)} %get-tuple-element.102.refs_2_), channel_id=1, source_target_pairs={{2,0},{4,2},{6,4},{7,6},{5,7},{3,5},{1,3},{0,1},{10,8},{12,10},{14... | collective-permute-start | bytes 786440 | tf_op jit(solution)/shard_map/left/ppermute | solution.py:237
  68.6 10.9 %collective-permute-start.25 = (bf16[32,4096]{1,0:T(8,128)(2,1)S(1)}, bf16[32,4096]{1,0:T(8,128)(2,1)S(1)}, u32[]{:S(2)}, u32[]{:S(2)}) collective-permute-start(bf16[32,4096]{1,0:T(8,128)(2,1)S(1)} %get-tuple-element.101.refs_3_), channel_id=1, source_target_pairs={{0,2},{2,4},{4,6},{6,7},{7,5},{5,3},{3,1},{1,0},{8,10},{10,12},{12... | collective-permute-start | bytes 786440 | tf_op jit(solution)/shard_map/right/ppermute | solution.py:233
  73.0 10.7 %collective-permute-start.28 = (bf16[32,4096]{1,0:T(8,128)(2,1)S(1)}, bf16[32,4096]{1,0:T(8,128)(2,1)S(1)}, u32[]{:S(2)}, u32[]{:S(2)}) collective-permute-start(bf16[32,4096]{1,0:T(8,128)(2,1)S(1)} %get-tuple-element.100.refs_5_), channel_id=1, source_target_pairs={{2,0},{4,2},{6,4},{7,6},{5,7},{3,5},{1,3},{0,1},{10,8},{12,10},{14... | collective-permute-start | bytes 786440 | tf_op jit(solution)/shard_map/left/ppermute | solution.py:237
  74.2 9.9 %collective-permute-start.29 = (bf16[32,4096]{1,0:T(8,128)(2,1)S(1)}, bf16[32,4096]{1,0:T(8,128)(2,1)S(1)}, u32[]{:S(2)}, u32[]{:S(2)}) collective-permute-start(bf16[32,4096]{1,0:T(8,128)(2,1)S(1)} %get-tuple-element.99.refs_6_), channel_id=1, source_target_pairs={{0,2},{2,4},{4,6},{6,7},{7,5},{5,3},{3,1},{1,0},{8,10},{10,12},{12... | collective-permute-start | bytes 786440 | tf_op jit(solution)/shard_map/right/ppermute | solution.py:233
  79.6 9.7 %collective-permute-start.26 = (bf16[32,4096]{1,0:T(8,128)(2,1)S(1)}, bf16[32,4096]{1,0:T(8,128)(2,1)S(1)}, u32[]{:S(2)}, u32[]{:S(2)}) collective-permute-start(bf16[32,4096]{1,0:T(8,128)(2,1)S(1)} %get-tuple-element.98.refs_2_), channel_id=1, source_target_pairs={{2,0},{4,2},{6,4},{7,6},{5,7},{3,5},{1,3},{0,1},{10,8},{12,10},{14... | collective-permute-start | bytes 786440 | tf_op jit(solution)/shard_map/left/ppermute | solution.py:237
  80.8 9.2 %collective-permute-start.27 = (bf16[32,4096]{1,0:T(8,128)(2,1)S(1)}, bf16[32,4096]{1,0:T(8,128)(2,1)S(1)}, u32[]{:S(2)}, u32[]{:S(2)}) collective-permute-start(bf16[32,4096]{1,0:T(8,128)(2,1)S(1)} %get-tuple-element.97.refs_3_), channel_id=1, source_target_pairs={{0,2},{2,4},{4,6},{6,7},{7,5},{5,3},{3,1},{1,0},{8,10},{10,12},{12... | collective-permute-start | bytes 786440 | tf_op jit(solution)/shard_map/right/ppermute | solution.py:233
  84.2 10.7 %collective-permute-start.32 = (bf16[32,4096]{1,0:T(8,128)(2,1)S(1)}, bf16[32,4096]{1,0:T(8,128)(2,1)S(1)}, u32[]{:S(2)}, u32[]{:S(2)}) collective-permute-start(bf16[32,4096]{1,0:T(8,128)(2,1)S(1)} %get-tuple-element.96.refs_2_), channel_id=1, source_target_pairs={{2,0},{4,2},{6,4},{7,6},{5,7},{3,5},{1,3},{0,1},{10,8},{12,10},{14... | collective-permute-start | bytes 786440 | tf_op jit(solution)/shard_map/left/ppermute | solution.py:237
  85.4 10.2 %collective-permute-start.33 = (bf16[32,4096]{1,0:T(8,128)(2,1)S(1)}, bf16[32,4096]{1,0:T(8,128)(2,1)S(1)}, u32[]{:S(2)}, u32[]{:S(2)}) collective-permute-start(bf16[32,4096]{1,0:T(8,128)(2,1)S(1)} %get-tuple-element.95.refs_3_), channel_id=1, source_target_pairs={{0,2},{2,4},{4,6},{6,7},{7,5},{5,3},{3,1},{1,0},{8,10},{10,12},{12... | collective-permute-start | bytes 786440 | tf_op jit(solution)/shard_map/right/ppermute | solution.py:233
  90.1 9.8 %collective-permute-start.30 = (bf16[32,4096]{1,0:T(8,128)(2,1)S(1)}, bf16[32,4096]{1,0:T(8,128)(2,1)S(1)}, u32[]{:S(2)}, u32[]{:S(2)}) collective-permute-start(bf16[32,4096]{1,0:T(8,128)(2,1)S(1)} %get-tuple-element.94.refs_2_), channel_id=1, source_target_pairs={{2,0},{4,2},{6,4},{7,6},{5,7},{3,5},{1,3},{0,1},{10,8},{12,10},{14... | collective-permute-start | bytes 786440 | tf_op jit(solution)/shard_map/left/ppermute | solution.py:237
  91.8 8.3 %collective-permute-start.31 = (bf16[32,4096]{1,0:T(8,128)(2,1)S(1)}, bf16[32,4096]{1,0:T(8,128)(2,1)S(1)}, u32[]{:S(2)}, u32[]{:S(2)}) collective-permute-start(bf16[32,4096]{1,0:T(8,128)(2,1)S(1)} %get-tuple-element.93.refs_3_), channel_id=1, source_target_pairs={{0,2},{2,4},{4,6},{6,7},{7,5},{5,3},{3,1},{1,0},{8,10},{10,12},{12... | collective-permute-start | bytes 786440 | tf_op jit(solution)/shard_map/right/ppermute | solution.py:233

commit v14 on v13

--- a/solution.py
+++ b/solution.py
@@ -139,26 +139,32 @@
     )(*pieces, *map(in_vmem, weights), *[in_hbm(x) for x, _, _ in load], *after)
 
 
-def gated(ours, theirs):
-    _, m, w = ours.shape
+def gated(ours, *theirs):
+    m, w = sum(size for _, size, _ in theirs), ours.shape[2]
     tile = min(w, 256)
 
-    def body(a_ref, b_ref, o_ref):
+    def body(a_ref, *refs):
+        o_ref = refs[-1]
+
         @pl.loop(0, w // tile)
         def _(j):
             cols = pl.ds(pl.multiple_of(j * tile, tile), tile)
-            v = a_ref[0, :, cols] + b_ref[0, :, cols]
-            u = a_ref[1, :, cols] + b_ref[1, :, cols]
-            o_ref[:, cols] = (v / (1.0 + jnp.exp(-v)) * u).astype(BF16)
+            at = 0
+            for b_ref, (_, size, first) in zip(refs, theirs):
+                mine, others = pl.ds(at, size), pl.ds(first, size)
+                v = a_ref[0, mine, cols] + b_ref[0, others, cols]
+                u = a_ref[1, mine, cols] + b_ref[1, others, cols]
+                o_ref[mine, cols] = (v / (1.0 + jnp.exp(-v)) * u).astype(BF16)
+                at += size
 
     return pl.pallas_call(
         body,
         name="gated",
-        in_specs=[VMEM, VMEM],
+        in_specs=[VMEM] * (1 + len(theirs)),
         out_specs=VMEM,
         out_shape=jax.ShapeDtypeStruct((m, w), BF16),
         **params(2 << 20),
-    )(ours, theirs)
+    )(ours, *[x for x, _, _ in theirs])
 
 
 def down(halves, weights, outs, after):
@@ -265,13 +271,18 @@
             elif d == 2:
                 ours += gate_up(rows_now, wide[2:], after)
                 waiting, done = held, ours[-1:]
-            else:
+            elif d < half - 1:
                 waiting |= held
                 groups.append(list(waiting))
                 out = gate_up(list(waiting.values()), wide, after)
                 theirs.append(out[0])
                 ours.append(out[1])
                 waiting, done = {}, out[:1]
+            else:
+                late = list(held.values())
+                groups.append(list(waiting | held))
+                ours += gate_up(list((waiting | held).values()), wide[2:], after)
+                waiting, done = {}, ours[-1:]
             near_r, near_l = gate(near_r, near_l, after=done, work=GATE)
             waiting |= {("near_r", d): near_r, ("near_l", d): near_l}
             after = [near_r]
@@ -286,30 +297,35 @@
                 theirs.append(out[0])
                 wide += out[1:]
                 after = out[:1]
+            if d == half - 2:
+                theirs += gate_up(list(waiting.values()), wide[:2], after)
+                after = theirs[-1:]
         far_r, far_l, *theirs = gate(far_r, far_l, *theirs, after=after)
         waiting |= {("far_r", half): far_r, ("far_l", half): far_l}
 
-        def hide(ours, got):
-            h = gated(ours, got)
+        def hide(*sums):
+            h = gated(*sums)
             return h, other(h)
 
         last = list(waiting.values())
         part_cols = down_weight.shape[1] * 3 // 8
         load = [(down_weight, part_cols, 0)]
-        last_theirs, low = gate_up(last, wide[:2], [], load)
+        last_theirs, low = gate_up(last + late, wide[:2], [], load)
         last_got = other(last_theirs)
         got = [other(x) for x in theirs]
         load = [(down_weight, part_cols, part_cols)]
         last_ours, high = gate_up(last, wide[2:], [last_theirs], load)
         weight = [low, high, down_weight]
-        last = hide(last_ours, last_got)
+        size = last_ours.shape[1]
+        last = hide(last_ours, (last_got, size, 0))
         outs = [(i * cut, cut, BF16) for i in range(4)]
         b_l, b_r, a_l, a_r = down([last], weight, outs, [])
-        hidden = [hide(*pair) for pair in zip(ours, got)]
+        taken = [[(x, x.shape[1], 0)] for x in got]
+        taken[-1].append((last_got, sum(x.shape[0] for x in late), size))
+        hidden = [hide(x, *parts) for x, parts in zip(ours, taken)]
 
         def put_down(which, after):
-            size = sum(h.shape[0] for h, _ in hidden[which])
-            outs = [(0, size, F32)]
+            outs = [(0, sum(h.shape[0] for h, _ in hidden[which]), F32)]
             (rest,) = down(hidden[which], weight, outs, after)
             at = 0
             for key in sum(groups[which], []):

time: 101 us -> 104 us (1.030)
  waiting for transfers between devices: 25.5 us -> 27.4 us
  Pallas kernels: 41.6 us -> 43.2 us
    pallas_call x5 -> x6, Pallas kernels: 21.8 us -> 23.4 us  [gate_up(): pl.pallas_call(body, name='gate_up', in_specs=[VMEM] * (count + len(weigh...]
    ppermute x6, waiting for transfers between devices: 0.74 us -> 1.8 us  [other(): return lax.ppermute(x, 'gx', swap)]
  transfers between devices with their start and end apart: 34 -> 34, of which waited for: 19 -> 20; matrix products, arithmetic and copies ran while one was open for 0% -> 0% of each run, Pallas kernels for 41% -> 38%
where the time goes in v14:
time: 104 us
  Pallas kernels  43.2 us (42%)
  starting transfers between devices  30.9 us (30%)
  waiting for transfers between devices  27.4 us (26%)
  other arithmetic  1.44 us (1%)
  local copies, waits for them, and re-layouts  1.07 us (1%)
    pallas_call x6, Pallas kernels, gate_up(): pl.pallas_call(body, name='gate_up', in_specs=[VMEM] * (count + len(weigh...  23.4 us
    ppermute x14, starting transfers between devices, right(): return lax.ppermute(x, 'gy', to_right)  20.4 us
    ppermute x14, waiting for transfers between devices, left(): return lax.ppermute(x, 'gy', to_left)  19.7 us
    pallas_call x3, Pallas kernels, down(): pl.pallas_call(body, name='down', in_specs=[VMEM] * (2 * count + 2) + [AN...  12 us
    ppermute x14, starting transfers between devices, left(): return lax.ppermute(x, 'gy', to_left)  9.54 us
    pallas_call x2, Pallas kernels, bring(): pl.pallas_call(body, name='bring', in_specs=[ANY] * (count + len(after)),...  6.96 us
    ppermute x14, waiting for transfers between devices, right(): return lax.ppermute(x, 'gy', to_right)  5.93 us
  transfers between devices with their start and end apart: 34, of which 20 were waited for; matrix products, arithmetic and copies ran while one was open for 0% of the time, Pallas kernels for 38%

profile of v14, /device:TPU:0, one launch (start us, length us, event | category | flops | bytes accessed | tf_op | source)
XLA Modules:
  0.0 104.3 jit_solution(12165945953372850823)
XLA Ops:
  0.0 1.1 %fusion.14 = (bf16[32,4096]{1,0:T(8,128)(2,1)S(1)}, bf16[32,4096]{1,0:T(8,128)(2,1)S(1)}) fusion(bf16[64,4096]{1,0:T(8,128)(2,1)} %param.4), kind=kLoop, calls=%fused_computation.27 | loop fusion | bytes 1048576 | tf_op jit(solution)/shard_map/slice | solution.py:256
  1.1 3.1 %collective-permute-start = (bf16[32,4096]{1,0:T(8,128)(2,1)S(1)}, bf16[32,4096]{1,0:T(8,128)(2,1)S(1)}, u32[]{:S(2)}, u32[]{:S(2)}) collective-permute-start(bf16[32,4096]{1,0:T(8,128)(2,1)S(1)} %get-tuple-element.100.refs_0_), channel_id=1, source_target_pairs={{0,2},{2,4},{4,6},{6,7},{7,5},{5,3},{3,1},{1,0},{8,10},{10,12},{12... | collective-permute-start | bytes 786440 | tf_op jit(solution)/shard_map/farR1/ppermute | solution.py:239
  4.2 2.0 %collective-permute-start.2 = (bf16[32,4096]{1,0:T(8,128)(2,1)S(1)}, bf16[32,4096]{1,0:T(8,128)(2,1)S(1)}, u32[]{:S(2)}, u32[]{:S(2)}) collective-permute-start(bf16[32,4096]{1,0:T(8,128)(2,1)S(1)} %get-tuple-element.99.refs_1_), channel_id=1, source_target_pairs={{0,2},{2,4},{4,6},{6,7},{7,5},{5,3},{3,1},{1,0},{8,10},{10,12},{12... | collective-permute-start | bytes 786440 | tf_op jit(solution)/shard_map/nearR1/ppermute | solution.py:239
  6.2 3.5 %bring.2.refs_1_.refs_6_.refs_4_ = bf16[4096,1024]{1,0:T(8,128)(2,1)S(1)} custom-call(bf16[4096,2048]{1,0:T(8,128)(2,1)} %refs_8_.2), custom_call_target="tpu_custom_call" | custom-call | flops 1100000000 | tf_op jit(solution)/shard_map/bring/pallas_call | solution.py:79
  9.7 3.5 %bring.3.refs_2_.refs_7_.refs_5_ = bf16[4096,1024]{1,0:T(8,128)(2,1)S(1)} custom-call(bf16[4096,2048]{1,0:T(8,128)(2,1)} %refs_9_.1, bf16[4096,1024]{1,0:T(8,128)(2,1)S(1)} %bring.2.refs_1_.refs_6_.refs_4_), custom_call_target="tpu_custom_call" | custom-call | flops 1100000000 | tf_op jit(solution)/shard_map/bring/pallas_call | solution.py:79
  13.4 1.9 %collective-permute-start.4 = (bf16[32,4096]{1,0:T(8,128)(2,1)S(1)}, bf16[32,4096]{1,0:T(8,128)(2,1)S(1)}, u32[]{:S(2)}, u32[]{:S(2)}) collective-permute-start(bf16[32,4096]{1,0:T(8,128)(2,1)S(1)} %get-tuple-element.46.refs_2_), channel_id=1, source_target_pairs={{0,2},{2,4},{4,6},{6,7},{7,5},{5,3},{3,1},{1,0},{8,10},{10,12},{12... | collective-permute-start | bytes 786440 | tf_op jit(solution)/shard_map/farR2/ppermute | solution.py:239
  15.4 1.4 %collective-permute-done.2.refs_0_ = bf16[32,4096]{1,0:T(8,128)(2,1)S(1)} collective-permute-done((bf16[32,4096]{1,0:T(8,128)(2,1)S(1)}, bf16[32,4096]{1,0:T(8,128)(2,1)S(1)}, u32[]{:S(2)}, u32[]{:S(2)}) %collective-permute-start.2) | collective-permute-done | bytes 262176 | tf_op jit(solution)/shard_map/nearR1/ppermute | solution.py:239
  16.8 1.9 %collective-permute-done.3.refs_1_ = bf16[32,4096]{1,0:T(8,128)(2,1)S(1)} collective-permute-done((bf16[32,4096]{1,0:T(8,128)(2,1)S(1)}, bf16[32,4096]{1,0:T(8,128)(2,1)S(1)}, u32[]{:S(2)}, u32[]{:S(2)}) %collective-permute-start.3) | collective-permute-done | bytes 262176 | tf_op jit(solution)/shard_map/nearL1/ppermute | solution.py:243
  18.7 1.6 %collective-permute-start.8 = (bf16[32,4096]{1,0:T(8,128)(2,1)S(1)}, bf16[32,4096]{1,0:T(8,128)(2,1)S(1)}, u32[]{:S(2)}, u32[]{:S(2)}) collective-permute-start(bf16[32,4096]{1,0:T(8,128)(2,1)S(1)} %get-tuple-element.48.refs_4_.refs_10_), channel_id=1, source_target_pairs={{0,2},{2,4},{4,6},{6,7},{7,5},{5,3},{3,1},{1,0},{8,10},{10,12},{12... | collective-permute-start | bytes 786440 | tf_op jit(solution)/shard_map/nearR2/ppermute | solution.py:239
  20.7 5.9 %gate_up.6 = (f32[2,192,1024]{2,1,0:T(8,128)S(1)}, bf16[4096,1024]{1,0:T(8,128)(2,1)S(1)}, bf16[4096,1024]{1,0:T(8,128)(2,1)S(1)}) custom-call(bf16[32,4096]{1,0:T(8,128)(2,1)S(1)} %get-tuple-element.100.refs_0_, bf16[32,4096]{1,0:T(8,128)(2,1)S(1)} %get-tuple-element.99.refs_1_, bf16[32,4096]{1,0:T(8,128)(2,1)S(1)} %get-tuple-element.46.refs_2_, ...), custom_call_target="tpu_custom_call" | custom-call | flops 1100000000 | tf_op jit(solution)/shard_map/gate_up/pallas_call | solution.py:131
  26.7 1.6 %collective-permute-start.6 = (bf16[32,4096]{1,0:T(8,128)(2,1)S(1)}, bf16[32,4096]{1,0:T(8,128)(2,1)S(1)}, u32[]{:S(2)}, u32[]{:S(2)}) collective-permute-start(bf16[32,4096]{1,0:T(8,128)(2,1)S(1)} %get-tuple-element.53.refs_8_.refs_0_), channel_id=1, source_target_pairs={{0,2},{2,4},{4,6},{6,7},{7,5},{5,3},{3,1},{1,0},{8,10},{10,12},{12... | collective-permute-start | bytes 786440 | tf_op jit(solution)/shard_map/farR3/ppermute | solution.py:239
  28.8 3.4 %gate_up.7.refs_2_.a_ref = f32[2,192,1024]{2,1,0:T(8,128)S(1)} custom-call(bf16[32,4096]{1,0:T(8,128)(2,1)S(1)} %get-tuple-element.100.refs_0_, bf16[32,4096]{1,0:T(8,128)(2,1)S(1)} %get-tuple-element.99.refs_1_, bf16[32,4096]{1,0:T(8,128)(2,1)S(1)} %get-tuple-element.46.refs_2_, bf16[32,4096]{1,0:T(8,128)(2,1)S(1)} %get-tuple-element.47.refs_3_, ...), custom_call_target="tpu_custom_call" | custom-call | flops 1100000000 | tf_op jit(solution)/shard_map/gate_up/pallas_call | solution.py:131
  32.2 1.6 %collective-permute-start.12 = (bf16[32,4096]{1,0:T(8,128)(2,1)S(1)}, bf16[32,4096]{1,0:T(8,128)(2,1)S(1)}, u32[]{:S(2)}, u32[]{:S(2)}) collective-permute-start(bf16[32,4096]{1,0:T(8,128)(2,1)S(1)} %get-tuple-element.55.refs_2_.refs_6_), channel_id=1, source_target_pairs={{0,2},{2,4},{4,6},{6,7},{7,5},{5,3},{3,1},{1,0},{8,10},{10,12},{12... | collective-permute-start | bytes 786440 | tf_op jit(solution)/shard_map/nearR3/ppermute | solution.py:239
  34.3 2.3 %gate_up.8.refs_2_.refs_3_ = f32[2,128,1024]{2,1,0:T(8,128)S(1)} custom-call(bf16[32,4096]{1,0:T(8,128)(2,1)S(1)} %get-tuple-element.53.refs_8_.refs_0_, bf16[32,4096]{1,0:T(8,128)(2,1)S(1)} %get-tuple-element.54.refs_1_, bf16[32,4096]{1,0:T(8,128)(2,1)S(1)} %get-tuple-element.55.refs_2_.refs_6_, bf16[32,4096]{1,0:T(8,128)(2,1)S(1)} %get-tuple-element.56.refs_3_, ...), custom_call_target="tpu_custom_call" | custom-call | flops 1100000000 | tf_op jit(solution)/shard_map/gate_up/pallas_call | solution.py:131
  36.9 1.6 %collective-permute-start.10 = (bf16[32,4096]{1,0:T(8,128)(2,1)S(1)}, bf16[32,4096]{1,0:T(8,128)(2,1)S(1)}, u32[]{:S(2)}, u32[]{:S(2)}) collective-permute-start(bf16[32,4096]{1,0:T(8,128)(2,1)S(1)} %get-tuple-element.57.refs_4_.refs_8_), channel_id=1, source_target_pairs={{0,2},{2,4},{4,6},{6,7},{7,5},{5,3},{3,1},{1,0},{8,10},{10,12},{12... | collective-permute-start | bytes 786440 | tf_op jit(solution)/shard_map/farR4/ppermute | solution.py:239
  39.0 3.4 %gate_up.9.refs_2_.a_ref = f32[2,192,1024]{2,1,0:T(8,128)S(1)} custom-call(bf16[32,4096]{1,0:T(8,128)(2,1)S(1)} %get-tuple-element.53.refs_8_.refs_0_, bf16[32,4096]{1,0:T(8,128)(2,1)S(1)} %get-tuple-element.54.refs_1_, bf16[32,4096]{1,0:T(8,128)(2,1)S(1)} %get-tuple-element.55.refs_2_.refs_6_, bf16[32,4096]{1,0:T(8,128)(2,1)S(1)} %get-tuple-element.56.refs_3_, ...), custom_call_target="tpu_custom_call" | custom-call | flops 1100000000 | tf_op jit(solution)/shard_map/gate_up/pallas_call | solution.py:131
  42.4 0.7 collective-permute-done.13.refs_1_
  43.1 1.3 %collective-permute-done.10.refs_0_ = bf16[32,4096]{1,0:T(8,128)(2,1)S(1)} collective-permute-done((bf16[32,4096]{1,0:T(8,128)(2,1)S(1)}, bf16[32,4096]{1,0:T(8,128)(2,1)S(1)}, u32[]{:S(2)}, u32[]{:S(2)}) %collective-permute-start.10) | collective-permute-done | bytes 262176 | tf_op jit(solution)/shard_map/farR4/ppermute | solution.py:239
  44.4 1.6 %collective-permute-done.11.refs_1_ = bf16[32,4096]{1,0:T(8,128)(2,1)S(1)} collective-permute-done((bf16[32,4096]{1,0:T(8,128)(2,1)S(1)}, bf16[32,4096]{1,0:T(8,128)(2,1)S(1)}, u32[]{:S(2)}, u32[]{:S(2)}) %collective-permute-start.11) | collective-permute-done | bytes 262176 | tf_op jit(solution)/shard_map/farL4/ppermute | solution.py:243
  46.0 3.8 %gate_up.10 = (f32[2,192,1024]{2,1,0:T(8,128)S(1)}, bf16[2048,1536]{1,0:T(8,128)(2,1)S(1)}) custom-call(bf16[32,4096]{1,0:T(8,128)(2,1)S(1)} %get-tuple-element.59.refs_4_.refs_0_, bf16[32,4096]{1,0:T(8,128)(2,1)S(1)} %get-tuple-element.61.refs_1_, bf16[32,4096]{1,0:T(8,128)(2,1)S(1)} %get-tuple-element.62.refs_2_, ...), custom_call_target="tpu_custom_call" | custom-call | flops 1100000000 | tf_op jit(solution)/shard_map/gate_up/pallas_call | solution.py:131
  49.9 0.5 collective-permute-start.14
  50.5 4.4 %gate_up.11 = (f32[2,128,1024]{2,1,0:T(8,128)S(1)}, bf16[2048,1536]{1,0:T(8,128)(2,1)S(1)}) custom-call(bf16[32,4096]{1,0:T(8,128)(2,1)S(1)} %get-tuple-element.59.refs_4_.refs_0_, bf16[32,4096]{1,0:T(8,128)(2,1)S(1)} %get-tuple-element.61.refs_1_, bf16[32,4096]{1,0:T(8,128)(2,1)S(1)} %get-tuple-element.62.refs_2_, ...), custom_call_target="tpu_custom_call" | custom-call | flops 1100000000 | tf_op jit(solution)/shard_map/gate_up/pallas_call | solution.py:131
  55.3 1.8 %collective-permute-done.16.refs_0_ = f32[2,128,1024]{2,1,0:T(8,128)S(1)} collective-permute-done((f32[2,128,1024]{2,1,0:T(8,128)S(1)}, f32[2,128,1024]{2,1,0:T(8,128)S(1)}, u32[]{:S(2)}, u32[]{:S(2)}) %collective-permute-start.16) | collective-permute-done | bytes 1048608 | tf_op jit(solution)/shard_map/swap/ppermute | solution.py:247
  57.6 3.2 %down.4 = (bf16[32,4096]{1,0:T(8,128)(2,1)S(1)}, bf16[32,4096]{1,0:T(8,128)(2,1)S(1)}, bf16[32,4096]{1,0:T(8,128)(2,1)S(1)}, bf16[32,4096]{1,0:T(8,128)(2,1)S(1)}) custom-call(bf16[128,1024]{1,0:T(8,128)(2,1)S(1)} %gated.5.refs_0_, bf16[128,1024]{1,0:T(8,128)(2,1)S(1)} %collective-permute-done.19.refs_1_, bf16[2048,1536]{1,0:T(8,128)(2,1)S(1)} %get-tuple-element.64.refs_2_, ...), custom_call_target="tpu_custom_call" | custom-call | tf_op jit(solution)/shard_map/down/pallas_call | solution.py:210
  60.8 0.5 collective-permute-start.22
  61.3 1.6 %collective-permute-start.23 = (bf16[32,4096]{1,0:T(8,128)(2,1)S(1)}, bf16[32,4096]{1,0:T(8,128)(2,1)S(1)}, u32[]{:S(2)}, u32[]{:S(2)}) collective-permute-start(bf16[32,4096]{1,0:T(8,128)(2,1)S(1)} %get-tuple-element.72), channel_id=1, source_target_pairs={{0,2},{2,4},{4,6},{6,7},{7,5},{5,3},{3,1},{1,0},{8,10},{10,12},{12... | collective-permute-start | bytes 786440 | tf_op jit(solution)/shard_map/right/ppermute | solution.py:239
  63.3 0.5 collective-permute-start.20
  63.8 1.6 %collective-permute-start.21 = (bf16[32,4096]{1,0:T(8,128)(2,1)S(1)}, bf16[32,4096]{1,0:T(8,128)(2,1)S(1)}, u32[]{:S(2)}, u32[]{:S(2)}) collective-permute-start(bf16[32,4096]{1,0:T(8,128)(2,1)S(1)} %get-tuple-element.70), channel_id=1, source_target_pairs={{0,2},{2,4},{4,6},{6,7},{7,5},{5,3},{3,1},{1,0},{8,10},{10,12},{12... | collective-permute-start | bytes 786440 | tf_op jit(solution)/shard_map/right/ppermute | solution.py:239
  65.4 4.4 %down.3.refs_2_ = f32[192,4096]{1,0:T(8,128)S(1)} custom-call(bf16[192,1024]{1,0:T(8,128)(2,1)S(1)} %gated.4.refs_0_, bf16[192,1024]{1,0:T(8,128)(2,1)S(1)} %collective-permute-done.18.refs_1_, bf16[2048,1536]{1,0:T(8,128)(2,1)S(1)} %get-tuple-element.64.refs_2_, bf16[2048,1536]{1,0:T(8,128)(2,1)S(1)} %get-tuple-element.66.refs_3_, bf16[2048,4096]{1,0:T(8,128)(2,1)} %refs_4_.5), custom_call_target="tpu_custom_call" | custom-call | tf_op jit(solution)/shard_map/down/pallas_call | solution.py:210
  70.0 0.5 collective-permute-done.23.refs_1_
  70.6 1.2 %collective-permute-start.24 = (bf16[32,4096]{1,0:T(8,128)(2,1)S(1)}, bf16[32,4096]{1,0:T(8,128)(2,1)S(1)}, u32[]{:S(2)}, u32[]{:S(2)}) collective-permute-start(bf16[32,4096]{1,0:T(8,128)(2,1)S(1)} %get-tuple-element.98.refs_2_), channel_id=1, source_target_pairs={{2,0},{4,2},{6,4},{7,6},{5,7},{3,5},{1,3},{0,1},{10,8},{12,10},{14... | collective-permute-start | bytes 786440 | tf_op jit(solution)/shard_map/left/ppermute | solution.py:243
  71.8 0.8 collective-permute-start.25
  72.7 3.0 %collective-permute-done.20.refs_0_ = bf16[32,4096]{1,0:T(8,128)(2,1)S(1)} collective-permute-done((bf16[32,4096]{1,0:T(8,128)(2,1)S(1)}, bf16[32,4096]{1,0:T(8,128)(2,1)S(1)}, u32[]{:S(2)}, u32[]{:S(2)}) %collective-permute-start.20) | collective-permute-done | bytes 262176 | tf_op jit(solution)/shard_map/left/ppermute | solution.py:243
  76.2 1.2 %collective-permute-start.28 = (bf16[32,4096]{1,0:T(8,128)(2,1)S(1)}, bf16[32,4096]{1,0:T(8,128)(2,1)S(1)}, u32[]{:S(2)}, u32[]{:S(2)}) collective-permute-start(bf16[32,4096]{1,0:T(8,128)(2,1)S(1)} %get-tuple-element.96.refs_5_), channel_id=1, source_target_pairs={{2,0},{4,2},{6,4},{7,6},{5,7},{3,5},{1,3},{0,1},{10,8},{12,10},{14... | collective-permute-start | bytes 786440 | tf_op jit(solution)/shard_map/left/ppermute | solution.py:243
  77.4 0.8 collective-permute-start.29
  78.3 4.4 %down.5.refs_2_ = f32[192,4096]{1,0:T(8,128)S(1)} custom-call(bf16[192,1024]{1,0:T(8,128)(2,1)S(1)} %gated.3.refs_0_, bf16[192,1024]{1,0:T(8,128)(2,1)S(1)} %collective-permute-done.15.refs_1_, bf16[2048,1536]{1,0:T(8,128)(2,1)S(1)} %copy-done.1, bf16[2048,1536]{1,0:T(8,128)(2,1)S(1)} %get-tuple-element.66.refs_3_, bf16[2048,4096]{1,0:T(8,128)(2,1)} %refs_4_.5, ...), custom_call_target="tpu_custom_call" | custom-call | tf_op jit(solution)/shard_map/down/pallas_call | solution.py:210
  82.8 1.2 %collective-permute-start.26 = (bf16[32,4096]{1,0:T(8,128)(2,1)S(1)}, bf16[32,4096]{1,0:T(8,128)(2,1)S(1)}, u32[]{:S(2)}, u32[]{:S(2)}) collective-permute-start(bf16[32,4096]{1,0:T(8,128)(2,1)S(1)} %get-tuple-element.94.refs_2_), channel_id=1, source_target_pairs={{2,0},{4,2},{6,4},{7,6},{5,7},{3,5},{1,3},{0,1},{10,8},{12,10},{14... | collective-permute-start | bytes 786440 | tf_op jit(solution)/shard_map/left/ppermute | solution.py:243
  84.0 0.8 collective-permute-start.27
  84.9 2.0 %collective-permute-done.28.refs_0_ = bf16[32,4096]{1,0:T(8,128)(2,1)S(1)} collective-permute-done((bf16[32,4096]{1,0:T(8,128)(2,1)S(1)}, bf16[32,4096]{1,0:T(8,128)(2,1)S(1)}, u32[]{:S(2)}, u32[]{:S(2)}) %collective-permute-start.28) | collective-permute-done | bytes 262176 | tf_op jit(solution)/shard_map/left/ppermute | solution.py:243
  87.4 1.2 %collective-permute-start.32 = (bf16[32,4096]{1,0:T(8,128)(2,1)S(1)}, bf16[32,4096]{1,0:T(8,128)(2,1)S(1)}, u32[]{:S(2)}, u32[]{:S(2)}) collective-permute-start(bf16[32,4096]{1,0:T(8,128)(2,1)S(1)} %get-tuple-element.92.refs_2_), channel_id=1, source_target_pairs={{2,0},{4,2},{6,4},{7,6},{5,7},{3,5},{1,3},{0,1},{10,8},{12,10},{14... | collective-permute-start | bytes 786440 | tf_op jit(solution)/shard_map/left/ppermute | solution.py:243
  88.7 0.8 collective-permute-start.33
  89.5 3.0 %collective-permute-done.26.refs_0_ = bf16[32,4096]{1,0:T(8,128)(2,1)S(1)} collective-permute-done((bf16[32,4096]{1,0:T(8,128)(2,1)S(1)}, bf16[32,4096]{1,0:T(8,128)(2,1)S(1)}, u32[]{:S(2)}, u32[]{:S(2)}) %collective-permute-start.26) | collective-permute-done | bytes 262176 | tf_op jit(solution)/shard_map/left/ppermute | solution.py:243
  92.5 0.8 collective-permute-done.27.refs_1_
  93.4 1.6 %collective-permute-start.30 = (bf16[32,4096]{1,0:T(8,128)(2,1)S(1)}, bf16[32,4096]{1,0:T(8,128)(2,1)S(1)}, u32[]{:S(2)}, u32[]{:S(2)}) collective-permute-start(bf16[32,4096]{1,0:T(8,128)(2,1)S(1)} %get-tuple-element.90.refs_2_), channel_id=1, source_target_pairs={{2,0},{4,2},{6,4},{7,6},{5,7},{3,5},{1,3},{0,1},{10,8},{12,10},{14... | collective-permute-start | bytes 786440 | tf_op jit(solution)/shard_map/left/ppermute | solution.py:243
  95.4 2.6 %collective-permute-done.32.refs_0_ = bf16[32,4096]{1,0:T(8,128)(2,1)S(1)} collective-permute-done((bf16[32,4096]{1,0:T(8,128)(2,1)S(1)}, bf16[32,4096]{1,0:T(8,128)(2,1)S(1)}, u32[]{:S(2)}, u32[]{:S(2)}) %collective-permute-start.32) | collective-permute-done | bytes 262176 | tf_op jit(solution)/shard_map/left/ppermute | solution.py:243
  98.1 0.8 collective-permute-done.33.refs_1_
  98.9 4.3 %collective-permute-done.30.refs_0_ = bf16[32,4096]{1,0:T(8,128)(2,1)S(1)} collective-permute-done((bf16[32,4096]{1,0:T(8,128)(2,1)S(1)}, bf16[32,4096]{1,0:T(8,128)(2,1)S(1)}, u32[]{:S(2)}, u32[]{:S(2)}) %collective-permute-start.30) | collective-permute-done | bytes 262176 | tf_op jit(solution)/shard_map/left/ppermute | solution.py:243
  103.5 0.8 pad_maximum_fusion
  (60 shorter events, 6.3 us)
Async XLA Ops:
  1.1 12.1 %collective-permute-start = (bf16[32,4096]{1,0:T(8,128)(2,1)S(1)}, bf16[32,4096]{1,0:T(8,128)(2,1)S(1)}, u32[]{:S(2)}, u32[]{:S(2)}) collective-permute-start(bf16[32,4096]{1,0:T(8,128)(2,1)S(1)} %get-tuple-element.100.refs_0_), channel_id=1, source_target_pairs={{0,2},{2,4},{4,6},{6,7},{7,5},{5,3},{3,1},{1,0},{8,10},{10,12},{12... | collective-permute-start | bytes 786440 | tf_op jit(solution)/shard_map/farR1/ppermute | solution.py:239
  4.1 9.2 %collective-permute-start.1 = (bf16[32,4096]{1,0:T(8,128)(2,1)S(1)}, bf16[32,4096]{1,0:T(8,128)(2,1)S(1)}, u32[]{:S(2)}, u32[]{:S(2)}) collective-permute-start(bf16[32,4096]{1,0:T(8,128)(2,1)S(1)} %get-tuple-element.99.refs_1_), channel_id=1, source_target_pairs={{2,0},{4,2},{6,4},{7,6},{5,7},{3,5},{1,3},{0,1},{10,8},{12,10},{14... | collective-permute-start | bytes 786440 | tf_op jit(solution)/shard_map/farL1/ppermute | solution.py:243
  4.2 12.7 %collective-permute-start.2 = (bf16[32,4096]{1,0:T(8,128)(2,1)S(1)}, bf16[32,4096]{1,0:T(8,128)(2,1)S(1)}, u32[]{:S(2)}, u32[]{:S(2)}) collective-permute-start(bf16[32,4096]{1,0:T(8,128)(2,1)S(1)} %get-tuple-element.99.refs_1_), channel_id=1, source_target_pairs={{0,2},{2,4},{4,6},{6,7},{7,5},{5,3},{3,1},{1,0},{8,10},{10,12},{12... | collective-permute-start | bytes 786440 | tf_op jit(solution)/shard_map/nearR1/ppermute | solution.py:239
  6.2 12.5 %collective-permute-start.3 = (bf16[32,4096]{1,0:T(8,128)(2,1)S(1)}, bf16[32,4096]{1,0:T(8,128)(2,1)S(1)}, u32[]{:S(2)}, u32[]{:S(2)}) collective-permute-start(bf16[32,4096]{1,0:T(8,128)(2,1)S(1)} %get-tuple-element.100.refs_0_), channel_id=1, source_target_pairs={{2,0},{4,2},{6,4},{7,6},{5,7},{3,5},{1,3},{0,1},{10,8},{12,10},{14... | collective-permute-start | bytes 786440 | tf_op jit(solution)/shard_map/nearL1/ppermute | solution.py:243
  13.4 13.3 %collective-permute-start.4 = (bf16[32,4096]{1,0:T(8,128)(2,1)S(1)}, bf16[32,4096]{1,0:T(8,128)(2,1)S(1)}, u32[]{:S(2)}, u32[]{:S(2)}) collective-permute-start(bf16[32,4096]{1,0:T(8,128)(2,1)S(1)} %get-tuple-element.46.refs_2_), channel_id=1, source_target_pairs={{0,2},{2,4},{4,6},{6,7},{7,5},{5,3},{3,1},{1,0},{8,10},{10,12},{12... | collective-permute-start | bytes 786440 | tf_op jit(solution)/shard_map/farR2/ppermute | solution.py:239
  15.3 11.4 %collective-permute-start.5 = (bf16[32,4096]{1,0:T(8,128)(2,1)S(1)}, bf16[32,4096]{1,0:T(8,128)(2,1)S(1)}, u32[]{:S(2)}, u32[]{:S(2)}) collective-permute-start(bf16[32,4096]{1,0:T(8,128)(2,1)S(1)} %get-tuple-element.47.refs_3_), channel_id=1, source_target_pairs={{2,0},{4,2},{6,4},{7,6},{5,7},{3,5},{1,3},{0,1},{10,8},{12,10},{14... | collective-permute-start | bytes 786440 | tf_op jit(solution)/shard_map/farL2/ppermute | solution.py:243
  18.7 13.5 %collective-permute-start.8 = (bf16[32,4096]{1,0:T(8,128)(2,1)S(1)}, bf16[32,4096]{1,0:T(8,128)(2,1)S(1)}, u32[]{:S(2)}, u32[]{:S(2)}) collective-permute-start(bf16[32,4096]{1,0:T(8,128)(2,1)S(1)} %get-tuple-element.48.refs_4_.refs_10_), channel_id=1, source_target_pairs={{0,2},{2,4},{4,6},{6,7},{7,5},{5,3},{3,1},{1,0},{8,10},{10,12},{12... | collective-permute-start | bytes 786440 | tf_op jit(solution)/shard_map/nearR2/ppermute | solution.py:239
  20.3 11.9 %collective-permute-start.9 = (bf16[32,4096]{1,0:T(8,128)(2,1)S(1)}, bf16[32,4096]{1,0:T(8,128)(2,1)S(1)}, u32[]{:S(2)}, u32[]{:S(2)}) collective-permute-start(bf16[32,4096]{1,0:T(8,128)(2,1)S(1)} %get-tuple-element.49.refs_5_), channel_id=1, source_target_pairs={{2,0},{4,2},{6,4},{7,6},{5,7},{3,5},{1,3},{0,1},{10,8},{12,10},{14... | collective-permute-start | bytes 786440 | tf_op jit(solution)/shard_map/nearL2/ppermute | solution.py:243
  26.7 10.0 %collective-permute-start.6 = (bf16[32,4096]{1,0:T(8,128)(2,1)S(1)}, bf16[32,4096]{1,0:T(8,128)(2,1)S(1)}, u32[]{:S(2)}, u32[]{:S(2)}) collective-permute-start(bf16[32,4096]{1,0:T(8,128)(2,1)S(1)} %get-tuple-element.53.refs_8_.refs_0_), channel_id=1, source_target_pairs={{0,2},{2,4},{4,6},{6,7},{7,5},{5,3},{3,1},{1,0},{8,10},{10,12},{12... | collective-permute-start | bytes 786440 | tf_op jit(solution)/shard_map/farR3/ppermute | solution.py:239
  28.3 8.6 %collective-permute-start.7 = (bf16[32,4096]{1,0:T(8,128)(2,1)S(1)}, bf16[32,4096]{1,0:T(8,128)(2,1)S(1)}, u32[]{:S(2)}, u32[]{:S(2)}) collective-permute-start(bf16[32,4096]{1,0:T(8,128)(2,1)S(1)} %get-tuple-element.54.refs_1_), channel_id=1, source_target_pairs={{2,0},{4,2},{6,4},{7,6},{5,7},{3,5},{1,3},{0,1},{10,8},{12,10},{14... | collective-permute-start | bytes 786440 | tf_op jit(solution)/shard_map/farL3/ppermute | solution.py:243
  32.2 10.1 %collective-permute-start.12 = (bf16[32,4096]{1,0:T(8,128)(2,1)S(1)}, bf16[32,4096]{1,0:T(8,128)(2,1)S(1)}, u32[]{:S(2)}, u32[]{:S(2)}) collective-permute-start(bf16[32,4096]{1,0:T(8,128)(2,1)S(1)} %get-tuple-element.55.refs_2_.refs_6_), channel_id=1, source_target_pairs={{0,2},{2,4},{4,6},{6,7},{7,5},{5,3},{3,1},{1,0},{8,10},{10,12},{12... | collective-permute-start | bytes 786440 | tf_op jit(solution)/shard_map/nearR3/ppermute | solution.py:239
  33.9 9.2 %collective-permute-start.13 = (bf16[32,4096]{1,0:T(8,128)(2,1)S(1)}, bf16[32,4096]{1,0:T(8,128)(2,1)S(1)}, u32[]{:S(2)}, u32[]{:S(2)}) collective-permute-start(bf16[32,4096]{1,0:T(8,128)(2,1)S(1)} %get-tuple-element.56.refs_3_), channel_id=1, source_target_pairs={{2,0},{4,2},{6,4},{7,6},{5,7},{3,5},{1,3},{0,1},{10,8},{12,10},{14... | collective-permute-start | bytes 786440 | tf_op jit(solution)/shard_map/nearL3/ppermute | solution.py:243
  36.9 7.4 %collective-permute-start.10 = (bf16[32,4096]{1,0:T(8,128)(2,1)S(1)}, bf16[32,4096]{1,0:T(8,128)(2,1)S(1)}, u32[]{:S(2)}, u32[]{:S(2)}) collective-permute-start(bf16[32,4096]{1,0:T(8,128)(2,1)S(1)} %get-tuple-element.57.refs_4_.refs_8_), channel_id=1, source_target_pairs={{0,2},{2,4},{4,6},{6,7},{7,5},{5,3},{3,1},{1,0},{8,10},{10,12},{12... | collective-permute-start | bytes 786440 | tf_op jit(solution)/shard_map/farR4/ppermute | solution.py:239
  38.5 7.4 %collective-permute-start.11 = (bf16[32,4096]{1,0:T(8,128)(2,1)S(1)}, bf16[32,4096]{1,0:T(8,128)(2,1)S(1)}, u32[]{:S(2)}, u32[]{:S(2)}) collective-permute-start(bf16[32,4096]{1,0:T(8,128)(2,1)S(1)} %get-tuple-element.58.refs_5_), channel_id=1, source_target_pairs={{2,0},{4,2},{6,4},{7,6},{5,7},{3,5},{1,3},{0,1},{10,8},{12,10},{14... | collective-permute-start | bytes 786440 | tf_op jit(solution)/shard_map/farL4/ppermute | solution.py:243
  49.8 15.6 %copy-start = (bf16[2048,1536]{1,0:T(8,128)(2,1)}, bf16[2048,1536]{1,0:T(8,128)(2,1)S(1)}, u32[]{:S(2)}) copy-start(bf16[2048,1536]{1,0:T(8,128)(2,1)S(1)} %get-tuple-element.64.refs_2_) | copy-start | bytes 18874372
  49.8 5.1 %collective-permute-start.17 = (f32[2,192,1024]{2,1,0:T(8,128)S(1)}, f32[2,192,1024]{2,1,0:T(8,128)S(1)}, u32[]{:S(2)}, u32[]{:S(2)}) collective-permute-start(f32[2,192,1024]{2,1,0:T(8,128)S(1)} %get-tuple-element.65.refs_7_), channel_id=1, source_target_pairs={{0,8},{8,0},{1,9},{9,1},{2,10},{10,2},{3,11},{11,3},{4,12},{12,4},... | collective-permute-start | bytes 4718600 | tf_op jit(solution)/shard_map/swap/ppermute | solution.py:247
  49.9 13.0 %collective-permute-start.14 = (f32[2,192,1024]{2,1,0:T(8,128)S(1)}, f32[2,192,1024]{2,1,0:T(8,128)S(1)}, u32[]{:S(2)}, u32[]{:S(2)}) collective-permute-start(f32[2,192,1024]{2,1,0:T(8,128)S(1)} %get-tuple-element.60), channel_id=1, source_target_pairs={{0,8},{8,0},{1,9},{9,1},{2,10},{10,2},{3,11},{11,3},{4,12},{12,4},... | collective-permute-start | bytes 4718600 | tf_op jit(solution)/shard_map/swap/ppermute | solution.py:247
  50.4 6.6 %collective-permute-start.16 = (f32[2,128,1024]{2,1,0:T(8,128)S(1)}, f32[2,128,1024]{2,1,0:T(8,128)S(1)}, u32[]{:S(2)}, u32[]{:S(2)}) collective-permute-start(f32[2,128,1024]{2,1,0:T(8,128)S(1)} %get-tuple-element.67), channel_id=1, source_target_pairs={{0,8},{8,0},{1,9},{9,1},{2,10},{10,2},{3,11},{11,3},{4,12},{12,4},... | collective-permute-start | bytes 3145736 | tf_op jit(solution)/shard_map/swap/ppermute | solution.py:247
  55.2 2.4 %collective-permute-start.19 = (bf16[128,1024]{1,0:T(8,128)(2,1)S(1)}, bf16[128,1024]{1,0:T(8,128)(2,1)S(1)}, u32[]{:S(2)}, u32[]{:S(2)}) collective-permute-start(bf16[128,1024]{1,0:T(8,128)(2,1)S(1)} %gated.5.refs_0_), channel_id=1, source_target_pairs={{0,8},{8,0},{1,9},{9,1},{2,10},{10,2},{3,11},{11,3},{4,12},{12,4},... | collective-permute-start | bytes 786440 | tf_op jit(solution)/shard_map/swap/ppermute | solution.py:247
  57.4 6.4 %collective-permute-start.18 = (bf16[192,1024]{1,0:T(8,128)(2,1)S(1)}, bf16[192,1024]{1,0:T(8,128)(2,1)S(1)}, u32[]{:S(2)}, u32[]{:S(2)}) collective-permute-start(bf16[192,1024]{1,0:T(8,128)(2,1)S(1)} %gated.4.refs_0_), channel_id=1, source_target_pairs={{0,8},{8,0},{1,9},{9,1},{2,10},{10,2},{3,11},{11,3},{4,12},{12,4},... | collective-permute-start | bytes 1179656 | tf_op jit(solution)/shard_map/swap/ppermute | solution.py:247
  60.8 9.2 %collective-permute-start.22 = (bf16[32,4096]{1,0:T(8,128)(2,1)S(1)}, bf16[32,4096]{1,0:T(8,128)(2,1)S(1)}, u32[]{:S(2)}, u32[]{:S(2)}) collective-permute-start(bf16[32,4096]{1,0:T(8,128)(2,1)S(1)} %get-tuple-element.71), channel_id=1, source_target_pairs={{2,0},{4,2},{6,4},{7,6},{5,7},{3,5},{1,3},{0,1},{10,8},{12,10},{14... | collective-permute-start | bytes 786440 | tf_op jit(solution)/shard_map/left/ppermute | solution.py:243
  61.3 9.2 %collective-permute-start.23 = (bf16[32,4096]{1,0:T(8,128)(2,1)S(1)}, bf16[32,4096]{1,0:T(8,128)(2,1)S(1)}, u32[]{:S(2)}, u32[]{:S(2)}) collective-permute-start(bf16[32,4096]{1,0:T(8,128)(2,1)S(1)} %get-tuple-element.72), channel_id=1, source_target_pairs={{0,2},{2,4},{4,6},{6,7},{7,5},{5,3},{3,1},{1,0},{8,10},{10,12},{12... | collective-permute-start | bytes 786440 | tf_op jit(solution)/shard_map/right/ppermute | solution.py:239
  63.2 15.1 %collective-permute-start.15 = (bf16[192,1024]{1,0:T(8,128)(2,1)S(1)}, bf16[192,1024]{1,0:T(8,128)(2,1)S(1)}, u32[]{:S(2)}, u32[]{:S(2)}) collective-permute-start(bf16[192,1024]{1,0:T(8,128)(2,1)S(1)} %gated.3.refs_0_), channel_id=1, source_target_pairs={{0,8},{8,0},{1,9},{9,1},{2,10},{10,2},{3,11},{11,3},{4,12},{12,4},... | collective-permute-start | bytes 1179656 | tf_op jit(solution)/shard_map/swap/ppermute | solution.py:247
  63.3 12.3 %collective-permute-start.20 = (bf16[32,4096]{1,0:T(8,128)(2,1)S(1)}, bf16[32,4096]{1,0:T(8,128)(2,1)S(1)}, u32[]{:S(2)}, u32[]{:S(2)}) collective-permute-start(bf16[32,4096]{1,0:T(8,128)(2,1)S(1)} %get-tuple-element.69), channel_id=1, source_target_pairs={{2,0},{4,2},{6,4},{7,6},{5,7},{3,5},{1,3},{0,1},{10,8},{12,10},{14... | collective-permute-start | bytes 786440 | tf_op jit(solution)/shard_map/left/ppermute | solution.py:243
  63.8 12.3 %collective-permute-start.21 = (bf16[32,4096]{1,0:T(8,128)(2,1)S(1)}, bf16[32,4096]{1,0:T(8,128)(2,1)S(1)}, u32[]{:S(2)}, u32[]{:S(2)}) collective-permute-start(bf16[32,4096]{1,0:T(8,128)(2,1)S(1)} %get-tuple-element.70), channel_id=1, source_target_pairs={{0,2},{2,4},{4,6},{6,7},{7,5},{5,3},{3,1},{1,0},{8,10},{10,12},{12... | collective-permute-start | bytes 786440 | tf_op jit(solution)/shard_map/right/ppermute | solution.py:239
  70.5 7.8 %copy-start.1 = (bf16[2048,1536]{1,0:T(8,128)(2,1)S(1)}, bf16[2048,1536]{1,0:T(8,128)(2,1)}, u32[]{:S(2)}) copy-start(bf16[2048,1536]{1,0:T(8,128)(2,1)} %copy-done) | copy-start | bytes 18874372
  70.6 12.1 %collective-permute-start.24 = (bf16[32,4096]{1,0:T(8,128)(2,1)S(1)}, bf16[32,4096]{1,0:T(8,128)(2,1)S(1)}, u32[]{:S(2)}, u32[]{:S(2)}) collective-permute-start(bf16[32,4096]{1,0:T(8,128)(2,1)S(1)} %get-tuple-element.98.refs_2_), channel_id=1, source_target_pairs={{2,0},{4,2},{6,4},{7,6},{5,7},{3,5},{1,3},{0,1},{10,8},{12,10},{14... | collective-permute-start | bytes 786440 | tf_op jit(solution)/shard_map/left/ppermute | solution.py:243
  71.8 10.9 %collective-permute-start.25 = (bf16[32,4096]{1,0:T(8,128)(2,1)S(1)}, bf16[32,4096]{1,0:T(8,128)(2,1)S(1)}, u32[]{:S(2)}, u32[]{:S(2)}) collective-permute-start(bf16[32,4096]{1,0:T(8,128)(2,1)S(1)} %get-tuple-element.97.refs_3_), channel_id=1, source_target_pairs={{0,2},{2,4},{4,6},{6,7},{7,5},{5,3},{3,1},{1,0},{8,10},{10,12},{12... | collective-permute-start | bytes 786440 | tf_op jit(solution)/shard_map/right/ppermute | solution.py:239
  76.2 10.7 %collective-permute-start.28 = (bf16[32,4096]{1,0:T(8,128)(2,1)S(1)}, bf16[32,4096]{1,0:T(8,128)(2,1)S(1)}, u32[]{:S(2)}, u32[]{:S(2)}) collective-permute-start(bf16[32,4096]{1,0:T(8,128)(2,1)S(1)} %get-tuple-element.96.refs_5_), channel_id=1, source_target_pairs={{2,0},{4,2},{6,4},{7,6},{5,7},{3,5},{1,3},{0,1},{10,8},{12,10},{14... | collective-permute-start | bytes 786440 | tf_op jit(solution)/shard_map/left/ppermute | solution.py:243
  77.4 9.9 %collective-permute-start.29 = (bf16[32,4096]{1,0:T(8,128)(2,1)S(1)}, bf16[32,4096]{1,0:T(8,128)(2,1)S(1)}, u32[]{:S(2)}, u32[]{:S(2)}) collective-permute-start(bf16[32,4096]{1,0:T(8,128)(2,1)S(1)} %get-tuple-element.95.refs_6_), channel_id=1, source_target_pairs={{0,2},{2,4},{4,6},{6,7},{7,5},{5,3},{3,1},{1,0},{8,10},{10,12},{12... | collective-permute-start | bytes 786440 | tf_op jit(solution)/shard_map/right/ppermute | solution.py:239
  82.8 9.7 %collective-permute-start.26 = (bf16[32,4096]{1,0:T(8,128)(2,1)S(1)}, bf16[32,4096]{1,0:T(8,128)(2,1)S(1)}, u32[]{:S(2)}, u32[]{:S(2)}) collective-permute-start(bf16[32,4096]{1,0:T(8,128)(2,1)S(1)} %get-tuple-element.94.refs_2_), channel_id=1, source_target_pairs={{2,0},{4,2},{6,4},{7,6},{5,7},{3,5},{1,3},{0,1},{10,8},{12,10},{14... | collective-permute-start | bytes 786440 | tf_op jit(solution)/shard_map/left/ppermute | solution.py:243
  84.0 9.2 %collective-permute-start.27 = (bf16[32,4096]{1,0:T(8,128)(2,1)S(1)}, bf16[32,4096]{1,0:T(8,128)(2,1)S(1)}, u32[]{:S(2)}, u32[]{:S(2)}) collective-permute-start(bf16[32,4096]{1,0:T(8,128)(2,1)S(1)} %get-tuple-element.93.refs_3_), channel_id=1, source_target_pairs={{0,2},{2,4},{4,6},{6,7},{7,5},{5,3},{3,1},{1,0},{8,10},{10,12},{12... | collective-permute-start | bytes 786440 | tf_op jit(solution)/shard_map/right/ppermute | solution.py:239
  87.4 10.7 %collective-permute-start.32 = (bf16[32,4096]{1,0:T(8,128)(2,1)S(1)}, bf16[32,4096]{1,0:T(8,128)(2,1)S(1)}, u32[]{:S(2)}, u32[]{:S(2)}) collective-permute-start(bf16[32,4096]{1,0:T(8,128)(2,1)S(1)} %get-tuple-element.92.refs_2_), channel_id=1, source_target_pairs={{2,0},{4,2},{6,4},{7,6},{5,7},{3,5},{1,3},{0,1},{10,8},{12,10},{14... | collective-permute-start | bytes 786440 | tf_op jit(solution)/shard_map/left/ppermute | solution.py:243
  88.7 10.2 %collective-permute-start.33 = (bf16[32,4096]{1,0:T(8,128)(2,1)S(1)}, bf16[32,4096]{1,0:T(8,128)(2,1)S(1)}, u32[]{:S(2)}, u32[]{:S(2)}) collective-permute-start(bf16[32,4096]{1,0:T(8,128)(2,1)S(1)} %get-tuple-element.91.refs_3_), channel_id=1, source_target_pairs={{0,2},{2,4},{4,6},{6,7},{7,5},{5,3},{3,1},{1,0},{8,10},{10,12},{12... | collective-permute-start | bytes 786440 | tf_op jit(solution)/shard_map/right/ppermute | solution.py:239
  93.4 9.8 %collective-permute-start.30 = (bf16[32,4096]{1,0:T(8,128)(2,1)S(1)}, bf16[32,4096]{1,0:T(8,128)(2,1)S(1)}, u32[]{:S(2)}, u32[]{:S(2)}) collective-permute-start(bf16[32,4096]{1,0:T(8,128)(2,1)S(1)} %get-tuple-element.90.refs_2_), channel_id=1, source_target_pairs={{2,0},{4,2},{6,4},{7,6},{5,7},{3,5},{1,3},{0,1},{10,8},{12,10},{14... | collective-permute-start | bytes 786440 | tf_op jit(solution)/shard_map/left/ppermute | solution.py:243
  95.0 8.3 %collective-permute-start.31 = (bf16[32,4096]{1,0:T(8,128)(2,1)S(1)}, bf16[32,4096]{1,0:T(8,128)(2,1)S(1)}, u32[]{:S(2)}, u32[]{:S(2)}) collective-permute-start(bf16[32,4096]{1,0:T(8,128)(2,1)S(1)} %get-tuple-element.89.refs_3_), channel_id=1, source_target_pairs={{0,2},{2,4},{4,6},{6,7},{7,5},{5,3},{3,1},{1,0},{8,10},{10,12},{12... | collective-permute-start | bytes 786440 | tf_op jit(solution)/shard_map/right/ppermute | solution.py:239

commit v15 on v13

--- a/solution.py
+++ b/solution.py
@@ -298,7 +298,7 @@
         load = [(down_weight, part_cols, 0)]
         last_theirs, low = gate_up(last, wide[:2], [], load)
         last_got = other(last_theirs)
-        got = [other(x) for x in theirs]
+        got = [other(x) for x in gate(*theirs, after=[last_theirs])]
         load = [(down_weight, part_cols, part_cols)]
         last_ours, high = gate_up(last, wide[2:], [last_theirs], load)
         weight = [low, high, down_weight]

time: 101 us -> 104 us (1.030)
  waiting for transfers between devices: 25.5 us -> 28.4 us
    ppermute x14, waiting for transfers between devices: 5.42 us -> 22.7 us  [right(): return lax.ppermute(x, 'gy', to_right)]
    ppermute x14, waiting for transfers between devices: 19.3 us -> 2.89 us  [left(): return lax.ppermute(x, 'gy', to_left)]
    ppermute x14, starting transfers between devices: 9.48 us -> 22.5 us  [left(): return lax.ppermute(x, 'gy', to_left)]
    ppermute x14, starting transfers between devices: 20.4 us -> 7.43 us  [right(): return lax.ppermute(x, 'gy', to_right)]
    ppermute x6, waiting for transfers between devices: 0.74 us -> 2.87 us  [other(): return lax.ppermute(x, 'gx', swap)]
  transfers between devices with their start and end apart: 34 -> 34, of which waited for: 19 -> 15; matrix products, arithmetic and copies ran while one was open for 0% -> 0% of each run, Pallas kernels for 41% -> 37%
where the time goes in v15:
time: 104 us
  Pallas kernels  41.6 us (40%)
  starting transfers between devices  31.3 us (30%)
  waiting for transfers between devices  28.4 us (27%)
  other arithmetic  1.44 us (1%)
  local copies, waits for them, and re-layouts  1.06 us (1%)
    ppermute x14, waiting for transfers between devices, right(): return lax.ppermute(x, 'gy', to_right)  22.7 us
    ppermute x14, starting transfers between devices, left(): return lax.ppermute(x, 'gy', to_left)  22.5 us
    pallas_call x5, Pallas kernels, gate_up(): pl.pallas_call(body, name='gate_up', in_specs=[VMEM] * (count + len(weigh...  21.8 us
    pallas_call x3, Pallas kernels, down(): pl.pallas_call(body, name='down', in_specs=[VMEM] * (2 * count + 2) + [AN...  12 us
    ppermute x14, starting transfers between devices, right(): return lax.ppermute(x, 'gy', to_right)  7.43 us
    pallas_call x2, Pallas kernels, bring(): pl.pallas_call(body, name='bring', in_specs=[ANY] * (count + len(after)),...  6.96 us
    ppermute x14, waiting for transfers between devices, left(): return lax.ppermute(x, 'gy', to_left)  2.89 us
    ppermute x6, waiting for transfers between devices, other(): return lax.ppermute(x, 'gx', swap)  2.87 us
  transfers between devices with their start and end apart: 34, of which 15 were waited for; matrix products, arithmetic and copies ran while one was open for 0% of the time, Pallas kernels for 37%

profile of v15, /device:TPU:0, one launch (start us, length us, event | category | flops | bytes accessed | tf_op | source)
XLA Modules:
  0.0 104.0 jit_solution(3055766829232719334)
XLA Ops:
  0.0 1.1 %fusion.14 = (bf16[32,4096]{1,0:T(8,128)(2,1)S(1)}, bf16[32,4096]{1,0:T(8,128)(2,1)S(1)}) fusion(bf16[64,4096]{1,0:T(8,128)(2,1)} %param.4), kind=kLoop, calls=%fused_computation.27 | loop fusion | bytes 1048576 | tf_op jit(solution)/shard_map/slice | solution.py:250
  1.1 3.0 %collective-permute-start.1 = (bf16[32,4096]{1,0:T(8,128)(2,1)S(1)}, bf16[32,4096]{1,0:T(8,128)(2,1)S(1)}, u32[]{:S(2)}, u32[]{:S(2)}) collective-permute-start(bf16[32,4096]{1,0:T(8,128)(2,1)S(1)} %get-tuple-element.107.refs_1_), channel_id=1, source_target_pairs={{2,0},{4,2},{6,4},{7,6},{5,7},{3,5},{1,3},{0,1},{10,8},{12,10},{14... | collective-permute-start | bytes 786440 | tf_op jit(solution)/shard_map/farL1/ppermute | solution.py:237
  4.2 2.0 %collective-permute-start.2 = (bf16[32,4096]{1,0:T(8,128)(2,1)S(1)}, bf16[32,4096]{1,0:T(8,128)(2,1)S(1)}, u32[]{:S(2)}, u32[]{:S(2)}) collective-permute-start(bf16[32,4096]{1,0:T(8,128)(2,1)S(1)} %get-tuple-element.107.refs_1_), channel_id=1, source_target_pairs={{0,2},{2,4},{4,6},{6,7},{7,5},{5,3},{3,1},{1,0},{8,10},{10,12},{12... | collective-permute-start | bytes 786440 | tf_op jit(solution)/shard_map/nearR1/ppermute | solution.py:233
  6.2 3.5 %bring.2.refs_1_.refs_6_.refs_4_ = bf16[4096,1024]{1,0:T(8,128)(2,1)S(1)} custom-call(bf16[4096,2048]{1,0:T(8,128)(2,1)} %refs_8_.1), custom_call_target="tpu_custom_call" | custom-call | flops 1100000000 | tf_op jit(solution)/shard_map/bring/pallas_call | solution.py:79
  9.7 3.5 %bring.3.refs_2_.refs_7_.refs_5_ = bf16[4096,1024]{1,0:T(8,128)(2,1)S(1)} custom-call(bf16[4096,2048]{1,0:T(8,128)(2,1)} %refs_9_.1, bf16[4096,1024]{1,0:T(8,128)(2,1)S(1)} %bring.2.refs_1_.refs_6_.refs_4_), custom_call_target="tpu_custom_call" | custom-call | flops 1100000000 | tf_op jit(solution)/shard_map/bring/pallas_call | solution.py:79
  13.3 1.9 %collective-permute-start.5 = (bf16[32,4096]{1,0:T(8,128)(2,1)S(1)}, bf16[32,4096]{1,0:T(8,128)(2,1)S(1)}, u32[]{:S(2)}, u32[]{:S(2)}) collective-permute-start(bf16[32,4096]{1,0:T(8,128)(2,1)S(1)} %get-tuple-element.51.refs_3_), channel_id=1, source_target_pairs={{2,0},{4,2},{6,4},{7,6},{5,7},{3,5},{1,3},{0,1},{10,8},{12,10},{14... | collective-permute-start | bytes 786440 | tf_op jit(solution)/shard_map/farL2/ppermute | solution.py:237
  15.3 3.3 %collective-permute-done.2.refs_0_ = bf16[32,4096]{1,0:T(8,128)(2,1)S(1)} collective-permute-done((bf16[32,4096]{1,0:T(8,128)(2,1)S(1)}, bf16[32,4096]{1,0:T(8,128)(2,1)S(1)}, u32[]{:S(2)}, u32[]{:S(2)}) %collective-permute-start.2) | collective-permute-done | bytes 262176 | tf_op jit(solution)/shard_map/nearR1/ppermute | solution.py:233
  19.0 1.7 %collective-permute-start.9 = (bf16[32,4096]{1,0:T(8,128)(2,1)S(1)}, bf16[32,4096]{1,0:T(8,128)(2,1)S(1)}, u32[]{:S(2)}, u32[]{:S(2)}) collective-permute-start(bf16[32,4096]{1,0:T(8,128)(2,1)S(1)} %get-tuple-element.53.refs_5_), channel_id=1, source_target_pairs={{2,0},{4,2},{6,4},{7,6},{5,7},{3,5},{1,3},{0,1},{10,8},{12,10},{14... | collective-permute-start | bytes 786440 | tf_op jit(solution)/shard_map/nearL2/ppermute | solution.py:237
  20.7 5.9 %gate_up.5 = (f32[2,192,1024]{2,1,0:T(8,128)S(1)}, bf16[4096,1024]{1,0:T(8,128)(2,1)S(1)}, bf16[4096,1024]{1,0:T(8,128)(2,1)S(1)}) custom-call(bf16[32,4096]{1,0:T(8,128)(2,1)S(1)} %get-tuple-element.108.refs_0_, bf16[32,4096]{1,0:T(8,128)(2,1)S(1)} %get-tuple-element.107.refs_1_, bf16[32,4096]{1,0:T(8,128)(2,1)S(1)} %get-tuple-element.50.refs_2_, ...), custom_call_target="tpu_custom_call" | custom-call | flops 1100000000 | tf_op jit(solution)/shard_map/gate_up/pallas_call | solution.py:131
  26.7 1.6 %collective-permute-start.7 = (bf16[32,4096]{1,0:T(8,128)(2,1)S(1)}, bf16[32,4096]{1,0:T(8,128)(2,1)S(1)}, u32[]{:S(2)}, u32[]{:S(2)}) collective-permute-start(bf16[32,4096]{1,0:T(8,128)(2,1)S(1)} %get-tuple-element.58.refs_1_), channel_id=1, source_target_pairs={{2,0},{4,2},{6,4},{7,6},{5,7},{3,5},{1,3},{0,1},{10,8},{12,10},{14... | collective-permute-start | bytes 786440 | tf_op jit(solution)/shard_map/farL3/ppermute | solution.py:237
  28.3 0.4 collective-permute-start.6
  28.7 3.4 %gate_up.6.refs_2_.a_ref = f32[2,192,1024]{2,1,0:T(8,128)S(1)} custom-call(bf16[32,4096]{1,0:T(8,128)(2,1)S(1)} %get-tuple-element.108.refs_0_, bf16[32,4096]{1,0:T(8,128)(2,1)S(1)} %get-tuple-element.107.refs_1_, bf16[32,4096]{1,0:T(8,128)(2,1)S(1)} %get-tuple-element.50.refs_2_, bf16[32,4096]{1,0:T(8,128)(2,1)S(1)} %get-tuple-element.51.refs_3_, ...), custom_call_target="tpu_custom_call" | custom-call | flops 1100000000 | tf_op jit(solution)/shard_map/gate_up/pallas_call | solution.py:131
  32.2 1.6 %collective-permute-start.13 = (bf16[32,4096]{1,0:T(8,128)(2,1)S(1)}, bf16[32,4096]{1,0:T(8,128)(2,1)S(1)}, u32[]{:S(2)}, u32[]{:S(2)}) collective-permute-start(bf16[32,4096]{1,0:T(8,128)(2,1)S(1)} %get-tuple-element.62.refs_3_), channel_id=1, source_target_pairs={{2,0},{4,2},{6,4},{7,6},{5,7},{3,5},{1,3},{0,1},{10,8},{12,10},{14... | collective-permute-start | bytes 786440 | tf_op jit(solution)/shard_map/nearL3/ppermute | solution.py:237
  33.8 0.4 collective-permute-start.12
  34.3 0.7 collective-permute-done.7.refs_1_
  35.0 1.9 %collective-permute-done.6.refs_0_ = bf16[32,4096]{1,0:T(8,128)(2,1)S(1)} collective-permute-done((bf16[32,4096]{1,0:T(8,128)(2,1)S(1)}, bf16[32,4096]{1,0:T(8,128)(2,1)S(1)}, u32[]{:S(2)}, u32[]{:S(2)}) %collective-permute-start.6) | collective-permute-done | bytes 262176 | tf_op jit(solution)/shard_map/farR3/ppermute | solution.py:233
  37.3 1.6 %collective-permute-start.11 = (bf16[32,4096]{1,0:T(8,128)(2,1)S(1)}, bf16[32,4096]{1,0:T(8,128)(2,1)S(1)}, u32[]{:S(2)}, u32[]{:S(2)}) collective-permute-start(bf16[32,4096]{1,0:T(8,128)(2,1)S(1)} %get-tuple-element.61.refs_5_), channel_id=1, source_target_pairs={{2,0},{4,2},{6,4},{7,6},{5,7},{3,5},{1,3},{0,1},{10,8},{12,10},{14... | collective-permute-start | bytes 786440 | tf_op jit(solution)/shard_map/farL4/ppermute | solution.py:237
  38.9 6.6 %gate_up.7 = (f32[2,192,1024]{2,1,0:T(8,128)S(1)}, f32[2,192,1024]{2,1,0:T(8,128)S(1)}) custom-call(bf16[32,4096]{1,0:T(8,128)(2,1)S(1)} %get-tuple-element.57.refs_8_.refs_0_, bf16[32,4096]{1,0:T(8,128)(2,1)S(1)} %get-tuple-element.58.refs_1_, bf16[32,4096]{1,0:T(8,128)(2,1)S(1)} %get-tuple-element.59.refs_2_, ...), custom_call_target="tpu_custom_call" | custom-call | flops 1100000000 | tf_op jit(solution)/shard_map/gate_up/pallas_call | solution.py:131
  45.9 2.9 %gate_up.8 = (f32[2,128,1024]{2,1,0:T(8,128)S(1)}, bf16[2048,1536]{1,0:T(8,128)(2,1)S(1)}) custom-call(bf16[32,4096]{1,0:T(8,128)(2,1)S(1)} %get-tuple-element.64.refs_4_.refs_0_, bf16[32,4096]{1,0:T(8,128)(2,1)S(1)} %get-tuple-element.67.refs_1_, bf16[32,4096]{1,0:T(8,128)(2,1)S(1)} %get-tuple-element.68.refs_2_, ...), custom_call_target="tpu_custom_call" | custom-call | flops 1100000000 | tf_op jit(solution)/shard_map/gate_up/pallas_call | solution.py:131
  48.9 0.5 collective-permute-start.18
  49.5 2.9 %gate_up.9 = (f32[2,128,1024]{2,1,0:T(8,128)S(1)}, bf16[2048,1536]{1,0:T(8,128)(2,1)S(1)}) custom-call(bf16[32,4096]{1,0:T(8,128)(2,1)S(1)} %get-tuple-element.64.refs_4_.refs_0_, bf16[32,4096]{1,0:T(8,128)(2,1)S(1)} %get-tuple-element.67.refs_1_, bf16[32,4096]{1,0:T(8,128)(2,1)S(1)} %get-tuple-element.68.refs_2_, ...), custom_call_target="tpu_custom_call" | custom-call | flops 1100000000 | tf_op jit(solution)/shard_map/gate_up/pallas_call | solution.py:131
  52.3 1.4 %collective-permute-done.18.b_ref = f32[2,128,1024]{2,1,0:T(8,128)S(1)} collective-permute-done((f32[2,128,1024]{2,1,0:T(8,128)S(1)}, f32[2,128,1024]{2,1,0:T(8,128)S(1)}, u32[]{:S(2)}, u32[]{:S(2)}) %collective-permute-start.18) | collective-permute-done | bytes 1048608 | tf_op jit(solution)/shard_map/swap/ppermute | solution.py:241
  55.0 1.4 %collective-permute-done.19.refs_1_ = bf16[128,1024]{1,0:T(8,128)(2,1)S(1)} collective-permute-done((bf16[128,1024]{1,0:T(8,128)(2,1)S(1)}, bf16[128,1024]{1,0:T(8,128)(2,1)S(1)}, u32[]{:S(2)}, u32[]{:S(2)}) %collective-permute-start.19) | collective-permute-done | bytes 262176 | tf_op jit(solution)/shard_map/swap/ppermute | solution.py:241
  56.4 3.2 %down.4 = (bf16[32,4096]{1,0:T(8,128)(2,1)S(1)}, bf16[32,4096]{1,0:T(8,128)(2,1)S(1)}, bf16[32,4096]{1,0:T(8,128)(2,1)S(1)}, bf16[32,4096]{1,0:T(8,128)(2,1)S(1)}) custom-call(bf16[128,1024]{1,0:T(8,128)(2,1)S(1)} %gated.5.refs_0_, bf16[128,1024]{1,0:T(8,128)(2,1)S(1)} %collective-permute-done.19.refs_1_, bf16[2048,1536]{1,0:T(8,128)(2,1)S(1)} %get-tuple-element.72.refs_2_, ...), custom_call_target="tpu_custom_call" | custom-call | tf_op jit(solution)/shard_map/down/pallas_call | solution.py:204
  59.6 1.6 %collective-permute-start.22 = (bf16[32,4096]{1,0:T(8,128)(2,1)S(1)}, bf16[32,4096]{1,0:T(8,128)(2,1)S(1)}, u32[]{:S(2)}, u32[]{:S(2)}) collective-permute-start(bf16[32,4096]{1,0:T(8,128)(2,1)S(1)} %get-tuple-element.79), channel_id=1, source_target_pairs={{2,0},{4,2},{6,4},{7,6},{5,7},{3,5},{1,3},{0,1},{10,8},{12,10},{14... | collective-permute-start | bytes 786440 | tf_op jit(solution)/shard_map/left/ppermute | solution.py:237
  61.3 0.5 collective-permute-start.23
  61.7 1.6 %collective-permute-start.20 = (bf16[32,4096]{1,0:T(8,128)(2,1)S(1)}, bf16[32,4096]{1,0:T(8,128)(2,1)S(1)}, u32[]{:S(2)}, u32[]{:S(2)}) collective-permute-start(bf16[32,4096]{1,0:T(8,128)(2,1)S(1)} %get-tuple-element.77), channel_id=1, source_target_pairs={{2,0},{4,2},{6,4},{7,6},{5,7},{3,5},{1,3},{0,1},{10,8},{12,10},{14... | collective-permute-start | bytes 786440 | tf_op jit(solution)/shard_map/left/ppermute | solution.py:237
  63.3 0.5 collective-permute-start.21
  64.2 4.4 %down.3.refs_2_ = f32[192,4096]{1,0:T(8,128)S(1)} custom-call(bf16[192,1024]{1,0:T(8,128)(2,1)S(1)} %gated.4.refs_0_, bf16[192,1024]{1,0:T(8,128)(2,1)S(1)} %collective-permute-done.17.refs_1_, bf16[2048,1536]{1,0:T(8,128)(2,1)S(1)} %get-tuple-element.72.refs_2_, bf16[2048,1536]{1,0:T(8,128)(2,1)S(1)} %get-tuple-element.73.refs_3_, bf16[2048,4096]{1,0:T(8,128)(2,1)} %refs_4_.5), custom_call_target="tpu_custom_call" | custom-call | tf_op jit(solution)/shard_map/down/pallas_call | solution.py:204
  68.9 1.6 %collective-permute-done.23.refs_1_ = bf16[32,4096]{1,0:T(8,128)(2,1)S(1)} collective-permute-done((bf16[32,4096]{1,0:T(8,128)(2,1)S(1)}, bf16[32,4096]{1,0:T(8,128)(2,1)S(1)}, u32[]{:S(2)}, u32[]{:S(2)}) %collective-permute-start.23) | collective-permute-done | bytes 262176 | tf_op jit(solution)/shard_map/right/ppermute | solution.py:233
  70.6 0.5 collective-permute-start.25
  71.1 1.6 %collective-permute-start.24 = (bf16[32,4096]{1,0:T(8,128)(2,1)S(1)}, bf16[32,4096]{1,0:T(8,128)(2,1)S(1)}, u32[]{:S(2)}, u32[]{:S(2)}) collective-permute-start(bf16[32,4096]{1,0:T(8,128)(2,1)S(1)} %get-tuple-element.106.refs_2_), channel_id=1, source_target_pairs={{2,0},{4,2},{6,4},{7,6},{5,7},{3,5},{1,3},{0,1},{10,8},{12,10},{14... | collective-permute-start | bytes 786440 | tf_op jit(solution)/shard_map/left/ppermute | solution.py:237
  72.6 1.8 %collective-permute-done.20.refs_0_ = bf16[32,4096]{1,0:T(8,128)(2,1)S(1)} collective-permute-done((bf16[32,4096]{1,0:T(8,128)(2,1)S(1)}, bf16[32,4096]{1,0:T(8,128)(2,1)S(1)}, u32[]{:S(2)}, u32[]{:S(2)}) %collective-permute-start.20) | collective-permute-done | bytes 262176 | tf_op jit(solution)/shard_map/left/ppermute | solution.py:237
  74.5 1.6 %collective-permute-done.21.refs_1_ = bf16[32,4096]{1,0:T(8,128)(2,1)S(1)} collective-permute-done((bf16[32,4096]{1,0:T(8,128)(2,1)S(1)}, bf16[32,4096]{1,0:T(8,128)(2,1)S(1)}, u32[]{:S(2)}, u32[]{:S(2)}) %collective-permute-start.21) | collective-permute-done | bytes 262176 | tf_op jit(solution)/shard_map/right/ppermute | solution.py:233
  76.2 0.5 collective-permute-start.29
  76.7 1.6 %collective-permute-start.28 = (bf16[32,4096]{1,0:T(8,128)(2,1)S(1)}, bf16[32,4096]{1,0:T(8,128)(2,1)S(1)}, u32[]{:S(2)}, u32[]{:S(2)}) collective-permute-start(bf16[32,4096]{1,0:T(8,128)(2,1)S(1)} %get-tuple-element.104.refs_5_), channel_id=1, source_target_pairs={{2,0},{4,2},{6,4},{7,6},{5,7},{3,5},{1,3},{0,1},{10,8},{12,10},{14... | collective-permute-start | bytes 786440 | tf_op jit(solution)/shard_map/left/ppermute | solution.py:237
  78.3 4.4 %down.5.refs_2_ = f32[192,4096]{1,0:T(8,128)S(1)} custom-call(bf16[192,1024]{1,0:T(8,128)(2,1)S(1)} %gated.3.refs_0_, bf16[192,1024]{1,0:T(8,128)(2,1)S(1)} %collective-permute-done.15.refs_1_, bf16[2048,1536]{1,0:T(8,128)(2,1)S(1)} %get-tuple-element.72.refs_2_, bf16[2048,1536]{1,0:T(8,128)(2,1)S(1)} %get-tuple-element.73.refs_3_, ...), custom_call_target="tpu_custom_call" | custom-call | tf_op jit(solution)/shard_map/down/pallas_call | solution.py:204
  82.8 0.5 collective-permute-start.27
  83.3 1.6 %collective-permute-start.26 = (bf16[32,4096]{1,0:T(8,128)(2,1)S(1)}, bf16[32,4096]{1,0:T(8,128)(2,1)S(1)}, u32[]{:S(2)}, u32[]{:S(2)}) collective-permute-start(bf16[32,4096]{1,0:T(8,128)(2,1)S(1)} %get-tuple-element.102.refs_2_), channel_id=1, source_target_pairs={{2,0},{4,2},{6,4},{7,6},{5,7},{3,5},{1,3},{0,1},{10,8},{12,10},{14... | collective-permute-start | bytes 786440 | tf_op jit(solution)/shard_map/left/ppermute | solution.py:237
  84.8 2.5 %collective-permute-done.29.refs_1_ = bf16[32,4096]{1,0:T(8,128)(2,1)S(1)} collective-permute-done((bf16[32,4096]{1,0:T(8,128)(2,1)S(1)}, bf16[32,4096]{1,0:T(8,128)(2,1)S(1)}, u32[]{:S(2)}, u32[]{:S(2)}) %collective-permute-start.29) | collective-permute-done | bytes 262176 | tf_op jit(solution)/shard_map/right/ppermute | solution.py:233
  87.4 0.5 collective-permute-start.33
  87.9 1.6 %collective-permute-start.32 = (bf16[32,4096]{1,0:T(8,128)(2,1)S(1)}, bf16[32,4096]{1,0:T(8,128)(2,1)S(1)}, u32[]{:S(2)}, u32[]{:S(2)}) collective-permute-start(bf16[32,4096]{1,0:T(8,128)(2,1)S(1)} %get-tuple-element.100.refs_2_), channel_id=1, source_target_pairs={{2,0},{4,2},{6,4},{7,6},{5,7},{3,5},{1,3},{0,1},{10,8},{12,10},{14... | collective-permute-start | bytes 786440 | tf_op jit(solution)/shard_map/left/ppermute | solution.py:237
  89.5 3.4 %collective-permute-done.27.refs_1_ = bf16[32,4096]{1,0:T(8,128)(2,1)S(1)} collective-permute-done((bf16[32,4096]{1,0:T(8,128)(2,1)S(1)}, bf16[32,4096]{1,0:T(8,128)(2,1)S(1)}, u32[]{:S(2)}, u32[]{:S(2)}) %collective-permute-start.27) | collective-permute-done | bytes 262176 | tf_op jit(solution)/shard_map/right/ppermute | solution.py:233
  93.0 0.5 collective-permute-start.31
  93.5 1.6 %collective-permute-start.30 = (bf16[32,4096]{1,0:T(8,128)(2,1)S(1)}, bf16[32,4096]{1,0:T(8,128)(2,1)S(1)}, u32[]{:S(2)}, u32[]{:S(2)}) collective-permute-start(bf16[32,4096]{1,0:T(8,128)(2,1)S(1)} %get-tuple-element.98.refs_2_), channel_id=1, source_target_pairs={{2,0},{4,2},{6,4},{7,6},{5,7},{3,5},{1,3},{0,1},{10,8},{12,10},{14... | collective-permute-start | bytes 786440 | tf_op jit(solution)/shard_map/left/ppermute | solution.py:237
  95.1 3.4 %collective-permute-done.33.refs_1_ = bf16[32,4096]{1,0:T(8,128)(2,1)S(1)} collective-permute-done((bf16[32,4096]{1,0:T(8,128)(2,1)S(1)}, bf16[32,4096]{1,0:T(8,128)(2,1)S(1)}, u32[]{:S(2)}, u32[]{:S(2)}) %collective-permute-start.33) | collective-permute-done | bytes 262176 | tf_op jit(solution)/shard_map/right/ppermute | solution.py:233
  98.6 4.5 %collective-permute-done.31.refs_1_ = bf16[32,4096]{1,0:T(8,128)(2,1)S(1)} collective-permute-done((bf16[32,4096]{1,0:T(8,128)(2,1)S(1)}, bf16[32,4096]{1,0:T(8,128)(2,1)S(1)}, u32[]{:S(2)}, u32[]{:S(2)}) %collective-permute-start.31) | collective-permute-done | bytes 262176 | tf_op jit(solution)/shard_map/right/ppermute | solution.py:233
  103.2 0.8 pad_maximum_fusion
  (56 shorter events, 4.2 us)
Async XLA Ops:
  1.1 12.1 %collective-permute-start.1 = (bf16[32,4096]{1,0:T(8,128)(2,1)S(1)}, bf16[32,4096]{1,0:T(8,128)(2,1)S(1)}, u32[]{:S(2)}, u32[]{:S(2)}) collective-permute-start(bf16[32,4096]{1,0:T(8,128)(2,1)S(1)} %get-tuple-element.107.refs_1_), channel_id=1, source_target_pairs={{2,0},{4,2},{6,4},{7,6},{5,7},{3,5},{1,3},{0,1},{10,8},{12,10},{14... | collective-permute-start | bytes 786440 | tf_op jit(solution)/shard_map/farL1/ppermute | solution.py:237
  4.1 9.2 %collective-permute-start = (bf16[32,4096]{1,0:T(8,128)(2,1)S(1)}, bf16[32,4096]{1,0:T(8,128)(2,1)S(1)}, u32[]{:S(2)}, u32[]{:S(2)}) collective-permute-start(bf16[32,4096]{1,0:T(8,128)(2,1)S(1)} %get-tuple-element.108.refs_0_), channel_id=1, source_target_pairs={{0,2},{2,4},{4,6},{6,7},{7,5},{5,3},{3,1},{1,0},{8,10},{10,12},{12... | collective-permute-start | bytes 786440 | tf_op jit(solution)/shard_map/farR1/ppermute | solution.py:233
  4.2 14.4 %collective-permute-start.2 = (bf16[32,4096]{1,0:T(8,128)(2,1)S(1)}, bf16[32,4096]{1,0:T(8,128)(2,1)S(1)}, u32[]{:S(2)}, u32[]{:S(2)}) collective-permute-start(bf16[32,4096]{1,0:T(8,128)(2,1)S(1)} %get-tuple-element.107.refs_1_), channel_id=1, source_target_pairs={{0,2},{2,4},{4,6},{6,7},{7,5},{5,3},{3,1},{1,0},{8,10},{10,12},{12... | collective-permute-start | bytes 786440 | tf_op jit(solution)/shard_map/nearR1/ppermute | solution.py:233
  6.2 12.5 %collective-permute-start.3 = (bf16[32,4096]{1,0:T(8,128)(2,1)S(1)}, bf16[32,4096]{1,0:T(8,128)(2,1)S(1)}, u32[]{:S(2)}, u32[]{:S(2)}) collective-permute-start(bf16[32,4096]{1,0:T(8,128)(2,1)S(1)} %get-tuple-element.108.refs_0_), channel_id=1, source_target_pairs={{2,0},{4,2},{6,4},{7,6},{5,7},{3,5},{1,3},{0,1},{10,8},{12,10},{14... | collective-permute-start | bytes 786440 | tf_op jit(solution)/shard_map/nearL1/ppermute | solution.py:237
  13.3 13.3 %collective-permute-start.5 = (bf16[32,4096]{1,0:T(8,128)(2,1)S(1)}, bf16[32,4096]{1,0:T(8,128)(2,1)S(1)}, u32[]{:S(2)}, u32[]{:S(2)}) collective-permute-start(bf16[32,4096]{1,0:T(8,128)(2,1)S(1)} %get-tuple-element.51.refs_3_), channel_id=1, source_target_pairs={{2,0},{4,2},{6,4},{7,6},{5,7},{3,5},{1,3},{0,1},{10,8},{12,10},{14... | collective-permute-start | bytes 786440 | tf_op jit(solution)/shard_map/farL2/ppermute | solution.py:237
  15.2 11.4 %collective-permute-start.4 = (bf16[32,4096]{1,0:T(8,128)(2,1)S(1)}, bf16[32,4096]{1,0:T(8,128)(2,1)S(1)}, u32[]{:S(2)}, u32[]{:S(2)}) collective-permute-start(bf16[32,4096]{1,0:T(8,128)(2,1)S(1)} %get-tuple-element.50.refs_2_), channel_id=1, source_target_pairs={{0,2},{2,4},{4,6},{6,7},{7,5},{5,3},{3,1},{1,0},{8,10},{10,12},{12... | collective-permute-start | bytes 786440 | tf_op jit(solution)/shard_map/farR2/ppermute | solution.py:233
  18.6 13.5 %collective-permute-start.8 = (bf16[32,4096]{1,0:T(8,128)(2,1)S(1)}, bf16[32,4096]{1,0:T(8,128)(2,1)S(1)}, u32[]{:S(2)}, u32[]{:S(2)}) collective-permute-start(bf16[32,4096]{1,0:T(8,128)(2,1)S(1)} %get-tuple-element.52.refs_4_.refs_10_), channel_id=1, source_target_pairs={{0,2},{2,4},{4,6},{6,7},{7,5},{5,3},{3,1},{1,0},{8,10},{10,12},{12... | collective-permute-start | bytes 786440 | tf_op jit(solution)/shard_map/nearR2/ppermute | solution.py:233
  19.0 13.1 %collective-permute-start.9 = (bf16[32,4096]{1,0:T(8,128)(2,1)S(1)}, bf16[32,4096]{1,0:T(8,128)(2,1)S(1)}, u32[]{:S(2)}, u32[]{:S(2)}) collective-permute-start(bf16[32,4096]{1,0:T(8,128)(2,1)S(1)} %get-tuple-element.53.refs_5_), channel_id=1, source_target_pairs={{2,0},{4,2},{6,4},{7,6},{5,7},{3,5},{1,3},{0,1},{10,8},{12,10},{14... | collective-permute-start | bytes 786440 | tf_op jit(solution)/shard_map/nearL2/ppermute | solution.py:237
  26.7 8.3 %collective-permute-start.7 = (bf16[32,4096]{1,0:T(8,128)(2,1)S(1)}, bf16[32,4096]{1,0:T(8,128)(2,1)S(1)}, u32[]{:S(2)}, u32[]{:S(2)}) collective-permute-start(bf16[32,4096]{1,0:T(8,128)(2,1)S(1)} %get-tuple-element.58.refs_1_), channel_id=1, source_target_pairs={{2,0},{4,2},{6,4},{7,6},{5,7},{3,5},{1,3},{0,1},{10,8},{12,10},{14... | collective-permute-start | bytes 786440 | tf_op jit(solution)/shard_map/farL3/ppermute | solution.py:237
  28.3 8.6 %collective-permute-start.6 = (bf16[32,4096]{1,0:T(8,128)(2,1)S(1)}, bf16[32,4096]{1,0:T(8,128)(2,1)S(1)}, u32[]{:S(2)}, u32[]{:S(2)}) collective-permute-start(bf16[32,4096]{1,0:T(8,128)(2,1)S(1)} %get-tuple-element.57.refs_8_.refs_0_), channel_id=1, source_target_pairs={{0,2},{2,4},{4,6},{6,7},{7,5},{5,3},{3,1},{1,0},{8,10},{10,12},{12... | collective-permute-start | bytes 786440 | tf_op jit(solution)/shard_map/farR3/ppermute | solution.py:233
  32.2 13.4 %collective-permute-start.13 = (bf16[32,4096]{1,0:T(8,128)(2,1)S(1)}, bf16[32,4096]{1,0:T(8,128)(2,1)S(1)}, u32[]{:S(2)}, u32[]{:S(2)}) collective-permute-start(bf16[32,4096]{1,0:T(8,128)(2,1)S(1)} %get-tuple-element.62.refs_3_), channel_id=1, source_target_pairs={{2,0},{4,2},{6,4},{7,6},{5,7},{3,5},{1,3},{0,1},{10,8},{12,10},{14... | collective-permute-start | bytes 786440 | tf_op jit(solution)/shard_map/nearL3/ppermute | solution.py:237
  33.8 11.8 %collective-permute-start.12 = (bf16[32,4096]{1,0:T(8,128)(2,1)S(1)}, bf16[32,4096]{1,0:T(8,128)(2,1)S(1)}, u32[]{:S(2)}, u32[]{:S(2)}) collective-permute-start(bf16[32,4096]{1,0:T(8,128)(2,1)S(1)} %get-tuple-element.59.refs_2_), channel_id=1, source_target_pairs={{0,2},{2,4},{4,6},{6,7},{7,5},{5,3},{3,1},{1,0},{8,10},{10,12},{12... | collective-permute-start | bytes 786440 | tf_op jit(solution)/shard_map/nearR3/ppermute | solution.py:233
  36.9 9.0 %collective-permute-start.10 = (bf16[32,4096]{1,0:T(8,128)(2,1)S(1)}, bf16[32,4096]{1,0:T(8,128)(2,1)S(1)}, u32[]{:S(2)}, u32[]{:S(2)}) collective-permute-start(bf16[32,4096]{1,0:T(8,128)(2,1)S(1)} %get-tuple-element.60.refs_4_.refs_10_), channel_id=1, source_target_pairs={{0,2},{2,4},{4,6},{6,7},{7,5},{5,3},{3,1},{1,0},{8,10},{10,12},{12... | collective-permute-start | bytes 786440 | tf_op jit(solution)/shard_map/farR4/ppermute | solution.py:233
  37.3 8.6 %collective-permute-start.11 = (bf16[32,4096]{1,0:T(8,128)(2,1)S(1)}, bf16[32,4096]{1,0:T(8,128)(2,1)S(1)}, u32[]{:S(2)}, u32[]{:S(2)}) collective-permute-start(bf16[32,4096]{1,0:T(8,128)(2,1)S(1)} %get-tuple-element.61.refs_5_), channel_id=1, source_target_pairs={{2,0},{4,2},{6,4},{7,6},{5,7},{3,5},{1,3},{0,1},{10,8},{12,10},{14... | collective-permute-start | bytes 786440 | tf_op jit(solution)/shard_map/farL4/ppermute | solution.py:237
  48.8 5.4 %collective-permute-start.16 = (f32[2,192,1024]{2,1,0:T(8,128)S(1)}, f32[2,192,1024]{2,1,0:T(8,128)S(1)}, u32[]{:S(2)}, u32[]{:S(2)}) collective-permute-start(f32[2,192,1024]{2,1,0:T(8,128)S(1)} %get-tuple-element.75), channel_id=1, source_target_pairs={{0,8},{8,0},{1,9},{9,1},{2,10},{10,2},{3,11},{11,3},{4,12},{12,4},... | collective-permute-start | bytes 4718600 | tf_op jit(solution)/shard_map/swap/ppermute | solution.py:241
  48.9 4.9 %collective-permute-start.18 = (f32[2,128,1024]{2,1,0:T(8,128)S(1)}, f32[2,128,1024]{2,1,0:T(8,128)S(1)}, u32[]{:S(2)}, u32[]{:S(2)}) collective-permute-start(f32[2,128,1024]{2,1,0:T(8,128)S(1)} %get-tuple-element.70.refs_2_.refs_7_), channel_id=1, source_target_pairs={{0,8},{8,0},{1,9},{9,1},{2,10},{10,2},{3,11},{11,3},{4,12},{12,4},... | collective-permute-start | bytes 3145736 | tf_op jit(solution)/shard_map/swap/ppermute | solution.py:241
  49.4 13.9 %collective-permute-start.14 = (f32[2,192,1024]{2,1,0:T(8,128)S(1)}, f32[2,192,1024]{2,1,0:T(8,128)S(1)}, u32[]{:S(2)}, u32[]{:S(2)}) collective-permute-start(f32[2,192,1024]{2,1,0:T(8,128)S(1)} %get-tuple-element.71), channel_id=1, source_target_pairs={{0,8},{8,0},{1,9},{9,1},{2,10},{10,2},{3,11},{11,3},{4,12},{12,4},... | collective-permute-start | bytes 4718600 | tf_op jit(solution)/shard_map/swap/ppermute | solution.py:241
  54.0 2.4 %collective-permute-start.19 = (bf16[128,1024]{1,0:T(8,128)(2,1)S(1)}, bf16[128,1024]{1,0:T(8,128)(2,1)S(1)}, u32[]{:S(2)}, u32[]{:S(2)}) collective-permute-start(bf16[128,1024]{1,0:T(8,128)(2,1)S(1)} %gated.5.refs_0_), channel_id=1, source_target_pairs={{0,8},{8,0},{1,9},{9,1},{2,10},{10,2},{3,11},{11,3},{4,12},{12,4},... | collective-permute-start | bytes 786440 | tf_op jit(solution)/shard_map/swap/ppermute | solution.py:241
  54.5 9.5 %collective-permute-start.17 = (bf16[192,1024]{1,0:T(8,128)(2,1)S(1)}, bf16[192,1024]{1,0:T(8,128)(2,1)S(1)}, u32[]{:S(2)}, u32[]{:S(2)}) collective-permute-start(bf16[192,1024]{1,0:T(8,128)(2,1)S(1)} %gated.4.refs_0_), channel_id=1, source_target_pairs={{0,8},{8,0},{1,9},{9,1},{2,10},{10,2},{3,11},{11,3},{4,12},{12,4},... | collective-permute-start | bytes 1179656 | tf_op jit(solution)/shard_map/swap/ppermute | solution.py:241
  59.6 9.2 %collective-permute-start.22 = (bf16[32,4096]{1,0:T(8,128)(2,1)S(1)}, bf16[32,4096]{1,0:T(8,128)(2,1)S(1)}, u32[]{:S(2)}, u32[]{:S(2)}) collective-permute-start(bf16[32,4096]{1,0:T(8,128)(2,1)S(1)} %get-tuple-element.79), channel_id=1, source_target_pairs={{2,0},{4,2},{6,4},{7,6},{5,7},{3,5},{1,3},{0,1},{10,8},{12,10},{14... | collective-permute-start | bytes 786440 | tf_op jit(solution)/shard_map/left/ppermute | solution.py:237
  61.3 9.2 %collective-permute-start.23 = (bf16[32,4096]{1,0:T(8,128)(2,1)S(1)}, bf16[32,4096]{1,0:T(8,128)(2,1)S(1)}, u32[]{:S(2)}, u32[]{:S(2)}) collective-permute-start(bf16[32,4096]{1,0:T(8,128)(2,1)S(1)} %get-tuple-element.80), channel_id=1, source_target_pairs={{0,2},{2,4},{4,6},{6,7},{7,5},{5,3},{3,1},{1,0},{8,10},{10,12},{12... | collective-permute-start | bytes 786440 | tf_op jit(solution)/shard_map/right/ppermute | solution.py:233
  61.7 12.7 %collective-permute-start.20 = (bf16[32,4096]{1,0:T(8,128)(2,1)S(1)}, bf16[32,4096]{1,0:T(8,128)(2,1)S(1)}, u32[]{:S(2)}, u32[]{:S(2)}) collective-permute-start(bf16[32,4096]{1,0:T(8,128)(2,1)S(1)} %get-tuple-element.77), channel_id=1, source_target_pairs={{2,0},{4,2},{6,4},{7,6},{5,7},{3,5},{1,3},{0,1},{10,8},{12,10},{14... | collective-permute-start | bytes 786440 | tf_op jit(solution)/shard_map/left/ppermute | solution.py:237
  63.3 12.8 %collective-permute-start.21 = (bf16[32,4096]{1,0:T(8,128)(2,1)S(1)}, bf16[32,4096]{1,0:T(8,128)(2,1)S(1)}, u32[]{:S(2)}, u32[]{:S(2)}) collective-permute-start(bf16[32,4096]{1,0:T(8,128)(2,1)S(1)} %get-tuple-element.78), channel_id=1, source_target_pairs={{0,2},{2,4},{4,6},{6,7},{7,5},{5,3},{3,1},{1,0},{8,10},{10,12},{12... | collective-permute-start | bytes 786440 | tf_op jit(solution)/shard_map/right/ppermute | solution.py:233
  64.1 14.2 %collective-permute-start.15 = (bf16[192,1024]{1,0:T(8,128)(2,1)S(1)}, bf16[192,1024]{1,0:T(8,128)(2,1)S(1)}, u32[]{:S(2)}, u32[]{:S(2)}) collective-permute-start(bf16[192,1024]{1,0:T(8,128)(2,1)S(1)} %gated.3.refs_0_), channel_id=1, source_target_pairs={{0,8},{8,0},{1,9},{9,1},{2,10},{10,2},{3,11},{11,3},{4,12},{12,4},... | collective-permute-start | bytes 1179656 | tf_op jit(solution)/shard_map/swap/ppermute | solution.py:241
  70.6 12.1 %collective-permute-start.25 = (bf16[32,4096]{1,0:T(8,128)(2,1)S(1)}, bf16[32,4096]{1,0:T(8,128)(2,1)S(1)}, u32[]{:S(2)}, u32[]{:S(2)}) collective-permute-start(bf16[32,4096]{1,0:T(8,128)(2,1)S(1)} %get-tuple-element.105.refs_3_), channel_id=1, source_target_pairs={{0,2},{2,4},{4,6},{6,7},{7,5},{5,3},{3,1},{1,0},{8,10},{10,12},{12... | collective-permute-start | bytes 786440 | tf_op jit(solution)/shard_map/right/ppermute | solution.py:233
  71.1 11.6 %collective-permute-start.24 = (bf16[32,4096]{1,0:T(8,128)(2,1)S(1)}, bf16[32,4096]{1,0:T(8,128)(2,1)S(1)}, u32[]{:S(2)}, u32[]{:S(2)}) collective-permute-start(bf16[32,4096]{1,0:T(8,128)(2,1)S(1)} %get-tuple-element.106.refs_2_), channel_id=1, source_target_pairs={{2,0},{4,2},{6,4},{7,6},{5,7},{3,5},{1,3},{0,1},{10,8},{12,10},{14... | collective-permute-start | bytes 786440 | tf_op jit(solution)/shard_map/left/ppermute | solution.py:237
  76.2 11.1 %collective-permute-start.29 = (bf16[32,4096]{1,0:T(8,128)(2,1)S(1)}, bf16[32,4096]{1,0:T(8,128)(2,1)S(1)}, u32[]{:S(2)}, u32[]{:S(2)}) collective-permute-start(bf16[32,4096]{1,0:T(8,128)(2,1)S(1)} %get-tuple-element.103.refs_6_), channel_id=1, source_target_pairs={{0,2},{2,4},{4,6},{6,7},{7,5},{5,3},{3,1},{1,0},{8,10},{10,12},{12... | collective-permute-start | bytes 786440 | tf_op jit(solution)/shard_map/right/ppermute | solution.py:233
  76.7 10.6 %collective-permute-start.28 = (bf16[32,4096]{1,0:T(8,128)(2,1)S(1)}, bf16[32,4096]{1,0:T(8,128)(2,1)S(1)}, u32[]{:S(2)}, u32[]{:S(2)}) collective-permute-start(bf16[32,4096]{1,0:T(8,128)(2,1)S(1)} %get-tuple-element.104.refs_5_), channel_id=1, source_target_pairs={{2,0},{4,2},{6,4},{7,6},{5,7},{3,5},{1,3},{0,1},{10,8},{12,10},{14... | collective-permute-start | bytes 786440 | tf_op jit(solution)/shard_map/left/ppermute | solution.py:237
  82.8 10.2 %collective-permute-start.27 = (bf16[32,4096]{1,0:T(8,128)(2,1)S(1)}, bf16[32,4096]{1,0:T(8,128)(2,1)S(1)}, u32[]{:S(2)}, u32[]{:S(2)}) collective-permute-start(bf16[32,4096]{1,0:T(8,128)(2,1)S(1)} %get-tuple-element.101.refs_3_), channel_id=1, source_target_pairs={{0,2},{2,4},{4,6},{6,7},{7,5},{5,3},{3,1},{1,0},{8,10},{10,12},{12... | collective-permute-start | bytes 786440 | tf_op jit(solution)/shard_map/right/ppermute | solution.py:233
  83.3 9.7 %collective-permute-start.26 = (bf16[32,4096]{1,0:T(8,128)(2,1)S(1)}, bf16[32,4096]{1,0:T(8,128)(2,1)S(1)}, u32[]{:S(2)}, u32[]{:S(2)}) collective-permute-start(bf16[32,4096]{1,0:T(8,128)(2,1)S(1)} %get-tuple-element.102.refs_2_), channel_id=1, source_target_pairs={{2,0},{4,2},{6,4},{7,6},{5,7},{3,5},{1,3},{0,1},{10,8},{12,10},{14... | collective-permute-start | bytes 786440 | tf_op jit(solution)/shard_map/left/ppermute | solution.py:237
  87.4 11.1 %collective-permute-start.33 = (bf16[32,4096]{1,0:T(8,128)(2,1)S(1)}, bf16[32,4096]{1,0:T(8,128)(2,1)S(1)}, u32[]{:S(2)}, u32[]{:S(2)}) collective-permute-start(bf16[32,4096]{1,0:T(8,128)(2,1)S(1)} %get-tuple-element.99.refs_3_), channel_id=1, source_target_pairs={{0,2},{2,4},{4,6},{6,7},{7,5},{5,3},{3,1},{1,0},{8,10},{10,12},{12... | collective-permute-start | bytes 786440 | tf_op jit(solution)/shard_map/right/ppermute | solution.py:233
  87.9 10.6 %collective-permute-start.32 = (bf16[32,4096]{1,0:T(8,128)(2,1)S(1)}, bf16[32,4096]{1,0:T(8,128)(2,1)S(1)}, u32[]{:S(2)}, u32[]{:S(2)}) collective-permute-start(bf16[32,4096]{1,0:T(8,128)(2,1)S(1)} %get-tuple-element.100.refs_2_), channel_id=1, source_target_pairs={{2,0},{4,2},{6,4},{7,6},{5,7},{3,5},{1,3},{0,1},{10,8},{12,10},{14... | collective-permute-start | bytes 786440 | tf_op jit(solution)/shard_map/left/ppermute | solution.py:237
  93.0 10.0 %collective-permute-start.31 = (bf16[32,4096]{1,0:T(8,128)(2,1)S(1)}, bf16[32,4096]{1,0:T(8,128)(2,1)S(1)}, u32[]{:S(2)}, u32[]{:S(2)}) collective-permute-start(bf16[32,4096]{1,0:T(8,128)(2,1)S(1)} %get-tuple-element.97.refs_3_), channel_id=1, source_target_pairs={{0,2},{2,4},{4,6},{6,7},{7,5},{5,3},{3,1},{1,0},{8,10},{10,12},{12... | collective-permute-start | bytes 786440 | tf_op jit(solution)/shard_map/right/ppermute | solution.py:233
  93.5 9.5 %collective-permute-start.30 = (bf16[32,4096]{1,0:T(8,128)(2,1)S(1)}, bf16[32,4096]{1,0:T(8,128)(2,1)S(1)}, u32[]{:S(2)}, u32[]{:S(2)}) collective-permute-start(bf16[32,4096]{1,0:T(8,128)(2,1)S(1)} %get-tuple-element.98.refs_2_), channel_id=1, source_target_pairs={{2,0},{4,2},{6,4},{7,6},{5,7},{3,5},{1,3},{0,1},{10,8},{12,10},{14... | collective-permute-start | bytes 786440 | tf_op jit(solution)/shard_map/left/ppermute | solution.py:237
